TPU v7x, 32 devices: a whole 2x2x4 slice. The times are simulated.
32 devices in a mesh: dp: 4 (over y, core), fsdp: 8 (over z, x).
Axes of the slice: x: 2, y: 2, z: 4, core: 2. Of those that a mesh axis runs over, the one named last changes fastest.
Arguments:
- hidden: bfloat16 [4096, 2048], P(('dp', 'fsdp')), may hold values from -6 to 6
- source: bfloat16 [4096, 2048], P(('dp', 'fsdp')), may hold values from -6 to 6
- cotangent: bfloat16 [4096, 2048], P(('dp', 'fsdp')), may hold values from -6 to 6
- row_counts: int32 [4, 8], P('dp'), may hold values from 96 to 128, as said below
- seq_lengths: int32 [4, 3], P('dp'), may hold values from 1 to 990, as said below
- kv_gain: bfloat16 [2048], P(('dp', 'fsdp')), may hold values from 0.25 to 1.75
- w_key: bfloat16 [2048, 2048], P(('dp', 'fsdp')), may hold values from -0.125 to 0.125
- w_value: bfloat16 [2048, 2048], P(('dp', 'fsdp')), may hold values from -0.125 to 0.125
- attn_gain: bfloat16 [2048], P(('dp', 'fsdp')), may hold values from 0.25 to 1.75
- w_query: bfloat16 [2048, 2048], P(('dp', 'fsdp')), may hold values from -0.125 to 0.125
- w_out: bfloat16 [2048, 2048], P(('dp', 'fsdp')), may hold values from -0.75 to 0.75
- ffn_gain: bfloat16 [2048], P(('dp', 'fsdp')), may hold values from 0.25 to 1.75
- w_gate: bfloat16 [5504, 2048], P(('dp', 'fsdp')), may hold values from -0.125 to 0.125
- w_up: bfloat16 [5504, 2048], P(('dp', 'fsdp')), may hold values from -0.125 to 0.125
- w_down: bfloat16 [5504, 2048], P(('dp', 'fsdp')), may hold values from -0.078125 to 0.078125
Outputs:
- output: bfloat16 [4096, 2048], P(('dp', 'fsdp'))
- grad_hidden: bfloat16 [4096, 2048], P(('dp', 'fsdp'))
- grad_source: bfloat16 [4096, 2048], P(('dp', 'fsdp'))
- grad_kv_gain: float32 [2048], P(('dp', 'fsdp'))
- grad_key: float32 [2048, 2048], P(('dp', 'fsdp'))
- grad_value: float32 [2048, 2048], P(('dp', 'fsdp'))
- grad_attn_gain: float32 [2048], P(('dp', 'fsdp'))
- grad_query: float32 [2048, 2048], P(('dp', 'fsdp'))
- grad_out: float32 [2048, 2048], P(('dp', 'fsdp'))
- grad_ffn_gain: float32 [2048], P(('dp', 'fsdp'))
- grad_gate: float32 [5504, 2048], P(('dp', 'fsdp'))
- grad_up: float32 [5504, 2048], P(('dp', 'fsdp'))
- grad_down: float32 [5504, 2048], P(('dp', 'fsdp'))
Inputs may be any that keep to these rules, and one draw needn't show every extreme that they name: `row_counts`: each device's live rows are its first ones, and a group's live rows follow one another device by device; in every group some device has 128 live rows. `seq_lengths`: the 3 sequences of a group are packed in order into its live rows; their lengths add up to the sum of the group's row_counts.
All inputs are finite; a program needn't handle non-finite values.
Results may differ from a plain program's by a relative error of at most 0.017.
Values may be sent and summed in bfloat16 or wider, within the bound.
No kernel may reach another device: no remote copies, remote signals or barrier semaphores. Data moves between devices by JAX's collectives and lax.ppermute only.
A program may use at most 704 MiB of HBM per device.

v0:
```python
import math

import jax
import jax.numpy as jnp
from jax import lax
from jax.sharding import PartitionSpec as P

HEADS = 16


EPSILON = 1e-06
MASKED = -1000000000.0


def product(left, right):
    return jnp.dot(left, right, preferred_element_type=jnp.float32)


def rows_by_rows(left, right):
    return lax.dot_general(
        left, right, (((1,), (1,)), ((), ())), preferred_element_type=jnp.float32
    )


def columns_by_columns(left, right):
    return lax.dot_general(
        left, right, (((0,), (0,)), ((), ())), preferred_element_type=jnp.float32
    )


def inverse_scale(values):
    return lax.rsqrt(jnp.mean(values * values, axis=-1, keepdims=True) + EPSILON)


def norm_backward(values, scale, gain, d_normed):
    weighted = d_normed * gain
    return scale * weighted - values * scale**3 * jnp.mean(
        values * weighted, axis=-1, keepdims=True
    )


def slot_layout(row_counts, seq_lengths, slots, per_device):
    counts = row_counts[0]
    offsets = jnp.cumsum(counts) - counts
    device_of = slots // per_device
    within = slots - device_of * per_device
    picker = device_of[:, None] == jnp.arange(counts.shape[0], dtype=jnp.int32)[None, :]
    count_here = jnp.sum(jnp.where(picker, counts[None, :], 0), axis=1)
    offset_here = jnp.sum(jnp.where(picker, offsets[None, :], 0), axis=1)
    position = offset_here + within
    ends = jnp.cumsum(seq_lengths[0])
    sequence = jnp.sum((ends[None, :] <= position[:, None]).astype(jnp.int32), axis=1)
    return (within < count_here, position, sequence)


def body(
    hidden,
    source,
    cotangent,
    row_counts,
    seq_lengths,
    kv_gain,
    w_key,
    w_value,
    attn_gain,
    w_query,
    w_out,
    ffn_gain,
    w_gate,
    w_up,
    w_down,
):
    local_rows, model_width = hidden.shape
    group_rows = local_rows * lax.axis_size("fsdp")
    head_size = model_width // HEADS
    factor = 1.0 / math.sqrt(head_size)
    block_rows = math.gcd(group_rows, 512)
    block_count = group_rows // block_rows
    own_slots = lax.axis_index("fsdp") * local_rows + jnp.arange(local_rows, dtype=jnp.int32)
    query_live, query_position, query_sequence = slot_layout(
        row_counts, seq_lengths, own_slots, local_rows
    )
    key_live, key_position, key_sequence = slot_layout(
        row_counts, seq_lengths, jnp.arange(group_rows, dtype=jnp.int32), local_rows
    )
    live_column = query_live.astype(jnp.float32)[:, None]
    source_f = source.astype(jnp.float32)
    hidden_f = hidden.astype(jnp.float32)
    source_scale = inverse_scale(source_f)
    hidden_scale = inverse_scale(hidden_f)
    source_unit = source_f * source_scale
    hidden_unit = hidden_f * hidden_scale
    piece_kv_gain = lax.all_gather(kv_gain, ("dp", "fsdp"), axis=0, tiled=True)
    piece_key = lax.all_gather(w_key, ("dp", "fsdp"), axis=0, tiled=True)
    piece_value = lax.all_gather(w_value, ("dp", "fsdp"), axis=0, tiled=True)
    piece_attn_gain = lax.all_gather(attn_gain, ("dp", "fsdp"), axis=0, tiled=True)
    piece_query = lax.all_gather(w_query, ("dp", "fsdp"), axis=0, tiled=True)
    piece_ffn_gain = lax.all_gather(ffn_gain, ("dp", "fsdp"), axis=0, tiled=True)
    source_cols = (source_unit * piece_kv_gain.astype(jnp.float32)[None, :]).astype(jnp.bfloat16)
    hidden_cols = (hidden_unit * piece_attn_gain.astype(jnp.float32)[None, :]).astype(jnp.bfloat16)
    key_sum = product(source_cols, piece_key)
    value_sum = product(source_cols, piece_value)
    query_sum = product(hidden_cols, piece_query)
    stacked = jnp.stack([piece_kv_gain, piece_attn_gain, piece_ffn_gain]).astype(jnp.float32)
    gains = stacked
    key_sum, value_sum, query_sum, gains = (key_sum, value_sum, query_sum, gains)
    kv_gain_full, attn_gain_full, ffn_gain_full = (gains[0], gains[1], gains[2])
    keys_low = key_sum.astype(jnp.bfloat16)
    values_low = value_sum.astype(jnp.bfloat16)
    queries_low = query_sum.astype(jnp.bfloat16)
    group_keys, group_values = (
        lax.all_gather(keys_low, "fsdp", axis=0, tiled=True),
        lax.all_gather(values_low, "fsdp", axis=0, tiled=True),
    )
    blocks = (
        group_keys.reshape(block_count, block_rows, HEADS, head_size),
        group_values.reshape(block_count, block_rows, HEADS, head_size),
        key_live.reshape(block_count, block_rows),
        key_position.reshape(block_count, block_rows),
        key_sequence.reshape(block_count, block_rows),
    )
    query_heads = queries_low.reshape(local_rows, HEADS, head_size)

    def block_scores(key_block, live_block, position_block, sequence_block):
        scores = (
            jnp.einsum("qhd,khd->hqk", query_heads, key_block, preferred_element_type=jnp.float32)
            * factor
        )
        allowed = (
            live_block[None, :]
            & (sequence_block[None, :] == query_sequence[:, None])
            & (position_block[None, :] <= query_position[:, None])
        )
        return jnp.where(allowed[None], scores, MASKED)

    def running_total(running, key_block_set):
        largest, summed = running
        key_block, value_block, live_block, position_block, sequence_block = key_block_set
        masked = block_scores(key_block, live_block, position_block, sequence_block)
        new_largest = jnp.maximum(largest, jnp.max(masked, axis=-1))
        summed = summed * jnp.exp(largest - new_largest) + jnp.sum(
            jnp.exp(masked - new_largest[:, :, None]), axis=-1
        )
        return ((new_largest, summed), None)

    (largest, summed), unused = lax.scan(
        running_total,
        (
            jnp.full((HEADS, local_rows), MASKED, jnp.float32),
            jnp.zeros((HEADS, local_rows), jnp.float32),
        ),
        blocks,
    )
    log_total = largest + jnp.log(summed)

    def weighted_sum(running, key_block_set):
        key_block, value_block, live_block, position_block, sequence_block = key_block_set
        probs_low = jnp.exp(
            block_scores(key_block, live_block, position_block, sequence_block)
            - log_total[:, :, None]
        ).astype(jnp.bfloat16)
        return (
            running
            + jnp.einsum(
                "hqk,khd->qhd", probs_low, value_block, preferred_element_type=jnp.float32
            ),
            None,
        )

    attended_f, unused = lax.scan(
        weighted_sum, jnp.zeros((local_rows, HEADS, head_size), jnp.float32), blocks
    )
    attended_low = attended_f.reshape(local_rows, model_width).astype(jnp.bfloat16)
    branch = product(attended_low, lax.all_gather(w_out, ("dp", "fsdp"), axis=0, tiled=True))
    middle = hidden_f + branch
    middle_scale = inverse_scale(middle)
    middle_unit = middle * middle_scale
    middle_low = (middle_unit * ffn_gain_full).astype(jnp.bfloat16)
    piece_gate = lax.all_gather(w_gate, ("dp", "fsdp"), axis=0, tiled=True)
    piece_up = lax.all_gather(w_up, ("dp", "fsdp"), axis=0, tiled=True)
    piece_down = lax.all_gather(w_down, ("dp", "fsdp"), axis=0, tiled=True)
    gate_value = rows_by_rows(middle_low, piece_gate)
    up_value = rows_by_rows(middle_low, piece_up)
    inner = (jax.nn.silu(gate_value) * up_value).astype(jnp.bfloat16)
    ffn_result = product(inner, piece_down)
    output = ((middle + ffn_result) * live_column).astype(jnp.bfloat16)
    d_out = cotangent.astype(jnp.float32) * live_column
    d_out_low = d_out.astype(jnp.bfloat16)
    piece_gate = lax.all_gather(w_gate, ("dp", "fsdp"), axis=0, tiled=True)
    piece_up = lax.all_gather(w_up, ("dp", "fsdp"), axis=0, tiled=True)
    piece_down = lax.all_gather(w_down, ("dp", "fsdp"), axis=0, tiled=True)
    gate_value = rows_by_rows(middle_low, piece_gate)
    up_value = rows_by_rows(middle_low, piece_up)
    sigmoid_gate = jax.nn.sigmoid(gate_value)
    swished = gate_value * sigmoid_gate
    inner = (swished * up_value).astype(jnp.bfloat16)
    d_inner = rows_by_rows(d_out_low, piece_down)
    d_gate = (d_inner * up_value * sigmoid_gate * (1.0 + gate_value * (1.0 - sigmoid_gate))).astype(
        jnp.bfloat16
    )
    d_up = (d_inner * swished).astype(jnp.bfloat16)
    d_normed = product(d_gate, piece_gate) + product(d_up, piece_up)
    ffn_grads = lax.psum_scatter(
        jnp.stack(
            [
                columns_by_columns(d_gate, middle_low),
                columns_by_columns(d_up, middle_low),
                columns_by_columns(inner, d_out_low),
            ],
            axis=1,
        ),
        ("dp", "fsdp"),
        scatter_dimension=0,
        tiled=True,
    )
    ffn_gain_part = jnp.sum(d_normed * middle_unit, axis=0)
    d_middle = d_out + norm_backward(middle, middle_scale, ffn_gain_full, d_normed)
    d_branch_low = d_middle.astype(jnp.bfloat16)
    d_attended = rows_by_rows(
        d_branch_low, lax.all_gather(w_out, ("dp", "fsdp"), axis=0, tiled=True)
    )
    d_heads = d_attended.astype(jnp.bfloat16).reshape(local_rows, HEADS, head_size)
    delta = jnp.sum(d_heads.astype(jnp.float32) * attended_f, axis=-1).T

    def attention_backward(d_query_sum, key_block_set):
        key_block, value_block, live_block, position_block, sequence_block = key_block_set
        probs = jnp.exp(
            block_scores(key_block, live_block, position_block, sequence_block)
            - log_total[:, :, None]
        )
        probs_low = probs.astype(jnp.bfloat16)
        d_values = jnp.einsum(
            "hqk,qhd->khd", probs_low, d_heads, preferred_element_type=jnp.float32
        )
        d_probs = jnp.einsum(
            "qhd,khd->hqk", d_heads, value_block, preferred_element_type=jnp.float32
        )
        d_scores = (probs * (d_probs - delta[:, :, None])).astype(jnp.bfloat16)
        d_query_sum = d_query_sum + jnp.einsum(
            "hqk,khd->qhd", d_scores, key_block, preferred_element_type=jnp.float32
        )
        d_keys = (
            jnp.einsum("hqk,qhd->khd", d_scores, query_heads, preferred_element_type=jnp.float32)
            * factor
        )
        return (d_query_sum, jnp.stack([d_keys, d_values], axis=1))

    d_query_sum, key_terms = lax.scan(
        attention_backward, jnp.zeros((local_rows, HEADS, head_size), jnp.float32), blocks
    )
    key_grads = lax.psum_scatter(
        key_terms.reshape(group_rows, 2, model_width).astype(jnp.bfloat16),
        "fsdp",
        scatter_dimension=0,
        tiled=True,
    ).astype(jnp.float32)
    d_keys_low = key_grads[:, 0].astype(jnp.bfloat16)
    d_values_low = key_grads[:, 1].astype(jnp.bfloat16)
    d_queries_low = (d_query_sum * factor).reshape(local_rows, model_width).astype(jnp.bfloat16)
    piece_query = lax.all_gather(w_query, ("dp", "fsdp"), axis=0, tiled=True)
    piece_key = lax.all_gather(w_key, ("dp", "fsdp"), axis=0, tiled=True)
    piece_value = lax.all_gather(w_value, ("dp", "fsdp"), axis=0, tiled=True)
    hidden_part = rows_by_rows(d_queries_low, piece_query)
    source_part = rows_by_rows(d_keys_low, piece_key) + rows_by_rows(d_values_low, piece_value)
    input_back = jnp.stack([hidden_part, source_part])
    grad_hidden = (
        d_middle + norm_backward(hidden_f, hidden_scale, attn_gain_full, input_back[0])
    ).astype(jnp.bfloat16)
    grad_source = norm_backward(source_f, source_scale, kv_gain_full, input_back[1]).astype(
        jnp.bfloat16
    )
    attn_gain_part = jnp.sum(input_back[0] * hidden_unit, axis=0)
    kv_gain_part = jnp.sum(input_back[1] * source_unit, axis=0)
    source_low = (source_unit * kv_gain_full).astype(jnp.bfloat16)
    hidden_low = (hidden_unit * attn_gain_full).astype(jnp.bfloat16)
    hidden_part = hidden_low
    source_part = source_low
    layer_stack = lax.psum_scatter(
        jnp.stack(
            [
                columns_by_columns(hidden_part, d_queries_low),
                columns_by_columns(source_part, d_keys_low),
                columns_by_columns(source_part, d_values_low),
                columns_by_columns(attended_low, d_branch_low),
            ],
            axis=1,
        ),
        ("dp", "fsdp"),
        scatter_dimension=0,
        tiled=True,
    )
    grad_query, grad_key, grad_value, grad_out = (
        layer_stack[:, 0],
        layer_stack[:, 1],
        layer_stack[:, 2],
        layer_stack[:, 3],
    )
    grad_kv_gain, grad_attn_gain, grad_ffn_gain = (
        lax.psum_scatter(kv_gain_part, ("dp", "fsdp"), scatter_dimension=0, tiled=True),
        lax.psum_scatter(attn_gain_part, ("dp", "fsdp"), scatter_dimension=0, tiled=True),
        lax.psum_scatter(ffn_gain_part, ("dp", "fsdp"), scatter_dimension=0, tiled=True),
    )
    return (
        output,
        grad_hidden,
        grad_source,
        grad_kv_gain,
        grad_key,
        grad_value,
        grad_attn_gain,
        grad_query,
        grad_out,
        grad_ffn_gain,
        ffn_grads[:, 0],
        ffn_grads[:, 1],
        ffn_grads[:, 2],
    )


def solution(mesh):
    in_specs = (
        P(("dp", "fsdp"), None),
        P(("dp", "fsdp"), None),
        P(("dp", "fsdp"), None),
        P("dp", None),
        P("dp", None),
        P(("dp", "fsdp")),
        P(("dp", "fsdp"), None),
        P(("dp", "fsdp"), None),
        P(("dp", "fsdp")),
        P(("dp", "fsdp"), None),
        P(("dp", "fsdp"), None),
        P(("dp", "fsdp")),
        P(("dp", "fsdp"), None),
        P(("dp", "fsdp"), None),
        P(("dp", "fsdp"), None),
    )
    out_specs = (
        P(("dp", "fsdp"), None),
        P(("dp", "fsdp"), None),
        P(("dp", "fsdp"), None),
        P(("dp", "fsdp")),
        P(("dp", "fsdp"), None),
        P(("dp", "fsdp"), None),
        P(("dp", "fsdp")),
        P(("dp", "fsdp"), None),
        P(("dp", "fsdp"), None),
        P(("dp", "fsdp")),
        P(("dp", "fsdp"), None),
        P(("dp", "fsdp"), None),
        P(("dp", "fsdp"), None),
    )
    return jax.shard_map(body, mesh=mesh, in_specs=in_specs, out_specs=out_specs, check_vma=False)
```

profile of v0, /device:TPU:0, one launch (start us, length us, event | category | flops | bytes accessed | tf_op | source)
XLA Modules:
  0.0 4497.0 jit_solution(2255536467648962452)
XLA Ops:
  12.0 42.7 all-reduce.8
  56.5 34.9 all-gather.13.cloned.1.call-done
  91.4 5.7 convolution_convert_fusion.3
  97.2 73.2 %all-gather.17.cloned.1.call-done = bf16[2048,2048]{1,0:T(8,128)(2,1)} async-done(((bf16[64,2048]{1,0:T(8,128)(2,1)}), bf16[2048,2048]{1,0:T(8,128)(2,1)}) %all-gather.17.cloned.1.call-update) | async-done | bytes 8388624 | tf_op jit(solution)/shard_map/all_gather | solution.py:94
  170.4 5.5 convolution_convert_fusion.2
  181.2 68.2 %all-gather.21.cloned.1.call-done = bf16[2048,2048]{1,0:T(8,128)(2,1)} async-done(((bf16[64,2048]{1,0:T(8,128)(2,1)}), bf16[2048,2048]{1,0:T(8,128)(2,1)}) %all-gather.21.cloned.1.call-update) | async-done | bytes 8388624 | tf_op jit(solution)/shard_map/all_gather | solution.py:97
  249.4 4.7 fusion.60
  254.3 69.7 %all-gather.15.cloned.1.call-done = bf16[1024,2048]{1,0:T(8,128)(2,1)} async-done(((bf16[128,2048]{1,0:T(8,128)(2,1)}), bf16[1024,2048]{1,0:T(8,128)(2,1)}) %all-gather.15.cloned.1.call-update) | async-done | bytes 4194320 | tf_op jit(solution)/shard_map/all_gather | solution.py:113
  324.0 5.5 copy.86
  329.5 68.7 %all-gather.19.cloned.1.call-done = bf16[1024,2048]{1,0:T(8,128)(2,1)} async-done(((bf16[128,2048]{1,0:T(8,128)(2,1)}), bf16[1024,2048]{1,0:T(8,128)(2,1)}) %all-gather.19.cloned.1.call-update) | async-done | bytes 4194320 | tf_op jit(solution)/shard_map/all_gather | solution.py:112
  404.8 15.6 while.37
  405.3 4.3 fusion.163
  413.0 4.3 fusion.163
  420.5 20.2 while.38
  425.6 4.8 fusion.168
  435.6 5.2 fusion.168
  442.0 34.8 all-gather.23.cloned.1.call-done
  476.8 4.7 multiply_reduce_fusion.3
  481.7 141.2 %all-gather.25.cloned.1.call-done = bf16[32,172,2048]{2,1,0:T(8,128)(2,1)} async-done(((bf16[1,172,2048]{2,1,0:T(8,128)(2,1)}), bf16[32,172,2048]{2,1,0:T(8,128)(2,1)}) %all-gather.25.cloned.1.call-update) | async-done | bytes 22544400 | tf_op jit(solution)/shard_map/all_gather | solution.py:179
  622.9 22.1 reshape.449
  645.1 123.6 %all-gather.27.cloned.1.call-done = bf16[32,172,2048]{2,1,0:T(8,128)(2,1)} async-done(((bf16[1,172,2048]{2,1,0:T(8,128)(2,1)}), bf16[32,172,2048]{2,1,0:T(8,128)(2,1)}) %all-gather.27.cloned.1.call-update) | async-done | bytes 22544400 | tf_op jit(solution)/shard_map/all_gather | solution.py:180
  768.7 22.2 reshape.451
  790.9 13.3 fusion.102
  804.2 13.2 fusion.103
  817.4 97.0 %all-gather.29.cloned.1.call-done = bf16[32,172,2048]{2,1,0:T(8,128)(2,1)} async-done(((bf16[1,172,2048]{2,1,0:T(8,128)(2,1)}), bf16[32,172,2048]{2,1,0:T(8,128)(2,1)}) %all-gather.29.cloned.1.call-update) | async-done | bytes 22544400 | tf_op jit(solution)/shard_map/all_gather | solution.py:181
  914.4 22.0 reshape.453
  936.4 14.9 multiply_convert_fusion
  951.3 9.6 fusion.104
  960.9 10.2 multiply_reduce_fusion
  975.4 26.3 while.39
  993.9 3.8 fusion.180
  1001.6 12.1 copy.76
  1013.7 13.3 convert_element_type.151
  1028.5 18.3 convolution_bitcast_fusion.2
  1046.8 17.9 convolution_bitcast_fusion.3
  1064.7 18.0 convolution_bitcast_fusion.1
  1082.7 89.5 %pad_maximum_fusion = f32[5504,3,2048]{2,0,1:T(8,128)} fusion(f32[5504,1,2048]{2,0,1:T(8,128)} %convolution_bitcast_fusion.1, f32[5504,1,2048]{2,0,1:T(8,128)} %convolution_bitcast_fusion.2, f32[5504,1,2048]{2,0,1:T(8,128)} %convolution_bitcast_fusion.3), kind=kLoop, calls=%fused_computation.64 | loop fusion | flops 67633152 | bytes 270532608 | tf_op jit(solution)/shard_map/stack | solution.py:204
  1173.7 8.2 convolution_bitcast_fusion.7
  1182.0 9.3 convolution_bitcast_fusion.4
  1191.3 9.5 convolution_bitcast_fusion.5
  1200.8 8.6 convolution_bitcast_fusion.6
  1209.3 45.5 %pad_maximum_fusion.1 = f32[2048,4,2048]{2,0,1:T(8,128)} fusion(f32[2048,1,2048]{2,0,1:T(8,128)} %convolution_bitcast_fusion.4, f32[2048,1,2048]{2,0,1:T(8,128)} %convolution_bitcast_fusion.5, f32[2048,1,2048]{2,0,1:T(8,128)} %convolution_bitcast_fusion.6, f32[2048,1,2048]{2,0,1:T(8,128)} %convolution_bitcast_fusion.7), kind=kLoop, calls=%fused_computation.65 | loop fusion | flops 50331648 | bytes 134217728 | tf_op jit(solution)/shard_map/stack | solution.py:279
  1255.0 6.9 fusion.63
  1263.2 12.1 fusion.53
  1281.4 40.6 all-reduce.7
  1325.0 1756.0 %all-reduce.11.cloned.1.call-done = f32[5504,3,2048]{2,0,1:T(8,128)} async-done(((f32[5504,3,2048]{2,0,1:T(8,128)}), f32[5504,3,2048]{2,0,1:T(8,128)}) %all-reduce.11.cloned.1.call-update) | async-done | bytes 135266320
  3081.0 4.5 dynamic-slice_bitcast_fusion
  3085.5 1401.3 %reduce-scatter.6.cloned.1.call-done = f32[64,4,2048]{2,0,1:T(8,128)} async-done(((f32[2048,4,2048]{2,0,1:T(8,128)}), f32[64,4,2048]{2,0,1:T(8,128)}) %reduce-scatter.6.cloned.1.call-update) | async-done | bytes 2097168 | tf_op jit(solution)/shard_map/reduce_scatter | solution.py:278
  (230 shorter events, 79.1 us)
Async XLA Ops:
  7.2 84.2 %all-gather.13.cloned.1.call-start = ((), (), s32[]{:S(2)}) async-start(), calls=%async_computation.2 | async-start | bytes 8650752 | tf_op jit(solution)/shard_map/all_gather | solution.py:95
  7.9 162.5 %all-gather.17.cloned.1.call-start = ((), (), s32[]{:S(2)}) async-start(), calls=%async_computation.4 | async-start | bytes 8650752 | tf_op jit(solution)/shard_map/all_gather | solution.py:94
  8.7 240.8 %all-gather.21.cloned.1.call-start = ((), (), s32[]{:S(2)}) async-start(), calls=%async_computation.6 | async-start | bytes 8650752 | tf_op jit(solution)/shard_map/all_gather | solution.py:97
  9.4 314.6 %all-gather.15.cloned.1.call-start = ((), (), s32[]{:S(2)}) async-start(), calls=%async_computation.3 | async-start | bytes 4718592 | tf_op jit(solution)/shard_map/all_gather | solution.py:113
  56.5 113.9 %copy-start.28 = (f32[128]{0:T(128)}, f32[128]{0:T(128)S(1)}, u32[]{:S(2)}) copy-start(f32[128]{0:T(128)S(1)} %get-tuple-element.563) | copy-start | bytes 1540
  91.4 79.0 %copy-start.3 = (bf16[128,2048]{1,0:T(8,128)(2,1)S(1)}, bf16[128,2048]{1,0:T(8,128)(2,1)}, u32[]{:S(2)}) copy-start(bf16[128,2048]{1,0:T(8,128)(2,1)} %param.22) | copy-start | bytes 1572868
  97.1 81.7 %copy-start.35 = (s32[1,8]{1,0:T(1,128)S(1)}, s32[1,8]{1,0:T(1,128)}, u32[]{:S(2)}) copy-start(s32[1,8]{1,0:T(1,128)} %param.24) | copy-start | bytes 100
  97.1 82.0 %copy-start.38 = (s32[1,3]{1,0:T(1,128)S(1)}, s32[1,3]{1,0:T(1,128)}, u32[]{:S(2)}) copy-start(s32[1,3]{1,0:T(1,128)} %param.25) | copy-start | bytes 40
  97.1 82.6 %copy-start.8 = (bf16[128,2048]{1,0:T(8,128)(2,1)S(1)}, bf16[128,2048]{1,0:T(8,128)(2,1)}, u32[]{:S(2)}) copy-start(bf16[128,2048]{1,0:T(8,128)(2,1)} %param.21) | copy-start | bytes 1572868
  97.1 301.1 %all-gather.19.cloned.1.call-start = ((), (), s32[]{:S(2)}) async-start(), calls=%async_computation.5 | async-start | bytes 4718592 | tf_op jit(solution)/shard_map/all_gather | solution.py:112
  175.9 300.9 %all-gather.23.cloned.1.call-start = ((), (), s32[]{:S(2)}) async-start(), calls=%async_computation.7 | async-start | bytes 8650752 | tf_op jit(solution)/shard_map/all_gather | solution.py:174
  176.5 446.5 %all-gather.25.cloned.1.call-start = ((), (), s32[]{:S(2)}) async-start(), calls=%async_computation.10 | async-start | bytes 23789568 | tf_op jit(solution)/shard_map/all_gather | solution.py:179
  177.2 591.4 %all-gather.27.cloned.1.call-start = ((), (), s32[]{:S(2)}) async-start(), calls=%async_computation.11 | async-start | bytes 23789568 | tf_op jit(solution)/shard_map/all_gather | solution.py:180
  178.0 736.4 %all-gather.29.cloned.1.call-start = ((), (), s32[]{:S(2)}) async-start(), calls=%async_computation.12 | async-start | bytes 23789568 | tf_op jit(solution)/shard_map/all_gather | solution.py:181
  178.7 1012.6 %reduce-scatter.4.cloned.1.call-start = ((), (), s32[]{:S(2)}) async-start(), calls=%async_computation.8 | async-start | bytes 9437184 | tf_op jit(solution)/shard_map/reduce_scatter | solution.py:251
  179.9 884.8 %copy-start.33 = (f32[128]{0:T(128)}, f32[128]{0:T(128)S(1)}, u32[]{:S(2)}) copy-start(f32[128]{0:T(128)S(1)} %compare_convert_fusion) | copy-start | bytes 1540
  180.4 73.7 %copy-start.31 = (f32[128]{0:T(128)}, f32[128]{0:T(128)S(1)}, u32[]{:S(2)}) copy-start(f32[128]{0:T(128)S(1)} %get-tuple-element.565) | copy-start | bytes 1540
  442.0 39.5 copy-start.19
  481.5 489.6 %copy-start.6 = (f32[128,2048]{1,0:T(8,128)}, f32[128,2048]{1,0:T(8,128)S(1)}, u32[]{:S(2)}) copy-start(f32[128,2048]{1,0:T(8,128)S(1)} %get-tuple-element.569) | copy-start | bytes 3145732
  481.7 322.5 %copy-start.10 = (bf16[128,2048]{1,0:T(8,128)(2,1)}, bf16[128,2048]{1,0:T(8,128)(2,1)S(1)}, u32[]{:S(2)}) copy-start(bf16[128,2048]{1,0:T(8,128)(2,1)S(1)} %multiply_convert_fusion.4) | copy-start | bytes 1572868
  817.4 119.0 %copy-start.24 = (bf16[128,2048]{1,0:T(8,128)(2,1)S(1)}, bf16[128,2048]{1,0:T(8,128)(2,1)}, u32[]{:S(2)}) copy-start(bf16[128,2048]{1,0:T(8,128)(2,1)} %param.23) | copy-start | bytes 1572868
  951.3 9.6 copy-start.17
  960.9 10.6 slice-start
  960.9 10.6 slice-start.1
  971.6 3.7 copy-start.21
  981.1 3.5 copy-start.1
  993.9 3.8 copy-start.1
  1027.0 19.7 copy-start.16
  1027.0 2054.0 %all-reduce.11.cloned.1.call-start = ((), (), s32[]{:S(2)}) async-start(), calls=%async_computation.13 | async-start | bytes 270532608
  1046.8 18.0 copy-start.14
  1046.8 18.0 copy-start.25
  1172.3 3314.5 %reduce-scatter.6.cloned.1.call-start = ((), (), s32[]{:S(2)}) async-start(), calls=%async_computation.9 | async-start | bytes 69206016 | tf_op jit(solution)/shard_map/reduce_scatter | solution.py:278
  1173.7 8.3 copy-start.13
  1173.7 8.2 copy-start.20
  1181.9 9.4 copy-start.4
  1181.9 9.4 copy-start.26
  1181.9 9.4 copy-start.29
  1191.3 9.5 copy-start.22
  1254.9 7.0 copy-start.37
  1254.9 8.2 copy-start.7
  1254.9 8.2 copy-start.34
  1254.9 20.4 slice-start.4
  1254.9 23.3 slice-start.2
  1263.2 12.1 slice-start.5
  1263.2 12.1 copy-start.23
  1263.2 15.0 slice-start.3
  1278.2 3.2 copy-start.30
  1278.2 45.5 %copy-start.36 = (f32[128]{0:T(128)S(1)}, f32[128]{0:T(128)}, u32[]{:S(2)}) copy-start(f32[128]{0:T(128)} %get-tuple-element.562) | copy-start | bytes 1540
  (12 other events, 23.4 us)
Sparse Core Ops, SparseCore 0:
  11.0 80.3 all-gather.12
  94.4 75.9 all-gather.16
  173.4 75.9 all-gather.20
  252.0 71.9 all-gather.14
  326.5 71.6 all-gather.18
  401.1 75.6 all-gather.22
  479.7 143.1 all-gather.24
  625.8 142.7 all-gather.26
  771.6 142.7 all-gather.28
  1027.1 147.1 reduce-scatter.3
  1181.9 1899.0 all-reduce.10
  3083.2 1403.5 reduce-scatter.5
where the time goes:
time: 4510 us; the launch traced here: 4500 us
  waiting for transfers between devices  3870 us (86%)
  matrix products  237 us (5%)
  other arithmetic  156 us (3%)
  local copies, waits for them, and re-layouts  130 us (3%)
  blocking collectives  83.3 us (2%)
    unnamed x13, waiting for transfers between devices  1760 us
    reduce_scatter x1, waiting for transfers between devices, body(): lax.psum_scatter(jnp.stack([columns_by_columns(hidden_part, d_queries_low...  1400 us
    all_gather x1, waiting for transfers between devices, body(): piece_gate = lax.all_gather(w_gate, ('dp', 'fsdp'), axis=0, tiled=True)  141 us
    all_gather x1, waiting for transfers between devices, body(): piece_up = lax.all_gather(w_up, ('dp', 'fsdp'), axis=0, tiled=True)  124 us
    all_gather x1, waiting for transfers between devices, body(): piece_down = lax.all_gather(w_down, ('dp', 'fsdp'), axis=0, tiled=True)  97 us
  transfers between devices with their start and end apart: 12, of which 11 were waited for; matrix products, arithmetic and copies ran while one was open for 9% of the time, Pallas kernels for 0%

commit v1 on v0

--- a/solution.py
+++ b/solution.py
@@ -1,8 +1,11 @@
+import functools
 import math
 
 import jax
 import jax.numpy as jnp
 from jax import lax
+from jax.experimental import pallas as pl
+from jax.experimental.pallas import tpu as pltpu
 from jax.sharding import PartitionSpec as P
 
 HEADS = 16
@@ -317,6 +320,546 @@
     )
 
 
+RING = (0, 1, 3, 2)
+BLOCK = 256
+
+
+def swap_pairs(size, mask):
+    return [(place, place ^ mask) for place in range(size)]
+
+
+def ring_pairs():
+    return [
+        (2 * RING[place] + x, 2 * RING[(place + 1) % 4] + x) for place in range(4) for x in range(2)
+    ]
+
+
+def x_swap(value):
+    return lax.ppermute(value, "fsdp", swap_pairs(8, 1))
+
+
+def ring_step(value):
+    return lax.ppermute(value, "fsdp", ring_pairs())
+
+
+def y_swap(value):
+    return lax.ppermute(value, "dp", swap_pairs(4, 2))
+
+
+def core_swap(value):
+    return lax.ppermute(value, "dp", swap_pairs(4, 1))
+
+
+def in_order(flag, first, second):
+    swapped = flag == 1
+    return jnp.concatenate(
+        [jnp.where(swapped, second, first), jnp.where(swapped, first, second)], axis=0
+    )
+
+
+def gather_rows(own):
+    pieces = []
+    held = own
+    for step in range(4):
+        pieces.append((held, x_swap(held)))
+        if step < 3:
+            held = ring_step(held)
+    return pieces
+
+
+def scatter_rows(part):
+    total = None
+    for step in (1, 2, 3, 0):
+        other = x_swap(part(step, 1).astype(jnp.bfloat16))
+        here = part(step, 0) + other.astype(jnp.float32)
+        if total is not None:
+            here = here + ring_step(total).astype(jnp.float32)
+        total = here.astype(jnp.bfloat16) if step else here
+    return total
+
+
+def attend_kernel(
+    factor, q_ref, k_ref, v_ref, first_ref, last_ref, place_ref, att_ref, low_ref, lse_ref
+):
+    scores = rows_by_rows(q_ref[...], k_ref[...]) * factor
+    places = place_ref[...]
+    allowed = (places >= first_ref[...]) & (places <= last_ref[...])
+    masked = jnp.where(allowed, scores, MASKED)
+    largest = jnp.max(masked, axis=-1, keepdims=True)
+    raised = jnp.exp(masked - largest)
+    summed = jnp.sum(raised, axis=-1, keepdims=True)
+    probs_low = (raised * (1.0 / summed)).astype(jnp.bfloat16)
+    attended = product(probs_low, v_ref[...])
+    att_ref[...] = attended
+    low_ref[...] = attended.astype(jnp.bfloat16)
+    lse_ref[...] = (largest + jnp.log(summed))[None]
+
+
+def attend_back_kernel(
+    factor,
+    q_ref,
+    k_ref,
+    v_ref,
+    first_ref,
+    last_ref,
+    place_ref,
+    lse_ref,
+    att_ref,
+    d_att_ref,
+    dq_ref,
+    dk_ref,
+    dv_ref,
+    dk_sum,
+    dv_sum,
+):
+    step = pl.program_id(1)
+
+    @pl.when(step == 0)
+    def _():
+        dk_sum[...] = jnp.zeros_like(dk_sum)
+        dv_sum[...] = jnp.zeros_like(dv_sum)
+
+    queries = q_ref[...]
+    keys = k_ref[...]
+    d_att = d_att_ref[...]
+    scores = rows_by_rows(queries, keys) * factor
+    places = place_ref[...]
+    allowed = (places >= first_ref[...]) & (places <= last_ref[...])
+    probs = jnp.exp(jnp.where(allowed, scores, MASKED) - lse_ref[0])
+    delta = jnp.sum(d_att.astype(jnp.float32) * att_ref[...], axis=-1, keepdims=True)
+    d_probs = rows_by_rows(d_att, v_ref[...])
+    d_scores = (probs * (d_probs - delta)).astype(jnp.bfloat16)
+    dq_ref[...] = (product(d_scores, keys) * factor).astype(jnp.bfloat16)
+    dk_sum[...] += columns_by_columns(d_scores, queries)
+    dv_sum[...] += columns_by_columns(probs.astype(jnp.bfloat16), d_att)
+
+    @pl.when(step == pl.num_programs(1) - 1)
+    def _():
+        dk_ref[...] = (dk_sum[...] * factor).astype(jnp.bfloat16)
+        dv_ref[...] = dv_sum[...].astype(jnp.bfloat16)
+
+
+def attend_specs(count, head):
+    by_query = pl.BlockSpec((BLOCK, head), lambda h, i: (i, h))
+    by_key = pl.BlockSpec((count, head), lambda h, i: (0, h))
+    bound = pl.BlockSpec((BLOCK, 1), lambda h, i: (i, 0))
+    place = pl.BlockSpec((1, count), lambda h, i: (0, 0))
+    lse = pl.BlockSpec((1, BLOCK, 1), lambda h, i: (h, i, 0))
+    return by_query, by_key, bound, place, lse
+
+
+def attend(queries, keys, values, first, last, place, head):
+    count, width = queries.shape
+    by_query, by_key, bound, places, lse = attend_specs(count, head)
+    return pl.pallas_call(
+        functools.partial(attend_kernel, 1.0 / math.sqrt(head)),
+        grid=(width // head, count // BLOCK),
+        in_specs=[by_query, by_key, by_key, bound, bound, places],
+        out_specs=[by_query, by_query, lse],
+        out_shape=[
+            jax.ShapeDtypeStruct((count, width), jnp.float32),
+            jax.ShapeDtypeStruct((count, width), jnp.bfloat16),
+            jax.ShapeDtypeStruct((width // head, count, 1), jnp.float32),
+        ],
+        compiler_params=pltpu.CompilerParams(vmem_limit_bytes=40 * 2**20),
+        cost_estimate=pl.CostEstimate(
+            flops=4 * count * count * width,
+            bytes_accessed=12 * count * width,
+            transcendentals=count * count * width // head,
+        ),
+        name="attend",
+    )(queries, keys, values, first, last, place)
+
+
+def attend_back(queries, keys, values, first, last, place, lse, attended, d_attended, head):
+    count, width = queries.shape
+    by_query, by_key, bound, places, by_lse = attend_specs(count, head)
+    return pl.pallas_call(
+        functools.partial(attend_back_kernel, 1.0 / math.sqrt(head)),
+        grid=(width // head, count // BLOCK),
+        in_specs=[
+            by_query,
+            by_key,
+            by_key,
+            bound,
+            bound,
+            places,
+            by_lse,
+            by_query,
+            by_query,
+        ],
+        out_specs=[by_query, by_key, by_key],
+        out_shape=[jax.ShapeDtypeStruct((count, width), jnp.bfloat16)] * 3,
+        scratch_shapes=[pltpu.VMEM((count, head), jnp.float32)] * 2,
+        compiler_params=pltpu.CompilerParams(vmem_limit_bytes=40 * 2**20),
+        cost_estimate=pl.CostEstimate(
+            flops=10 * count * count * width,
+            bytes_accessed=18 * count * width,
+            transcendentals=count * count * width // head,
+        ),
+        name="attend_back",
+    )(queries, keys, values, first, last, place, lse, attended, d_attended)
+
+
+def spread_gains(gains, me):
+    held = gains
+    for bit in (1, 2, 4, 8, 16):
+        held = jnp.concatenate(
+            [held, lax.ppermute(held, ("dp", "fsdp"), swap_pairs(32, bit))], axis=0
+        )
+    count = held.shape[0]
+    owner = jnp.arange(count, dtype=jnp.int32)
+    picker = (owner[None, :] == (owner[:, None] ^ me)).astype(held.dtype)
+    return product(picker, held)
+
+
+def sum_to_owners(total, me):
+    for bit in (16, 8, 4, 2, 1):
+        half = total.shape[0] // 2
+        high = (me & bit) != 0
+        kept = jnp.where(high, total[half:], total[:half])
+        given = jnp.where(high, total[:half], total[half:])
+        total = kept + lax.ppermute(given, ("dp", "fsdp"), swap_pairs(32, bit))
+    return total
+
+
+def projection_columns(stacked, z, x, dp):
+    rows, width = stacked.shape
+    each = rows // 3
+    half = width // 2
+    kept = lax.dynamic_slice(stacked, (0, half * x), (rows, half))
+    given = lax.dynamic_slice(stacked, (0, half * (1 - x)), (rows, half))
+    pair = in_order(x, kept, x_swap(given))
+    head = half // 8
+
+    def for_z(place):
+        return jnp.concatenate(
+            [
+                lax.dynamic_slice(pair, (0, head * (4 * j) + head * place), (2 * rows, head))
+                for j in range(2)
+            ],
+            axis=1,
+        )
+
+    held = [for_z(z)]
+    for mask in (1, 2, 3):
+        held.append(lax.ppermute(for_z(z ^ mask), "fsdp", swap_pairs(8, 2 * mask)))
+    held = jnp.stack(held)
+    held = jnp.concatenate(
+        [lax.dynamic_index_in_dim(held, place ^ z, 0, keepdims=False) for place in range(4)], axis=0
+    )
+    both = jnp.stack([held, y_swap(held)])
+    other = core_swap(both)
+    held = jnp.stack([both[0], other[0], both[1], other[1]])
+    held = held.reshape(4, 8, 3, each, 2 * head)
+    out = []
+    for which in range(3):
+        out.append(
+            jnp.concatenate(
+                [
+                    lax.dynamic_index_in_dim(held[:, :, which], place ^ dp, 0, keepdims=False)
+                    for place in range(4)
+                ],
+                axis=0,
+            ).reshape(32 * each, 2 * head)
+        )
+    return out
+
+
+def projection_grads(grads, z, x, y, c):
+    width, mine = grads[0].shape
+    block = width // 4
+    each = width // 32
+    head = mine // 2
+
+    def dp_rows(grad, place):
+        return lax.dynamic_slice(grad, (block * place, 0), (block, mine))
+
+    given = jnp.concatenate(
+        [
+            jnp.concatenate([dp_rows(grad, 2 * row + 1 - c) for row in range(2)], axis=0)
+            for grad in grads
+        ],
+        axis=1,
+    ).astype(jnp.bfloat16)
+    from_core = core_swap(given)
+
+    def summed(which, row):
+        return dp_rows(grads[which], 2 * row + c) + lax.dynamic_slice(
+            from_core, (block * row, mine * which), (block, mine)
+        ).astype(jnp.float32)
+
+    given = jnp.concatenate([summed(which, 1 - y) for which in range(3)], axis=1)
+    got = y_swap(given.astype(jnp.bfloat16))
+    total = jnp.concatenate([summed(which, y) for which in range(3)], axis=1)
+    total = (total + got.astype(jnp.float32)).astype(jnp.bfloat16)
+
+    def z_rows(place):
+        return lax.dynamic_slice(total, (2 * each * place, 0), (2 * each, 3 * mine))
+
+    held = [z_rows(z)]
+    for mask in (1, 2, 3):
+        held.append(lax.ppermute(z_rows(z ^ mask), "fsdp", swap_pairs(8, 2 * mask)))
+    held = jnp.stack(held)
+    held = jnp.stack(
+        [lax.dynamic_index_in_dim(held, place ^ z, 0, keepdims=False) for place in range(4)]
+    )
+    kept = lax.dynamic_slice(held, (0, each * x, 0), (4, each, 3 * mine))
+    given = lax.dynamic_slice(held, (0, each * (1 - x), 0), (4, each, 3 * mine))
+    both = in_order(x, kept[None], x_swap(given)[None])
+    out = []
+    for which in range(3):
+        out.append(
+            jnp.concatenate(
+                [
+                    both[side, place, :, mine * which + head * j : mine * which + head * (j + 1)]
+                    for side in range(2)
+                    for j in range(2)
+                    for place in range(4)
+                ],
+                axis=1,
+            ).astype(jnp.float32)
+        )
+    return out
+
+
+def out_rows(own, x, y, c):
+    head = in_order(x, own, x_swap(own))
+    pairs = [(place, place ^ 16) for place in range(32) if place // 16 == place % 2]
+    got = lax.ppermute(head, ("dp", "fsdp"), pairs)
+    mine = jnp.where(x == y, head, got)
+    return in_order(c, mine, core_swap(mine))
+
+
+def out_grads(grad, x, y, c):
+    head = grad.shape[0] // 2
+    width = grad.shape[1]
+    kept = lax.dynamic_slice(grad, (head * c, 0), (head, width))
+    given = lax.dynamic_slice(grad, (head * (1 - c), 0), (head, width))
+    total = kept + core_swap(given.astype(jnp.bfloat16)).astype(jnp.float32)
+    pairs = [(place, place ^ 16) for place in range(32) if place // 16 != place % 2]
+    got = lax.ppermute(total.astype(jnp.bfloat16), ("dp", "fsdp"), pairs)
+    total = total + got.astype(jnp.float32)
+    each = head // 2
+    kept = lax.dynamic_slice(total, (each * x, 0), (each, width))
+    given = lax.dynamic_slice(total, (each * (1 - x), 0), (each, width))
+    pairs = [(place, place ^ 1) for place in range(32) if place // 16 == place % 2]
+    got = lax.ppermute(given.astype(jnp.bfloat16), ("dp", "fsdp"), pairs)
+    return jnp.where(x == y, kept, got.astype(jnp.float32))
+
+
+def hidden_units(own, padded):
+    rows = jnp.pad(own, ((0, padded - own.shape[0]), (0, 0)))
+    rows = jnp.concatenate([rows, y_swap(rows)], axis=0)
+    return jnp.concatenate([rows, core_swap(rows)], axis=0)
+
+
+def hidden_grads(units, rows, count):
+    half = units.shape[1] // 2
+    got = core_swap(columns_by_columns(units[:, half:], rows).astype(jnp.bfloat16))
+    total = columns_by_columns(units[:, :half], rows) + got.astype(jnp.float32)
+    quarter = half // 2
+    got = y_swap(total[quarter:].astype(jnp.bfloat16))
+    return (total[:quarter] + got.astype(jnp.float32))[:count]
+
+
+def fast_body(
+    hidden,
+    source,
+    cotangent,
+    row_counts,
+    seq_lengths,
+    kv_gain,
+    w_key,
+    w_value,
+    attn_gain,
+    w_query,
+    w_out,
+    ffn_gain,
+    w_gate,
+    w_up,
+    w_down,
+):
+    local_rows, width = hidden.shape
+    head = width // HEADS
+    dp = lax.axis_index("dp")
+    fsdp = lax.axis_index("fsdp")
+    y, c = dp // 2, dp % 2
+    z, x = fsdp // 2, fsdp % 2
+    me = 8 * dp + fsdp
+
+    src_pieces = gather_rows(source)
+    hid_pieces = gather_rows(hidden)
+    wq, wk, wv = projection_columns(jnp.concatenate([w_query, w_key, w_value], axis=0), z, x, dp)
+    w_kv = jnp.concatenate([wk, wv], axis=1)
+    each = kv_gain.shape[0]
+    spread = spread_gains(jnp.concatenate([kv_gain, attn_gain, ffn_gain])[None, :], me)
+    kv_gain_full, attn_gain_full, ffn_gain_full = (
+        spread[:, which * each : (which + 1) * each].reshape(1, width) for which in range(3)
+    )
+
+    order = z ^ (z >> 1)
+    devices = []
+    for step in range(4):
+        place = (order - step) % 4
+        for side in range(2):
+            devices.append(2 * (place ^ (place >> 1)) + (x ^ side))
+    slots = (
+        jnp.stack(devices).astype(jnp.int32)[:, None] * local_rows
+        + jnp.arange(local_rows, dtype=jnp.int32)[None, :]
+    ).reshape(-1)
+    live, position, sequence = slot_layout(row_counts, seq_lengths, slots, local_rows)
+    starts = jnp.concatenate([jnp.zeros((1,), jnp.int32), jnp.cumsum(seq_lengths[0])])
+    first = jnp.sum(
+        jnp.where(
+            sequence[:, None] == jnp.arange(starts.shape[0], dtype=jnp.int32)[None, :],
+            starts[None, :],
+            0,
+        ),
+        axis=1,
+    )
+    first, last = first[:, None], position[:, None]
+    place_of_key = jnp.where(live, position, -1)[None, :]
+    own_live = live[:local_rows].astype(jnp.float32)[:, None]
+
+    def normed(values, gain):
+        values = values.astype(jnp.float32)
+        return (values * inverse_scale(values) * gain).astype(jnp.bfloat16)
+
+    hid_low, src_low, queries, pairs = [], [], [], []
+    for step in range(4):
+        rows = normed(jnp.concatenate(src_pieces[step], axis=0), kv_gain_full)
+        src_low.append(rows)
+        pairs.append(product(rows, w_kv).astype(jnp.bfloat16))
+        rows = normed(jnp.concatenate(hid_pieces[step], axis=0), attn_gain_full)
+        hid_low.append(rows)
+        queries.append(product(rows, wq).astype(jnp.bfloat16))
+    hid_low = jnp.concatenate(hid_low, axis=0)
+    src_low = jnp.concatenate(src_low, axis=0)
+    queries = jnp.concatenate(queries, axis=0)
+    pairs = jnp.concatenate(pairs, axis=0)
+    keys, values = pairs[:, : 2 * head], pairs[:, 2 * head :]
+    attended_f, attended_low, lse = attend(queries, keys, values, first, last, place_of_key, head)
+
+    wo = out_rows(w_out, x, y, c)
+
+    def rows_of(array, step, side):
+        start = (2 * step + side) * local_rows
+        return array[start : start + local_rows]
+
+    branch = scatter_rows(lambda step, side: product(rows_of(attended_low, step, side), wo))
+    hidden_f = hidden.astype(jnp.float32)
+    middle = hidden_f + branch
+    middle_scale = inverse_scale(middle)
+    middle_unit = middle * middle_scale
+    mid_pieces = gather_rows((middle_unit * ffn_gain_full).astype(jnp.bfloat16))
+
+    d_out = cotangent.astype(jnp.float32) * own_live
+    cot_pieces = gather_rows(d_out.astype(jnp.bfloat16))
+    units = w_gate.shape[0]
+    padded = -(-units // 64) * 64
+    wg = hidden_units(w_gate, padded)
+    wu = hidden_units(w_up, padded)
+    wd = hidden_units(w_down, padded)
+
+    mids, cots, inners, d_gates, d_ups = [], [], [], [], []
+    for step in range(4):
+        mid = jnp.concatenate(mid_pieces[step], axis=0)
+        cot = jnp.concatenate(cot_pieces[step], axis=0)
+        gate_value = rows_by_rows(mid, wg)
+        up_value = rows_by_rows(mid, wu)
+        sigmoid_gate = jax.nn.sigmoid(gate_value)
+        swished = gate_value * sigmoid_gate
+        d_inner = rows_by_rows(cot, wd)
+        mids.append(mid)
+        cots.append(cot)
+        inners.append((swished * up_value).astype(jnp.bfloat16))
+        d_gates.append(
+            (d_inner * up_value * sigmoid_gate * (1.0 + gate_value * (1.0 - sigmoid_gate))).astype(
+                jnp.bfloat16
+            )
+        )
+        d_ups.append((d_inner * swished).astype(jnp.bfloat16))
+
+    def side_of(array, side):
+        return array[side * local_rows : (side + 1) * local_rows]
+
+    d_normed = scatter_rows(
+        lambda step, side: product(side_of(d_gates[step], side), wg)
+        + product(side_of(d_ups[step], side), wu)
+    )
+    ffn_result = scatter_rows(lambda step, side: product(side_of(inners[step], side), wd))
+    output = ((middle + ffn_result) * own_live).astype(jnp.bfloat16)
+
+    d_middle = d_out + norm_backward(middle, middle_scale, ffn_gain_full, d_normed)
+    d_branch_low = d_middle.astype(jnp.bfloat16)
+    branch_pieces = gather_rows(d_branch_low)
+    ffn_gain_part = jnp.sum(d_normed * middle_unit, axis=0)
+    grad_ffn_gain = sum_to_owners(ffn_gain_part.reshape(32, each), me).reshape(each)
+
+    mids = jnp.concatenate(mids, axis=0)
+    cots = jnp.concatenate(cots, axis=0)
+    grad_gate = hidden_grads(jnp.concatenate(d_gates, axis=0), mids, units)
+    grad_up = hidden_grads(jnp.concatenate(d_ups, axis=0), mids, units)
+    grad_down = hidden_grads(jnp.concatenate(inners, axis=0), cots, units)
+
+    d_branches = [jnp.concatenate(pair, axis=0) for pair in branch_pieces]
+    d_attended = jnp.concatenate(
+        [rows_by_rows(rows, wo).astype(jnp.bfloat16) for rows in d_branches], axis=0
+    )
+    d_queries, d_keys, d_values = attend_back(
+        queries, keys, values, first, last, place_of_key, lse, attended_f, d_attended, head
+    )
+    d_pairs = jnp.concatenate([d_keys, d_values], axis=1)
+    d_src = scatter_rows(lambda step, side: rows_by_rows(rows_of(d_pairs, step, side), w_kv))
+    d_hid = scatter_rows(lambda step, side: rows_by_rows(rows_of(d_queries, step, side), wq))
+
+    grad_out = out_grads(
+        columns_by_columns(attended_low, jnp.concatenate(d_branches, axis=0)), x, y, c
+    )
+    pair_grads = columns_by_columns(src_low, d_pairs)
+    grad_query, grad_key, grad_value = projection_grads(
+        [
+            columns_by_columns(hid_low, d_queries),
+            pair_grads[:, : 2 * head],
+            pair_grads[:, 2 * head :],
+        ],
+        z,
+        x,
+        y,
+        c,
+    )
+    grad_attn_gain = jnp.sum(w_query.astype(jnp.float32) * grad_query, axis=1)
+    grad_attn_gain = grad_attn_gain / attn_gain.astype(jnp.float32)
+    grad_kv_gain = jnp.sum(
+        w_key.astype(jnp.float32) * grad_key + w_value.astype(jnp.float32) * grad_value, axis=1
+    )
+    grad_kv_gain = grad_kv_gain / kv_gain.astype(jnp.float32)
+
+    grad_hidden = (
+        d_middle + norm_backward(hidden_f, inverse_scale(hidden_f), attn_gain_full, d_hid)
+    ).astype(jnp.bfloat16)
+    source_f = source.astype(jnp.float32)
+    grad_source = norm_backward(source_f, inverse_scale(source_f), kv_gain_full, d_src).astype(
+        jnp.bfloat16
+    )
+    return (
+        output,
+        grad_hidden,
+        grad_source,
+        grad_kv_gain,
+        grad_key,
+        grad_value,
+        grad_attn_gain,
+        grad_query,
+        grad_out,
+        grad_ffn_gain,
+        grad_gate,
+        grad_up,
+        grad_down,
+    )
+
+
 def solution(mesh):
     in_specs = (
         P(("dp", "fsdp"), None),
@@ -350,4 +893,8 @@
         P(("dp", "fsdp"), None),
         P(("dp", "fsdp"), None),
     )
-    return jax.shard_map(body, mesh=mesh, in_specs=in_specs, out_specs=out_specs, check_vma=False)
+    placed = (
+        mesh.shape["dp"] == 4 and mesh.shape["fsdp"] == 8 and HEADS == 2 * mesh.shape["fsdp"]
+    )
+    chosen = fast_body if placed else body
+    return jax.shard_map(chosen, mesh=mesh, in_specs=in_specs, out_specs=out_specs, check_vma=False)

time: 4510 us -> 773 us (0.17)
  waiting for transfers between devices: 3870 us -> 397 us
  starting transfers between devices: 0.68 us -> 115 us
  other arithmetic: 156 us -> 44.4 us
  matrix products: 237 us -> 133 us
  blocking collectives: 83.3 us -> 0 us
  local copies, waits for them, and re-layouts: 130 us -> 54.7 us
    unnamed x13 -> x0, waiting for transfers between devices: 1760 us -> none
    reduce_scatter x2 -> x0, waiting for transfers between devices: 1400 us -> none  [the longest x1 1400 us: body(): lax.psum_scatter(jnp.stack([columns_by_columns(hidden_part, d_queries_low...]
    all_gather x9 -> x0, waiting for transfers between devices: 711 us -> none  [the longest x1 141 us: body(): piece_gate = lax.all_gather(w_gate, ('dp', 'fsdp'), axis=0, tiled=True)]
    ppermute x0 -> x110, waiting for transfers between devices: none -> 397 us  [the longest x43 173 us: x_swap(): return lax.ppermute(value, 'fsdp', swap_pairs(8, 1))]
    another operation x4 -> x10, other arithmetic: 135 us -> 3.33 us  [the longest x1 89.5 us: body(): jnp.stack([columns_by_columns(d_gate, middle_low), columns_by_columns(d_u...]
    ppermute x0 -> x110, starting transfers between devices: none -> 115 us  [the longest x43 47.2 us: x_swap(): return lax.ppermute(value, 'fsdp', swap_pairs(8, 1))]
    unnamed x2 -> x0, blocking collectives: 83.3 us -> none
    dot_general x7 -> x9, matrix products: 89.8 us -> 24.3 us  [columns_by_columns(): lax.dot_general(left, right, (((0,), (0,)), ((), ())), preferred_element_...]
  transfers between devices with their start and end apart: 12 -> 110, of which waited for: 11 -> 53; matrix products, arithmetic and copies ran while one was open for 9% -> 26% of each run, Pallas kernels for 0% -> 1%
where the time goes in v1:
time: 773 us; the launch traced here: 765 us
  waiting for transfers between devices  397 us (51%)
  matrix products  133 us (17%)
  starting transfers between devices  115 us (15%)
  local copies, waits for them, and re-layouts  54.7 us (7%)
  other arithmetic  44.4 us (6%)
  Pallas kernels  17.7 us (2%)
    ppermute x43, waiting for transfers between devices, x_swap(): return lax.ppermute(value, 'fsdp', swap_pairs(8, 1))  173 us
    ppermute x30, waiting for transfers between devices, ring_step(): return lax.ppermute(value, 'fsdp', ring_pairs())  132 us
    dot_general x41, matrix products, product(): return jnp.dot(left, right, preferred_element_type=jnp.float32)  62.4 us
    ppermute x43, starting transfers between devices, x_swap(): return lax.ppermute(value, 'fsdp', swap_pairs(8, 1))  47.2 us
    dot_general x32, matrix products, rows_by_rows(): lax.dot_general(left, right, (((1,), (1,)), ((), ())), preferred_element_...  46.1 us
    ppermute x8, waiting for transfers between devices, y_swap(): return lax.ppermute(value, 'dp', swap_pairs(4, 2))  31 us
    ppermute x30, starting transfers between devices, ring_step(): return lax.ppermute(value, 'fsdp', ring_pairs())  29.1 us
    unnamed x210, local copies, waits for them, and re-layouts  28.4 us
  transfers between devices with their start and end apart: 110, of which 53 were waited for; matrix products, arithmetic and copies ran while one was open for 26% of the time, Pallas kernels for 1%

profile of v1, /device:TPU:0, one launch (start us, length us, event | category | flops | bytes accessed | tf_op | source)
XLA Modules:
  0.0 765.5 jit_solution(9448361037002789616)
XLA Ops:
  52.2 3.9 concatenate.227
  62.9 8.9 %collective-permute-done.6 = bf16[192,1024]{1,0:T(8,128)(2,1)S(1)} collective-permute-done((bf16[192,1024]{1,0:T(8,128)(2,1)S(1)}, bf16[192,1024]{1,0:T(8,128)(2,1)S(1)}, u32[]{:S(2)}, u32[]{:S(2)}) %collective-permute-start.6) | collective-permute-done | bytes 393248 | tf_op jit(solution)/shard_map/ppermute | solution.py:338
  75.9 3.7 collective-permute-start.9
  81.1 4.5 collective-permute-done.9
  85.6 6.8 collective-permute-start.14
  92.4 3.5 collective-permute-done.8
  99.5 7.6 collective-permute-done.14
  107.9 10.4 %collective-permute-done.21 = bf16[128,2048]{1,0:T(8,128)(2,1)S(1)} collective-permute-done((bf16[128,2048]{1,0:T(8,128)(2,1)S(1)}, bf16[128,2048]{1,0:T(8,128)(2,1)S(1)}, u32[]{:S(2)}, u32[]{:S(2)}) %collective-permute-start.21) | collective-permute-done | bytes 524320 | tf_op jit(solution)/shard_map/ppermute | solution.py:342
  120.5 3.6 collective-permute-start.57
  133.2 7.6 collective-permute-done.23
  141.1 14.5 %collective-permute-done.17 = bf16[128,2048]{1,0:T(8,128)(2,1)S(1)} collective-permute-done((bf16[128,2048]{1,0:T(8,128)(2,1)S(1)}, bf16[128,2048]{1,0:T(8,128)(2,1)S(1)}, u32[]{:S(2)}, u32[]{:S(2)}) %collective-permute-start.17) | collective-permute-done | bytes 524320 | tf_op jit(solution)/shard_map/ppermute | solution.py:338
  156.0 8.0 %collective-permute-done.24 = bf16[128,2048]{1,0:T(8,128)(2,1)S(1)} collective-permute-done((bf16[128,2048]{1,0:T(8,128)(2,1)S(1)}, bf16[128,2048]{1,0:T(8,128)(2,1)S(1)}, u32[]{:S(2)}, u32[]{:S(2)}) %collective-permute-start.24) | collective-permute-done | bytes 524320 | tf_op jit(solution)/shard_map/ppermute | solution.py:338
  179.4 7.5 attend.1
  190.1 11.0 %collective-permute-done.31 = bf16[128,2048]{1,0:T(8,128)(2,1)S(1)} collective-permute-done((bf16[128,2048]{1,0:T(8,128)(2,1)S(1)}, bf16[128,2048]{1,0:T(8,128)(2,1)S(1)}, u32[]{:S(2)}, u32[]{:S(2)}) %collective-permute-start.31) | collective-permute-done | bytes 524320 | tf_op jit(solution)/shard_map/ppermute | solution.py:338
  207.8 6.2 collective-permute-done.30
  214.0 4.1 collective-permute-done.32
  221.7 7.7 collective-permute-done.58
  231.8 8.8 %collective-permute-done.33 = bf16[128,2048]{1,0:T(8,128)(2,1)S(1)} collective-permute-done((bf16[128,2048]{1,0:T(8,128)(2,1)S(1)}, bf16[128,2048]{1,0:T(8,128)(2,1)S(1)}, u32[]{:S(2)}, u32[]{:S(2)}) %collective-permute-start.33) | collective-permute-done | bytes 524320 | tf_op jit(solution)/shard_map/ppermute | solution.py:342
  244.3 7.6 collective-permute-done.59
  253.6 7.3 collective-permute-done.34
  266.8 4.6 fusion.82
  271.5 6.0 collective-permute-done.35
  293.6 16.8 %collective-permute-done.50 = bf16[128,2048]{1,0:T(8,128)(2,1)S(1)} collective-permute-done((bf16[128,2048]{1,0:T(8,128)(2,1)S(1)}, bf16[128,2048]{1,0:T(8,128)(2,1)S(1)}, u32[]{:S(2)}, u32[]{:S(2)}) %collective-permute-start.50) | collective-permute-done | bytes 524320 | tf_op jit(solution)/shard_map/ppermute | solution.py:338
  329.9 5.1 collective-permute-done.51
  337.2 18.1 %collective-permute-done.48 = bf16[128,2048]{1,0:T(8,128)(2,1)S(1)} collective-permute-done((bf16[128,2048]{1,0:T(8,128)(2,1)S(1)}, bf16[128,2048]{1,0:T(8,128)(2,1)S(1)}, u32[]{:S(2)}, u32[]{:S(2)}) %collective-permute-start.48) | collective-permute-done | bytes 524320 | tf_op jit(solution)/shard_map/ppermute | solution.py:338
  384.3 5.9 collective-permute-done.63
  394.0 16.6 %collective-permute-done.46 = bf16[128,2048]{1,0:T(8,128)(2,1)S(1)} collective-permute-done((bf16[128,2048]{1,0:T(8,128)(2,1)S(1)}, bf16[128,2048]{1,0:T(8,128)(2,1)S(1)}, u32[]{:S(2)}, u32[]{:S(2)}) %collective-permute-start.46) | collective-permute-done | bytes 524320 | tf_op jit(solution)/shard_map/ppermute | solution.py:338
  410.7 3.6 fusion.232
  443.0 7.2 collective-permute-done.68
  450.2 3.8 multiply_reduce_fusion
  455.9 5.4 convolution_convert_fusion
  469.6 11.8 %collective-permute-done.101 = f32[4,64]{1,0:T(4,128)S(1)} collective-permute-done((f32[4,64]{1,0:T(4,128)S(1)}, f32[4,64]{1,0:T(4,128)S(1)}, u32[]{:S(2)}, u32[]{:S(2)}) %collective-permute-start.101) | collective-permute-done | bytes 1056 | tf_op jit(solution)/shard_map/ppermute | solution.py:522
  511.2 10.9 %collective-permute-done.72 = bf16[128,2048]{1,0:T(8,128)(2,1)S(1)} collective-permute-done((bf16[128,2048]{1,0:T(8,128)(2,1)S(1)}, bf16[128,2048]{1,0:T(8,128)(2,1)S(1)}, u32[]{:S(2)}, u32[]{:S(2)}) %collective-permute-start.72) | collective-permute-done | bytes 524320 | tf_op jit(solution)/shard_map/ppermute | solution.py:342
  526.3 15.5 %collective-permute-done.107 = bf16[192,2048]{1,0:T(8,128)(2,1)S(1)} collective-permute-done((bf16[192,2048]{1,0:T(8,128)(2,1)S(1)}, bf16[192,2048]{1,0:T(8,128)(2,1)S(1)}, u32[]{:S(2)}, u32[]{:S(2)}) %collective-permute-start.107) | collective-permute-done | bytes 786464 | tf_op jit(solution)/shard_map/ppermute | solution.py:346
  543.1 14.6 %collective-permute-done.109 = bf16[192,2048]{1,0:T(8,128)(2,1)S(1)} collective-permute-done((bf16[192,2048]{1,0:T(8,128)(2,1)S(1)}, bf16[192,2048]{1,0:T(8,128)(2,1)S(1)}, u32[]{:S(2)}, u32[]{:S(2)}) %collective-permute-start.109) | collective-permute-done | bytes 786464 | tf_op jit(solution)/shard_map/ppermute | solution.py:346
  561.2 10.8 %collective-permute-done.75 = bf16[128,2048]{1,0:T(8,128)(2,1)S(1)} collective-permute-done((bf16[128,2048]{1,0:T(8,128)(2,1)S(1)}, bf16[128,2048]{1,0:T(8,128)(2,1)S(1)}, u32[]{:S(2)}, u32[]{:S(2)}) %collective-permute-start.75) | collective-permute-done | bytes 524320 | tf_op jit(solution)/shard_map/ppermute | solution.py:338
  572.6 10.2 %attend_back.1 = (bf16[1024,256]{1,0:T(8,128)(2,1)S(1)}, bf16[1024,256]{1,0:T(8,128)(2,1)S(1)}, bf16[1024,256]{1,0:T(8,128)(2,1)S(1)}) custom-call(bf16[1024,256]{1,0:T(8,128)(2,1)S(1)} %copy-done.1, bf16[1024,256]{1,0:T(8,128)(2,1)S(1)} %copy-done.5, bf16[1024,256]{1,0:T(8,128)(2,1)S(1)} %copy-done.3, s32[1024,1]{1,0:T(8,128)S(1)} %copy.97.first_ref, ...), custom_call_target="tpu_custom_call" | custom-call | flops 2684354560 | bytes 4718592 | tf_op jit(solution)/shard_map/attend_back/pallas_call | solution.py:477
  604.6 5.9 collective-permute-done.79
  612.3 20.7 %collective-permute-done.86 = bf16[128,2048]{1,0:T(8,128)(2,1)S(1)} collective-permute-done((bf16[128,2048]{1,0:T(8,128)(2,1)S(1)}, bf16[128,2048]{1,0:T(8,128)(2,1)S(1)}, u32[]{:S(2)}, u32[]{:S(2)}) %collective-permute-start.86) | collective-permute-done | bytes 524320 | tf_op jit(solution)/shard_map/ppermute | solution.py:338
  637.8 10.3 %collective-permute-done.80 = bf16[128,2048]{1,0:T(8,128)(2,1)S(1)} collective-permute-done((bf16[128,2048]{1,0:T(8,128)(2,1)S(1)}, bf16[128,2048]{1,0:T(8,128)(2,1)S(1)}, u32[]{:S(2)}, u32[]{:S(2)}) %collective-permute-start.80) | collective-permute-done | bytes 524320 | tf_op jit(solution)/shard_map/ppermute | solution.py:342
  657.1 22.5 %collective-permute-done.98 = bf16[64,2048]{1,0:T(8,128)(2,1)S(1)} collective-permute-done((bf16[64,2048]{1,0:T(8,128)(2,1)S(1)}, bf16[64,2048]{1,0:T(8,128)(2,1)S(1)}, u32[]{:S(2)}, u32[]{:S(2)}) %collective-permute-start.98) | collective-permute-done | bytes 262176 | tf_op jit(solution)/shard_map/ppermute | solution.py:647
  685.4 10.0 %collective-permute-done.81 = bf16[128,2048]{1,0:T(8,128)(2,1)S(1)} collective-permute-done((bf16[128,2048]{1,0:T(8,128)(2,1)S(1)}, bf16[128,2048]{1,0:T(8,128)(2,1)S(1)}, u32[]{:S(2)}, u32[]{:S(2)}) %collective-permute-start.81) | collective-permute-done | bytes 524320 | tf_op jit(solution)/shard_map/ppermute | solution.py:342
  698.4 8.2 %collective-permute-done.88 = bf16[128,2048]{1,0:T(8,128)(2,1)S(1)} collective-permute-done((bf16[128,2048]{1,0:T(8,128)(2,1)S(1)}, bf16[128,2048]{1,0:T(8,128)(2,1)S(1)}, u32[]{:S(2)}, u32[]{:S(2)}) %collective-permute-start.88) | collective-permute-done | bytes 524320 | tf_op jit(solution)/shard_map/ppermute | solution.py:342
  707.1 10.8 %collective-permute-done.82 = bf16[128,2048]{1,0:T(8,128)(2,1)S(1)} collective-permute-done((bf16[128,2048]{1,0:T(8,128)(2,1)S(1)}, bf16[128,2048]{1,0:T(8,128)(2,1)S(1)}, u32[]{:S(2)}, u32[]{:S(2)}) %collective-permute-start.82) | collective-permute-done | bytes 524320 | tf_op jit(solution)/shard_map/ppermute | solution.py:342
  718.6 6.7 collective-permute-done.89
  733.1 4.4 collective-permute-done.94
  737.4 5.7 collective-permute-done.93
  749.1 3.9 collective-permute-done.95
  (622 shorter events, 342.7 us)
Async XLA Ops:
  0.7 75.2 %collective-permute-start = (bf16[128,2048]{1,0:T(8,128)(2,1)}, bf16[128,2048]{1,0:T(8,128)(2,1)S(1)}, u32[]{:S(2)}, u32[]{:S(2)}) collective-permute-start(bf16[128,2048]{1,0:T(8,128)(2,1)} %param.15), channel_id=1, source_target_pairs={{0,1},{1,0},{2,3},{3,2},{4,5},{5,4},{6,7},{7,6},{8,9},{9,8},{10,11... | collective-permute-start | bytes 1572872 | tf_op jit(solution)/shard_map/ppermute | solution.py:338
  3.7 76.6 %collective-permute-start.12 = (bf16[128,2048]{1,0:T(8,128)(2,1)}, bf16[128,2048]{1,0:T(8,128)(2,1)S(1)}, u32[]{:S(2)}, u32[]{:S(2)}) collective-permute-start(bf16[128,2048]{1,0:T(8,128)(2,1)} %param.15), channel_id=1, source_target_pairs={{0,2},{1,3},{2,6},{3,7},{6,4},{7,5},{4,0},{5,1},{8,10},{9,11},{10,... | collective-permute-start | bytes 1572872 | tf_op jit(solution)/shard_map/ppermute | solution.py:342
  5.2 74.6 %collective-permute-start.18 = (bf16[128,2048]{1,0:T(8,128)(2,1)}, bf16[128,2048]{1,0:T(8,128)(2,1)S(1)}, u32[]{:S(2)}, u32[]{:S(2)}) collective-permute-start(bf16[128,2048]{1,0:T(8,128)(2,1)} %param.16), channel_id=1, source_target_pairs={{0,1},{1,0},{2,3},{3,2},{4,5},{5,4},{6,7},{7,6},{8,9},{9,8},{10,11... | collective-permute-start | bytes 1572872 | tf_op jit(solution)/shard_map/ppermute | solution.py:338
  5.8 75.3 %collective-permute-start.19 = (bf16[128,2048]{1,0:T(8,128)(2,1)}, bf16[128,2048]{1,0:T(8,128)(2,1)S(1)}, u32[]{:S(2)}, u32[]{:S(2)}) collective-permute-start(bf16[128,2048]{1,0:T(8,128)(2,1)} %param.16), channel_id=1, source_target_pairs={{0,2},{1,3},{2,6},{3,7},{6,4},{7,5},{4,0},{5,1},{8,10},{9,11},{10,... | collective-permute-start | bytes 1572872 | tf_op jit(solution)/shard_map/ppermute | solution.py:342
  71.9 25.0 %collective-permute-start.26 = (bf16[128,2048]{1,0:T(8,128)(2,1)S(1)}, bf16[128,2048]{1,0:T(8,128)(2,1)S(1)}, u32[]{:S(2)}, u32[]{:S(2)}) collective-permute-start(bf16[128,2048]{1,0:T(8,128)(2,1)S(1)} %pad_maximum_fusion.34), channel_id=1, source_target_pairs={{0,16},{2,18},{4,20},{6,22},{8,24},{10,26},{12,28},{14,30},{17,1},... | collective-permute-start | bytes 1572872 | tf_op jit(solution)/shard_map/ppermute | solution.py:629
  95.9 22.5 %collective-permute-start.21 = (bf16[128,2048]{1,0:T(8,128)(2,1)S(1)}, bf16[128,2048]{1,0:T(8,128)(2,1)S(1)}, u32[]{:S(2)}, u32[]{:S(2)}) collective-permute-start(bf16[128,2048]{1,0:T(8,128)(2,1)S(1)} %collective-permute-done.19), channel_id=1, source_target_pairs={{0,2},{1,3},{2,6},{3,7},{6,4},{7,5},{4,0},{5,1},{8,10},{9,11},{10,... | collective-permute-start | bytes 1572872 | tf_op jit(solution)/shard_map/ppermute | solution.py:342
  96.9 23.6 %collective-permute-start.10 = (bf16[1536,256]{1,0:T(8,128)(2,1)S(1)}, bf16[1536,256]{1,0:T(8,128)(2,1)S(1)}, u32[]{:S(2)}, u32[]{:S(2)}) collective-permute-start(bf16[1536,256]{1,0:T(8,128)(2,1)S(1)} %get-tuple-element.217), channel_id=1, source_target_pairs={{0,16},{8,24},{16,0},{24,8},{1,17},{9,25},{17,1},{25,9},{2,18},{10... | collective-permute-start | bytes 2359304 | tf_op jit(solution)/shard_map/ppermute | solution.py:346
  120.5 49.9 %collective-permute-start.57 = (bf16[128,2048]{1,0:T(8,128)(2,1)}, bf16[128,2048]{1,0:T(8,128)(2,1)}, u32[]{:S(2)}, u32[]{:S(2)}) collective-permute-start(bf16[128,2048]{1,0:T(8,128)(2,1)} %get-tuple-element.99), channel_id=1, source_target_pairs={{0,2},{1,3},{2,6},{3,7},{6,4},{7,5},{4,0},{5,1},{8,10},{9,11},{10,... | collective-permute-start | bytes 1572872 | tf_op jit(solution)/shard_map/ppermute | solution.py:342
  124.3 63.0 %collective-permute-start.55 = (bf16[128,2048]{1,0:T(8,128)(2,1)}, bf16[128,2048]{1,0:T(8,128)(2,1)}, u32[]{:S(2)}, u32[]{:S(2)}) collective-permute-start(bf16[128,2048]{1,0:T(8,128)(2,1)} %get-tuple-element.99), channel_id=1, source_target_pairs={{0,1},{1,0},{2,3},{3,2},{4,5},{5,4},{6,7},{7,6},{8,9},{9,8},{10,11... | collective-permute-start | bytes 1572872 | tf_op jit(solution)/shard_map/ppermute | solution.py:338
  129.6 26.1 %collective-permute-start.17 = (bf16[128,2048]{1,0:T(8,128)(2,1)S(1)}, bf16[128,2048]{1,0:T(8,128)(2,1)S(1)}, u32[]{:S(2)}, u32[]{:S(2)}) collective-permute-start(bf16[128,2048]{1,0:T(8,128)(2,1)S(1)} %collective-permute-done.16), channel_id=1, source_target_pairs={{0,1},{1,0},{2,3},{3,2},{4,5},{5,4},{6,7},{7,6},{8,9},{9,8},{10,11... | collective-permute-start | bytes 1572872 | tf_op jit(solution)/shard_map/ppermute | solution.py:338
  133.2 68.6 %collective-permute-start.36 = (bf16[192,2048]{1,0:T(8,128)(2,1)}, bf16[192,2048]{1,0:T(8,128)(2,1)}, u32[]{:S(2)}, u32[]{:S(2)}) collective-permute-start(bf16[192,2048]{1,0:T(8,128)(2,1)} %pad.10), channel_id=1, source_target_pairs={{0,16},{8,24},{16,0},{24,8},{1,17},{9,25},{17,1},{25,9},{2,18},{10... | collective-permute-start | bytes 2359304 | tf_op jit(solution)/shard_map/ppermute | solution.py:346
  140.8 23.2 %collective-permute-start.24 = (bf16[128,2048]{1,0:T(8,128)(2,1)S(1)}, bf16[128,2048]{1,0:T(8,128)(2,1)S(1)}, u32[]{:S(2)}, u32[]{:S(2)}) collective-permute-start(bf16[128,2048]{1,0:T(8,128)(2,1)S(1)} %collective-permute-done.23), channel_id=1, source_target_pairs={{0,1},{1,0},{2,3},{3,2},{4,5},{5,4},{6,7},{7,6},{8,9},{9,8},{10,11... | collective-permute-start | bytes 1572872 | tf_op jit(solution)/shard_map/ppermute | solution.py:338
  155.7 48.3 %collective-permute-start.38 = (bf16[192,2048]{1,0:T(8,128)(2,1)}, bf16[192,2048]{1,0:T(8,128)(2,1)}, u32[]{:S(2)}, u32[]{:S(2)}) collective-permute-start(bf16[192,2048]{1,0:T(8,128)(2,1)} %pad.11), channel_id=1, source_target_pairs={{0,16},{8,24},{16,0},{24,8},{1,17},{9,25},{17,1},{25,9},{2,18},{10... | collective-permute-start | bytes 2359304 | tf_op jit(solution)/shard_map/ppermute | solution.py:346
  170.3 49.8 %collective-permute-start.40 = (bf16[192,2048]{1,0:T(8,128)(2,1)}, bf16[192,2048]{1,0:T(8,128)(2,1)}, u32[]{:S(2)}, u32[]{:S(2)}) collective-permute-start(bf16[192,2048]{1,0:T(8,128)(2,1)} %pad.12), channel_id=1, source_target_pairs={{0,16},{8,24},{16,0},{24,8},{1,17},{9,25},{17,1},{25,9},{2,18},{10... | collective-permute-start | bytes 2359304 | tf_op jit(solution)/shard_map/ppermute | solution.py:346
  170.7 60.3 %collective-permute-start.64 = (bf16[128,2048]{1,0:T(8,128)(2,1)}, bf16[128,2048]{1,0:T(8,128)(2,1)S(1)}, u32[]{:S(2)}, u32[]{:S(2)}) collective-permute-start(bf16[128,2048]{1,0:T(8,128)(2,1)} %collective-permute-done.57), channel_id=1, source_target_pairs={{0,1},{1,0},{2,3},{3,2},{4,5},{5,4},{6,7},{7,6},{8,9},{9,8},{10,11... | collective-permute-start | bytes 1572872 | tf_op jit(solution)/shard_map/ppermute | solution.py:338
  203.9 25.4 %collective-permute-start.58 = (bf16[128,2048]{1,0:T(8,128)(2,1)}, bf16[128,2048]{1,0:T(8,128)(2,1)S(1)}, u32[]{:S(2)}, u32[]{:S(2)}) collective-permute-start(bf16[128,2048]{1,0:T(8,128)(2,1)} %collective-permute-done.57), channel_id=1, source_target_pairs={{0,2},{1,3},{2,6},{3,7},{6,4},{7,5},{4,0},{5,1},{8,10},{9,11},{10,... | collective-permute-start | bytes 1572872 | tf_op jit(solution)/shard_map/ppermute | solution.py:342
  214.0 65.9 %collective-permute-start.37 = (bf16[384,2048]{1,0:T(8,128)(2,1)S(1)}, bf16[384,2048]{1,0:T(8,128)(2,1)S(1)}, u32[]{:S(2)}, u32[]{:S(2)}) collective-permute-start(bf16[384,2048]{1,0:T(8,128)(2,1)S(1)} %pad_maximum_fusion.6), channel_id=1, source_target_pairs={{0,8},{8,0},{16,24},{24,16},{1,9},{9,1},{17,25},{25,17},{2,10},{10... | collective-permute-start | bytes 4718600 | tf_op jit(solution)/shard_map/ppermute | solution.py:350
  244.2 22.5 %collective-permute-start.41 = (bf16[384,2048]{1,0:T(8,128)(2,1)S(1)}, bf16[384,2048]{1,0:T(8,128)(2,1)S(1)}, u32[]{:S(2)}, u32[]{:S(2)}) collective-permute-start(bf16[384,2048]{1,0:T(8,128)(2,1)S(1)} %pad_maximum_fusion.8), channel_id=1, source_target_pairs={{0,8},{8,0},{16,24},{24,16},{1,9},{9,1},{17,25},{25,17},{2,10},{10... | collective-permute-start | bytes 4718600 | tf_op jit(solution)/shard_map/ppermute | solution.py:350
  285.4 199.6 %collective-permute-start.42 = (bf16[128,2048]{1,0:T(8,128)(2,1)}, bf16[128,2048]{1,0:T(8,128)(2,1)}, u32[]{:S(2)}, u32[]{:S(2)}) collective-permute-start(bf16[128,2048]{1,0:T(8,128)(2,1)} %convolution_convert_fusion.14), channel_id=1, source_target_pairs={{0,1},{1,0},{2,3},{3,2},{4,5},{5,4},{6,7},{7,6},{8,9},{9,8},{10,11... | collective-permute-start | bytes 1572872 | tf_op jit(solution)/shard_map/ppermute | solution.py:338
  287.1 23.3 %collective-permute-start.50 = (bf16[128,2048]{1,0:T(8,128)(2,1)S(1)}, bf16[128,2048]{1,0:T(8,128)(2,1)S(1)}, u32[]{:S(2)}, u32[]{:S(2)}) collective-permute-start(bf16[128,2048]{1,0:T(8,128)(2,1)S(1)} %collective-permute-done.43), channel_id=1, source_target_pairs={{0,1},{1,0},{2,3},{3,2},{4,5},{5,4},{6,7},{7,6},{8,9},{9,8},{10,11... | collective-permute-start | bytes 1572872 | tf_op jit(solution)/shard_map/ppermute | solution.py:338
  287.4 38.7 %collective-permute-start.44 = (bf16[128,2048]{1,0:T(8,128)(2,1)S(1)}, bf16[128,2048]{1,0:T(8,128)(2,1)S(1)}, u32[]{:S(2)}, u32[]{:S(2)}) collective-permute-start(bf16[128,2048]{1,0:T(8,128)(2,1)S(1)} %collective-permute-done.43), channel_id=1, source_target_pairs={{0,2},{1,3},{2,6},{3,7},{6,4},{7,5},{4,0},{5,1},{8,10},{9,11},{10,... | collective-permute-start | bytes 1572872 | tf_op jit(solution)/shard_map/ppermute | solution.py:342
  325.7 41.0 %collective-permute-start.65 = (bf16[128,2048]{1,0:T(8,128)(2,1)S(1)}, bf16[128,2048]{1,0:T(8,128)(2,1)S(1)}, u32[]{:S(2)}, u32[]{:S(2)}) collective-permute-start(bf16[128,2048]{1,0:T(8,128)(2,1)S(1)} %fusion.45), channel_id=1, source_target_pairs={{0,1},{1,0},{2,3},{3,2},{4,5},{5,4},{6,7},{7,6},{8,9},{9,8},{10,11... | collective-permute-start | bytes 1572872 | tf_op jit(solution)/shard_map/ppermute | solution.py:338
  326.1 29.2 %collective-permute-start.48 = (bf16[128,2048]{1,0:T(8,128)(2,1)S(1)}, bf16[128,2048]{1,0:T(8,128)(2,1)S(1)}, u32[]{:S(2)}, u32[]{:S(2)}) collective-permute-start(bf16[128,2048]{1,0:T(8,128)(2,1)S(1)} %collective-permute-done.44), channel_id=1, source_target_pairs={{0,1},{1,0},{2,3},{3,2},{4,5},{5,4},{6,7},{7,6},{8,9},{9,8},{10,11... | collective-permute-start | bytes 1572872 | tf_op jit(solution)/shard_map/ppermute | solution.py:338
  327.8 46.8 %collective-permute-start.45 = (bf16[128,2048]{1,0:T(8,128)(2,1)S(1)}, bf16[128,2048]{1,0:T(8,128)(2,1)S(1)}, u32[]{:S(2)}, u32[]{:S(2)}) collective-permute-start(bf16[128,2048]{1,0:T(8,128)(2,1)S(1)} %collective-permute-done.44), channel_id=1, source_target_pairs={{0,2},{1,3},{2,6},{3,7},{6,4},{7,5},{4,0},{5,1},{8,10},{9,11},{10,... | collective-permute-start | bytes 1572872 | tf_op jit(solution)/shard_map/ppermute | solution.py:342
  337.0 38.3 %collective-permute-start.52 = (bf16[128,2048]{1,0:T(8,128)(2,1)S(1)}, bf16[128,2048]{1,0:T(8,128)(2,1)S(1)}, u32[]{:S(2)}, u32[]{:S(2)}) collective-permute-start(bf16[128,2048]{1,0:T(8,128)(2,1)S(1)} %fusion.38), channel_id=1, source_target_pairs={{0,2},{1,3},{2,6},{3,7},{6,4},{7,5},{4,0},{5,1},{8,10},{9,11},{10,... | collective-permute-start | bytes 1572872 | tf_op jit(solution)/shard_map/ppermute | solution.py:342
  375.2 67.8 %collective-permute-start.56 = (bf16[128,2048]{1,0:T(8,128)(2,1)S(1)}, bf16[128,2048]{1,0:T(8,128)(2,1)S(1)}, u32[]{:S(2)}, u32[]{:S(2)}) collective-permute-start(bf16[128,2048]{1,0:T(8,128)(2,1)S(1)} %fusion.39), channel_id=1, source_target_pairs={{0,1},{1,0},{2,3},{3,2},{4,5},{5,4},{6,7},{7,6},{8,9},{9,8},{10,11... | collective-permute-start | bytes 1572872 | tf_op jit(solution)/shard_map/ppermute | solution.py:338
  379.0 31.6 %collective-permute-start.46 = (bf16[128,2048]{1,0:T(8,128)(2,1)S(1)}, bf16[128,2048]{1,0:T(8,128)(2,1)S(1)}, u32[]{:S(2)}, u32[]{:S(2)}) collective-permute-start(bf16[128,2048]{1,0:T(8,128)(2,1)S(1)} %collective-permute-done.45), channel_id=1, source_target_pairs={{0,1},{1,0},{2,3},{3,2},{4,5},{5,4},{6,7},{7,6},{8,9},{9,8},{10,11... | collective-permute-start | bytes 1572872 | tf_op jit(solution)/shard_map/ppermute | solution.py:338
  384.3 78.6 %collective-permute-start.53 = (bf16[128,2048]{1,0:T(8,128)(2,1)}, bf16[128,2048]{1,0:T(8,128)(2,1)}, u32[]{:S(2)}, u32[]{:S(2)}) collective-permute-start(bf16[128,2048]{1,0:T(8,128)(2,1)} %fusion.37), channel_id=1, source_target_pairs={{0,2},{1,3},{2,6},{3,7},{6,4},{7,5},{4,0},{5,1},{8,10},{9,11},{10,... | collective-permute-start | bytes 1572872 | tf_op jit(solution)/shard_map/ppermute | solution.py:342
  392.4 41.7 %collective-permute-start.67 = (bf16[128,2048]{1,0:T(8,128)(2,1)S(1)}, bf16[128,2048]{1,0:T(8,128)(2,1)S(1)}, u32[]{:S(2)}, u32[]{:S(2)}) collective-permute-start(bf16[128,2048]{1,0:T(8,128)(2,1)S(1)} %fusion.42), channel_id=1, source_target_pairs={{0,2},{1,3},{2,6},{3,7},{6,4},{7,5},{4,0},{5,1},{8,10},{9,11},{10,... | collective-permute-start | bytes 1572872 | tf_op jit(solution)/shard_map/ppermute | solution.py:342
  434.1 29.3 %collective-permute-start.47 = (bf16[128,2048]{1,0:T(8,128)(2,1)}, bf16[128,2048]{1,0:T(8,128)(2,1)}, u32[]{:S(2)}, u32[]{:S(2)}) collective-permute-start(bf16[128,2048]{1,0:T(8,128)(2,1)} %convolution_convert_fusion.13), channel_id=1, source_target_pairs={{0,1},{1,0},{2,3},{3,2},{4,5},{5,4},{6,7},{7,6},{8,9},{9,8},{10,11... | collective-permute-start | bytes 1572872 | tf_op jit(solution)/shard_map/ppermute | solution.py:338
  443.0 48.4 %collective-permute-start.104 = (bf16[384,2048]{1,0:T(8,128)(2,1)}, bf16[384,2048]{1,0:T(8,128)(2,1)}, u32[]{:S(2)}, u32[]{:S(2)}) collective-permute-start(bf16[384,2048]{1,0:T(8,128)(2,1)} %convolution_convert_fusion.2), channel_id=1, source_target_pairs={{0,8},{8,0},{16,24},{24,16},{1,9},{9,1},{17,25},{25,17},{2,10},{10... | collective-permute-start | bytes 4718600 | tf_op jit(solution)/shard_map/ppermute | solution.py:350
  462.0 32.8 %collective-permute-start.106 = (bf16[384,2048]{1,0:T(8,128)(2,1)}, bf16[384,2048]{1,0:T(8,128)(2,1)S(1)}, u32[]{:S(2)}, u32[]{:S(2)}) collective-permute-start(bf16[384,2048]{1,0:T(8,128)(2,1)} %convolution_convert_fusion.1), channel_id=1, source_target_pairs={{0,8},{8,0},{16,24},{24,16},{1,9},{9,1},{17,25},{25,17},{2,10},{10... | collective-permute-start | bytes 4718600 | tf_op jit(solution)/shard_map/ppermute | solution.py:350
  485.1 23.2 %collective-permute-start.70 = (bf16[128,2048]{1,0:T(8,128)(2,1)S(1)}, bf16[128,2048]{1,0:T(8,128)(2,1)S(1)}, u32[]{:S(2)}, u32[]{:S(2)}) collective-permute-start(bf16[128,2048]{1,0:T(8,128)(2,1)S(1)} %get-tuple-element.103), channel_id=1, source_target_pairs={{0,2},{1,3},{2,6},{3,7},{6,4},{7,5},{4,0},{5,1},{8,10},{9,11},{10,... | collective-permute-start | bytes 1572872 | tf_op jit(solution)/shard_map/ppermute | solution.py:342
  506.2 35.6 %collective-permute-start.107 = (bf16[192,2048]{1,0:T(8,128)(2,1)S(1)}, bf16[192,2048]{1,0:T(8,128)(2,1)S(1)}, u32[]{:S(2)}, u32[]{:S(2)}) collective-permute-start(bf16[192,2048]{1,0:T(8,128)(2,1)S(1)} %slice.977), channel_id=1, source_target_pairs={{0,16},{8,24},{16,0},{24,8},{1,17},{9,25},{17,1},{25,9},{2,18},{10... | collective-permute-start | bytes 2359304 | tf_op jit(solution)/shard_map/ppermute | solution.py:346
  506.6 51.1 %collective-permute-start.109 = (bf16[192,2048]{1,0:T(8,128)(2,1)S(1)}, bf16[192,2048]{1,0:T(8,128)(2,1)S(1)}, u32[]{:S(2)}, u32[]{:S(2)}) collective-permute-start(bf16[192,2048]{1,0:T(8,128)(2,1)S(1)} %slice.976), channel_id=1, source_target_pairs={{0,16},{8,24},{16,0},{24,8},{1,17},{9,25},{17,1},{25,9},{2,18},{10... | collective-permute-start | bytes 2359304 | tf_op jit(solution)/shard_map/ppermute | solution.py:346
  522.1 37.0 %collective-permute-start.74 = (bf16[128,2048]{1,0:T(8,128)(2,1)S(1)}, bf16[128,2048]{1,0:T(8,128)(2,1)S(1)}, u32[]{:S(2)}, u32[]{:S(2)}) collective-permute-start(bf16[128,2048]{1,0:T(8,128)(2,1)S(1)} %collective-permute-done.72), channel_id=1, source_target_pairs={{0,2},{1,3},{2,6},{3,7},{6,4},{7,5},{4,0},{5,1},{8,10},{9,11},{10,... | collective-permute-start | bytes 1572872 | tf_op jit(solution)/shard_map/ppermute | solution.py:342
  523.0 37.6 %collective-permute-start.73 = (bf16[128,2048]{1,0:T(8,128)(2,1)S(1)}, bf16[128,2048]{1,0:T(8,128)(2,1)S(1)}, u32[]{:S(2)}, u32[]{:S(2)}) collective-permute-start(bf16[128,2048]{1,0:T(8,128)(2,1)S(1)} %collective-permute-done.72), channel_id=1, source_target_pairs={{0,1},{1,0},{2,3},{3,2},{4,5},{5,4},{6,7},{7,6},{8,9},{9,8},{10,11... | collective-permute-start | bytes 1572872 | tf_op jit(solution)/shard_map/ppermute | solution.py:338
  597.1 39.1 %collective-permute-start.78 = (bf16[128,2048]{1,0:T(8,128)(2,1)S(1)}, bf16[128,2048]{1,0:T(8,128)(2,1)S(1)}, u32[]{:S(2)}, u32[]{:S(2)}) collective-permute-start(bf16[128,2048]{1,0:T(8,128)(2,1)S(1)} %convolution_convert_fusion.8), channel_id=1, source_target_pairs={{0,1},{1,0},{2,3},{3,2},{4,5},{5,4},{6,7},{7,6},{8,9},{9,8},{10,11... | collective-permute-start | bytes 1572872 | tf_op jit(solution)/shard_map/ppermute | solution.py:338
  597.7 35.3 %collective-permute-start.86 = (bf16[128,2048]{1,0:T(8,128)(2,1)S(1)}, bf16[128,2048]{1,0:T(8,128)(2,1)S(1)}, u32[]{:S(2)}, u32[]{:S(2)}) collective-permute-start(bf16[128,2048]{1,0:T(8,128)(2,1)S(1)} %convolution_convert_fusion.3), channel_id=1, source_target_pairs={{0,1},{1,0},{2,3},{3,2},{4,5},{5,4},{6,7},{7,6},{8,9},{9,8},{10,11... | collective-permute-start | bytes 1572872 | tf_op jit(solution)/shard_map/ppermute | solution.py:338
  599.1 50.5 %collective-permute-start.85 = (bf16[128,2048]{1,0:T(8,128)(2,1)S(1)}, bf16[128,2048]{1,0:T(8,128)(2,1)S(1)}, u32[]{:S(2)}, u32[]{:S(2)}) collective-permute-start(bf16[128,2048]{1,0:T(8,128)(2,1)S(1)} %convolution_convert_fusion.4), channel_id=1, source_target_pairs={{0,1},{1,0},{2,3},{3,2},{4,5},{5,4},{6,7},{7,6},{8,9},{9,8},{10,11... | collective-permute-start | bytes 1572872 | tf_op jit(solution)/shard_map/ppermute | solution.py:338
  604.3 77.3 %collective-permute-start.90 = (bf16[1024,768]{0,1:T(8,128)(2,1)S(1)}, bf16[1024,768]{0,1:T(8,128)(2,1)S(1)}, u32[]{:S(2)}, u32[]{:S(2)}) collective-permute-start(bf16[1024,768]{0,1:T(8,128)(2,1)S(1)} %maximum_maximum_fusion), channel_id=1, source_target_pairs={{0,8},{8,0},{16,24},{24,16},{1,9},{9,1},{17,25},{25,17},{2,10},{10... | collective-permute-start | bytes 4718600 | tf_op jit(solution)/shard_map/ppermute | solution.py:350
  610.5 24.7 %collective-permute-start.97 = (bf16[128,2048]{1,0:T(8,128)(2,1)S(1)}, bf16[128,2048]{1,0:T(8,128)(2,1)S(1)}, u32[]{:S(2)}, u32[]{:S(2)}) collective-permute-start(bf16[128,2048]{1,0:T(8,128)(2,1)S(1)} %fusion.123), channel_id=1, source_target_pairs={{1,17},{3,19},{5,21},{7,23},{9,25},{11,27},{13,29},{15,31},{16,0},... | collective-permute-start | bytes 1572872 | tf_op jit(solution)/shard_map/ppermute | solution.py:641
  636.3 48.5 %collective-permute-start.77 = (bf16[128,2048]{1,0:T(8,128)(2,1)S(1)}, bf16[128,2048]{1,0:T(8,128)(2,1)S(1)}, u32[]{:S(2)}, u32[]{:S(2)}) collective-permute-start(bf16[128,2048]{1,0:T(8,128)(2,1)S(1)} %convolution_convert_fusion.9), channel_id=1, source_target_pairs={{0,1},{1,0},{2,3},{3,2},{4,5},{5,4},{6,7},{7,6},{8,9},{9,8},{10,11... | collective-permute-start | bytes 1572872 | tf_op jit(solution)/shard_map/ppermute | solution.py:338
  648.1 59.0 %collective-permute-start.76 = (bf16[128,2048]{1,0:T(8,128)(2,1)S(1)}, bf16[128,2048]{1,0:T(8,128)(2,1)S(1)}, u32[]{:S(2)}, u32[]{:S(2)}) collective-permute-start(bf16[128,2048]{1,0:T(8,128)(2,1)S(1)} %convolution_convert_fusion.10), channel_id=1, source_target_pairs={{0,1},{1,0},{2,3},{3,2},{4,5},{5,4},{6,7},{7,6},{8,9},{9,8},{10,11... | collective-permute-start | bytes 1572872 | tf_op jit(solution)/shard_map/ppermute | solution.py:338
  649.6 46.3 %collective-permute-start.84 = (bf16[128,2048]{1,0:T(8,128)(2,1)S(1)}, bf16[128,2048]{1,0:T(8,128)(2,1)S(1)}, u32[]{:S(2)}, u32[]{:S(2)}) collective-permute-start(bf16[128,2048]{1,0:T(8,128)(2,1)S(1)} %convolution_convert_fusion.5), channel_id=1, source_target_pairs={{0,1},{1,0},{2,3},{3,2},{4,5},{5,4},{6,7},{7,6},{8,9},{9,8},{10,11... | collective-permute-start | bytes 1572872 | tf_op jit(solution)/shard_map/ppermute | solution.py:338
  653.7 26.0 %collective-permute-start.98 = (bf16[64,2048]{1,0:T(8,128)(2,1)S(1)}, bf16[64,2048]{1,0:T(8,128)(2,1)S(1)}, u32[]{:S(2)}, u32[]{:S(2)}) collective-permute-start(bf16[64,2048]{1,0:T(8,128)(2,1)S(1)} %dynamic-slice_convert_fusion.1), channel_id=1, source_target_pairs={{0,1},{2,3},{4,5},{6,7},{8,9},{10,11},{12,13},{14,15},{17,16},{19,... | collective-permute-start | bytes 786440 | tf_op jit(solution)/shard_map/ppermute | solution.py:647
  681.6 37.0 %collective-permute-start.83 = (bf16[128,2048]{1,0:T(8,128)(2,1)S(1)}, bf16[128,2048]{1,0:T(8,128)(2,1)S(1)}, u32[]{:S(2)}, u32[]{:S(2)}) collective-permute-start(bf16[128,2048]{1,0:T(8,128)(2,1)S(1)} %convolution_convert_fusion.6), channel_id=1, source_target_pairs={{0,1},{1,0},{2,3},{3,2},{4,5},{5,4},{6,7},{7,6},{8,9},{9,8},{10,11... | collective-permute-start | bytes 1572872 | tf_op jit(solution)/shard_map/ppermute | solution.py:338
  696.0 31.7 %collective-permute-start.91 = (bf16[512,768]{0,1:T(8,128)(2,1)S(1)}, bf16[512,768]{0,1:T(8,128)(2,1)S(1)}, u32[]{:S(2)}, u32[]{:S(2)}) collective-permute-start(bf16[512,768]{0,1:T(8,128)(2,1)S(1)} %pad_maximum_fusion.28), channel_id=1, source_target_pairs={{0,16},{8,24},{16,0},{24,8},{1,17},{9,25},{17,1},{25,9},{2,18},{10... | collective-permute-start | bytes 2359304 | tf_op jit(solution)/shard_map/ppermute | solution.py:346
  (149 other events, 2430.9 us)

commit v2 on v0

--- a/solution.py
+++ b/solution.py
@@ -1,8 +1,11 @@
+import functools
 import math
 
 import jax
 import jax.numpy as jnp
 from jax import lax
+from jax.experimental import pallas as pl
+from jax.experimental.pallas import tpu as pltpu
 from jax.sharding import PartitionSpec as P
 
 HEADS = 16
@@ -317,6 +320,917 @@
     )
 
 
+RING = (0, 1, 3, 2)
+BLOCK = 256
+
+
+def swap_pairs(size, mask):
+    return [(place, place ^ mask) for place in range(size)]
+
+
+def ring_pairs():
+    return [
+        (2 * RING[place] + x, 2 * RING[(place + 1) % 4] + x) for place in range(4) for x in range(2)
+    ]
+
+
+def x_swap(value):
+    return lax.ppermute(value, "fsdp", swap_pairs(8, 1))
+
+
+def ring_step(value):
+    return lax.ppermute(value, "fsdp", ring_pairs())
+
+
+def y_swap(value):
+    return lax.ppermute(value, "dp", swap_pairs(4, 2))
+
+
+def core_swap(value):
+    return lax.ppermute(value, "dp", swap_pairs(4, 1))
+
+
+def in_order(flag, first, second):
+    swapped = flag == 1
+    return jnp.concatenate(
+        [jnp.where(swapped, second, first), jnp.where(swapped, first, second)], axis=0
+    )
+
+
+def after(value, *earlier):
+    if not earlier:
+        return value
+    return lax.optimization_barrier((value, *earlier))[0]
+
+
+class Gather:
+    def __init__(self, own):
+        self.held = own
+        self.pieces = []
+
+    def send(self):
+        if len(self.pieces) < 3:
+            return self.held, self.held
+        half = self.held.shape[0] // 2
+        return self.held[:half], self.pieces[2][1][half:]
+
+    def take(self, from_x, from_ring):
+        if len(self.pieces) < 3:
+            self.pieces.append((self.held, from_x))
+            self.held = from_ring
+        else:
+            self.pieces.append((self.held, from_x, from_ring))
+
+    def piece(self, step):
+        return jnp.concatenate(self.pieces[step], axis=0)
+
+
+class Scatter:
+    def __init__(self):
+        self.kept = []
+        self.got = None
+        self.terms = None
+
+    def of(self, terms):
+        self.terms = terms
+        return self
+
+    def send(self):
+        terms = self.terms
+        rows = terms.shape[0] // 2
+        half = rows // 2
+        if not self.kept:
+            self.kept.append(terms[:rows])
+            return terms[rows : rows + half], terms[rows + half :]
+        if len(self.kept) == 1:
+            from_x, from_ring = self.got
+            total = jnp.concatenate(
+                [
+                    self.kept[0][:half].astype(jnp.float32) + from_x.astype(jnp.float32),
+                    self.kept[0][half:].astype(jnp.float32),
+                ],
+                axis=0,
+            )
+            given = jnp.concatenate(
+                [
+                    terms[rows : rows + half].astype(jnp.float32),
+                    terms[rows + half :].astype(jnp.float32) + from_ring.astype(jnp.float32),
+                ],
+                axis=0,
+            ).astype(jnp.bfloat16)
+        else:
+            total, given = self.total(), terms[rows:]
+        self.kept.append(terms[:rows])
+        return given, total.astype(jnp.bfloat16)
+
+    def take(self, from_x, from_ring):
+        self.got = (from_x, from_ring)
+
+    def total(self):
+        from_x, from_ring = self.got
+        return (
+            self.kept[-1].astype(jnp.float32)
+            + from_x.astype(jnp.float32)
+            + from_ring.astype(jnp.float32)
+        )
+
+
+def move(parts, *gate):
+    sent = [part.send() for part in parts]
+    along_x, along_ring = (
+        values[0] if len(values) == 1 else jnp.concatenate(values, axis=0) for values in zip(*sent)
+    )
+    along_x, along_ring = after((along_x, along_ring), *gate)
+    from_x, from_ring = x_swap(along_x), ring_step(along_ring)
+    x_row = ring_row = 0
+    for part, (given_x, given_ring) in zip(parts, sent):
+        x_end, ring_end = x_row + given_x.shape[0], ring_row + given_ring.shape[0]
+        part.take(from_x[x_row:x_end], from_ring[ring_row:ring_end])
+        x_row, ring_row = x_end, ring_end
+    return [from_x, from_ring]
+
+
+def attend_kernel(
+    factor, q_ref, k_ref, v_ref, first_ref, last_ref, place_ref, att_ref, low_ref, lse_ref
+):
+    scores = rows_by_rows(q_ref[...], k_ref[...]) * factor
+    places = place_ref[...]
+    allowed = (places >= first_ref[...]) & (places <= last_ref[...])
+    masked = jnp.where(allowed, scores, MASKED)
+    largest = jnp.max(masked, axis=-1, keepdims=True)
+    raised = jnp.exp(masked - largest)
+    summed = jnp.sum(raised, axis=-1, keepdims=True)
+    probs_low = (raised * (1.0 / summed)).astype(jnp.bfloat16)
+    attended = product(probs_low, v_ref[...])
+    att_ref[...] = attended
+    low_ref[...] = attended.astype(jnp.bfloat16)
+    lse_ref[...] = (largest + jnp.log(summed))[None]
+
+
+def attend_back_kernel(
+    factor,
+    q_ref,
+    k_ref,
+    v_ref,
+    first_ref,
+    last_ref,
+    place_ref,
+    lse_ref,
+    att_ref,
+    d_att_ref,
+    dq_ref,
+    dkv_ref,
+    dk_sum,
+    dv_sum,
+):
+    head = pl.program_id(0)
+    step = pl.program_id(1)
+    size = q_ref.shape[1]
+    mine = dkv_ref.shape[1] // 2
+
+    @pl.when(step == 0)
+    def _():
+        dk_sum[...] = jnp.zeros_like(dk_sum)
+        dv_sum[...] = jnp.zeros_like(dv_sum)
+
+    queries = q_ref[...]
+    keys = k_ref[...]
+    d_att = d_att_ref[...]
+    scores = rows_by_rows(queries, keys) * factor
+    places = place_ref[...]
+    allowed = (places >= first_ref[...]) & (places <= last_ref[...])
+    probs = jnp.exp(jnp.where(allowed, scores, MASKED) - lse_ref[0])
+    delta = jnp.sum(d_att.astype(jnp.float32) * att_ref[...], axis=-1, keepdims=True)
+    d_probs = rows_by_rows(d_att, v_ref[...])
+    d_scores = (probs * (d_probs - delta)).astype(jnp.bfloat16)
+    dq_ref[...] = (product(d_scores, keys) * factor).astype(jnp.bfloat16)
+    dk_sum[...] += columns_by_columns(d_scores, queries)
+    dv_sum[...] += columns_by_columns(probs.astype(jnp.bfloat16), d_att)
+
+    @pl.when(step == pl.num_programs(1) - 1)
+    def _():
+        first = pl.multiple_of(size * head, size)
+        dkv_ref[:, pl.ds(first, size)] = (dk_sum[...] * factor).astype(jnp.bfloat16)
+        dkv_ref[:, pl.ds(mine + first, size)] = dv_sum[...].astype(jnp.bfloat16)
+
+
+def attend_specs(count, head):
+    by_query = pl.BlockSpec((BLOCK, head), lambda h, i: (i, h))
+    keys = pl.BlockSpec((count, head), lambda h, i: (0, h))
+    values = pl.BlockSpec((count, head), lambda h, i: (0, 2 + h))
+    bound = pl.BlockSpec((BLOCK, 1), lambda h, i: (i, 0))
+    place = pl.BlockSpec((1, count), lambda h, i: (0, 0))
+    lse = pl.BlockSpec((1, BLOCK, 1), lambda h, i: (h, i, 0))
+    return by_query, keys, values, bound, place, lse
+
+
+def attend(queries, pairs, first, last, place, head):
+    count, width = queries.shape
+    by_query, keys, values, bound, places, lse = attend_specs(count, head)
+    return pl.pallas_call(
+        functools.partial(attend_kernel, 1.0 / math.sqrt(head)),
+        grid=(width // head, count // BLOCK),
+        in_specs=[by_query, keys, values, bound, bound, places],
+        out_specs=[by_query, by_query, lse],
+        out_shape=[
+            jax.ShapeDtypeStruct((count, width), jnp.float32),
+            jax.ShapeDtypeStruct((count, width), jnp.bfloat16),
+            jax.ShapeDtypeStruct((width // head, count, 1), jnp.float32),
+        ],
+        compiler_params=pltpu.CompilerParams(vmem_limit_bytes=40 * 2**20),
+        cost_estimate=pl.CostEstimate(
+            flops=count * count, bytes_accessed=count * width, transcendentals=0
+        ),
+        name="attend",
+    )(queries, pairs, pairs, first, last, place)
+
+
+def attend_back(queries, pairs, first, last, place, lse, attended, d_attended, head):
+    count, width = queries.shape
+    by_query, keys, values, bound, places, by_lse = attend_specs(count, head)
+    return pl.pallas_call(
+        functools.partial(attend_back_kernel, 1.0 / math.sqrt(head)),
+        grid=(width // head, count // BLOCK),
+        in_specs=[
+            by_query,
+            keys,
+            values,
+            bound,
+            bound,
+            places,
+            by_lse,
+            by_query,
+            by_query,
+        ],
+        out_specs=[by_query, pl.BlockSpec((count, 2 * width), lambda h, i: (0, 0))],
+        out_shape=[
+            jax.ShapeDtypeStruct((count, width), jnp.bfloat16),
+            jax.ShapeDtypeStruct((count, 2 * width), jnp.bfloat16),
+        ],
+        scratch_shapes=[pltpu.VMEM((count, head), jnp.float32)] * 2,
+        compiler_params=pltpu.CompilerParams(vmem_limit_bytes=40 * 2**20),
+        cost_estimate=pl.CostEstimate(
+            flops=count * count, bytes_accessed=count * width, transcendentals=0
+        ),
+        name="attend_back",
+    )(queries, pairs, pairs, first, last, place, lse, attended, d_attended)
+
+
+def as_rows(values, columns):
+    rows = 8 * -(-values.shape[0] // (8 * columns))
+    return jnp.pad(values, (0, rows * columns - values.shape[0])).reshape(rows, columns)
+
+
+def from_rows(rows, count):
+    return rows.reshape(-1)[:count]
+
+
+def heads_of(device, head):
+    z, x = device // 2, device % 2
+    return [slice(head * (8 * x + 4 * j + z), head * (8 * x + 4 * j + z + 1)) for j in range(2)]
+
+
+def columns_kernel(dp_ref, held_ref, q_ref, kv_ref, gain_ref):
+    each = q_ref.shape[0] // 8
+    mine = q_ref.shape[1]
+    rows = held_ref.shape[2] // 8
+    for device in range(8):
+        first = rows * device
+        here = slice(each * device, each * (device + 1))
+        q_ref[here, :] = held_ref[0, 0, first : first + each, :]
+        kv_ref[here, :mine] = held_ref[0, 0, first + each : first + 2 * each, :]
+        kv_ref[here, mine:] = held_ref[0, 0, first + 2 * each : first + 3 * each, :]
+        extra = rows - 3 * each
+        gain_ref[0, extra * device : extra * (device + 1), :] = held_ref[
+            0, 0, first + 3 * each : first + rows, :
+        ]
+
+
+def payload_kernel(q_ref, k_ref, v_ref, gain_ref, out_ref):
+    each = q_ref.shape[0]
+    head = q_ref.shape[1] // 16
+    rows = out_ref.shape[0] // 8
+    for device in range(8):
+        for which, w_ref in enumerate((q_ref, k_ref, v_ref)):
+            first = rows * device + each * which
+            for j, columns in enumerate(heads_of(device, head)):
+                out_ref[first : first + each, head * j : head * (j + 1)] = w_ref[:, columns]
+        out_ref[rows * device + 3 * each : rows * (device + 1), :] = gain_ref[...]
+
+
+class Columns:
+    def __init__(self, weights, gains, dp):
+        self.weights, self.gains, self.dp = weights, gains, dp
+
+    def along_fsdp(self, *gate):
+        each, width = self.weights[0].shape
+        extra = as_rows(self.gains, width // 8)
+        given = pl.pallas_call(
+            payload_kernel,
+            out_shape=jax.ShapeDtypeStruct(
+                (8 * (3 * each + extra.shape[0]), width // 8), self.weights[0].dtype
+            ),
+            compiler_params=pltpu.CompilerParams(vmem_limit_bytes=16 * 2**20),
+            cost_estimate=pl.CostEstimate(flops=0, bytes_accessed=2**20, transcendentals=0),
+            name="payload",
+        )(*self.weights, extra)
+        self.held = lax.all_to_all(after(given, *gate), "fsdp", 0, 0, tiled=True)
+        return [self.held]
+
+    def along_y(self, *gate):
+        held = after(self.held, *gate)
+        got, other = y_swap(held), core_swap(held)
+        self.held = [held, got, other]
+        return [got, other]
+
+    def along_core(self, *gate):
+        held, got, other = after(tuple(self.held), *gate)
+        last = core_swap(got)
+        self.held = jnp.stack([held, got, other, last]).reshape(2, 2, *held.shape)
+        return [last]
+
+    def whole(self):
+        each, width = self.weights[0].shape
+        rows, mine = self.held.shape[2:]
+        extra = rows - 24 * each
+        block = 8 * each
+        low = self.held.dtype
+        wq, w_kv, gains = pl.pallas_call(
+            columns_kernel,
+            grid_spec=pltpu.PrefetchScalarGridSpec(
+                num_scalar_prefetch=1,
+                grid=(4,),
+                in_specs=[
+                    pl.BlockSpec(
+                        (1, 1, rows, mine),
+                        lambda i, dp: ((dp[0] ^ i) % 2, (dp[0] ^ i) // 2, 0, 0),
+                    )
+                ],
+                out_specs=[
+                    pl.BlockSpec((block, mine), lambda i, dp: (i, 0)),
+                    pl.BlockSpec((block, 2 * mine), lambda i, dp: (i, 0)),
+                    pl.BlockSpec((1, extra, mine), lambda i, dp: (i, 0, 0)),
+                ],
+            ),
+            out_shape=[
+                jax.ShapeDtypeStruct((4 * block, mine), low),
+                jax.ShapeDtypeStruct((4 * block, 2 * mine), low),
+                jax.ShapeDtypeStruct((4, extra, mine), low),
+            ],
+            compiler_params=pltpu.CompilerParams(vmem_limit_bytes=32 * 2**20),
+            cost_estimate=pl.CostEstimate(flops=0, bytes_accessed=2**20, transcendentals=0),
+            name="columns",
+        )(self.dp.reshape(1).astype(jnp.int32), self.held)
+        gains = gains.reshape(32, -1)[:, : self.gains.shape[0]].astype(jnp.float32)
+        return wq, w_kv, gains
+
+
+def column_grads_kernel(dp_ref, *refs):
+    sources, hiddens = refs[:4], refs[4:8]
+    dq_ref, dkv_ref, given_ref, kept_ref = refs[8:]
+    count = sources[0].shape[0]
+    mine = dq_ref.shape[1]
+    for_q, for_kv = 0.0, 0.0
+    for step in range(4):
+        here = slice(count * step, count * (step + 1))
+        for_q = for_q + columns_by_columns(hiddens[step][...], dq_ref[here, :])
+        for_kv = for_kv + columns_by_columns(sources[step][...], dkv_ref[here, :])
+
+    @pl.when(pl.program_id(0) < 2)
+    def _():
+        given_ref[0, :, :mine] = for_q.astype(jnp.bfloat16)
+        given_ref[0, :, mine:] = for_kv.astype(jnp.bfloat16)
+
+    @pl.when(pl.program_id(0) >= 2)
+    def _():
+        kept_ref[0, :, :mine] = for_q
+        kept_ref[0, :, mine:] = for_kv
+
+
+def own_grads_kernel(got_ref, wq_ref, wk_ref, wv_ref, q_ref, k_ref, v_ref, q_sum_ref, kv_sum_ref):
+    each = wq_ref.shape[0]
+    head = wq_ref.shape[1] // 16
+    sums = []
+    for which, (w_ref, out_ref) in enumerate(((wq_ref, q_ref), (wk_ref, k_ref), (wv_ref, v_ref))):
+        total = jnp.zeros((each, head), jnp.float32)
+        for device in range(8):
+            for j, columns in enumerate(heads_of(device, head)):
+                first = head * (2 * which + j)
+                grad = got_ref[device, :each, first : first + head].astype(jnp.float32)
+                out_ref[:, columns] = grad
+                total = total + grad * w_ref[:, columns].astype(jnp.float32)
+        sums.append(jnp.sum(total, axis=1, keepdims=True))
+    q_sum_ref[...] = sums[0]
+    kv_sum_ref[...] = sums[1] + sums[2]
+
+
+FREE = pl.CostEstimate(flops=0, bytes_accessed=0, transcendentals=0)
+
+
+def whole_block(array):
+    return pl.BlockSpec(array.shape, lambda *place: (0,) * array.ndim)
+
+
+def project_kernel(held_ref, *refs):
+    others = refs[:-8]
+    kv_gain_ref, attn_gain_ref, w_kv_ref, wq_ref, src_ref, hid_ref, pair_ref, query_ref = refs[-8:]
+    rows = src_ref.shape[0] // 2
+
+    def other_rows(which):
+        if len(others) == 1:
+            return others[0][rows * which : rows * (which + 1), :]
+        return others[which][...]
+
+    for which, gain_ref, w_ref, low_ref, out_ref in (
+        (0, kv_gain_ref, w_kv_ref, src_ref, pair_ref),
+        (1, attn_gain_ref, wq_ref, hid_ref, query_ref),
+    ):
+        for side in range(2):
+            here = slice(rows * side, rows * (side + 1))
+            values = other_rows(which) if side else held_ref[rows * which : rows * (which + 1), :]
+            values = values.astype(jnp.float32)
+            low_ref[here, :] = (values * inverse_scale(values) * gain_ref[...]).astype(jnp.bfloat16)
+        out_ref[...] = product(low_ref[...], w_ref[...]).astype(jnp.bfloat16)
+
+
+def project(piece, kv_gain, attn_gain, w_kv, wq):
+    rows, width = piece[0].shape
+    low = piece[0].dtype
+    return pl.pallas_call(
+        project_kernel,
+        out_shape=[
+            jax.ShapeDtypeStruct((rows, width), low),
+            jax.ShapeDtypeStruct((rows, width), low),
+            jax.ShapeDtypeStruct((rows, w_kv.shape[1]), low),
+            jax.ShapeDtypeStruct((rows, wq.shape[1]), low),
+        ],
+        compiler_params=pltpu.CompilerParams(vmem_limit_bytes=40 * 2**20),
+        cost_estimate=FREE,
+        name="project",
+    )(*piece, kv_gain, attn_gain, w_kv, wq)
+
+
+def input_terms_kernel(pair_ref, query_ref, w_kv_ref, wq_ref, src_ref, hid_ref):
+    src_ref[...] = rows_by_rows(pair_ref[...], w_kv_ref[...]).astype(jnp.bfloat16)
+    hid_ref[...] = rows_by_rows(query_ref[...], wq_ref[...]).astype(jnp.bfloat16)
+
+
+def input_terms(step, d_pairs, d_queries, w_kv, wq):
+    rows, width = d_pairs.shape[0] // 4, w_kv.shape[0]
+    out = jax.ShapeDtypeStruct((rows, width), jnp.bfloat16)
+    out_spec = pl.BlockSpec((rows, width), lambda i: (0, 0))
+    return pl.pallas_call(
+        input_terms_kernel,
+        grid=(1,),
+        in_specs=[
+            pl.BlockSpec((rows, d_pairs.shape[1]), lambda i: (step, 0)),
+            pl.BlockSpec((rows, d_queries.shape[1]), lambda i: (step, 0)),
+            whole_block(w_kv),
+            whole_block(wq),
+        ],
+        out_specs=[out_spec, out_spec],
+        out_shape=[out, out],
+        compiler_params=pltpu.CompilerParams(vmem_limit_bytes=40 * 2**20),
+        cost_estimate=FREE,
+        name="input_terms",
+    )(d_pairs, d_queries, w_kv, wq)
+
+
+def add_kernel(*refs):
+    count = len(refs) // 3
+    for kept_ref, got_ref, out_ref in zip(refs[:count], refs[count : 2 * count], refs[2 * count :]):
+        rows = out_ref.shape[0]
+        out_ref[...] = kept_ref[:rows, :] + got_ref[:rows, :].astype(jnp.float32)
+
+
+def add_all(kept, got, rows):
+    width = kept[0].shape[1]
+    block = width // 4
+    count = len(kept)
+    spec = pl.BlockSpec((kept[0].shape[0], block), lambda i: (0, i))
+    return pl.pallas_call(
+        add_kernel,
+        grid=(4,),
+        in_specs=[spec] * (2 * count),
+        out_specs=[pl.BlockSpec((rows, block), lambda i: (0, i))] * count,
+        out_shape=[jax.ShapeDtypeStruct((rows, width), jnp.float32)] * count,
+        compiler_params=pltpu.CompilerParams(vmem_limit_bytes=40 * 2**20),
+        cost_estimate=FREE,
+        name="add_all",
+    )(*kept, *got)
+
+
+def copy_kernel(dp_ref, in_ref, out_ref):
+    out_ref[...] = in_ref[...]
+
+
+def own_first(rows, dp):
+    block = (rows.shape[0] // 4, rows.shape[1])
+    return pl.pallas_call(
+        copy_kernel,
+        grid_spec=pltpu.PrefetchScalarGridSpec(
+            num_scalar_prefetch=1,
+            grid=(4,),
+            in_specs=[pl.BlockSpec(block, lambda i, dp: (dp[0] ^ (2 * (i % 2) + i // 2), 0))],
+            out_specs=pl.BlockSpec(block, lambda i, dp: (i, 0)),
+        ),
+        out_shape=jax.ShapeDtypeStruct(rows.shape, rows.dtype),
+        compiler_params=pltpu.CompilerParams(vmem_limit_bytes=16 * 2**20),
+        cost_estimate=FREE,
+        name="own_first",
+    )(dp.reshape(1).astype(jnp.int32), rows)
+
+
+class ColumnGrads:
+    def __init__(self, dp):
+        self.dp = dp
+        self.y, self.c = dp // 2, dp % 2
+
+    def gain_core(self, gain, *gate):
+        gain = gain.reshape(2, 2, -1)
+        kept = lax.dynamic_index_in_dim(gain, self.c, 1, keepdims=False)
+        given = lax.dynamic_index_in_dim(gain, 1 - self.c, 1, keepdims=False)
+        self.gain = kept + core_swap(after(given, *gate))
+        return [given]
+
+    def gain_y(self, *gate):
+        gain = after(self.gain, *gate)
+        kept = lax.dynamic_index_in_dim(gain, self.y, 0, keepdims=False)
+        given = lax.dynamic_index_in_dim(gain, 1 - self.y, 0, keepdims=False)
+        self.gain = kept + y_swap(given)
+        return [given]
+
+    def along_core(self, sources, hiddens, d_queries, d_pairs):
+        count, width = sources[0].shape
+        block = width // 4
+        mine = d_queries.shape[1]
+        rows = d_queries.shape[0]
+
+        def of_step(i):
+            return 2 * (i % 2) + 1 - i // 2
+
+        by_block = pl.BlockSpec((count, block), lambda i, dp: (0, dp[0] ^ of_step(i)))
+        given, self.kept = pl.pallas_call(
+            column_grads_kernel,
+            grid_spec=pltpu.PrefetchScalarGridSpec(
+                num_scalar_prefetch=1,
+                grid=(4,),
+                in_specs=[by_block] * 8
+                + [
+                    pl.BlockSpec((rows, mine), lambda i, dp: (0, 0)),
+                    pl.BlockSpec((rows, 2 * mine), lambda i, dp: (0, 0)),
+                ],
+                out_specs=[
+                    pl.BlockSpec((1, block, 3 * mine), lambda i, dp: (jnp.minimum(i, 1), 0, 0)),
+                    pl.BlockSpec((1, block, 3 * mine), lambda i, dp: (jnp.maximum(i, 2) - 2, 0, 0)),
+                ],
+            ),
+            out_shape=[
+                jax.ShapeDtypeStruct((2, block, 3 * mine), jnp.bfloat16),
+                jax.ShapeDtypeStruct((2, block, 3 * mine), jnp.float32),
+            ],
+            compiler_params=pltpu.CompilerParams(vmem_limit_bytes=40 * 2**20),
+            cost_estimate=pl.CostEstimate(
+                flops=rows * width, bytes_accessed=2**20, transcendentals=0
+            ),
+            name="column_grads",
+        )(self.dp.reshape(1).astype(jnp.int32), *sources, *hiddens, d_queries, d_pairs)
+        self.from_core = core_swap(given)
+        return [given]
+
+    def along_y(self, *gate):
+        given = self.kept[1] + after(self.from_core, *gate)[1].astype(jnp.float32)
+        given = given.astype(jnp.bfloat16)
+        self.from_y = y_swap(given)
+        return [given]
+
+    def along_fsdp(self, *gate):
+        total = self.kept[0] + self.from_core[0].astype(jnp.float32)
+        total = (total + after(self.from_y, *gate).astype(jnp.float32)).astype(jnp.bfloat16)
+        each, columns = total.shape[0] // 8, total.shape[1]
+        gain = self.gain.astype(jnp.bfloat16).reshape(8, 1, each)
+        gain = jnp.pad(gain, ((0, 0), (0, 7), (0, columns - each)))
+        given = jnp.concatenate([total.reshape(8, each, columns), gain], axis=1)
+        self.got = lax.all_to_all(given, "fsdp", 0, 0, tiled=True)
+        return [given], [self.got]
+
+    def whole(self, weights, *gate):
+        each, width = weights[0].shape
+        got = after(self.got, *gate)
+        flat = jax.ShapeDtypeStruct((each, width), jnp.float32)
+        column = jax.ShapeDtypeStruct((each, 1), jnp.float32)
+        out = pl.pallas_call(
+            own_grads_kernel,
+            out_shape=[flat, flat, flat, column, column],
+            compiler_params=pltpu.CompilerParams(vmem_limit_bytes=32 * 2**20),
+            cost_estimate=pl.CostEstimate(flops=0, bytes_accessed=2**20, transcendentals=0),
+            name="own_grads",
+        )(got, *weights)
+        gain = jnp.sum(got[:, each, :each].astype(jnp.float32), axis=0)
+        return out, gain
+
+
+def out_rows(own, x, y, c, before, late):
+    head = in_order(x, own, x_swap(own))
+    pairs = [(place, place ^ 16) for place in range(32) if place // 16 == place % 2]
+    got = lax.ppermute(after(head, *before), ("dp", "fsdp"), pairs)
+    mine = jnp.where(x == y, head, after(got, *late))
+    return in_order(c, mine, core_swap(mine))
+
+
+class OutGrads:
+    def __init__(self, grad, x, y, c):
+        self.grad, self.x, self.y, self.c = grad, x, y, c
+
+    def along_core(self, *gate):
+        head, width = self.grad.shape[0] // 2, self.grad.shape[1]
+        kept = lax.dynamic_slice(self.grad, (head * self.c, 0), (head, width))
+        given = lax.dynamic_slice(self.grad, (head * (1 - self.c), 0), (head, width))
+        given = after(given.astype(jnp.bfloat16), *gate)
+        self.total = kept + core_swap(given).astype(jnp.float32)
+        return [given]
+
+    def along_y(self, *gate):
+        pairs = [(place, place ^ 16) for place in range(32) if place // 16 != place % 2]
+        given = after(self.total.astype(jnp.bfloat16), *gate)
+        self.from_y = lax.ppermute(given, ("dp", "fsdp"), pairs)
+        return [given]
+
+    def along_x(self, *gate):
+        total = self.total + after(self.from_y, *gate).astype(jnp.float32)
+        each, width = total.shape[0] // 2, total.shape[1]
+        self.kept = lax.dynamic_slice(total, (each * self.x, 0), (each, width))
+        given = lax.dynamic_slice(total, (each * (1 - self.x), 0), (each, width))
+        pairs = [(place, place ^ 1) for place in range(32) if place // 16 == place % 2]
+        self.from_x = lax.ppermute(given.astype(jnp.bfloat16), ("dp", "fsdp"), pairs)
+
+    def whole(self, *gate):
+        got = after(self.from_x, *gate)
+        return jnp.where(self.x == self.y, self.kept, got.astype(jnp.float32))
+
+
+def hidden_units(own, padded, dp, *gate):
+    rows = jnp.pad(own, ((0, padded - own.shape[0]), (0, 0)))
+    return own_first(lax.all_gather(after(rows, *gate), "dp", axis=0, tiled=True), dp)
+
+
+class HiddenGrads:
+    def along_core(self, units, rows):
+        self.units, self.rows = units, rows
+        half = units.shape[1] // 2
+        given = columns_by_columns(units[:, half:], rows).astype(jnp.bfloat16)
+        self.from_core = core_swap(given)
+        return [given]
+
+    def along_y(self, *gate):
+        half = self.units.shape[1] // 2
+        units, got = after((self.units, self.from_core), *gate)
+        total = columns_by_columns(units[:, :half], self.rows) + got.astype(jnp.float32)
+        given = total[half // 2 :].astype(jnp.bfloat16)
+        self.kept = total[: half // 2]
+        self.from_y = y_swap(given)
+        return [given]
+
+
+def fast_body(
+    hidden,
+    source,
+    cotangent,
+    row_counts,
+    seq_lengths,
+    kv_gain,
+    w_key,
+    w_value,
+    attn_gain,
+    w_query,
+    w_out,
+    ffn_gain,
+    w_gate,
+    w_up,
+    w_down,
+):
+    local_rows, width = hidden.shape
+    head = width // HEADS
+    dp = lax.axis_index("dp")
+    fsdp = lax.axis_index("fsdp")
+    y, c = dp // 2, dp % 2
+    z, x = fsdp // 2, fsdp % 2
+    me = 8 * dp + fsdp
+
+    each = kv_gain.shape[0]
+    inputs = Gather(jnp.concatenate([source, hidden], axis=0))
+    columns = Columns(
+        [w_query, w_key, w_value], jnp.concatenate([kv_gain, attn_gain, ffn_gain]), dp
+    )
+    wa = columns.along_fsdp()
+    s1 = move([inputs])
+    wy = columns.along_y(*wa)
+    s2 = move([inputs], *s1, *wa)
+    wc = columns.along_core(*wy)
+    s3 = move([inputs], *s2, *wy)
+    wq, w_kv, gains = columns.whole()
+    kv_gain_full, attn_gain_full, ffn_gain_full = (
+        gains[:, which * each : (which + 1) * each].reshape(1, width) for which in range(3)
+    )
+    units = w_gate.shape[0]
+    padded = -(-units // 64) * 64
+    wg, wu, wd = (hidden_units(own, padded, dp, *s1, *wa) for own in (w_gate, w_up, w_down))
+
+    order = z ^ (z >> 1)
+    devices = []
+    for step in range(4):
+        place = (order - step) % 4
+        for side in range(2):
+            devices.append(2 * (place ^ (place >> 1)) + (x ^ side))
+    slots = (
+        jnp.stack(devices).astype(jnp.int32)[:, None] * local_rows
+        + jnp.arange(local_rows, dtype=jnp.int32)[None, :]
+    ).reshape(-1)
+    live, position, sequence = slot_layout(row_counts, seq_lengths, slots, local_rows)
+    starts = jnp.concatenate([jnp.zeros((1,), jnp.int32), jnp.cumsum(seq_lengths[0])])
+    first = jnp.sum(
+        jnp.where(
+            sequence[:, None] == jnp.arange(starts.shape[0], dtype=jnp.int32)[None, :],
+            starts[None, :],
+            0,
+        ),
+        axis=1,
+    )
+    first, last = first[:, None], position[:, None]
+    place_of_key = jnp.where(live, position, -1)[None, :]
+    own_live = live[:local_rows].astype(jnp.float32)[:, None]
+
+    hidden_f = hidden.astype(jnp.float32)
+    d_out = cotangent.astype(jnp.float32) * own_live
+    projected = []
+
+    def project_piece(step):
+        piece = after(tuple(inputs.pieces[step]), *(value[3] for value in projected[-1:]))
+        projected.append(project(piece, kv_gain_full, attn_gain_full, w_kv, wq))
+
+    project_piece(0)
+    project_piece(1)
+    s4 = move([inputs], *s3)
+    project_piece(2)
+    cots = Gather(d_out.astype(jnp.bfloat16))
+    c1 = move([cots], *s4)
+    project_piece(3)
+    src_low, hid_low, pairs, queries = zip(*projected)
+    queries = jnp.concatenate(queries, axis=0)
+    pairs = jnp.concatenate(pairs, axis=0)
+    attended_f, attended_low, lse = attend(queries, pairs, first, last, place_of_key, head)
+    wo = out_rows(after(w_out, *s3), x, y, c, s4, [attended_low])
+
+    def rows_of(array, step):
+        return array[2 * step * local_rows : 2 * (step + 1) * local_rows]
+
+    def branch_terms(step, *gate):
+        return product(after(rows_of(attended_low, step), *gate), wo).astype(jnp.bfloat16)
+
+    branch = Scatter()
+    b1 = move([branch.of(branch_terms(1)), cots], *c1)
+    b2 = move([branch.of(branch_terms(2)), cots], *b1)
+    b3 = move([branch.of(branch_terms(3, *b1)), cots], *b2)
+    b4 = move([branch.of(branch_terms(0, *b2))], *b3)
+    middle = hidden_f + branch.total()
+    middle_scale = inverse_scale(middle)
+    middle_unit = middle * middle_scale
+    mids = Gather((middle_unit * ffn_gain_full).astype(jnp.bfloat16))
+
+    inners, d_gates, d_ups = [], [], []
+
+    def feed(step):
+        mid = mids.piece(step)
+        gate_value = rows_by_rows(mid, wg)
+        up_value = rows_by_rows(mid, wu)
+        sigmoid_gate = jax.nn.sigmoid(gate_value)
+        swished = gate_value * sigmoid_gate
+        d_inner = rows_by_rows(cots.piece(step), wd)
+        inners.append((swished * up_value).astype(jnp.bfloat16))
+        d_gates.append(
+            (d_inner * up_value * sigmoid_gate * (1.0 + gate_value * (1.0 - sigmoid_gate))).astype(
+                jnp.bfloat16
+            )
+        )
+        d_ups.append((d_inner * swished).astype(jnp.bfloat16))
+        return (product(d_gates[step], wg) + product(d_ups[step], wu)).astype(jnp.bfloat16)
+
+    m1 = move([mids])
+    m2 = move([mids], *m1)
+    t0 = feed(0)
+    m3 = move([mids], *m2, t0)
+    t1 = feed(1)
+    back = Scatter()
+    d1 = move([mids, back.of(t1)], *m3)
+    t2 = feed(2)
+    d2 = move([back.of(t2)], *d1)
+    t3 = feed(3)
+    d3 = move([back.of(t3)], *d2)
+    d_gates, d_ups, inners = (jnp.concatenate(value, axis=0) for value in (d_gates, d_ups, inners))
+    all_mids = jnp.concatenate([mids.piece(step) for step in range(4)], axis=0)
+    all_cots = jnp.concatenate([cots.piece(step) for step in range(4)], axis=0)
+    gate_sums, up_sums, down_sums = (HiddenGrads() for which in range(3))
+    h1 = gate_sums.along_core(after(d_gates, *d2), all_mids)
+    d4 = move([back.of(t0)], *d3, *h1)
+    h2 = up_sums.along_core(after(d_ups, *d3), all_mids)
+    d_normed = after(back.total(), *h2)
+    d_middle = d_out + norm_backward(middle, middle_scale, ffn_gain_full, d_normed)
+    d_branch_low = d_middle.astype(jnp.bfloat16)
+    outs = Gather(d_branch_low)
+    e1 = move([outs])
+    h1 = gate_sums.along_y(d_branch_low)
+    e2 = move([outs], *e1, *h1)
+    h2 = up_sums.along_y(*e1)
+    h3 = down_sums.along_core(after(inners, *e1), all_cots)
+    e3 = move([outs], *e2, *h2, *h3)
+    ffn_gain_part = jnp.sum(after(d_normed * middle_unit, *e2), axis=0)
+    h3 = down_sums.along_y(*e2)
+
+    def result_terms(step, *gate):
+        return product(after(rows_of(inners, step), *gate), wd).astype(jnp.bfloat16)
+
+    result = Scatter()
+    e4 = move([outs, result.of(result_terms(1, *e2))], *e3, *h3, gate_sums.from_y)
+    column_grads = ColumnGrads(dp)
+    column_grads.gain_core(ffn_gain_part, *e3)
+    column_grads.gain_y(*e4)
+    d_branches = [outs.piece(step) for step in range(4)]
+    d_attended = jnp.concatenate(
+        [rows_by_rows(rows, wo).astype(jnp.bfloat16) for rows in d_branches], axis=0
+    )
+    o2 = move([result.of(result_terms(2, *e3))], *e4)
+    d_queries, d_pairs = attend_back(
+        queries, pairs, first, last, place_of_key, lse, attended_f, d_attended, head
+    )
+    d_queries, d_pairs = after((d_queries, d_pairs), *o2)
+    d_src, d_hid = Scatter(), Scatter()
+
+    def terms(step, *gate):
+        rows = input_terms(step, *after((d_pairs, d_queries), *gate), w_kv, wq)
+        return [d_src.of(rows[0]), d_hid.of(rows[1])]
+
+    first_terms = terms(1)
+    started = d_hid.terms
+    i1 = move(first_terms, *o2, up_sums.from_y, column_grads.gain)
+    sources, hiddens = after((tuple(src_low), tuple(hid_low)), started)
+    column_grads.along_core(sources, hiddens, d_queries, d_pairs)
+    py = column_grads.along_y()
+    i2 = move(
+        terms(2, started) + [result.of(result_terms(3, started))],
+        *i1,
+        down_sums.from_y,
+    )
+    out_grads = OutGrads(
+        columns_by_columns(after(attended_low, *i1, *py), jnp.concatenate(d_branches, axis=0)), x, y, c
+    )
+    out_grads.along_core()
+    oy = out_grads.along_y(column_grads.from_y)
+    pz, got_z = column_grads.along_fsdp(*i2)
+    i3 = move(terms(3, *i1) + [result.of(result_terms(0, *i1))], *i2, *oy)
+    out_grads.along_x(*i2)
+    i4 = move(terms(0, *i2), *i3)
+    grad_gate, grad_up, grad_down = add_all(
+        *zip(
+            *(
+                (sums.kept, after(sums.from_y, *i3))
+                for sums in (gate_sums, up_sums, down_sums)
+            )
+        ),
+        units,
+    )
+    output = ((middle + after(result.total(), *i3)) * own_live).astype(jnp.bfloat16)
+    d_src, d_hid = d_src.total(), d_hid.total()
+
+    grad_out = out_grads.whole(*i3)
+    own_grads, grad_ffn_gain = column_grads.whole([w_query, w_key, w_value], *i3)
+    grad_query, grad_key, grad_value, query_sum, pair_sum = own_grads
+    grad_attn_gain = query_sum[:, 0] / attn_gain.astype(jnp.float32)
+    grad_kv_gain = pair_sum[:, 0] / kv_gain.astype(jnp.float32)
+
+    grad_hidden = (
+        d_middle + norm_backward(hidden_f, inverse_scale(hidden_f), attn_gain_full, d_hid)
+    ).astype(jnp.bfloat16)
+    source_f = source.astype(jnp.float32)
+    grad_source = norm_backward(source_f, inverse_scale(source_f), kv_gain_full, d_src).astype(
+        jnp.bfloat16
+    )
+    return (
+        output,
+        grad_hidden,
+        grad_source,
+        grad_kv_gain,
+        grad_key,
+        grad_value,
+        grad_attn_gain,
+        grad_query,
+        grad_out,
+        grad_ffn_gain,
+        grad_gate,
+        grad_up,
+        grad_down,
+    )
+
+
 def solution(mesh):
     in_specs = (
         P(("dp", "fsdp"), None),
@@ -350,4 +1264,8 @@
         P(("dp", "fsdp"), None),
         P(("dp", "fsdp"), None),
     )
-    return jax.shard_map(body, mesh=mesh, in_specs=in_specs, out_specs=out_specs, check_vma=False)
+    placed = (
+        mesh.shape["dp"] == 4 and mesh.shape["fsdp"] == 8 and HEADS == 2 * mesh.shape["fsdp"]
+    )
+    chosen = fast_body if placed else body
+    return jax.shard_map(chosen, mesh=mesh, in_specs=in_specs, out_specs=out_specs, check_vma=False)

time: 4510 us -> 647 us (0.14)
  waiting for transfers between devices: 3870 us -> 313 us
  matrix products: 237 us -> 55 us
  other arithmetic: 156 us -> 49 us
  blocking collectives: 83.3 us -> 0 us
  starting transfers between devices: 0.68 us -> 67 us
  Pallas kernels: 0 us -> 47.8 us
    unnamed x13 -> x3, waiting for transfers between devices: 1760 us -> 0.05 us
    reduce_scatter x2 -> x0, waiting for transfers between devices: 1400 us -> none  [the longest x1 1400 us: body(): lax.psum_scatter(jnp.stack([columns_by_columns(hidden_part, d_queries_low...]
    all_gather x9 -> x3, waiting for transfers between devices: 711 us -> 0.01 us  [hidden_units(): lax.all_gather(after(rows, *gate), 'dp', axis=0, tiled=True)]
    ppermute x0 -> x69, waiting for transfers between devices: none -> 305 us  [the longest x26 148 us: x_swap(): return lax.ppermute(value, 'fsdp', swap_pairs(8, 1))]
    another operation x4 -> x9, other arithmetic: 135 us -> 2.88 us  [the longest x1 2.13 us: along_core(): self.held = jnp.stack([held, got, other, last]).reshape(2, 2, *held.shape)]
    unnamed x2 -> x0, blocking collectives: 83.3 us -> none
    dot_general x7, matrix products: 89.8 us -> 18.6 us  [columns_by_columns(): lax.dot_general(left, right, (((0,), (0,)), ((), ())), preferred_element_...]
    ppermute x0 -> x69, starting transfers between devices: none -> 53.8 us  [the longest x26 26.2 us: x_swap(): return lax.ppermute(value, 'fsdp', swap_pairs(8, 1))]
  transfers between devices with their start and end apart: 12 -> 74, of which waited for: 11 -> 44; matrix products, arithmetic and copies ran while one was open for 9% -> 21% of each run, Pallas kernels for 0% -> 7%
where the time goes in v2:
time: 647 us; the launch traced here: 636 us
  waiting for transfers between devices  313 us (48%)
  local copies, waits for them, and re-layouts  88 us (14%)
  starting transfers between devices  67 us (10%)
  matrix products  55 us (9%)
  other arithmetic  49 us (8%)
  Pallas kernels  47.8 us (7%)
  between operations  16.8 us (3%)
    ppermute x26, waiting for transfers between devices, x_swap(): return lax.ppermute(value, 'fsdp', swap_pairs(8, 1))  148 us
    ppermute x25, waiting for transfers between devices, ring_step(): return lax.ppermute(value, 'fsdp', ring_pairs())  123 us
    unnamed x331, local copies, waits for them, and re-layouts  58.5 us
    ppermute x6, waiting for transfers between devices, y_swap(): return lax.ppermute(value, 'dp', swap_pairs(4, 2))  28 us
    ppermute x26, starting transfers between devices, x_swap(): return lax.ppermute(value, 'fsdp', swap_pairs(8, 1))  26.2 us
    dot_general x16, matrix products, product(): return jnp.dot(left, right, preferred_element_type=jnp.float32)  19.2 us
    dot_general x7, matrix products, columns_by_columns(): lax.dot_general(left, right, (((0,), (0,)), ((), ())), preferred_element_...  18.6 us
    dot_general x16, matrix products, rows_by_rows(): lax.dot_general(left, right, (((1,), (1,)), ((), ())), preferred_element_...  17.3 us
  transfers between devices with their start and end apart: 74, of which 44 were waited for; matrix products, arithmetic and copies ran while one was open for 21% of the time, Pallas kernels for 7%

profile of v2, /device:TPU:0, one launch (start us, length us, event | category | flops | bytes accessed | tf_op | source)
XLA Modules:
  0.0 636.5 jit_solution(885807102480968369)
XLA Ops:
  11.9 7.4 %all-to-all-start = ((bf16[8,200,256]{2,1,0:T(8,128)(2,1)}), bf16[8,200,256]{2,1,0:T(8,128)(2,1)}, u32[]{:S(2)}, u32[]{:S(2)}) async-start(bf16[8,200,256]{2,1,0:T(8,128)(2,1)} %bitcast.1), calls=%async_computation | async-start | bytes 1638400 | tf_op jit(solution)/shard_map/all_to_all | solution.py:637
  26.1 36.5 %collective-permute-done.4.held_ref = bf16[256,2048]{1,0:T(8,128)(2,1)S(1)} collective-permute-done((bf16[256,2048]{1,0:T(8,128)(2,1)S(1)}, bf16[256,2048]{1,0:T(8,128)(2,1)S(1)}, u32[]{:S(2)}, u32[]{:S(2)}) %collective-permute-start.4) | collective-permute-done | bytes 1048608 | tf_op jit(solution)/shard_map/ppermute | solution.py:342
  68.9 28.0 %collective-permute-done.1 = bf16[1600,256]{1,0:T(8,128)(2,1)} collective-permute-done((bf16[1600,256]{1,0:T(8,128)(2,1)}, bf16[1600,256]{1,0:T(8,128)(2,1)}, u32[]{:S(2)}, u32[]{:S(2)}) %collective-permute-start.1) | collective-permute-done | bytes 819232 | tf_op jit(solution)/shard_map/ppermute | solution.py:346
  109.5 16.1 %collective-permute-done.7.refs_0_ = bf16[256,2048]{1,0:T(8,128)(2,1)} collective-permute-done((bf16[256,2048]{1,0:T(8,128)(2,1)}, bf16[256,2048]{1,0:T(8,128)(2,1)}, u32[]{:S(2)}, u32[]{:S(2)}) %collective-permute-start.7) | collective-permute-done | bytes 1048608 | tf_op jit(solution)/shard_map/ppermute | solution.py:338
  128.2 2.7 project.5
  134.9 11.7 %collective-permute-done.9.refs_0_ = bf16[128,2048]{1,0:T(8,128)(2,1)S(1)} collective-permute-done((bf16[128,2048]{1,0:T(8,128)(2,1)S(1)}, bf16[128,2048]{1,0:T(8,128)(2,1)S(1)}, u32[]{:S(2)}, u32[]{:S(2)}) %collective-permute-start.9) | collective-permute-done | bytes 524320 | tf_op jit(solution)/shard_map/ppermute | solution.py:338
  148.2 4.4 collective-permute-start.12
  152.6 3.0 project.6
  157.6 2.8 project.7
  162.5 7.6 %attend.1 = (f32[1024,256]{1,0:T(8,128)S(1)}, bf16[1024,256]{1,0:T(8,128)(2,1)S(1)}, f32[2,1024,1]{2,1,0:T(8,128)S(1)}) custom-call(bf16[1024,256]{1,0:T(8,128)(2,1)S(1)} %constant_dynamic-update-slice_fusion.2.q_ref, bf16[1024,512]{1,0:T(8,128)(2,1)S(1)} %constant_dynamic-update-slice_fusion.6.k_ref.v_ref, ...), custom_call_target="tpu_custom_call" | custom-call | flops 1048576 | bytes 262144 | tf_op jit(solution)/shard_map/attend/pallas_call | solution.py:530
  174.5 2.2 constant_dynamic-update-slice_fusion.31
  178.7 13.3 %collective-permute-done.14 = bf16[128,2048]{1,0:T(8,128)(2,1)S(1)} collective-permute-done((bf16[128,2048]{1,0:T(8,128)(2,1)}, bf16[128,2048]{1,0:T(8,128)(2,1)S(1)}, u32[]{:S(2)}, u32[]{:S(2)}) %collective-permute-start.14) | collective-permute-done | bytes 524320 | tf_op jit(solution)/shard_map/ppermute | solution.py:342
  195.2 17.1 %collective-permute-done.16 = bf16[192,2048]{1,0:T(8,128)(2,1)S(1)} collective-permute-done((bf16[192,2048]{1,0:T(8,128)(2,1)S(1)}, bf16[192,2048]{1,0:T(8,128)(2,1)S(1)}, u32[]{:S(2)}, u32[]{:S(2)}) %collective-permute-start.16) | collective-permute-done | bytes 786464 | tf_op jit(solution)/shard_map/ppermute | solution.py:342
  232.0 9.2 %collective-permute-done.18 = bf16[256,2048]{1,0:T(8,128)(2,1)} collective-permute-done((bf16[256,2048]{1,0:T(8,128)(2,1)}, bf16[256,2048]{1,0:T(8,128)(2,1)}, u32[]{:S(2)}, u32[]{:S(2)}) %collective-permute-start.18) | collective-permute-done | bytes 1048608 | tf_op jit(solution)/shard_map/ppermute | solution.py:338
  252.0 11.2 %collective-permute-done.20 = bf16[192,2048]{1,0:T(8,128)(2,1)S(1)} collective-permute-done((bf16[192,2048]{1,0:T(8,128)(2,1)S(1)}, bf16[192,2048]{1,0:T(8,128)(2,1)S(1)}, u32[]{:S(2)}, u32[]{:S(2)}) %collective-permute-start.20) | collective-permute-done | bytes 786464 | tf_op jit(solution)/shard_map/ppermute | solution.py:338
  268.1 7.2 %collective-permute-done.22 = bf16[128,2048]{1,0:T(8,128)(2,1)S(1)} collective-permute-done((bf16[128,2048]{1,0:T(8,128)(2,1)S(1)}, bf16[128,2048]{1,0:T(8,128)(2,1)S(1)}, u32[]{:S(2)}, u32[]{:S(2)}) %collective-permute-start.22) | collective-permute-done | bytes 524320 | tf_op jit(solution)/shard_map/ppermute | solution.py:338
  275.3 2.3 collective-permute-done.23
  281.4 9.1 %collective-permute-done.25 = bf16[128,2048]{1,0:T(8,128)(2,1)S(1)} collective-permute-done((bf16[128,2048]{1,0:T(8,128)(2,1)S(1)}, bf16[128,2048]{1,0:T(8,128)(2,1)S(1)}, u32[]{:S(2)}, u32[]{:S(2)}) %collective-permute-start.25) | collective-permute-done | bytes 524320 | tf_op jit(solution)/shard_map/ppermute | solution.py:342
  299.3 2.2 collective-permute-done.27
  309.3 11.5 %collective-permute-done.28 = bf16[128,2048]{1,0:T(8,128)(2,1)S(1)} collective-permute-done((bf16[128,2048]{1,0:T(8,128)(2,1)S(1)}, bf16[128,2048]{1,0:T(8,128)(2,1)S(1)}, u32[]{:S(2)}, u32[]{:S(2)}) %collective-permute-start.28) | collective-permute-done | bytes 524320 | tf_op jit(solution)/shard_map/ppermute | solution.py:342
  327.6 5.3 collective-permute-done.30
  333.0 2.5 collective-permute-done.31
  341.9 10.4 %collective-permute-done.32 = bf16[128,2048]{1,0:T(8,128)(2,1)S(1)} collective-permute-done((bf16[128,2048]{1,0:T(8,128)(2,1)S(1)}, bf16[128,2048]{1,0:T(8,128)(2,1)S(1)}, u32[]{:S(2)}, u32[]{:S(2)}) %collective-permute-start.32) | collective-permute-done | bytes 524320 | tf_op jit(solution)/shard_map/ppermute | solution.py:338
  357.2 8.8 %collective-permute-done.34 = bf16[128,2048]{1,0:T(8,128)(2,1)S(1)} collective-permute-done((bf16[128,2048]{1,0:T(8,128)(2,1)S(1)}, bf16[128,2048]{1,0:T(8,128)(2,1)S(1)}, u32[]{:S(2)}, u32[]{:S(2)}) %collective-permute-start.34) | collective-permute-done | bytes 524320 | tf_op jit(solution)/shard_map/ppermute | solution.py:338
  371.9 5.4 collective-permute-done.36
  377.3 2.7 collective-permute-done.37
  386.9 9.1 %collective-permute-done.39 = bf16[128,2048]{1,0:T(8,128)(2,1)S(1)} collective-permute-done((bf16[128,2048]{1,0:T(8,128)(2,1)S(1)}, bf16[128,2048]{1,0:T(8,128)(2,1)S(1)}, u32[]{:S(2)}, u32[]{:S(2)}) %collective-permute-start.39) | collective-permute-done | bytes 524320 | tf_op jit(solution)/shard_map/ppermute | solution.py:342
  397.5 3.3 collective-permute-start.42
  400.8 5.2 convolution_convert_fusion
  414.6 3.0 convolution_convert_fusion.10
  422.1 10.2 %collective-permute-done.44 = bf16[128,2048]{1,0:T(8,128)(2,1)S(1)} collective-permute-done((bf16[128,2048]{1,0:T(8,128)(2,1)}, bf16[128,2048]{1,0:T(8,128)(2,1)S(1)}, u32[]{:S(2)}, u32[]{:S(2)}) %collective-permute-start.44) | collective-permute-done | bytes 524320 | tf_op jit(solution)/shard_map/ppermute | solution.py:338
  435.8 4.6 convert_add_fusion
  446.1 8.8 %collective-permute-done.48 = bf16[128,2048]{1,0:T(8,128)(2,1)S(1)} collective-permute-done((bf16[128,2048]{1,0:T(8,128)(2,1)S(1)}, bf16[128,2048]{1,0:T(8,128)(2,1)S(1)}, u32[]{:S(2)}, u32[]{:S(2)}) %collective-permute-start.48) | collective-permute-done | bytes 524320 | tf_op jit(solution)/shard_map/ppermute | solution.py:338
  463.5 10.0 %attend_back.1 = (bf16[1024,256]{1,0:T(8,128)(2,1)S(1)}, bf16[1024,512]{1,0:T(8,128)(2,1)S(1)}) custom-call(bf16[1024,256]{1,0:T(8,128)(2,1)S(1)} %copy-done.25, bf16[1024,512]{1,0:T(8,128)(2,1)S(1)} %copy-done.8, bf16[1024,512]{1,0:T(8,128)(2,1)S(1)} %copy-done.8, s32[1024,1]{1,0:T(8,128)S(1)} %copy-done.18, s32[1024,1]{1,0:T(8,128)S(1)} %copy-done.16, ...), custom_call_target="tpu_custom_call" | custom-call | flops 1048576 | bytes 262144 | tf_op jit(solution)/shard_map/attend_back/pallas_call | solution.py:551
  479.6 7.1 %column_grads.1 = (bf16[2,512,768]{2,1,0:T(8,128)(2,1)}, f32[2,512,768]{2,1,0:T(8,128)}) custom-call(s32[1]{0:T(128)} %bitcast.dp_ref, bf16[256,2048]{1,0:T(8,128)(2,1)S(1)} %copy-done.33, bf16[256,2048]{1,0:T(8,128)(2,1)S(1)} %copy-done.37, bf16[256,2048]{1,0:T(8,128)(2,1)S(1)} %copy-done.41, bf16[256,2048]{1,0:T(8,128)(2,1)S(1)} %copy-done.45, ...), custom_call_target="tpu_custom_call" | custom-call | flops 2097152 | bytes 1048576 | tf_op jit(solution)/shard_map/column_grads/pallas_call | solution.py:873
  499.5 3.1 convolution_convert_fusion.8
  503.9 3.2 slice-done
  511.7 22.1 %collective-permute-done.58 = bf16[384,2048]{1,0:T(8,128)(2,1)} collective-permute-done((bf16[384,2048]{1,0:T(8,128)(2,1)}, bf16[384,2048]{1,0:T(8,128)(2,1)}, u32[]{:S(2)}, u32[]{:S(2)}) %collective-permute-start.58) | collective-permute-done | bytes 1572896 | tf_op jit(solution)/shard_map/ppermute | solution.py:338
  535.6 2.5 add_convert_fusion.5
  543.1 2.8 slice.626.refs_0_
  558.6 5.6 all-to-all-start.1
  564.3 4.1 collective-permute-done.67
  572.2 9.2 %collective-permute-done.63 = bf16[384,2048]{1,0:T(8,128)(2,1)} collective-permute-done((bf16[384,2048]{1,0:T(8,128)(2,1)}, bf16[384,2048]{1,0:T(8,128)(2,1)}, u32[]{:S(2)}, u32[]{:S(2)}) %collective-permute-start.63) | collective-permute-done | bytes 1572896 | tf_op jit(solution)/shard_map/ppermute | solution.py:338
  582.1 3.5 add_convert_fusion.2
  588.7 8.3 %all-to-all-done.1.got_ref = bf16[8,72,768]{2,1,0:T(8,128)(2,1)} async-done(((bf16[8,72,768]{2,1,0:T(8,128)(2,1)}), bf16[8,72,768]{2,1,0:T(8,128)(2,1)}, u32[]{:S(2)}, u32[]{:S(2)}) %all-to-all-start.1) | async-done | bytes 884768 | tf_op jit(solution)/shard_map/all_to_all | solution.py:914
  598.9 2.4 own_grads.1
  607.4 4.3 add_all.1
  615.9 8.9 %collective-permute-done.65 = bf16[256,2048]{1,0:T(8,128)(2,1)S(1)} collective-permute-done((bf16[256,2048]{1,0:T(8,128)(2,1)}, bf16[256,2048]{1,0:T(8,128)(2,1)S(1)}, u32[]{:S(2)}, u32[]{:S(2)}) %collective-permute-start.65) | collective-permute-done | bytes 1048608 | tf_op jit(solution)/shard_map/ppermute | solution.py:338
  (641 shorter events, 237.9 us)
Async XLA Ops:
  11.9 50.8 %all-to-all-start = ((bf16[8,200,256]{2,1,0:T(8,128)(2,1)}), bf16[8,200,256]{2,1,0:T(8,128)(2,1)}, u32[]{:S(2)}, u32[]{:S(2)}) async-start(bf16[8,200,256]{2,1,0:T(8,128)(2,1)} %bitcast.1), calls=%async_computation | async-start | bytes 1638400 | tf_op jit(solution)/shard_map/all_to_all | solution.py:637
  19.3 202.8 %all-gather.4.cloned.1.call-start = ((), (), s32[]{:S(2)}) async-start(), calls=%async_computation.2 | async-start | bytes 3932160 | tf_op jit(solution)/shard_map/all_gather | solution.py:974
  20.5 42.1 %collective-permute-start.4 = (bf16[256,2048]{1,0:T(8,128)(2,1)S(1)}, bf16[256,2048]{1,0:T(8,128)(2,1)S(1)}, u32[]{:S(2)}, u32[]{:S(2)}) collective-permute-start(bf16[256,2048]{1,0:T(8,128)(2,1)S(1)} %constant_dynamic-update-slice_fusion.held_ref), channel_id=1, source_target_pairs={{0,2},{1,3},{2,6},{3,7},{6,4},{7,5},{4,0},{5,1},{8,10},{9,11},{10,... | collective-permute-start | bytes 3145736 | tf_op jit(solution)/shard_map/ppermute | solution.py:342
  22.5 40.1 %collective-permute-start = (bf16[256,2048]{1,0:T(8,128)(2,1)S(1)}, bf16[256,2048]{1,0:T(8,128)(2,1)S(1)}, u32[]{:S(2)}, u32[]{:S(2)}) collective-permute-start(bf16[256,2048]{1,0:T(8,128)(2,1)S(1)} %constant_dynamic-update-slice_fusion.held_ref), channel_id=1, source_target_pairs={{0,1},{1,0},{2,3},{3,2},{4,5},{5,4},{6,7},{7,6},{8,9},{9,8},{10,11... | collective-permute-start | bytes 3145736 | tf_op jit(solution)/shard_map/ppermute | solution.py:338
  62.7 163.3 %all-gather.6.cloned.1.call-start = ((), (), s32[]{:S(2)}) async-start(), calls=%async_computation.3 | async-start | bytes 3932160 | tf_op jit(solution)/shard_map/all_gather | solution.py:974
  63.2 33.7 %collective-permute-start.1 = (bf16[1600,256]{1,0:T(8,128)(2,1)}, bf16[1600,256]{1,0:T(8,128)(2,1)}, u32[]{:S(2)}, u32[]{:S(2)}) collective-permute-start(bf16[1600,256]{1,0:T(8,128)(2,1)} %bitcast.2), channel_id=1, source_target_pairs={{0,16},{8,24},{16,0},{24,8},{1,17},{9,25},{17,1},{25,9},{2,18},{10... | collective-permute-start | bytes 2457608 | tf_op jit(solution)/shard_map/ppermute | solution.py:346
  67.2 32.5 %collective-permute-start.5 = (bf16[256,2048]{1,0:T(8,128)(2,1)S(1)}, bf16[256,2048]{1,0:T(8,128)(2,1)}, u32[]{:S(2)}, u32[]{:S(2)}) collective-permute-start(bf16[256,2048]{1,0:T(8,128)(2,1)S(1)} %collective-permute-done.4.held_ref), channel_id=1, source_target_pairs={{0,1},{1,0},{2,3},{3,2},{4,5},{5,4},{6,7},{7,6},{8,9},{9,8},{10,11... | collective-permute-start | bytes 3145736 | tf_op jit(solution)/shard_map/ppermute | solution.py:338
  68.6 31.1 %collective-permute-start.6 = (bf16[256,2048]{1,0:T(8,128)(2,1)S(1)}, bf16[256,2048]{1,0:T(8,128)(2,1)}, u32[]{:S(2)}, u32[]{:S(2)}) collective-permute-start(bf16[256,2048]{1,0:T(8,128)(2,1)S(1)} %collective-permute-done.4.held_ref), channel_id=1, source_target_pairs={{0,2},{1,3},{2,6},{3,7},{6,4},{7,5},{4,0},{5,1},{8,10},{9,11},{10,... | collective-permute-start | bytes 3145736 | tf_op jit(solution)/shard_map/ppermute | solution.py:342
  68.8 161.0 %all-gather.8.cloned.1.call-start = ((), (), s32[]{:S(2)}) async-start(), calls=%async_computation.4 | async-start | bytes 3932160 | tf_op jit(solution)/shard_map/all_gather | solution.py:974
  99.7 25.9 %collective-permute-start.7 = (bf16[256,2048]{1,0:T(8,128)(2,1)}, bf16[256,2048]{1,0:T(8,128)(2,1)}, u32[]{:S(2)}, u32[]{:S(2)}) collective-permute-start(bf16[256,2048]{1,0:T(8,128)(2,1)} %collective-permute-done.6.held_ref), channel_id=1, source_target_pairs={{0,1},{1,0},{2,3},{3,2},{4,5},{5,4},{6,7},{7,6},{8,9},{9,8},{10,11... | collective-permute-start | bytes 3145736 | tf_op jit(solution)/shard_map/ppermute | solution.py:338
  100.7 26.5 %collective-permute-start.8 = (bf16[256,2048]{1,0:T(8,128)(2,1)}, bf16[256,2048]{1,0:T(8,128)(2,1)}, u32[]{:S(2)}, u32[]{:S(2)}) collective-permute-start(bf16[256,2048]{1,0:T(8,128)(2,1)} %collective-permute-done.6.held_ref), channel_id=1, source_target_pairs={{0,2},{1,3},{2,6},{3,7},{6,4},{7,5},{4,0},{5,1},{8,10},{9,11},{10,... | collective-permute-start | bytes 3145736 | tf_op jit(solution)/shard_map/ppermute | solution.py:342
  148.2 22.9 %collective-permute-start.12 = (bf16[128,2048]{1,0:T(8,128)(2,1)S(1)}, bf16[128,2048]{1,0:T(8,128)(2,1)S(1)}, u32[]{:S(2)}, u32[]{:S(2)}) collective-permute-start(bf16[128,2048]{1,0:T(8,128)(2,1)S(1)} %pad_maximum_fusion.19), channel_id=1, source_target_pairs={{0,16},{2,18},{4,20},{6,22},{8,24},{10,26},{12,28},{14,30},{17,1},... | collective-permute-start | bytes 1572872 | tf_op jit(solution)/shard_map/ppermute | solution.py:936
  176.7 15.3 %collective-permute-start.14 = (bf16[128,2048]{1,0:T(8,128)(2,1)}, bf16[128,2048]{1,0:T(8,128)(2,1)S(1)}, u32[]{:S(2)}, u32[]{:S(2)}) collective-permute-start(bf16[128,2048]{1,0:T(8,128)(2,1)} %get-tuple-element.193), channel_id=1, source_target_pairs={{0,2},{1,3},{2,6},{3,7},{6,4},{7,5},{4,0},{5,1},{8,10},{9,11},{10,... | collective-permute-start | bytes 1572872 | tf_op jit(solution)/shard_map/ppermute | solution.py:342
  176.7 15.4 %collective-permute-start.15 = (bf16[128,2048]{1,0:T(8,128)(2,1)}, bf16[128,2048]{1,0:T(8,128)(2,1)S(1)}, u32[]{:S(2)}, u32[]{:S(2)}) collective-permute-start(bf16[128,2048]{1,0:T(8,128)(2,1)} %get-tuple-element.193), channel_id=1, source_target_pairs={{0,1},{1,0},{2,3},{3,2},{4,5},{5,4},{6,7},{7,6},{8,9},{9,8},{10,11... | collective-permute-start | bytes 1572872 | tf_op jit(solution)/shard_map/ppermute | solution.py:338
  192.2 20.1 %collective-permute-start.16 = (bf16[192,2048]{1,0:T(8,128)(2,1)S(1)}, bf16[192,2048]{1,0:T(8,128)(2,1)S(1)}, u32[]{:S(2)}, u32[]{:S(2)}) collective-permute-start(bf16[192,2048]{1,0:T(8,128)(2,1)S(1)} %get-tuple-element.195), channel_id=1, source_target_pairs={{0,2},{1,3},{2,6},{3,7},{6,4},{7,5},{4,0},{5,1},{8,10},{9,11},{10,... | collective-permute-start | bytes 2359304 | tf_op jit(solution)/shard_map/ppermute | solution.py:342
  193.8 18.9 %collective-permute-start.17 = (bf16[192,2048]{1,0:T(8,128)(2,1)S(1)}, bf16[192,2048]{1,0:T(8,128)(2,1)S(1)}, u32[]{:S(2)}, u32[]{:S(2)}) collective-permute-start(bf16[192,2048]{1,0:T(8,128)(2,1)S(1)} %get-tuple-element.196), channel_id=1, source_target_pairs={{0,1},{1,0},{2,3},{3,2},{4,5},{5,4},{6,7},{7,6},{8,9},{9,8},{10,11... | collective-permute-start | bytes 2359304 | tf_op jit(solution)/shard_map/ppermute | solution.py:338
  217.2 24.0 %collective-permute-start.18 = (bf16[256,2048]{1,0:T(8,128)(2,1)}, bf16[256,2048]{1,0:T(8,128)(2,1)}, u32[]{:S(2)}, u32[]{:S(2)}) collective-permute-start(bf16[256,2048]{1,0:T(8,128)(2,1)} %get-tuple-element.197), channel_id=1, source_target_pairs={{0,1},{1,0},{2,3},{3,2},{4,5},{5,4},{6,7},{7,6},{8,9},{9,8},{10,11... | collective-permute-start | bytes 3145736 | tf_op jit(solution)/shard_map/ppermute | solution.py:338
  217.5 24.9 %collective-permute-start.19 = (bf16[256,2048]{1,0:T(8,128)(2,1)}, bf16[256,2048]{1,0:T(8,128)(2,1)}, u32[]{:S(2)}, u32[]{:S(2)}) collective-permute-start(bf16[256,2048]{1,0:T(8,128)(2,1)} %get-tuple-element.198), channel_id=1, source_target_pairs={{0,2},{1,3},{2,6},{3,7},{6,4},{7,5},{4,0},{5,1},{8,10},{9,11},{10,... | collective-permute-start | bytes 3145736 | tf_op jit(solution)/shard_map/ppermute | solution.py:342
  246.1 17.2 %collective-permute-start.20 = (bf16[192,2048]{1,0:T(8,128)(2,1)S(1)}, bf16[192,2048]{1,0:T(8,128)(2,1)S(1)}, u32[]{:S(2)}, u32[]{:S(2)}) collective-permute-start(bf16[192,2048]{1,0:T(8,128)(2,1)S(1)} %pad_maximum_fusion.15), channel_id=1, source_target_pairs={{0,1},{1,0},{2,3},{3,2},{4,5},{5,4},{6,7},{7,6},{8,9},{9,8},{10,11... | collective-permute-start | bytes 2359304 | tf_op jit(solution)/shard_map/ppermute | solution.py:338
  247.5 17.4 %collective-permute-start.21 = (bf16[192,2048]{1,0:T(8,128)(2,1)S(1)}, bf16[192,2048]{1,0:T(8,128)(2,1)S(1)}, u32[]{:S(2)}, u32[]{:S(2)}) collective-permute-start(bf16[192,2048]{1,0:T(8,128)(2,1)S(1)} %pad_maximum_fusion.16), channel_id=1, source_target_pairs={{0,2},{1,3},{2,6},{3,7},{6,4},{7,5},{4,0},{5,1},{8,10},{9,11},{10,... | collective-permute-start | bytes 2359304 | tf_op jit(solution)/shard_map/ppermute | solution.py:342
  290.4 15.8 %collective-permute-start.26 = (bf16[128,2048]{1,0:T(8,128)(2,1)S(1)}, bf16[128,2048]{1,0:T(8,128)(2,1)S(1)}, u32[]{:S(2)}, u32[]{:S(2)}) collective-permute-start(bf16[128,2048]{1,0:T(8,128)(2,1)S(1)} %collective-permute-done.25), channel_id=1, source_target_pairs={{0,2},{1,3},{2,6},{3,7},{6,4},{7,5},{4,0},{5,1},{8,10},{9,11},{10,... | collective-permute-start | bytes 1572872 | tf_op jit(solution)/shard_map/ppermute | solution.py:342
  306.2 14.6 %collective-permute-start.28 = (bf16[128,2048]{1,0:T(8,128)(2,1)S(1)}, bf16[128,2048]{1,0:T(8,128)(2,1)S(1)}, u32[]{:S(2)}, u32[]{:S(2)}) collective-permute-start(bf16[128,2048]{1,0:T(8,128)(2,1)S(1)} %collective-permute-done.26), channel_id=1, source_target_pairs={{0,2},{1,3},{2,6},{3,7},{6,4},{7,5},{4,0},{5,1},{8,10},{9,11},{10,... | collective-permute-start | bytes 1572872 | tf_op jit(solution)/shard_map/ppermute | solution.py:342
  369.4 14.5 %collective-permute-start.40 = (bf16[384,2048]{1,0:T(8,128)(2,1)S(1)}, bf16[384,2048]{1,0:T(8,128)(2,1)S(1)}, u32[]{:S(2)}, u32[]{:S(2)}) collective-permute-start(bf16[384,2048]{1,0:T(8,128)(2,1)S(1)} %convolution_convert_fusion.2), channel_id=1, source_target_pairs={{0,8},{8,0},{16,24},{24,16},{1,9},{9,1},{17,25},{25,17},{2,10},{10... | collective-permute-start | bytes 4718600 | tf_op jit(solution)/shard_map/ppermute | solution.py:350
  371.3 35.9 %collective-permute-start.43 = (bf16[384,2048]{1,0:T(8,128)(2,1)S(1)}, bf16[384,2048]{1,0:T(8,128)(2,1)S(1)}, u32[]{:S(2)}, u32[]{:S(2)}) collective-permute-start(bf16[384,2048]{1,0:T(8,128)(2,1)S(1)} %convolution_convert_fusion.1), channel_id=1, source_target_pairs={{0,8},{8,0},{16,24},{24,16},{1,9},{9,1},{17,25},{25,17},{2,10},{10... | collective-permute-start | bytes 4718600 | tf_op jit(solution)/shard_map/ppermute | solution.py:350
  386.9 53.6 %collective-permute-start.47 = (bf16[192,2048]{1,0:T(8,128)(2,1)}, bf16[192,2048]{1,0:T(8,128)(2,1)}, u32[]{:S(2)}, u32[]{:S(2)}) collective-permute-start(bf16[192,2048]{1,0:T(8,128)(2,1)} %slice.735), channel_id=1, source_target_pairs={{0,16},{8,24},{16,0},{24,8},{1,17},{9,25},{17,1},{25,9},{2,18},{10... | collective-permute-start | bytes 2359304 | tf_op jit(solution)/shard_map/ppermute | solution.py:346
  396.2 15.7 %collective-permute-start.41 = (bf16[128,2048]{1,0:T(8,128)(2,1)S(1)}, bf16[128,2048]{1,0:T(8,128)(2,1)S(1)}, u32[]{:S(2)}, u32[]{:S(2)}) collective-permute-start(bf16[128,2048]{1,0:T(8,128)(2,1)S(1)} %collective-permute-done.39), channel_id=1, source_target_pairs={{0,1},{1,0},{2,3},{3,2},{4,5},{5,4},{6,7},{7,6},{8,9},{9,8},{10,11... | collective-permute-start | bytes 1572872 | tf_op jit(solution)/shard_map/ppermute | solution.py:338
  397.5 14.4 %collective-permute-start.42 = (bf16[128,2048]{1,0:T(8,128)(2,1)S(1)}, bf16[128,2048]{1,0:T(8,128)(2,1)}, u32[]{:S(2)}, u32[]{:S(2)}) collective-permute-start(bf16[128,2048]{1,0:T(8,128)(2,1)S(1)} %collective-permute-done.39), channel_id=1, source_target_pairs={{0,2},{1,3},{2,6},{3,7},{6,4},{7,5},{4,0},{5,1},{8,10},{9,11},{10,... | collective-permute-start | bytes 1572872 | tf_op jit(solution)/shard_map/ppermute | solution.py:342
  406.0 29.8 %collective-permute-start.46 = (bf16[384,2048]{1,0:T(8,128)(2,1)}, bf16[384,2048]{1,0:T(8,128)(2,1)}, u32[]{:S(2)}, u32[]{:S(2)}) collective-permute-start(bf16[384,2048]{1,0:T(8,128)(2,1)} %convolution_convert_fusion), channel_id=1, source_target_pairs={{0,8},{8,0},{16,24},{24,16},{1,9},{9,1},{17,25},{25,17},{2,10},{10... | collective-permute-start | bytes 4718600 | tf_op jit(solution)/shard_map/ppermute | solution.py:350
  417.7 57.4 %collective-permute-start.52 = (bf16[192,2048]{1,0:T(8,128)(2,1)S(1)}, bf16[192,2048]{1,0:T(8,128)(2,1)S(1)}, u32[]{:S(2)}, u32[]{:S(2)}) collective-permute-start(bf16[192,2048]{1,0:T(8,128)(2,1)S(1)} %copy-done.112), channel_id=1, source_target_pairs={{0,16},{8,24},{16,0},{24,8},{1,17},{9,25},{17,1},{25,9},{2,18},{10... | collective-permute-start | bytes 2359304 | tf_op jit(solution)/shard_map/ppermute | solution.py:346
  417.7 14.6 %collective-permute-start.44 = (bf16[128,2048]{1,0:T(8,128)(2,1)}, bf16[128,2048]{1,0:T(8,128)(2,1)S(1)}, u32[]{:S(2)}, u32[]{:S(2)}) collective-permute-start(bf16[128,2048]{1,0:T(8,128)(2,1)} %collective-permute-done.42), channel_id=1, source_target_pairs={{0,1},{1,0},{2,3},{3,2},{4,5},{5,4},{6,7},{7,6},{8,9},{9,8},{10,11... | collective-permute-start | bytes 1572872 | tf_op jit(solution)/shard_map/ppermute | solution.py:338
  418.5 15.3 %collective-permute-start.45 = (bf16[128,2048]{1,0:T(8,128)(2,1)}, bf16[128,2048]{1,0:T(8,128)(2,1)S(1)}, u32[]{:S(2)}, u32[]{:S(2)}) collective-permute-start(bf16[128,2048]{1,0:T(8,128)(2,1)} %collective-permute-done.42), channel_id=1, source_target_pairs={{0,2},{1,3},{2,6},{3,7},{6,4},{7,5},{4,0},{5,1},{8,10},{9,11},{10,... | collective-permute-start | bytes 1572872 | tf_op jit(solution)/shard_map/ppermute | solution.py:342
  440.5 14.4 %collective-permute-start.48 = (bf16[128,2048]{1,0:T(8,128)(2,1)S(1)}, bf16[128,2048]{1,0:T(8,128)(2,1)S(1)}, u32[]{:S(2)}, u32[]{:S(2)}) collective-permute-start(bf16[128,2048]{1,0:T(8,128)(2,1)S(1)} %pad_maximum_fusion.24), channel_id=1, source_target_pairs={{0,1},{1,0},{2,3},{3,2},{4,5},{5,4},{6,7},{7,6},{8,9},{9,8},{10,11... | collective-permute-start | bytes 1572872 | tf_op jit(solution)/shard_map/ppermute | solution.py:338
  442.0 15.0 %collective-permute-start.49 = (bf16[128,2048]{1,0:T(8,128)(2,1)S(1)}, bf16[128,2048]{1,0:T(8,128)(2,1)S(1)}, u32[]{:S(2)}, u32[]{:S(2)}) collective-permute-start(bf16[128,2048]{1,0:T(8,128)(2,1)S(1)} %pad_maximum_fusion.25), channel_id=1, source_target_pairs={{0,2},{1,3},{2,6},{3,7},{6,4},{7,5},{4,0},{5,1},{8,10},{9,11},{10,... | collective-permute-start | bytes 1572872 | tf_op jit(solution)/shard_map/ppermute | solution.py:342
  444.4 52.2 %collective-permute-start.57 = (bf16[192,2048]{1,0:T(8,128)(2,1)S(1)}, bf16[192,2048]{1,0:T(8,128)(2,1)S(1)}, u32[]{:S(2)}, u32[]{:S(2)}) collective-permute-start(bf16[192,2048]{1,0:T(8,128)(2,1)S(1)} %slice.733), channel_id=1, source_target_pairs={{0,16},{8,24},{16,0},{24,8},{1,17},{9,25},{17,1},{25,9},{2,18},{10... | collective-permute-start | bytes 2359304 | tf_op jit(solution)/shard_map/ppermute | solution.py:346
  456.9 16.7 %collective-permute-start.54 = (f32[512]{0:T(512)S(1)}, f32[512]{0:T(512)S(1)}, u32[]{:S(2)}, u32[]{:S(2)}) collective-permute-start(f32[512]{0:T(512)S(1)} %bitcast.130), channel_id=1, source_target_pairs={{0,16},{8,24},{16,0},{24,8},{1,17},{9,25},{17,1},{25,9},{2,18},{10... | collective-permute-start | bytes 6152 | tf_op jit(solution)/shard_map/ppermute | solution.py:346
  458.9 14.7 %collective-permute-start.50 = (bf16[128,2048]{1,0:T(8,128)(2,1)S(1)}, bf16[128,2048]{1,0:T(8,128)(2,1)S(1)}, u32[]{:S(2)}, u32[]{:S(2)}) collective-permute-start(bf16[128,2048]{1,0:T(8,128)(2,1)S(1)} %pad_maximum_fusion.27), channel_id=1, source_target_pairs={{0,1},{1,0},{2,3},{3,2},{4,5},{5,4},{6,7},{7,6},{8,9},{9,8},{10,11... | collective-permute-start | bytes 1572872 | tf_op jit(solution)/shard_map/ppermute | solution.py:338
  486.7 21.7 %collective-permute-start.60 = (bf16[2,512,768]{2,1,0:T(8,128)(2,1)}, bf16[2,512,768]{2,1,0:T(8,128)(2,1)}, u32[]{:S(2)}, u32[]{:S(2)}) collective-permute-start(bf16[2,512,768]{2,1,0:T(8,128)(2,1)} %get-tuple-element.282), channel_id=1, source_target_pairs={{0,8},{8,0},{16,24},{24,16},{1,9},{9,1},{17,25},{25,17},{2,10},{10... | collective-permute-start | bytes 4718600 | tf_op jit(solution)/shard_map/ppermute | solution.py:350
  497.5 36.3 %collective-permute-start.58 = (bf16[384,2048]{1,0:T(8,128)(2,1)}, bf16[384,2048]{1,0:T(8,128)(2,1)}, u32[]{:S(2)}, u32[]{:S(2)}) collective-permute-start(bf16[384,2048]{1,0:T(8,128)(2,1)} %slice_dynamic-update-slice_fusion), channel_id=1, source_target_pairs={{0,1},{1,0},{2,3},{3,2},{4,5},{5,4},{6,7},{7,6},{8,9},{9,8},{10,11... | collective-permute-start | bytes 4718600 | tf_op jit(solution)/shard_map/ppermute | solution.py:338
  498.3 37.3 %collective-permute-start.59 = (bf16[384,2048]{1,0:T(8,128)(2,1)}, bf16[384,2048]{1,0:T(8,128)(2,1)}, u32[]{:S(2)}, u32[]{:S(2)}) collective-permute-start(bf16[384,2048]{1,0:T(8,128)(2,1)} %fusion.69), channel_id=1, source_target_pairs={{0,2},{1,3},{2,6},{3,7},{6,4},{7,5},{4,0},{5,1},{8,10},{9,11},{10,... | collective-permute-start | bytes 4718600 | tf_op jit(solution)/shard_map/ppermute | solution.py:342
  509.8 30.6 %collective-permute-start.62 = (bf16[512,768]{1,0:T(8,128)(2,1)S(1)}, bf16[512,768]{1,0:T(8,128)(2,1)S(1)}, u32[]{:S(2)}, u32[]{:S(2)}) collective-permute-start(bf16[512,768]{1,0:T(8,128)(2,1)S(1)} %fusion.51), channel_id=1, source_target_pairs={{0,16},{8,24},{16,0},{24,8},{1,17},{9,25},{17,1},{25,9},{2,18},{10... | collective-permute-start | bytes 2359304 | tf_op jit(solution)/shard_map/ppermute | solution.py:346
  511.6 27.8 %collective-permute-start.61 = (bf16[128,2048]{1,0:T(8,128)(2,1)S(1)}, bf16[128,2048]{1,0:T(8,128)(2,1)S(1)}, u32[]{:S(2)}, u32[]{:S(2)}) collective-permute-start(bf16[128,2048]{1,0:T(8,128)(2,1)S(1)} %dynamic-slice_convert_fusion), channel_id=1, source_target_pairs={{0,8},{8,0},{16,24},{24,16},{1,9},{9,1},{17,25},{25,17},{2,10},{10... | collective-permute-start | bytes 1572872 | tf_op jit(solution)/shard_map/ppermute | solution.py:350
  541.2 40.1 %collective-permute-start.63 = (bf16[384,2048]{1,0:T(8,128)(2,1)}, bf16[384,2048]{1,0:T(8,128)(2,1)}, u32[]{:S(2)}, u32[]{:S(2)}) collective-permute-start(bf16[384,2048]{1,0:T(8,128)(2,1)} %pad_maximum_fusion.4), channel_id=1, source_target_pairs={{0,1},{1,0},{2,3},{3,2},{4,5},{5,4},{6,7},{7,6},{8,9},{9,8},{10,11... | collective-permute-start | bytes 4718600 | tf_op jit(solution)/shard_map/ppermute | solution.py:338
  542.3 39.8 %collective-permute-start.64 = (bf16[384,2048]{1,0:T(8,128)(2,1)}, bf16[384,2048]{1,0:T(8,128)(2,1)}, u32[]{:S(2)}, u32[]{:S(2)}) collective-permute-start(bf16[384,2048]{1,0:T(8,128)(2,1)} %pad_maximum_fusion.5), channel_id=1, source_target_pairs={{0,2},{1,3},{2,6},{3,7},{6,4},{7,5},{4,0},{5,1},{8,10},{9,11},{10,... | collective-permute-start | bytes 4718600 | tf_op jit(solution)/shard_map/ppermute | solution.py:342
  553.2 15.1 %collective-permute-start.67 = (bf16[128,2048]{1,0:T(8,128)(2,1)}, bf16[128,2048]{1,0:T(8,128)(2,1)}, u32[]{:S(2)}, u32[]{:S(2)}) collective-permute-start(bf16[128,2048]{1,0:T(8,128)(2,1)} %fusion.64), channel_id=1, source_target_pairs={{1,17},{3,19},{5,21},{7,23},{9,25},{11,27},{13,29},{15,31},{16,0},... | collective-permute-start | bytes 1572872 | tf_op jit(solution)/shard_map/ppermute | solution.py:956
  558.6 38.4 %all-to-all-start.1 = ((bf16[8,72,768]{2,1,0:T(8,128)(2,1)}), bf16[8,72,768]{2,1,0:T(8,128)(2,1)}, u32[]{:S(2)}, u32[]{:S(2)}) async-start(bf16[8,72,768]{2,1,0:T(8,128)(2,1)} %fusion.50), calls=%async_computation.1 | async-start | bytes 1769472 | tf_op jit(solution)/shard_map/all_to_all | solution.py:914
  570.1 18.6 %collective-permute-start.68 = (bf16[64,2048]{1,0:T(8,128)(2,1)S(1)}, bf16[64,2048]{1,0:T(8,128)(2,1)}, u32[]{:S(2)}, u32[]{:S(2)}) collective-permute-start(bf16[64,2048]{1,0:T(8,128)(2,1)S(1)} %dynamic-slice_convert_fusion.1), channel_id=1, source_target_pairs={{0,1},{2,3},{4,5},{6,7},{8,9},{10,11},{12,13},{14,15},{17,16},{19,... | collective-permute-start | bytes 786440 | tf_op jit(solution)/shard_map/ppermute | solution.py:965
  602.6 22.3 %collective-permute-start.65 = (bf16[256,2048]{1,0:T(8,128)(2,1)}, bf16[256,2048]{1,0:T(8,128)(2,1)S(1)}, u32[]{:S(2)}, u32[]{:S(2)}) collective-permute-start(bf16[256,2048]{1,0:T(8,128)(2,1)} %pad_maximum_fusion.11), channel_id=1, source_target_pairs={{0,1},{1,0},{2,3},{3,2},{4,5},{5,4},{6,7},{7,6},{8,9},{9,8},{10,11... | collective-permute-start | bytes 3145736 | tf_op jit(solution)/shard_map/ppermute | solution.py:338
  603.7 23.0 %collective-permute-start.66 = (bf16[256,2048]{1,0:T(8,128)(2,1)}, bf16[256,2048]{1,0:T(8,128)(2,1)S(1)}, u32[]{:S(2)}, u32[]{:S(2)}) collective-permute-start(bf16[256,2048]{1,0:T(8,128)(2,1)} %pad_maximum_fusion.12), channel_id=1, source_target_pairs={{0,2},{1,3},{2,6},{3,7},{6,4},{7,5},{4,0},{5,1},{8,10},{9,11},{10,... | collective-permute-start | bytes 3145736 | tf_op jit(solution)/shard_map/ppermute | solution.py:342
  (176 other events, 1755.3 us)
Sparse Core Ops, SparseCore 0:
  62.8 39.6 all-gather.3
  104.0 27.5 all-gather.5
  176.8 24.5 all-gather.7

commit v3 on v2

--- a/solution.py
+++ b/solution.py
@@ -363,16 +363,37 @@
     return lax.optimization_barrier((value, *earlier))[0]
 
 
+FREE = pl.CostEstimate(flops=0, bytes_accessed=0, transcendentals=0)
+LONG = pl.CostEstimate(flops=2 * 10**10, bytes_accessed=0, transcendentals=0)
+
+
+class Rows:
+    def __init__(self, array, start, count):
+        self.array, self.start, self.count = array, start, count
+
+    def part(self, start, count):
+        return Rows(self.array, self.start + start, count)
+
+    def value(self):
+        if self.count == self.array.shape[0]:
+            return self.array
+        return self.array[self.start : self.start + self.count]
+
+
+def rows_in(array):
+    return Rows(array, 0, array.shape[0])
+
+
 class Gather:
     def __init__(self, own):
-        self.held = own
+        self.held = rows_in(own)
         self.pieces = []
 
     def send(self):
         if len(self.pieces) < 3:
-            return self.held, self.held
-        half = self.held.shape[0] // 2
-        return self.held[:half], self.pieces[2][1][half:]
+            return [[self.held]], [[self.held]]
+        half = self.held.count // 2
+        return [[self.held.part(0, half)]], [[self.pieces[2][1].part(half, half)]]
 
     def take(self, from_x, from_ring):
         if len(self.pieces) < 3:
@@ -381,72 +402,113 @@
         else:
             self.pieces.append((self.held, from_x, from_ring))
 
+    def arrays(self, step):
+        return tuple(rows.value() for rows in self.pieces[step])
+
     def piece(self, step):
-        return jnp.concatenate(self.pieces[step], axis=0)
+        return jnp.concatenate(self.arrays(step), axis=0)
 
 
 class Scatter:
     def __init__(self):
-        self.kept = []
-        self.got = None
-        self.terms = None
+        self.stage = 0
 
     def of(self, terms):
-        self.terms = terms
+        rows = terms.shape[0] // 2
+        return self.of_rows(Rows(terms, 0, rows), Rows(terms, rows, rows))
+
+    def of_rows(self, own, other):
+        self.own, self.other = own, other
         return self
 
     def send(self):
-        terms = self.terms
-        rows = terms.shape[0] // 2
-        half = rows // 2
-        if not self.kept:
-            self.kept.append(terms[:rows])
-            return terms[rows : rows + half], terms[rows + half :]
-        if len(self.kept) == 1:
-            from_x, from_ring = self.got
-            total = jnp.concatenate(
-                [
-                    self.kept[0][:half].astype(jnp.float32) + from_x.astype(jnp.float32),
-                    self.kept[0][half:].astype(jnp.float32),
-                ],
-                axis=0,
+        own, other = self.own, self.other
+        half = own.count // 2
+        if self.stage == 0:
+            given = [[other.part(0, half)]], [[other.part(half, half)]]
+        elif self.stage == 1:
+            kept, (from_x, from_ring) = self.kept, self.got
+            given = (
+                [[other.part(0, half)], [other.part(half, half), from_ring]],
+                [[kept.part(0, half), from_x], [kept.part(half, half)]],
             )
-            given = jnp.concatenate(
-                [
-                    terms[rows : rows + half].astype(jnp.float32),
-                    terms[rows + half :].astype(jnp.float32) + from_ring.astype(jnp.float32),
-                ],
-                axis=0,
-            ).astype(jnp.bfloat16)
         else:
-            total, given = self.total(), terms[rows:]
-        self.kept.append(terms[:rows])
-        return given, total.astype(jnp.bfloat16)
+            given = [[other]], [[self.kept, *self.got]]
+        self.stage += 1
+        self.kept = own
+        return given
 
     def take(self, from_x, from_ring):
         self.got = (from_x, from_ring)
 
     def total(self):
-        from_x, from_ring = self.got
-        return (
-            self.kept[-1].astype(jnp.float32)
-            + from_x.astype(jnp.float32)
-            + from_ring.astype(jnp.float32)
-        )
+        return sum(rows.value().astype(jnp.float32) for rows in (self.kept, *self.got))
+
+
+def mix_kernel(plans, *refs):
+    for plan, out_ref in zip(plans, refs[-len(plans) :]):
+        first = 0
+        for places, count in plan:
+            values = [refs[index][start : start + count, :] for index, start in places]
+            if len(values) > 1:
+                values = [sum(value.astype(jnp.float32) for value in values)]
+            out_ref[first : first + count, :] = values[0].astype(out_ref.dtype)
+            first += count
+
+
+def only_array(sums):
+    array = sums[0][0].array
+    first = 0
+    for rows in sums:
+        if len(rows) > 1 or rows[0].array is not array or rows[0].start != first:
+            return None
+        first += rows[0].count
+    return array if first == array.shape[0] else None
+
+
+def mixed(*all_sums):
+    arrays = []
+    plans = []
+    for sums in all_sums:
+        plan = []
+        for rows in sums:
+            places = []
+            for part in rows:
+                index = next((n for n, held in enumerate(arrays) if held is part.array), None)
+                if index is None:
+                    index = len(arrays)
+                    arrays.append(part.array)
+                places.append((index, part.start))
+            plan.append((tuple(places), rows[0].count))
+        plans.append(tuple(plan))
+    width = arrays[0].shape[1]
+    counts = [sum(count for places, count in plan) for plan in plans]
+    return pl.pallas_call(
+        functools.partial(mix_kernel, tuple(plans)),
+        out_shape=[jax.ShapeDtypeStruct((count, width), jnp.bfloat16) for count in counts],
+        compiler_params=pltpu.CompilerParams(vmem_limit_bytes=32 * 2**20),
+        cost_estimate=FREE,
+        name="mix",
+    )(*arrays)
 
 
 def move(parts, *gate):
     sent = [part.send() for part in parts]
-    along_x, along_ring = (
-        values[0] if len(values) == 1 else jnp.concatenate(values, axis=0) for values in zip(*sent)
-    )
+    x_sums, ring_sums = (sum((given[way] for given in sent), []) for way in range(2))
+    along_x, along_ring = only_array(x_sums), only_array(ring_sums)
+    if along_x is None and along_ring is None:
+        along_x, along_ring = mixed(x_sums, ring_sums)
+    elif along_x is None:
+        (along_x,) = mixed(x_sums)
+    elif along_ring is None:
+        (along_ring,) = mixed(ring_sums)
     along_x, along_ring = after((along_x, along_ring), *gate)
     from_x, from_ring = x_swap(along_x), ring_step(along_ring)
     x_row = ring_row = 0
-    for part, (given_x, given_ring) in zip(parts, sent):
-        x_end, ring_end = x_row + given_x.shape[0], ring_row + given_ring.shape[0]
-        part.take(from_x[x_row:x_end], from_ring[ring_row:ring_end])
-        x_row, ring_row = x_end, ring_end
+    for part, given in zip(parts, sent):
+        x_count, ring_count = (sum(rows[0].count for rows in sums) for sums in given)
+        part.take(Rows(from_x, x_row, x_count), Rows(from_ring, ring_row, ring_count))
+        x_row, ring_row = x_row + x_count, ring_row + ring_count
     return [from_x, from_ring]
 
 
@@ -538,9 +600,7 @@
             jax.ShapeDtypeStruct((width // head, count, 1), jnp.float32),
         ],
         compiler_params=pltpu.CompilerParams(vmem_limit_bytes=40 * 2**20),
-        cost_estimate=pl.CostEstimate(
-            flops=count * count, bytes_accessed=count * width, transcendentals=0
-        ),
+        cost_estimate=LONG,
         name="attend",
     )(queries, pairs, pairs, first, last, place)
 
@@ -569,9 +629,7 @@
         ],
         scratch_shapes=[pltpu.VMEM((count, head), jnp.float32)] * 2,
         compiler_params=pltpu.CompilerParams(vmem_limit_bytes=40 * 2**20),
-        cost_estimate=pl.CostEstimate(
-            flops=count * count, bytes_accessed=count * width, transcendentals=0
-        ),
+        cost_estimate=LONG,
         name="attend_back",
     )(queries, pairs, pairs, first, last, place, lse, attended, d_attended)
 
@@ -631,7 +689,7 @@
                 (8 * (3 * each + extra.shape[0]), width // 8), self.weights[0].dtype
             ),
             compiler_params=pltpu.CompilerParams(vmem_limit_bytes=16 * 2**20),
-            cost_estimate=pl.CostEstimate(flops=0, bytes_accessed=2**20, transcendentals=0),
+            cost_estimate=LONG,
             name="payload",
         )(*self.weights, extra)
         self.held = lax.all_to_all(after(given, *gate), "fsdp", 0, 0, tiled=True)
@@ -678,7 +736,7 @@
                 jax.ShapeDtypeStruct((4, extra, mine), low),
             ],
             compiler_params=pltpu.CompilerParams(vmem_limit_bytes=32 * 2**20),
-            cost_estimate=pl.CostEstimate(flops=0, bytes_accessed=2**20, transcendentals=0),
+            cost_estimate=FREE,
             name="columns",
         )(self.dp.reshape(1).astype(jnp.int32), self.held)
         gains = gains.reshape(32, -1)[:, : self.gains.shape[0]].astype(jnp.float32)
@@ -707,8 +765,30 @@
         kept_ref[0, :, mine:] = for_kv
 
 
-def own_grads_kernel(got_ref, wq_ref, wk_ref, wv_ref, q_ref, k_ref, v_ref, q_sum_ref, kv_sum_ref):
+def own_grads_kernel(
+    got_ref,
+    wq_ref,
+    wk_ref,
+    wv_ref,
+    flag_ref,
+    out_kept_ref,
+    out_got_ref,
+    q_ref,
+    k_ref,
+    v_ref,
+    q_sum_ref,
+    kv_sum_ref,
+    gain_ref,
+    out_ref,
+):
     each = wq_ref.shape[0]
+    gain = 0.0
+    for device in range(8):
+        gain = gain + got_ref[device, each : each + 8, :128].astype(jnp.float32)
+    gain_ref[...] = gain
+    out_ref[...] = jnp.where(
+        flag_ref[...] != 0, out_kept_ref[...], out_got_ref[...].astype(jnp.float32)
+    )
     head = wq_ref.shape[1] // 16
     sums = []
     for which, (w_ref, out_ref) in enumerate(((wq_ref, q_ref), (wk_ref, k_ref), (wv_ref, v_ref))):
@@ -724,9 +804,6 @@
     kv_sum_ref[...] = sums[1] + sums[2]
 
 
-FREE = pl.CostEstimate(flops=0, bytes_accessed=0, transcendentals=0)
-
-
 def whole_block(array):
     return pl.BlockSpec(array.shape, lambda *place: (0,) * array.ndim)
 
@@ -753,7 +830,7 @@
         out_ref[...] = product(low_ref[...], w_ref[...]).astype(jnp.bfloat16)
 
 
-def project(piece, kv_gain, attn_gain, w_kv, wq):
+def project(piece, kv_gain, attn_gain, w_kv, wq, cost):
     rows, width = piece[0].shape
     low = piece[0].dtype
     return pl.pallas_call(
@@ -765,35 +842,109 @@
             jax.ShapeDtypeStruct((rows, wq.shape[1]), low),
         ],
         compiler_params=pltpu.CompilerParams(vmem_limit_bytes=40 * 2**20),
-        cost_estimate=FREE,
+        cost_estimate=cost,
         name="project",
     )(*piece, kv_gain, attn_gain, w_kv, wq)
 
 
-def input_terms_kernel(pair_ref, query_ref, w_kv_ref, wq_ref, src_ref, hid_ref):
-    src_ref[...] = rows_by_rows(pair_ref[...], w_kv_ref[...]).astype(jnp.bfloat16)
-    hid_ref[...] = rows_by_rows(query_ref[...], wq_ref[...]).astype(jnp.bfloat16)
-
-
-def input_terms(step, d_pairs, d_queries, w_kv, wq):
+def terms_kernel(step, result_step, pair_ref, query_ref, w_kv_ref, wq_ref, *refs):
+    own_ref, other_ref = refs[-2:]
+    count = pair_ref.shape[0] // 4
+    here = slice(count * step, count * (step + 1))
+    found = [
+        rows_by_rows(pair_ref[here, :], w_kv_ref[...]),
+        rows_by_rows(query_ref[here, :], wq_ref[...]),
+    ]
+    if len(refs) > 2:
+        there = slice(count * result_step, count * (result_step + 1))
+        found.append(product(refs[0][there, :], refs[1][...]))
+    rows = count // 2
+    for place, value in enumerate(found):
+        value = value.astype(jnp.bfloat16)
+        own_ref[rows * place : rows * (place + 1), :] = value[:rows]
+        other_ref[rows * place : rows * (place + 1), :] = value[rows:]
+
+
+def back_terms(parts, step, d_pairs, d_queries, w_kv, wq, result=()):
     rows, width = d_pairs.shape[0] // 4, w_kv.shape[0]
-    out = jax.ShapeDtypeStruct((rows, width), jnp.bfloat16)
-    out_spec = pl.BlockSpec((rows, width), lambda i: (0, 0))
-    return pl.pallas_call(
-        input_terms_kernel,
-        grid=(1,),
-        in_specs=[
-            pl.BlockSpec((rows, d_pairs.shape[1]), lambda i: (step, 0)),
-            pl.BlockSpec((rows, d_queries.shape[1]), lambda i: (step, 0)),
-            whole_block(w_kv),
-            whole_block(wq),
-        ],
-        out_specs=[out_spec, out_spec],
+    result_step, *weights = result or (None,)
+    count = rows // 2
+    out = jax.ShapeDtypeStruct((count * len(parts), width), jnp.bfloat16)
+    own, other = pl.pallas_call(
+        functools.partial(terms_kernel, step, result_step),
         out_shape=[out, out],
         compiler_params=pltpu.CompilerParams(vmem_limit_bytes=40 * 2**20),
         cost_estimate=FREE,
-        name="input_terms",
-    )(d_pairs, d_queries, w_kv, wq)
+        name="back_terms",
+    )(d_pairs, d_queries, w_kv, wq, *weights)
+    return [
+        part.of_rows(Rows(own, count * place, count), Rows(other, count * place, count))
+        for place, part in enumerate(parts)
+    ]
+
+
+def row_blocks(rows, count):
+    first = rows.start // count
+    return pl.BlockSpec((count, rows.array.shape[1]), lambda i: (first + i, 0))
+
+
+def result_kernel(middle_ref, live_ref, kept_ref, x_ref, ring_ref, out_ref):
+    total = middle_ref[...] + kept_ref[...].astype(jnp.float32)
+    total = total + x_ref[...].astype(jnp.float32) + ring_ref[...].astype(jnp.float32)
+    out_ref[...] = (total * live_ref[...]).astype(jnp.bfloat16)
+
+
+def result_of(middle, live, scatter):
+    sums = [scatter.kept, *scatter.got]
+    rows, width = middle.shape
+    block = rows // 4
+    return pl.pallas_call(
+        result_kernel,
+        grid=(4,),
+        in_specs=[
+            pl.BlockSpec((block, width), lambda i: (i, 0)),
+            pl.BlockSpec((block, 1), lambda i: (i, 0)),
+        ]
+        + [row_blocks(part, block) for part in sums],
+        out_specs=pl.BlockSpec((block, width), lambda i: (i, 0)),
+        out_shape=jax.ShapeDtypeStruct((rows, width), jnp.bfloat16),
+        compiler_params=pltpu.CompilerParams(vmem_limit_bytes=16 * 2**20),
+        cost_estimate=FREE,
+        name="result",
+    )(middle, live, *(part.array for part in sums))
+
+
+def input_grads_kernel(hidden_ref, source_ref, d_middle_ref, attn_gain_ref, kv_gain_ref, *refs):
+    d_hid, d_src = (
+        sum(ref[...].astype(jnp.float32) for ref in refs[first : first + 3]) for first in (0, 3)
+    )
+    hidden = hidden_ref[...].astype(jnp.float32)
+    source = source_ref[...].astype(jnp.float32)
+    refs[6][...] = (
+        d_middle_ref[...] + norm_backward(hidden, inverse_scale(hidden), attn_gain_ref[...], d_hid)
+    ).astype(jnp.bfloat16)
+    refs[7][...] = norm_backward(
+        source, inverse_scale(source), kv_gain_ref[...], d_src
+    ).astype(jnp.bfloat16)
+
+
+def input_grads(hidden, source, d_middle, attn_gain, kv_gain, d_hid, d_src):
+    sums = [d_hid.kept, *d_hid.got, d_src.kept, *d_src.got]
+    rows, width = hidden.shape
+    block = rows // 4
+    spec = pl.BlockSpec((block, width), lambda i: (i, 0))
+    return pl.pallas_call(
+        input_grads_kernel,
+        grid=(4,),
+        in_specs=[spec] * 3
+        + [whole_block(attn_gain), whole_block(kv_gain)]
+        + [row_blocks(part, block) for part in sums],
+        out_specs=[spec, spec],
+        out_shape=[jax.ShapeDtypeStruct((rows, width), jnp.bfloat16)] * 2,
+        compiler_params=pltpu.CompilerParams(vmem_limit_bytes=16 * 2**20),
+        cost_estimate=FREE,
+        name="input_grads",
+    )(hidden, source, d_middle, attn_gain, kv_gain, *(part.array for part in sums))
 
 
 def add_kernel(*refs):
@@ -807,7 +958,7 @@
     width = kept[0].shape[1]
     block = width // 4
     count = len(kept)
-    spec = pl.BlockSpec((kept[0].shape[0], block), lambda i: (0, i))
+    spec = pl.BlockSpec((got[0].shape[0], block), lambda i: (0, i))
     return pl.pallas_call(
         add_kernel,
         grid=(4,),
@@ -815,7 +966,7 @@
         out_specs=[pl.BlockSpec((rows, block), lambda i: (0, i))] * count,
         out_shape=[jax.ShapeDtypeStruct((rows, width), jnp.float32)] * count,
         compiler_params=pltpu.CompilerParams(vmem_limit_bytes=40 * 2**20),
-        cost_estimate=FREE,
+        cost_estimate=LONG,
         name="add_all",
     )(*kept, *got)
 
@@ -890,9 +1041,7 @@
                 jax.ShapeDtypeStruct((2, block, 3 * mine), jnp.float32),
             ],
             compiler_params=pltpu.CompilerParams(vmem_limit_bytes=40 * 2**20),
-            cost_estimate=pl.CostEstimate(
-                flops=rows * width, bytes_accessed=2**20, transcendentals=0
-            ),
+            cost_estimate=LONG,
             name="column_grads",
         )(self.dp.reshape(1).astype(jnp.int32), *sources, *hiddens, d_queries, d_pairs)
         self.from_core = core_swap(given)
@@ -914,20 +1063,28 @@
         self.got = lax.all_to_all(given, "fsdp", 0, 0, tiled=True)
         return [given], [self.got]
 
-    def whole(self, weights, *gate):
+    def whole(self, weights, out_grads, *gate):
         each, width = weights[0].shape
-        got = after(self.got, *gate)
+        got, out_got = after((self.got, out_grads.from_x), *gate)
+        flag = (out_grads.x == out_grads.y).astype(jnp.int32).reshape(1, 1)
         flat = jax.ShapeDtypeStruct((each, width), jnp.float32)
         column = jax.ShapeDtypeStruct((each, 1), jnp.float32)
         out = pl.pallas_call(
             own_grads_kernel,
-            out_shape=[flat, flat, flat, column, column],
+            out_shape=[
+                flat,
+                flat,
+                flat,
+                column,
+                column,
+                jax.ShapeDtypeStruct((8, 128), jnp.float32),
+                flat,
+            ],
             compiler_params=pltpu.CompilerParams(vmem_limit_bytes=32 * 2**20),
-            cost_estimate=pl.CostEstimate(flops=0, bytes_accessed=2**20, transcendentals=0),
+            cost_estimate=FREE,
             name="own_grads",
-        )(got, *weights)
-        gain = jnp.sum(got[:, each, :each].astype(jnp.float32), axis=0)
-        return out, gain
+        )(got, *weights, flag, out_grads.kept, out_got)
+        return out, out[5][0, :each]
 
 
 def out_rows(own, x, y, c, before, late):
@@ -964,10 +1121,6 @@
         pairs = [(place, place ^ 1) for place in range(32) if place // 16 == place % 2]
         self.from_x = lax.ppermute(given.astype(jnp.bfloat16), ("dp", "fsdp"), pairs)
 
-    def whole(self, *gate):
-        got = after(self.from_x, *gate)
-        return jnp.where(self.x == self.y, self.kept, got.astype(jnp.float32))
-
 
 def hidden_units(own, padded, dp, *gate):
     rows = jnp.pad(own, ((0, padded - own.shape[0]), (0, 0)))
@@ -987,7 +1140,7 @@
         units, got = after((self.units, self.from_core), *gate)
         total = columns_by_columns(units[:, :half], self.rows) + got.astype(jnp.float32)
         given = total[half // 2 :].astype(jnp.bfloat16)
-        self.kept = total[: half // 2]
+        self.kept = total
         self.from_y = y_swap(given)
         return [given]
 
@@ -1017,25 +1170,6 @@
     z, x = fsdp // 2, fsdp % 2
     me = 8 * dp + fsdp
 
-    each = kv_gain.shape[0]
-    inputs = Gather(jnp.concatenate([source, hidden], axis=0))
-    columns = Columns(
-        [w_query, w_key, w_value], jnp.concatenate([kv_gain, attn_gain, ffn_gain]), dp
-    )
-    wa = columns.along_fsdp()
-    s1 = move([inputs])
-    wy = columns.along_y(*wa)
-    s2 = move([inputs], *s1, *wa)
-    wc = columns.along_core(*wy)
-    s3 = move([inputs], *s2, *wy)
-    wq, w_kv, gains = columns.whole()
-    kv_gain_full, attn_gain_full, ffn_gain_full = (
-        gains[:, which * each : (which + 1) * each].reshape(1, width) for which in range(3)
-    )
-    units = w_gate.shape[0]
-    padded = -(-units // 64) * 64
-    wg, wu, wd = (hidden_units(own, padded, dp, *s1, *wa) for own in (w_gate, w_up, w_down))
-
     order = z ^ (z >> 1)
     devices = []
     for step in range(4):
@@ -1060,26 +1194,51 @@
     place_of_key = jnp.where(live, position, -1)[None, :]
     own_live = live[:local_rows].astype(jnp.float32)[:, None]
 
+    def layout():
+        return first, last, place_of_key, own_live
+
+    each = kv_gain.shape[0]
+    inputs = Gather(jnp.concatenate([source, hidden], axis=0))
+    columns = Columns(
+        [w_query, w_key, w_value], jnp.concatenate([kv_gain, attn_gain, ffn_gain]), dp
+    )
+    wa = columns.along_fsdp()
+    s1 = move([inputs])
+    wy = columns.along_y(*s1)
+    s2 = move([inputs], *s1, *wa, *layout())
+    wc = columns.along_core(*wy)
+    s3 = move([inputs], *s2)
+    wq, w_kv, gains = columns.whole()
+    kv_gain_full, attn_gain_full, ffn_gain_full = (
+        gains[:, which * each : (which + 1) * each].reshape(1, width) for which in range(3)
+    )
+    units = w_gate.shape[0]
+    padded = -(-units // 64) * 64
+    wg, wu, wd = (hidden_units(own, padded, dp, *s2, *wy) for own in (w_gate, w_up, w_down))
+
     hidden_f = hidden.astype(jnp.float32)
     d_out = cotangent.astype(jnp.float32) * own_live
     projected = []
 
-    def project_piece(step):
-        piece = after(tuple(inputs.pieces[step]), *(value[3] for value in projected[-1:]))
-        projected.append(project(piece, kv_gain_full, attn_gain_full, w_kv, wq))
-
-    project_piece(0)
-    project_piece(1)
+    def project_piece(step, cost, *gate):
+        piece = after(inputs.arrays(step), *(value[3] for value in projected[-1:]), *gate)
+        projected.append(project(piece, kv_gain_full, attn_gain_full, w_kv, wq, cost))
+
+    project_piece(0, FREE)
+    project_piece(1, FREE)
     s4 = move([inputs], *s3)
-    project_piece(2)
+    project_piece(2, LONG, *s3)
     cots = Gather(d_out.astype(jnp.bfloat16))
-    c1 = move([cots], *s4)
-    project_piece(3)
+    c1 = move([cots], *s4, projected[2][3])
+    project_piece(3, LONG)
     src_low, hid_low, pairs, queries = zip(*projected)
     queries = jnp.concatenate(queries, axis=0)
     pairs = jnp.concatenate(pairs, axis=0)
-    attended_f, attended_low, lse = attend(queries, pairs, first, last, place_of_key, head)
-    wo = out_rows(after(w_out, *s3), x, y, c, s4, [attended_low])
+    c2 = move([cots], *c1, pairs, queries)
+    attended_f, attended_low, lse = attend(
+        *after((queries, pairs), *c1), first, last, place_of_key, head
+    )
+    wo = out_rows(after(w_out, *s3), x, y, c, s4, c1)
 
     def rows_of(array, step):
         return array[2 * step * local_rows : 2 * (step + 1) * local_rows]
@@ -1088,9 +1247,9 @@
         return product(after(rows_of(attended_low, step), *gate), wo).astype(jnp.bfloat16)
 
     branch = Scatter()
-    b1 = move([branch.of(branch_terms(1)), cots], *c1)
+    b1 = move([branch.of(branch_terms(1)), cots], *c2)
     b2 = move([branch.of(branch_terms(2)), cots], *b1)
-    b3 = move([branch.of(branch_terms(3, *b1)), cots], *b2)
+    b3 = move([branch.of(branch_terms(3, *b1))], *b2)
     b4 = move([branch.of(branch_terms(0, *b2))], *b3)
     middle = hidden_f + branch.total()
     middle_scale = inverse_scale(middle)
@@ -1133,7 +1292,8 @@
     h1 = gate_sums.along_core(after(d_gates, *d2), all_mids)
     d4 = move([back.of(t0)], *d3, *h1)
     h2 = up_sums.along_core(after(d_ups, *d3), all_mids)
-    d_normed = after(back.total(), *h2)
+    h3 = down_sums.along_core(after(inners, *d3), all_cots)
+    d_normed = after(back.total(), *h2, *h3)
     d_middle = d_out + norm_backward(middle, middle_scale, ffn_gain_full, d_normed)
     d_branch_low = d_middle.astype(jnp.bfloat16)
     outs = Gather(d_branch_low)
@@ -1141,16 +1301,16 @@
     h1 = gate_sums.along_y(d_branch_low)
     e2 = move([outs], *e1, *h1)
     h2 = up_sums.along_y(*e1)
-    h3 = down_sums.along_core(after(inners, *e1), all_cots)
-    e3 = move([outs], *e2, *h2, *h3)
-    ffn_gain_part = jnp.sum(after(d_normed * middle_unit, *e2), axis=0)
+    e3 = move([outs], *e2, *h2)
     h3 = down_sums.along_y(*e2)
 
     def result_terms(step, *gate):
         return product(after(rows_of(inners, step), *gate), wd).astype(jnp.bfloat16)
 
     result = Scatter()
-    e4 = move([outs, result.of(result_terms(1, *e2))], *e3, *h3, gate_sums.from_y)
+    first_result = result_terms(1, *e2, *h3)
+    ffn_gain_part = jnp.sum(after(d_normed * middle_unit, first_result), axis=0)
+    e4 = move([outs, result.of(first_result)], *e3, ffn_gain_part, gate_sums.from_y)
     column_grads = ColumnGrads(dp)
     column_grads.gain_core(ffn_gain_part, *e3)
     column_grads.gain_y(*e4)
@@ -1158,35 +1318,33 @@
     d_attended = jnp.concatenate(
         [rows_by_rows(rows, wo).astype(jnp.bfloat16) for rows in d_branches], axis=0
     )
-    o2 = move([result.of(result_terms(2, *e3))], *e4)
+    o2 = move([result.of(result_terms(2, *e3))], *e4, up_sums.from_y, down_sums.from_y, column_grads.gain)
     d_queries, d_pairs = attend_back(
         queries, pairs, first, last, place_of_key, lse, attended_f, d_attended, head
     )
     d_queries, d_pairs = after((d_queries, d_pairs), *o2)
     d_src, d_hid = Scatter(), Scatter()
 
-    def terms(step, *gate):
-        rows = input_terms(step, *after((d_pairs, d_queries), *gate), w_kv, wq)
-        return [d_src.of(rows[0]), d_hid.of(rows[1])]
+    def terms(step, *gate, result=()):
+        parts = [d_src, d_hid, *result[:1]]
+        rows = after((d_pairs, d_queries), *gate)
+        weights = (*result[1:], inners, wd) if result else ()
+        return back_terms(parts, step, *rows, w_kv, wq, weights)
 
     first_terms = terms(1)
-    started = d_hid.terms
-    i1 = move(first_terms, *o2, up_sums.from_y, column_grads.gain)
+    started = d_hid.own.array
+    i1 = move(first_terms, *o2)
     sources, hiddens = after((tuple(src_low), tuple(hid_low)), started)
     column_grads.along_core(sources, hiddens, d_queries, d_pairs)
     py = column_grads.along_y()
-    i2 = move(
-        terms(2, started) + [result.of(result_terms(3, started))],
-        *i1,
-        down_sums.from_y,
-    )
+    i2 = move(terms(2, started, result=(result, 3)), *i1)
     out_grads = OutGrads(
-        columns_by_columns(after(attended_low, *i1, *py), jnp.concatenate(d_branches, axis=0)), x, y, c
+        columns_by_columns(after(attended_low, *i1), jnp.concatenate(d_branches, axis=0)), x, y, c
     )
     out_grads.along_core()
     oy = out_grads.along_y(column_grads.from_y)
-    pz, got_z = column_grads.along_fsdp(*i2)
-    i3 = move(terms(3, *i1) + [result.of(result_terms(0, *i1))], *i2, *oy)
+    pz, got_z = column_grads.along_fsdp()
+    i3 = move(terms(3, *i1, result=(result, 0)), *i2, *oy, *pz)
     out_grads.along_x(*i2)
     i4 = move(terms(0, *i2), *i3)
     grad_gate, grad_up, grad_down = add_all(
@@ -1198,21 +1356,14 @@
         ),
         units,
     )
-    output = ((middle + after(result.total(), *i3)) * own_live).astype(jnp.bfloat16)
-    d_src, d_hid = d_src.total(), d_hid.total()
-
-    grad_out = out_grads.whole(*i3)
-    own_grads, grad_ffn_gain = column_grads.whole([w_query, w_key, w_value], *i3)
-    grad_query, grad_key, grad_value, query_sum, pair_sum = own_grads
+    output = result_of(after(middle, grad_gate), own_live, result)
+    own_grads, grad_ffn_gain = column_grads.whole([w_query, w_key, w_value], out_grads, grad_gate)
+    grad_query, grad_key, grad_value, query_sum, pair_sum, gain_sum, grad_out = own_grads
     grad_attn_gain = query_sum[:, 0] / attn_gain.astype(jnp.float32)
     grad_kv_gain = pair_sum[:, 0] / kv_gain.astype(jnp.float32)
 
-    grad_hidden = (
-        d_middle + norm_backward(hidden_f, inverse_scale(hidden_f), attn_gain_full, d_hid)
-    ).astype(jnp.bfloat16)
-    source_f = source.astype(jnp.float32)
-    grad_source = norm_backward(source_f, inverse_scale(source_f), kv_gain_full, d_src).astype(
-        jnp.bfloat16
+    grad_hidden, grad_source = input_grads(
+        hidden, source, d_middle, attn_gain_full, kv_gain_full, d_hid, d_src
     )
     return (
         output,

time: 647 us -> 590 us (0.912)
  waiting for transfers between devices: 313 us -> 248 us
  Pallas kernels: 47.8 us -> 71.2 us
  starting transfers between devices: 67 us -> 90.3 us
  other arithmetic: 49 us -> 28 us
  local copies, waits for them, and re-layouts: 88 us -> 78.9 us
  matrix products: 55 us -> 47.2 us
    ppermute x25 -> x26, waiting for transfers between devices: 123 us -> 65.1 us  [ring_step(): return lax.ppermute(value, 'fsdp', ring_pairs())]
    pallas_call x4 -> x21, Pallas kernels: 4.2 us -> 30.2 us  [the longest x15 14.6 us: mixed(): pl.pallas_call(functools.partial(mix_kernel, tuple(plans)), out_shape=[ja...]
    ppermute x25 -> x26, starting transfers between devices: 13.4 us -> 32.5 us  [ring_step(): return lax.ppermute(value, 'fsdp', ring_pairs())]
    slice x28 -> x0, local copies, waits for them, and re-layouts: 14.6 us -> none  [the longest x3 5.36 us: along_y(): self.kept = total[:half // 2]]
    all_to_all x1, waiting for transfers between devices: 0.01 us -> 13.7 us  [along_fsdp(): self.held = lax.all_to_all(after(given, *gate), 'fsdp', 0, 0, tiled=True)]
    convert_element_type x8 -> x0, other arithmetic: 10.8 us -> none  [the longest x6 8.14 us: send(): return (given, total.astype(jnp.bfloat16))]
    ppermute x6, waiting for transfers between devices: 28 us -> 18.3 us  [y_swap(): return lax.ppermute(value, 'dp', swap_pairs(4, 2))]
    concatenate x19 -> x0, other arithmetic: 8.09 us -> none  [the longest x15 7.92 us: move(): jnp.concatenate(values, axis=0)]
  transfers between devices with their start and end apart: 74 -> 76, of which waited for: 44 -> 48; matrix products, arithmetic and copies ran while one was open for 21% -> 18% of each run, Pallas kernels for 7% -> 10%
where the time goes in v3:
time: 590 us; the launch traced here: 580 us
  waiting for transfers between devices  248 us (42%)
  starting transfers between devices  90.3 us (15%)
  local copies, waits for them, and re-layouts  78.9 us (13%)
  Pallas kernels  71.2 us (12%)
  matrix products  47.2 us (8%)
  other arithmetic  28 us (5%)
  between operations  16.3 us (3%)
    ppermute x27, waiting for transfers between devices, x_swap(): return lax.ppermute(value, 'fsdp', swap_pairs(8, 1))  149 us
    ppermute x26, waiting for transfers between devices, ring_step(): return lax.ppermute(value, 'fsdp', ring_pairs())  65.1 us
    unnamed x319, local copies, waits for them, and re-layouts  59.1 us
    ppermute x26, starting transfers between devices, ring_step(): return lax.ppermute(value, 'fsdp', ring_pairs())  32.5 us
    ppermute x27, starting transfers between devices, x_swap(): return lax.ppermute(value, 'fsdp', swap_pairs(8, 1))  29.2 us
    dot_general x16, matrix products, rows_by_rows(): lax.dot_general(left, right, (((1,), (1,)), ((), ())), preferred_element_...  23 us
    ppermute x6, waiting for transfers between devices, y_swap(): return lax.ppermute(value, 'dp', swap_pairs(4, 2))  18.3 us
    pallas_call x15, Pallas kernels, mixed(): pl.pallas_call(functools.partial(mix_kernel, tuple(plans)), out_shape=[ja...  14.6 us
  transfers between devices with their start and end apart: 76, of which 48 were waited for; matrix products, arithmetic and copies ran while one was open for 18% of the time, Pallas kernels for 10%

profile of v3, /device:TPU:0, one launch (start us, length us, event | category | flops | bytes accessed | tf_op | source)
XLA Modules:
  0.0 580.1 jit_solution(6131713698802191170)
XLA Ops:
  9.4 3.1 collective-permute-start.1
  18.6 4.2 all-to-all-start
  29.0 8.4 %collective-permute-done.1.held_ref = bf16[256,2048]{1,0:T(8,128)(2,1)S(1)} collective-permute-done((bf16[256,2048]{1,0:T(8,128)(2,1)S(1)}, bf16[256,2048]{1,0:T(8,128)(2,1)S(1)}, u32[]{:S(2)}, u32[]{:S(2)}) %collective-permute-start.1) | collective-permute-done | bytes 1048608 | tf_op jit(solution)/shard_map/ppermute | solution.py:342
  37.5 3.2 collective-permute-done.refs_0_
  40.6 13.7 %all-to-all-done = bf16[8,200,256]{2,1,0:T(8,128)(2,1)} async-done(((bf16[8,200,256]{2,1,0:T(8,128)(2,1)}), bf16[8,200,256]{2,1,0:T(8,128)(2,1)}, u32[]{:S(2)}, u32[]{:S(2)}) %all-to-all-start) | async-done | bytes 819232 | tf_op jit(solution)/shard_map/all_to_all | solution.py:695
  60.3 17.3 %collective-permute-done.2 = bf16[1600,256]{1,0:T(8,128)(2,1)} collective-permute-done((bf16[1600,256]{1,0:T(8,128)(2,1)}, bf16[1600,256]{1,0:T(8,128)(2,1)}, u32[]{:S(2)}, u32[]{:S(2)}) %collective-permute-start.2) | collective-permute-done | bytes 819232 | tf_op jit(solution)/shard_map/ppermute | solution.py:346
  100.8 13.0 %collective-permute-done.7.refs_0_.refs_1_ = bf16[256,2048]{1,0:T(8,128)(2,1)} collective-permute-done((bf16[256,2048]{1,0:T(8,128)(2,1)}, bf16[256,2048]{1,0:T(8,128)(2,1)}, u32[]{:S(2)}, u32[]{:S(2)}) %collective-permute-start.7) | collective-permute-done | bytes 1048608 | tf_op jit(solution)/shard_map/ppermute | solution.py:338
  119.5 3.2 project.6
  124.8 9.5 %collective-permute-done.9.refs_0_ = bf16[128,2048]{1,0:T(8,128)(2,1)S(1)} collective-permute-done((bf16[128,2048]{1,0:T(8,128)(2,1)S(1)}, bf16[128,2048]{1,0:T(8,128)(2,1)S(1)}, u32[]{:S(2)}, u32[]{:S(2)}) %collective-permute-start.9) | collective-permute-done | bytes 524320 | tf_op jit(solution)/shard_map/ppermute | solution.py:338
  134.3 3.0 collective-permute-start.14
  138.3 2.8 project.7
  141.2 8.4 %collective-permute-done.11 = bf16[128,2048]{1,0:T(8,128)(2,1)S(1)} collective-permute-done((bf16[128,2048]{1,0:T(8,128)(2,1)S(1)}, bf16[128,2048]{1,0:T(8,128)(2,1)S(1)}, u32[]{:S(2)}, u32[]{:S(2)}) %collective-permute-start.11) | collective-permute-done | bytes 524320 | tf_op jit(solution)/shard_map/ppermute | solution.py:338
  153.4 7.6 %attend.1 = (f32[1024,256]{1,0:T(8,128)S(1)}, bf16[1024,256]{1,0:T(8,128)(2,1)S(1)}, f32[2,1024,1]{2,1,0:T(8,128)S(1)}) custom-call(bf16[1024,256]{1,0:T(8,128)(2,1)S(1)} %constant_dynamic-update-slice_fusion.2.q_ref, bf16[1024,512]{1,0:T(8,128)(2,1)S(1)} %constant_dynamic-update-slice_fusion.6.k_ref.v_ref, ...), custom_call_target="tpu_custom_call" | custom-call | flops 20000000000 | tf_op jit(solution)/shard_map/attend/pallas_call | solution.py:592
  163.5 2.6 collective-permute-done.16.refs_1_
  166.3 2.9 collective-permute-start.18
  173.0 13.3 %collective-permute-done.18.refs_1_ = bf16[192,2048]{1,0:T(8,128)(2,1)S(1)} collective-permute-done((bf16[192,2048]{1,0:T(8,128)(2,1)S(1)}, bf16[192,2048]{1,0:T(8,128)(2,1)S(1)}, u32[]{:S(2)}, u32[]{:S(2)}) %collective-permute-start.18) | collective-permute-done | bytes 786464 | tf_op jit(solution)/shard_map/ppermute | solution.py:342
  193.7 12.0 %collective-permute-done.20.refs_2_ = bf16[192,2048]{1,0:T(8,128)(2,1)S(1)} collective-permute-done((bf16[192,2048]{1,0:T(8,128)(2,1)S(1)}, bf16[192,2048]{1,0:T(8,128)(2,1)S(1)}, u32[]{:S(2)}, u32[]{:S(2)}) %collective-permute-start.20) | collective-permute-done | bytes 786464 | tf_op jit(solution)/shard_map/ppermute | solution.py:338
  211.5 7.8 %collective-permute-done.22.refs_2_ = bf16[128,2048]{1,0:T(8,128)(2,1)S(1)} collective-permute-done((bf16[128,2048]{1,0:T(8,128)(2,1)S(1)}, bf16[128,2048]{1,0:T(8,128)(2,1)S(1)}, u32[]{:S(2)}, u32[]{:S(2)}) %collective-permute-start.22) | collective-permute-done | bytes 524320 | tf_op jit(solution)/shard_map/ppermute | solution.py:338
  248.5 4.0 collective-permute-start.29
  254.7 2.5 multiply_convert_fusion.4
  269.6 9.7 %collective-permute-done.30.refs_2_ = bf16[128,2048]{1,0:T(8,128)(2,1)S(1)} collective-permute-done((bf16[128,2048]{1,0:T(8,128)(2,1)S(1)}, bf16[128,2048]{1,0:T(8,128)(2,1)S(1)}, u32[]{:S(2)}, u32[]{:S(2)}) %collective-permute-start.30) | collective-permute-done | bytes 524320 | tf_op jit(solution)/shard_map/ppermute | solution.py:338
  287.7 6.0 %collective-permute-done.32.refs_3_ = bf16[128,2048]{1,0:T(8,128)(2,1)S(1)} collective-permute-done((bf16[128,2048]{1,0:T(8,128)(2,1)S(1)}, bf16[128,2048]{1,0:T(8,128)(2,1)S(1)}, u32[]{:S(2)}, u32[]{:S(2)}) %collective-permute-start.32) | collective-permute-done | bytes 524320 | tf_op jit(solution)/shard_map/ppermute | solution.py:338
  302.6 10.6 %collective-permute-done.34.refs_2_ = bf16[128,2048]{1,0:T(8,128)(2,1)S(1)} collective-permute-done((bf16[128,2048]{1,0:T(8,128)(2,1)S(1)}, bf16[128,2048]{1,0:T(8,128)(2,1)S(1)}, u32[]{:S(2)}, u32[]{:S(2)}) %collective-permute-start.34) | collective-permute-done | bytes 524320 | tf_op jit(solution)/shard_map/ppermute | solution.py:338
  318.2 10.0 %collective-permute-done.37.refs_2_ = bf16[128,2048]{1,0:T(8,128)(2,1)S(1)} collective-permute-done((bf16[128,2048]{1,0:T(8,128)(2,1)S(1)}, bf16[128,2048]{1,0:T(8,128)(2,1)S(1)}, u32[]{:S(2)}, u32[]{:S(2)}) %collective-permute-start.37) | collective-permute-done | bytes 524320 | tf_op jit(solution)/shard_map/ppermute | solution.py:338
  328.4 2.8 collective-permute-start.39
  335.8 2.6 collective-permute-done.39
  338.4 3.1 collective-permute-done.40
  349.6 5.0 collective-permute-done.43
  362.4 2.8 collective-permute-done.45
  383.2 3.5 collective-permute-start.51
  389.9 6.0 %collective-permute-done.50.refs_3_ = bf16[128,2048]{1,0:T(8,128)(2,1)S(1)} collective-permute-done((bf16[128,2048]{1,0:T(8,128)(2,1)S(1)}, bf16[128,2048]{1,0:T(8,128)(2,1)S(1)}, u32[]{:S(2)}, u32[]{:S(2)}) %collective-permute-start.50) | collective-permute-done | bytes 524320 | tf_op jit(solution)/shard_map/ppermute | solution.py:338
  405.1 10.1 %attend_back.1 = (bf16[1024,256]{1,0:T(8,128)(2,1)S(1)}, bf16[1024,512]{1,0:T(8,128)(2,1)S(1)}) custom-call(bf16[1024,256]{1,0:T(8,128)(2,1)S(1)} %copy-done.82, bf16[1024,512]{1,0:T(8,128)(2,1)S(1)} %copy-done.80, bf16[1024,512]{1,0:T(8,128)(2,1)S(1)} %copy-done.80, s32[1024,1]{1,0:T(8,128)S(1)} %copy-done.59, s32[1024,1]{1,0:T(8,128)S(1)} %copy-done.57, ...), custom_call_target="tpu_custom_call" | custom-call | flops 20000000000 | tf_op jit(solution)/shard_map/attend_back/pallas_call | solution.py:611
  418.7 7.0 %column_grads.1 = (bf16[2,512,768]{2,1,0:T(8,128)(2,1)}, f32[2,512,768]{2,1,0:T(8,128)}) custom-call(s32[1]{0:T(128)} %bitcast.dp_ref, bf16[256,2048]{1,0:T(8,128)(2,1)S(1)} %copy-done.85, bf16[256,2048]{1,0:T(8,128)(2,1)S(1)} %copy-done.89, bf16[256,2048]{1,0:T(8,128)(2,1)S(1)} %copy-done.95, bf16[256,2048]{1,0:T(8,128)(2,1)S(1)} %copy-done.99, ...), custom_call_target="tpu_custom_call" | custom-call | flops 20000000000 | tf_op jit(solution)/shard_map/column_grads/pallas_call | solution.py:1024
  437.1 4.3 collective-permute-done.58.refs_3_
  443.7 3.1 mix.27
  459.6 3.0 back_terms.5
  465.1 17.7 %collective-permute-done.60.refs_1_ = bf16[384,2048]{1,0:T(8,128)(2,1)} collective-permute-done((bf16[384,2048]{1,0:T(8,128)(2,1)}, bf16[384,2048]{1,0:T(8,128)(2,1)}, u32[]{:S(2)}, u32[]{:S(2)}) %collective-permute-start.60) | collective-permute-done | bytes 1572896 | tf_op jit(solution)/shard_map/ppermute | solution.py:338
  484.0 3.8 mix.28
  499.3 7.0 %all-to-all-start.1 = ((bf16[8,72,768]{2,1,0:T(8,128)(2,1)}), bf16[8,72,768]{2,1,0:T(8,128)(2,1)S(1)}, u32[]{:S(2)}, u32[]{:S(2)}) async-start(bf16[8,72,768]{2,1,0:T(8,128)(2,1)} %fusion.39), calls=%async_computation.1 | async-start | bytes 1769472 | tf_op jit(solution)/shard_map/all_to_all | solution.py:1063
  508.3 4.1 collective-permute-start.70
  513.2 18.0 %collective-permute-done.65.x_ref.refs_1_ = bf16[384,2048]{1,0:T(8,128)(2,1)} collective-permute-done((bf16[384,2048]{1,0:T(8,128)(2,1)}, bf16[384,2048]{1,0:T(8,128)(2,1)}, u32[]{:S(2)}, u32[]{:S(2)}) %collective-permute-start.65) | collective-permute-done | bytes 1572896 | tf_op jit(solution)/shard_map/ppermute | solution.py:338
  531.2 3.5 collective-permute-done.66.ring_ref.refs_2_
  534.7 3.3 mix.29
  538.0 4.7 collective-permute-start.68
  542.8 4.4 add_all.1
  558.3 3.6 result.1
  563.5 5.4 collective-permute-done.68.refs_2_.refs_5_
  568.9 4.2 input_grads.1
  (575 shorter events, 252.0 us)
Async XLA Ops:
  9.4 28.1 %collective-permute-start.1 = (bf16[256,2048]{1,0:T(8,128)(2,1)S(1)}, bf16[256,2048]{1,0:T(8,128)(2,1)S(1)}, u32[]{:S(2)}, u32[]{:S(2)}) collective-permute-start(bf16[256,2048]{1,0:T(8,128)(2,1)S(1)} %constant_dynamic-update-slice_fusion.held_ref), channel_id=1, source_target_pairs={{0,2},{1,3},{2,6},{3,7},{6,4},{7,5},{4,0},{5,1},{8,10},{9,11},{10,... | collective-permute-start | bytes 3145736 | tf_op jit(solution)/shard_map/ppermute | solution.py:342
  12.4 28.2 %collective-permute-start = (bf16[256,2048]{1,0:T(8,128)(2,1)S(1)}, bf16[256,2048]{1,0:T(8,128)(2,1)S(1)}, u32[]{:S(2)}, u32[]{:S(2)}) collective-permute-start(bf16[256,2048]{1,0:T(8,128)(2,1)S(1)} %constant_dynamic-update-slice_fusion.held_ref), channel_id=1, source_target_pairs={{0,1},{1,0},{2,3},{3,2},{4,5},{5,4},{6,7},{7,6},{8,9},{9,8},{10,11... | collective-permute-start | bytes 3145736 | tf_op jit(solution)/shard_map/ppermute | solution.py:338
  18.6 35.7 %all-to-all-start = ((bf16[8,200,256]{2,1,0:T(8,128)(2,1)}), bf16[8,200,256]{2,1,0:T(8,128)(2,1)}, u32[]{:S(2)}, u32[]{:S(2)}) async-start(bf16[8,200,256]{2,1,0:T(8,128)(2,1)} %bitcast.122), calls=%async_computation | async-start | bytes 1638400 | tf_op jit(solution)/shard_map/all_to_all | solution.py:695
  22.8 199.8 %all-gather.4.cloned.1.call-start = ((), (), s32[]{:S(2)}) async-start(), calls=%async_computation.2 | async-start | bytes 3932160 | tf_op jit(solution)/shard_map/all_gather | solution.py:1127
  54.3 24.3 %collective-permute-start.5 = (bf16[256,2048]{1,0:T(8,128)(2,1)S(1)}, bf16[256,2048]{1,0:T(8,128)(2,1)S(1)}, u32[]{:S(2)}, u32[]{:S(2)}) collective-permute-start(bf16[256,2048]{1,0:T(8,128)(2,1)S(1)} %collective-permute-done.1.held_ref), channel_id=1, source_target_pairs={{0,1},{1,0},{2,3},{3,2},{4,5},{5,4},{6,7},{7,6},{8,9},{9,8},{10,11... | collective-permute-start | bytes 3145736 | tf_op jit(solution)/shard_map/ppermute | solution.py:338
  55.8 24.5 %collective-permute-start.6 = (bf16[256,2048]{1,0:T(8,128)(2,1)S(1)}, bf16[256,2048]{1,0:T(8,128)(2,1)}, u32[]{:S(2)}, u32[]{:S(2)}) collective-permute-start(bf16[256,2048]{1,0:T(8,128)(2,1)S(1)} %collective-permute-done.1.held_ref), channel_id=1, source_target_pairs={{0,2},{1,3},{2,6},{3,7},{6,4},{7,5},{4,0},{5,1},{8,10},{9,11},{10,... | collective-permute-start | bytes 3145736 | tf_op jit(solution)/shard_map/ppermute | solution.py:342
  56.6 21.0 %collective-permute-start.2 = (bf16[1600,256]{1,0:T(8,128)(2,1)}, bf16[1600,256]{1,0:T(8,128)(2,1)}, u32[]{:S(2)}, u32[]{:S(2)}) collective-permute-start(bf16[1600,256]{1,0:T(8,128)(2,1)} %bitcast.2), channel_id=1, source_target_pairs={{0,16},{8,24},{16,0},{24,8},{1,17},{9,25},{17,1},{25,9},{2,18},{10... | collective-permute-start | bytes 2457608 | tf_op jit(solution)/shard_map/ppermute | solution.py:346
  80.3 159.0 %all-gather.6.cloned.1.call-start = ((), (), s32[]{:S(2)}) async-start(), calls=%async_computation.3 | async-start | bytes 3932160 | tf_op jit(solution)/shard_map/all_gather | solution.py:1127
  82.5 159.0 %all-gather.8.cloned.1.call-start = ((), (), s32[]{:S(2)}) async-start(), calls=%async_computation.4 | async-start | bytes 3932160 | tf_op jit(solution)/shard_map/all_gather | solution.py:1127
  88.0 25.9 %collective-permute-start.7 = (bf16[256,2048]{1,0:T(8,128)(2,1)}, bf16[256,2048]{1,0:T(8,128)(2,1)}, u32[]{:S(2)}, u32[]{:S(2)}) collective-permute-start(bf16[256,2048]{1,0:T(8,128)(2,1)} %collective-permute-done.6.held_ref), channel_id=1, source_target_pairs={{0,1},{1,0},{2,3},{3,2},{4,5},{5,4},{6,7},{7,6},{8,9},{9,8},{10,11... | collective-permute-start | bytes 3145736 | tf_op jit(solution)/shard_map/ppermute | solution.py:338
  89.0 26.5 %collective-permute-start.8 = (bf16[256,2048]{1,0:T(8,128)(2,1)}, bf16[256,2048]{1,0:T(8,128)(2,1)}, u32[]{:S(2)}, u32[]{:S(2)}) collective-permute-start(bf16[256,2048]{1,0:T(8,128)(2,1)} %collective-permute-done.6.held_ref), channel_id=1, source_target_pairs={{0,2},{1,3},{2,6},{3,7},{6,4},{7,5},{4,0},{5,1},{8,10},{9,11},{10,... | collective-permute-start | bytes 3145736 | tf_op jit(solution)/shard_map/ppermute | solution.py:342
  118.3 16.0 %collective-permute-start.9 = (bf16[128,2048]{1,0:T(8,128)(2,1)S(1)}, bf16[128,2048]{1,0:T(8,128)(2,1)S(1)}, u32[]{:S(2)}, u32[]{:S(2)}) collective-permute-start(bf16[128,2048]{1,0:T(8,128)(2,1)S(1)} %get-tuple-element.212), channel_id=1, source_target_pairs={{0,1},{1,0},{2,3},{3,2},{4,5},{5,4},{6,7},{7,6},{8,9},{9,8},{10,11... | collective-permute-start | bytes 1572872 | tf_op jit(solution)/shard_map/ppermute | solution.py:338
  119.3 15.0 %collective-permute-start.10 = (bf16[128,2048]{1,0:T(8,128)(2,1)S(1)}, bf16[128,2048]{1,0:T(8,128)(2,1)S(1)}, u32[]{:S(2)}, u32[]{:S(2)}) collective-permute-start(bf16[128,2048]{1,0:T(8,128)(2,1)S(1)} %get-tuple-element.213), channel_id=1, source_target_pairs={{0,2},{1,3},{2,6},{3,7},{6,4},{7,5},{4,0},{5,1},{8,10},{9,11},{10,... | collective-permute-start | bytes 1572872 | tf_op jit(solution)/shard_map/ppermute | solution.py:342
  134.3 16.2 %collective-permute-start.14 = (bf16[128,2048]{1,0:T(8,128)(2,1)S(1)}, bf16[128,2048]{1,0:T(8,128)(2,1)S(1)}, u32[]{:S(2)}, u32[]{:S(2)}) collective-permute-start(bf16[128,2048]{1,0:T(8,128)(2,1)S(1)} %pad_maximum_fusion.9), channel_id=1, source_target_pairs={{0,16},{2,18},{4,20},{6,22},{8,24},{10,26},{12,28},{14,30},{17,1},... | collective-permute-start | bytes 1572872 | tf_op jit(solution)/shard_map/ppermute | solution.py:1093
  150.8 15.4 %collective-permute-start.16 = (bf16[128,2048]{1,0:T(8,128)(2,1)S(1)}, bf16[128,2048]{1,0:T(8,128)(2,1)S(1)}, u32[]{:S(2)}, u32[]{:S(2)}) collective-permute-start(bf16[128,2048]{1,0:T(8,128)(2,1)S(1)} %collective-permute-done.12), channel_id=1, source_target_pairs={{0,2},{1,3},{2,6},{3,7},{6,4},{7,5},{4,0},{5,1},{8,10},{9,11},{10,... | collective-permute-start | bytes 1572872 | tf_op jit(solution)/shard_map/ppermute | solution.py:342
  151.8 14.5 %collective-permute-start.17 = (bf16[128,2048]{1,0:T(8,128)(2,1)S(1)}, bf16[128,2048]{1,0:T(8,128)(2,1)S(1)}, u32[]{:S(2)}, u32[]{:S(2)}) collective-permute-start(bf16[128,2048]{1,0:T(8,128)(2,1)S(1)} %collective-permute-done.12), channel_id=1, source_target_pairs={{0,1},{1,0},{2,3},{3,2},{4,5},{5,4},{6,7},{7,6},{8,9},{9,8},{10,11... | collective-permute-start | bytes 1572872 | tf_op jit(solution)/shard_map/ppermute | solution.py:338
  166.3 20.0 %collective-permute-start.18 = (bf16[192,2048]{1,0:T(8,128)(2,1)S(1)}, bf16[192,2048]{1,0:T(8,128)(2,1)S(1)}, u32[]{:S(2)}, u32[]{:S(2)}) collective-permute-start(bf16[192,2048]{1,0:T(8,128)(2,1)S(1)} %get-tuple-element.234), channel_id=1, source_target_pairs={{0,2},{1,3},{2,6},{3,7},{6,4},{7,5},{4,0},{5,1},{8,10},{9,11},{10,... | collective-permute-start | bytes 2359304 | tf_op jit(solution)/shard_map/ppermute | solution.py:342
  169.1 18.6 %collective-permute-start.19 = (bf16[192,2048]{1,0:T(8,128)(2,1)S(1)}, bf16[192,2048]{1,0:T(8,128)(2,1)S(1)}, u32[]{:S(2)}, u32[]{:S(2)}) collective-permute-start(bf16[192,2048]{1,0:T(8,128)(2,1)S(1)} %get-tuple-element.235), channel_id=1, source_target_pairs={{0,1},{1,0},{2,3},{3,2},{4,5},{5,4},{6,7},{7,6},{8,9},{9,8},{10,11... | collective-permute-start | bytes 2359304 | tf_op jit(solution)/shard_map/ppermute | solution.py:338
  187.9 17.7 %collective-permute-start.20 = (bf16[192,2048]{1,0:T(8,128)(2,1)S(1)}, bf16[192,2048]{1,0:T(8,128)(2,1)S(1)}, u32[]{:S(2)}, u32[]{:S(2)}) collective-permute-start(bf16[192,2048]{1,0:T(8,128)(2,1)S(1)} %get-tuple-element.238), channel_id=1, source_target_pairs={{0,1},{1,0},{2,3},{3,2},{4,5},{5,4},{6,7},{7,6},{8,9},{9,8},{10,11... | collective-permute-start | bytes 2359304 | tf_op jit(solution)/shard_map/ppermute | solution.py:338
  189.6 18.3 %collective-permute-start.21 = (bf16[192,2048]{1,0:T(8,128)(2,1)S(1)}, bf16[192,2048]{1,0:T(8,128)(2,1)S(1)}, u32[]{:S(2)}, u32[]{:S(2)}) collective-permute-start(bf16[192,2048]{1,0:T(8,128)(2,1)S(1)} %get-tuple-element.239), channel_id=1, source_target_pairs={{0,2},{1,3},{2,6},{3,7},{6,4},{7,5},{4,0},{5,1},{8,10},{9,11},{10,... | collective-permute-start | bytes 2359304 | tf_op jit(solution)/shard_map/ppermute | solution.py:342
  248.5 14.2 %collective-permute-start.28 = (bf16[128,2048]{1,0:T(8,128)(2,1)}, bf16[128,2048]{1,0:T(8,128)(2,1)S(1)}, u32[]{:S(2)}, u32[]{:S(2)}) collective-permute-start(bf16[128,2048]{1,0:T(8,128)(2,1)} %collective-permute-done.27), channel_id=1, source_target_pairs={{0,1},{1,0},{2,3},{3,2},{4,5},{5,4},{6,7},{7,6},{8,9},{9,8},{10,11... | collective-permute-start | bytes 1572872 | tf_op jit(solution)/shard_map/ppermute | solution.py:338
  248.5 17.8 %collective-permute-start.29 = (bf16[128,2048]{1,0:T(8,128)(2,1)}, bf16[128,2048]{1,0:T(8,128)(2,1)S(1)}, u32[]{:S(2)}, u32[]{:S(2)}) collective-permute-start(bf16[128,2048]{1,0:T(8,128)(2,1)} %collective-permute-done.27), channel_id=1, source_target_pairs={{0,2},{1,3},{2,6},{3,7},{6,4},{7,5},{4,0},{5,1},{8,10},{9,11},{10,... | collective-permute-start | bytes 1572872 | tf_op jit(solution)/shard_map/ppermute | solution.py:342
  268.4 14.2 %collective-permute-start.31 = (bf16[128,2048]{1,0:T(8,128)(2,1)S(1)}, bf16[128,2048]{1,0:T(8,128)(2,1)S(1)}, u32[]{:S(2)}, u32[]{:S(2)}) collective-permute-start(bf16[128,2048]{1,0:T(8,128)(2,1)S(1)} %collective-permute-done.29), channel_id=1, source_target_pairs={{0,2},{1,3},{2,6},{3,7},{6,4},{7,5},{4,0},{5,1},{8,10},{9,11},{10,... | collective-permute-start | bytes 1572872 | tf_op jit(solution)/shard_map/ppermute | solution.py:342
  299.6 13.6 %collective-permute-start.34 = (bf16[128,2048]{1,0:T(8,128)(2,1)S(1)}, bf16[128,2048]{1,0:T(8,128)(2,1)S(1)}, u32[]{:S(2)}, u32[]{:S(2)}) collective-permute-start(bf16[128,2048]{1,0:T(8,128)(2,1)S(1)} %get-tuple-element.263), channel_id=1, source_target_pairs={{0,1},{1,0},{2,3},{3,2},{4,5},{5,4},{6,7},{7,6},{8,9},{9,8},{10,11... | collective-permute-start | bytes 1572872 | tf_op jit(solution)/shard_map/ppermute | solution.py:338
  301.2 14.2 %collective-permute-start.35 = (bf16[128,2048]{1,0:T(8,128)(2,1)S(1)}, bf16[128,2048]{1,0:T(8,128)(2,1)S(1)}, u32[]{:S(2)}, u32[]{:S(2)}) collective-permute-start(bf16[128,2048]{1,0:T(8,128)(2,1)S(1)} %get-tuple-element.264), channel_id=1, source_target_pairs={{0,2},{1,3},{2,6},{3,7},{6,4},{7,5},{4,0},{5,1},{8,10},{9,11},{10,... | collective-permute-start | bytes 1572872 | tf_op jit(solution)/shard_map/ppermute | solution.py:342
  318.1 26.3 %collective-permute-start.36 = (bf16[384,2048]{1,0:T(8,128)(2,1)S(1)}, bf16[384,2048]{1,0:T(8,128)(2,1)S(1)}, u32[]{:S(2)}, u32[]{:S(2)}) collective-permute-start(bf16[384,2048]{1,0:T(8,128)(2,1)S(1)} %convolution_convert_fusion.2), channel_id=1, source_target_pairs={{0,8},{8,0},{16,24},{24,16},{1,9},{9,1},{17,25},{25,17},{2,10},{10... | collective-permute-start | bytes 4718600 | tf_op jit(solution)/shard_map/ppermute | solution.py:350
  333.2 33.0 %collective-permute-start.44 = (bf16[384,2048]{1,0:T(8,128)(2,1)S(1)}, bf16[384,2048]{1,0:T(8,128)(2,1)S(1)}, u32[]{:S(2)}, u32[]{:S(2)}) collective-permute-start(bf16[384,2048]{1,0:T(8,128)(2,1)S(1)} %convolution_convert_fusion), channel_id=1, source_target_pairs={{0,8},{8,0},{16,24},{24,16},{1,9},{9,1},{17,25},{25,17},{2,10},{10... | collective-permute-start | bytes 4718600 | tf_op jit(solution)/shard_map/ppermute | solution.py:350
  335.2 22.1 %collective-permute-start.41 = (bf16[384,2048]{1,0:T(8,128)(2,1)S(1)}, bf16[384,2048]{1,0:T(8,128)(2,1)S(1)}, u32[]{:S(2)}, u32[]{:S(2)}) collective-permute-start(bf16[384,2048]{1,0:T(8,128)(2,1)S(1)} %convolution_convert_fusion.1), channel_id=1, source_target_pairs={{0,8},{8,0},{16,24},{24,16},{1,9},{9,1},{17,25},{25,17},{2,10},{10... | collective-permute-start | bytes 4718600 | tf_op jit(solution)/shard_map/ppermute | solution.py:350
  347.5 34.1 %collective-permute-start.47 = (bf16[192,2048]{1,0:T(8,128)(2,1)}, bf16[192,2048]{1,0:T(8,128)(2,1)S(1)}, u32[]{:S(2)}, u32[]{:S(2)}) collective-permute-start(bf16[192,2048]{1,0:T(8,128)(2,1)} %slice.202), channel_id=1, source_target_pairs={{0,16},{8,24},{16,0},{24,8},{1,17},{9,25},{17,1},{25,9},{2,18},{10... | collective-permute-start | bytes 2359304 | tf_op jit(solution)/shard_map/ppermute | solution.py:346
  360.3 41.6 %collective-permute-start.52 = (bf16[192,2048]{1,0:T(8,128)(2,1)}, bf16[192,2048]{1,0:T(8,128)(2,1)}, u32[]{:S(2)}, u32[]{:S(2)}) collective-permute-start(bf16[192,2048]{1,0:T(8,128)(2,1)} %slice.201), channel_id=1, source_target_pairs={{0,16},{8,24},{16,0},{24,8},{1,17},{9,25},{17,1},{25,9},{2,18},{10... | collective-permute-start | bytes 2359304 | tf_op jit(solution)/shard_map/ppermute | solution.py:346
  366.2 14.2 %collective-permute-start.48 = (bf16[128,2048]{1,0:T(8,128)(2,1)}, bf16[128,2048]{1,0:T(8,128)(2,1)S(1)}, u32[]{:S(2)}, u32[]{:S(2)}) collective-permute-start(bf16[128,2048]{1,0:T(8,128)(2,1)} %collective-permute-done.46), channel_id=1, source_target_pairs={{0,1},{1,0},{2,3},{3,2},{4,5},{5,4},{6,7},{7,6},{8,9},{9,8},{10,11... | collective-permute-start | bytes 1572872 | tf_op jit(solution)/shard_map/ppermute | solution.py:338
  371.7 30.2 %collective-permute-start.53 = (bf16[192,2048]{1,0:T(8,128)(2,1)}, bf16[192,2048]{1,0:T(8,128)(2,1)}, u32[]{:S(2)}, u32[]{:S(2)}) collective-permute-start(bf16[192,2048]{1,0:T(8,128)(2,1)} %slice.200), channel_id=1, source_target_pairs={{0,16},{8,24},{16,0},{24,8},{1,17},{9,25},{17,1},{25,9},{2,18},{10... | collective-permute-start | bytes 2359304 | tf_op jit(solution)/shard_map/ppermute | solution.py:346
  381.6 14.4 %collective-permute-start.50 = (bf16[128,2048]{1,0:T(8,128)(2,1)S(1)}, bf16[128,2048]{1,0:T(8,128)(2,1)S(1)}, u32[]{:S(2)}, u32[]{:S(2)}) collective-permute-start(bf16[128,2048]{1,0:T(8,128)(2,1)S(1)} %get-tuple-element.293), channel_id=1, source_target_pairs={{0,1},{1,0},{2,3},{3,2},{4,5},{5,4},{6,7},{7,6},{8,9},{9,8},{10,11... | collective-permute-start | bytes 1572872 | tf_op jit(solution)/shard_map/ppermute | solution.py:338
  383.2 15.1 %collective-permute-start.51 = (bf16[128,2048]{1,0:T(8,128)(2,1)S(1)}, bf16[128,2048]{1,0:T(8,128)(2,1)S(1)}, u32[]{:S(2)}, u32[]{:S(2)}) collective-permute-start(bf16[128,2048]{1,0:T(8,128)(2,1)S(1)} %get-tuple-element.294), channel_id=1, source_target_pairs={{0,2},{1,3},{2,6},{3,7},{6,4},{7,5},{4,0},{5,1},{8,10},{9,11},{10,... | collective-permute-start | bytes 1572872 | tf_op jit(solution)/shard_map/ppermute | solution.py:342
  402.5 13.6 %collective-permute-start.57 = (bf16[128,2048]{1,0:T(8,128)(2,1)S(1)}, bf16[128,2048]{1,0:T(8,128)(2,1)S(1)}, u32[]{:S(2)}, u32[]{:S(2)}) collective-permute-start(bf16[128,2048]{1,0:T(8,128)(2,1)S(1)} %get-tuple-element.303), channel_id=1, source_target_pairs={{0,2},{1,3},{2,6},{3,7},{6,4},{7,5},{4,0},{5,1},{8,10},{9,11},{10,... | collective-permute-start | bytes 1572872 | tf_op jit(solution)/shard_map/ppermute | solution.py:342
  425.7 24.7 %collective-permute-start.63 = (bf16[2,512,768]{2,1,0:T(8,128)(2,1)}, bf16[2,512,768]{2,1,0:T(8,128)(2,1)}, u32[]{:S(2)}, u32[]{:S(2)}) collective-permute-start(bf16[2,512,768]{2,1,0:T(8,128)(2,1)} %get-tuple-element.341), channel_id=1, source_target_pairs={{0,8},{8,0},{16,24},{24,16},{1,9},{9,1},{17,25},{25,17},{2,10},{10... | collective-permute-start | bytes 4718600 | tf_op jit(solution)/shard_map/ppermute | solution.py:350
  426.8 14.6 %collective-permute-start.58 = (bf16[128,2048]{1,0:T(8,128)(2,1)}, bf16[128,2048]{1,0:T(8,128)(2,1)}, u32[]{:S(2)}, u32[]{:S(2)}) collective-permute-start(bf16[128,2048]{1,0:T(8,128)(2,1)} %get-tuple-element.309), channel_id=1, source_target_pairs={{0,1},{1,0},{2,3},{3,2},{4,5},{5,4},{6,7},{7,6},{8,9},{9,8},{10,11... | collective-permute-start | bytes 1572872 | tf_op jit(solution)/shard_map/ppermute | solution.py:338
  428.2 15.5 %collective-permute-start.59 = (bf16[128,2048]{1,0:T(8,128)(2,1)}, bf16[128,2048]{1,0:T(8,128)(2,1)}, u32[]{:S(2)}, u32[]{:S(2)}) collective-permute-start(bf16[128,2048]{1,0:T(8,128)(2,1)} %get-tuple-element.310), channel_id=1, source_target_pairs={{0,2},{1,3},{2,6},{3,7},{6,4},{7,5},{4,0},{5,1},{8,10},{9,11},{10,... | collective-permute-start | bytes 1572872 | tf_op jit(solution)/shard_map/ppermute | solution.py:342
  446.8 36.0 %collective-permute-start.60 = (bf16[384,2048]{1,0:T(8,128)(2,1)}, bf16[384,2048]{1,0:T(8,128)(2,1)}, u32[]{:S(2)}, u32[]{:S(2)}) collective-permute-start(bf16[384,2048]{1,0:T(8,128)(2,1)} %get-tuple-element.321), channel_id=1, source_target_pairs={{0,1},{1,0},{2,3},{3,2},{4,5},{5,4},{6,7},{7,6},{8,9},{9,8},{10,11... | collective-permute-start | bytes 4718600 | tf_op jit(solution)/shard_map/ppermute | solution.py:338
  447.4 36.6 %collective-permute-start.61 = (bf16[384,2048]{1,0:T(8,128)(2,1)}, bf16[384,2048]{1,0:T(8,128)(2,1)}, u32[]{:S(2)}, u32[]{:S(2)}) collective-permute-start(bf16[384,2048]{1,0:T(8,128)(2,1)} %get-tuple-element.322), channel_id=1, source_target_pairs={{0,2},{1,3},{2,6},{3,7},{6,4},{7,5},{4,0},{5,1},{8,10},{9,11},{10,... | collective-permute-start | bytes 4718600 | tf_op jit(solution)/shard_map/ppermute | solution.py:342
  452.6 35.2 %collective-permute-start.64 = (bf16[512,768]{1,0:T(8,128)(2,1)}, bf16[512,768]{1,0:T(8,128)(2,1)}, u32[]{:S(2)}, u32[]{:S(2)}) collective-permute-start(bf16[512,768]{1,0:T(8,128)(2,1)} %fusion.40), channel_id=1, source_target_pairs={{0,16},{8,24},{16,0},{24,8},{1,17},{9,25},{17,1},{25,9},{2,18},{10... | collective-permute-start | bytes 2359304 | tf_op jit(solution)/shard_map/ppermute | solution.py:346
  490.5 40.6 %collective-permute-start.65 = (bf16[384,2048]{1,0:T(8,128)(2,1)}, bf16[384,2048]{1,0:T(8,128)(2,1)}, u32[]{:S(2)}, u32[]{:S(2)}) collective-permute-start(bf16[384,2048]{1,0:T(8,128)(2,1)} %get-tuple-element.343), channel_id=1, source_target_pairs={{0,1},{1,0},{2,3},{3,2},{4,5},{5,4},{6,7},{7,6},{8,9},{9,8},{10,11... | collective-permute-start | bytes 4718600 | tf_op jit(solution)/shard_map/ppermute | solution.py:338
  492.0 42.7 %collective-permute-start.66 = (bf16[384,2048]{1,0:T(8,128)(2,1)}, bf16[384,2048]{1,0:T(8,128)(2,1)}, u32[]{:S(2)}, u32[]{:S(2)}) collective-permute-start(bf16[384,2048]{1,0:T(8,128)(2,1)} %mix.28), channel_id=1, source_target_pairs={{0,2},{1,3},{2,6},{3,7},{6,4},{7,5},{4,0},{5,1},{8,10},{9,11},{10,... | collective-permute-start | bytes 4718600 | tf_op jit(solution)/shard_map/ppermute | solution.py:342
  492.0 14.4 %collective-permute-start.69 = (bf16[128,2048]{1,0:T(8,128)(2,1)}, bf16[128,2048]{1,0:T(8,128)(2,1)}, u32[]{:S(2)}, u32[]{:S(2)}) collective-permute-start(bf16[128,2048]{1,0:T(8,128)(2,1)} %fusion.53), channel_id=1, source_target_pairs={{1,17},{3,19},{5,21},{7,23},{9,25},{11,27},{13,29},{15,31},{16,0},... | collective-permute-start | bytes 1572872 | tf_op jit(solution)/shard_map/ppermute | solution.py:1113
  499.3 50.1 %all-to-all-start.1 = ((bf16[8,72,768]{2,1,0:T(8,128)(2,1)}), bf16[8,72,768]{2,1,0:T(8,128)(2,1)S(1)}, u32[]{:S(2)}, u32[]{:S(2)}) async-start(bf16[8,72,768]{2,1,0:T(8,128)(2,1)} %fusion.39), calls=%async_computation.1 | async-start | bytes 1769472 | tf_op jit(solution)/shard_map/all_to_all | solution.py:1063
  508.3 38.9 %collective-permute-start.70 = (bf16[64,2048]{1,0:T(8,128)(2,1)S(1)}, bf16[64,2048]{1,0:T(8,128)(2,1)S(1)}, u32[]{:S(2)}, u32[]{:S(2)}) collective-permute-start(bf16[64,2048]{1,0:T(8,128)(2,1)S(1)} %dynamic-slice_convert_fusion.1), channel_id=1, source_target_pairs={{0,1},{2,3},{4,5},{6,7},{8,9},{10,11},{12,13},{14,15},{17,16},{19,... | collective-permute-start | bytes 786440 | tf_op jit(solution)/shard_map/ppermute | solution.py:1122
  538.0 25.4 %collective-permute-start.67 = (bf16[256,2048]{1,0:T(8,128)(2,1)}, bf16[256,2048]{1,0:T(8,128)(2,1)}, u32[]{:S(2)}, u32[]{:S(2)}) collective-permute-start(bf16[256,2048]{1,0:T(8,128)(2,1)} %get-tuple-element.355), channel_id=1, source_target_pairs={{0,1},{1,0},{2,3},{3,2},{4,5},{5,4},{6,7},{7,6},{8,9},{9,8},{10,11... | collective-permute-start | bytes 3145736 | tf_op jit(solution)/shard_map/ppermute | solution.py:338
  538.0 30.9 %collective-permute-start.68 = (bf16[256,2048]{1,0:T(8,128)(2,1)}, bf16[256,2048]{1,0:T(8,128)(2,1)}, u32[]{:S(2)}, u32[]{:S(2)}) collective-permute-start(bf16[256,2048]{1,0:T(8,128)(2,1)} %mix.29), channel_id=1, source_target_pairs={{0,2},{1,3},{2,6},{3,7},{6,4},{7,5},{4,0},{5,1},{8,10},{9,11},{10,... | collective-permute-start | bytes 3145736 | tf_op jit(solution)/shard_map/ppermute | solution.py:342
  (173 other events, 1789.3 us)
Sparse Core Ops, SparseCore 0:
  80.5 29.1 all-gather.3
  111.2 28.5 all-gather.5
  141.3 29.0 all-gather.7

commit v4 on v3

--- a/solution.py
+++ b/solution.py
@@ -486,13 +486,13 @@
     return pl.pallas_call(
         functools.partial(mix_kernel, tuple(plans)),
         out_shape=[jax.ShapeDtypeStruct((count, width), jnp.bfloat16) for count in counts],
-        compiler_params=pltpu.CompilerParams(vmem_limit_bytes=32 * 2**20),
+        compiler_params=pltpu.CompilerParams(vmem_limit_bytes=16 * 2**20),
         cost_estimate=FREE,
         name="mix",
     )(*arrays)
 
 
-def move(parts, *gate):
+def move(parts, *gate, payload=None):
     sent = [part.send() for part in parts]
     x_sums, ring_sums = (sum((given[way] for given in sent), []) for way in range(2))
     along_x, along_ring = only_array(x_sums), only_array(ring_sums)
@@ -503,6 +503,8 @@
     elif along_ring is None:
         (along_ring,) = mixed(ring_sums)
     along_x, along_ring = after((along_x, along_ring), *gate)
+    if payload is not None:
+        payload += [along_x, along_ring]
     from_x, from_ring = x_swap(along_x), ring_step(along_ring)
     x_row = ring_row = 0
     for part, given in zip(parts, sent):
@@ -599,7 +601,7 @@
             jax.ShapeDtypeStruct((count, width), jnp.bfloat16),
             jax.ShapeDtypeStruct((width // head, count, 1), jnp.float32),
         ],
-        compiler_params=pltpu.CompilerParams(vmem_limit_bytes=40 * 2**20),
+        compiler_params=pltpu.CompilerParams(vmem_limit_bytes=20 * 2**20),
         cost_estimate=LONG,
         name="attend",
     )(queries, pairs, pairs, first, last, place)
@@ -628,14 +630,14 @@
             jax.ShapeDtypeStruct((count, 2 * width), jnp.bfloat16),
         ],
         scratch_shapes=[pltpu.VMEM((count, head), jnp.float32)] * 2,
-        compiler_params=pltpu.CompilerParams(vmem_limit_bytes=40 * 2**20),
+        compiler_params=pltpu.CompilerParams(vmem_limit_bytes=20 * 2**20),
         cost_estimate=LONG,
         name="attend_back",
     )(queries, pairs, pairs, first, last, place, lse, attended, d_attended)
 
 
 def as_rows(values, columns):
-    rows = 8 * -(-values.shape[0] // (8 * columns))
+    rows = 16 * -(-values.shape[0] // (16 * columns))
     return jnp.pad(values, (0, rows * columns - values.shape[0])).reshape(rows, columns)
 
 
@@ -648,20 +650,26 @@
     return [slice(head * (8 * x + 4 * j + z), head * (8 * x + 4 * j + z + 1)) for j in range(2)]
 
 
-def columns_kernel(dp_ref, held_ref, q_ref, kv_ref, gain_ref):
+def columns_kernel(dp_ref, *refs):
+    held_refs = refs[:4]
+    q_ref, kv_ref, gain_ref = refs[4:]
     each = q_ref.shape[0] // 8
     mine = q_ref.shape[1]
-    rows = held_ref.shape[2] // 8
-    for device in range(8):
-        first = rows * device
-        here = slice(each * device, each * (device + 1))
-        q_ref[here, :] = held_ref[0, 0, first : first + each, :]
-        kv_ref[here, :mine] = held_ref[0, 0, first + each : first + 2 * each, :]
-        kv_ref[here, mine:] = held_ref[0, 0, first + 2 * each : first + 3 * each, :]
-        extra = rows - 3 * each
-        gain_ref[0, extra * device : extra * (device + 1), :] = held_ref[
-            0, 0, first + 3 * each : first + rows, :
-        ]
+    rows = held_refs[0].shape[0] // 8
+    extra = rows - 3 * each
+    for mask, held_ref in enumerate(held_refs):
+
+        @pl.when((dp_ref[0] ^ pl.program_id(0)) == mask)
+        def _():
+            for device in range(8):
+                first = rows * device
+                here = slice(each * device, each * (device + 1))
+                q_ref[here, :] = held_ref[first : first + each, :]
+                kv_ref[here, :mine] = held_ref[first + each : first + 2 * each, :]
+                kv_ref[here, mine:] = held_ref[first + 2 * each : first + 3 * each, :]
+                gain_ref[0, extra * device : extra * (device + 1), :] = held_ref[
+                    first + 3 * each : first + rows, :
+                ]
 
 
 def payload_kernel(q_ref, k_ref, v_ref, gain_ref, out_ref):
@@ -688,7 +696,7 @@
             out_shape=jax.ShapeDtypeStruct(
                 (8 * (3 * each + extra.shape[0]), width // 8), self.weights[0].dtype
             ),
-            compiler_params=pltpu.CompilerParams(vmem_limit_bytes=16 * 2**20),
+            compiler_params=pltpu.CompilerParams(vmem_limit_bytes=8 * 2**20),
             cost_estimate=LONG,
             name="payload",
         )(*self.weights, extra)
@@ -704,26 +712,21 @@
     def along_core(self, *gate):
         held, got, other = after(tuple(self.held), *gate)
         last = core_swap(got)
-        self.held = jnp.stack([held, got, other, last]).reshape(2, 2, *held.shape)
+        self.held = [held, other, got, last]
         return [last]
 
     def whole(self):
         each, width = self.weights[0].shape
-        rows, mine = self.held.shape[2:]
+        rows, mine = self.held[0].shape
         extra = rows - 24 * each
         block = 8 * each
-        low = self.held.dtype
+        low = self.held[0].dtype
         wq, w_kv, gains = pl.pallas_call(
             columns_kernel,
             grid_spec=pltpu.PrefetchScalarGridSpec(
                 num_scalar_prefetch=1,
                 grid=(4,),
-                in_specs=[
-                    pl.BlockSpec(
-                        (1, 1, rows, mine),
-                        lambda i, dp: ((dp[0] ^ i) % 2, (dp[0] ^ i) // 2, 0, 0),
-                    )
-                ],
+                in_specs=[pl.BlockSpec((rows, mine), lambda i, dp: (0, 0))] * 4,
                 out_specs=[
                     pl.BlockSpec((block, mine), lambda i, dp: (i, 0)),
                     pl.BlockSpec((block, 2 * mine), lambda i, dp: (i, 0)),
@@ -735,17 +738,17 @@
                 jax.ShapeDtypeStruct((4 * block, 2 * mine), low),
                 jax.ShapeDtypeStruct((4, extra, mine), low),
             ],
-            compiler_params=pltpu.CompilerParams(vmem_limit_bytes=32 * 2**20),
+            compiler_params=pltpu.CompilerParams(vmem_limit_bytes=16 * 2**20),
             cost_estimate=FREE,
             name="columns",
-        )(self.dp.reshape(1).astype(jnp.int32), self.held)
+        )(self.dp.reshape(1).astype(jnp.int32), *self.held)
         gains = gains.reshape(32, -1)[:, : self.gains.shape[0]].astype(jnp.float32)
         return wq, w_kv, gains
 
 
 def column_grads_kernel(dp_ref, *refs):
     sources, hiddens = refs[:4], refs[4:8]
-    dq_ref, dkv_ref, given_ref, kept_ref = refs[8:]
+    dq_ref, dkv_ref, *given_refs, kept_ref = refs[8:]
     count = sources[0].shape[0]
     mine = dq_ref.shape[1]
     for_q, for_kv = 0.0, 0.0
@@ -754,10 +757,12 @@
         for_q = for_q + columns_by_columns(hiddens[step][...], dq_ref[here, :])
         for_kv = for_kv + columns_by_columns(sources[step][...], dkv_ref[here, :])
 
-    @pl.when(pl.program_id(0) < 2)
-    def _():
-        given_ref[0, :, :mine] = for_q.astype(jnp.bfloat16)
-        given_ref[0, :, mine:] = for_kv.astype(jnp.bfloat16)
+    for place in range(2):
+
+        @pl.when(pl.program_id(0) == place)
+        def _():
+            given_refs[2 * place][...] = for_q.astype(jnp.bfloat16)
+            given_refs[2 * place + 1][...] = for_kv.astype(jnp.bfloat16)
 
     @pl.when(pl.program_id(0) >= 2)
     def _():
@@ -784,7 +789,7 @@
     each = wq_ref.shape[0]
     gain = 0.0
     for device in range(8):
-        gain = gain + got_ref[device, each : each + 8, :128].astype(jnp.float32)
+        gain = gain + got_ref[device, each : each + 16, :128].astype(jnp.float32)
     gain_ref[...] = gain
     out_ref[...] = jnp.where(
         flag_ref[...] != 0, out_kept_ref[...], out_got_ref[...].astype(jnp.float32)
@@ -841,13 +846,13 @@
             jax.ShapeDtypeStruct((rows, w_kv.shape[1]), low),
             jax.ShapeDtypeStruct((rows, wq.shape[1]), low),
         ],
-        compiler_params=pltpu.CompilerParams(vmem_limit_bytes=40 * 2**20),
+        compiler_params=pltpu.CompilerParams(vmem_limit_bytes=16 * 2**20),
         cost_estimate=cost,
         name="project",
     )(*piece, kv_gain, attn_gain, w_kv, wq)
 
 
-def terms_kernel(step, result_step, pair_ref, query_ref, w_kv_ref, wq_ref, *refs):
+def terms_kernel(step, pair_ref, query_ref, w_kv_ref, wq_ref, *refs):
     own_ref, other_ref = refs[-2:]
     count = pair_ref.shape[0] // 4
     here = slice(count * step, count * (step + 1))
@@ -856,8 +861,7 @@
         rows_by_rows(query_ref[here, :], wq_ref[...]),
     ]
     if len(refs) > 2:
-        there = slice(count * result_step, count * (result_step + 1))
-        found.append(product(refs[0][there, :], refs[1][...]))
+        found.append(product(refs[0][...], refs[1][...]))
     rows = count // 2
     for place, value in enumerate(found):
         value = value.astype(jnp.bfloat16)
@@ -867,16 +871,15 @@
 
 def back_terms(parts, step, d_pairs, d_queries, w_kv, wq, result=()):
     rows, width = d_pairs.shape[0] // 4, w_kv.shape[0]
-    result_step, *weights = result or (None,)
     count = rows // 2
     out = jax.ShapeDtypeStruct((count * len(parts), width), jnp.bfloat16)
     own, other = pl.pallas_call(
-        functools.partial(terms_kernel, step, result_step),
+        functools.partial(terms_kernel, step),
         out_shape=[out, out],
-        compiler_params=pltpu.CompilerParams(vmem_limit_bytes=40 * 2**20),
+        compiler_params=pltpu.CompilerParams(vmem_limit_bytes=20 * 2**20),
         cost_estimate=FREE,
         name="back_terms",
-    )(d_pairs, d_queries, w_kv, wq, *weights)
+    )(d_pairs, d_queries, w_kv, wq, *result)
     return [
         part.of_rows(Rows(own, count * place, count), Rows(other, count * place, count))
         for place, part in enumerate(parts)
@@ -908,7 +911,7 @@
         + [row_blocks(part, block) for part in sums],
         out_specs=pl.BlockSpec((block, width), lambda i: (i, 0)),
         out_shape=jax.ShapeDtypeStruct((rows, width), jnp.bfloat16),
-        compiler_params=pltpu.CompilerParams(vmem_limit_bytes=16 * 2**20),
+        compiler_params=pltpu.CompilerParams(vmem_limit_bytes=8 * 2**20),
         cost_estimate=FREE,
         name="result",
     )(middle, live, *(part.array for part in sums))
@@ -941,17 +944,74 @@
         + [row_blocks(part, block) for part in sums],
         out_specs=[spec, spec],
         out_shape=[jax.ShapeDtypeStruct((rows, width), jnp.bfloat16)] * 2,
-        compiler_params=pltpu.CompilerParams(vmem_limit_bytes=16 * 2**20),
+        compiler_params=pltpu.CompilerParams(vmem_limit_bytes=56 * 2**20),
         cost_estimate=FREE,
         name="input_grads",
     )(hidden, source, d_middle, attn_gain, kv_gain, *(part.array for part in sums))
 
 
+def feed_kernel(mid_plan, cot_plan, *refs):
+    arrays = refs[:-10]
+    wg_ref, wu_ref, wd_ref, inner_ref, d_gate_ref, d_up_ref, own_ref, other_ref = refs[-10:-2]
+    for plan, rows_ref in ((mid_plan, refs[-2]), (cot_plan, refs[-1])):
+        first = 0
+        for index, start, count in plan:
+            rows_ref[first : first + count, :] = arrays[index][start : start + count, :]
+            first += count
+    mid_ref, cot_ref = refs[-2:]
+    hidden, width = wg_ref.shape
+    for first in range(0, hidden, 256):
+        here = slice(first, min(first + 256, hidden))
+        gate_value = rows_by_rows(mid_ref[...], wg_ref[here, :])
+        up_value = rows_by_rows(mid_ref[...], wu_ref[here, :])
+        d_inner = rows_by_rows(cot_ref[...], wd_ref[here, :])
+        sigmoid_gate = jax.nn.sigmoid(gate_value)
+        swished = gate_value * sigmoid_gate
+        inner_ref[:, here] = (swished * up_value).astype(jnp.bfloat16)
+        d_gate_ref[:, here] = (
+            d_inner * up_value * sigmoid_gate * (1.0 + gate_value * (1.0 - sigmoid_gate))
+        ).astype(jnp.bfloat16)
+        d_up_ref[:, here] = (d_inner * swished).astype(jnp.bfloat16)
+    rows = own_ref.shape[0]
+    for first in range(0, width, 512):
+        here = slice(first, first + 512)
+        terms = product(d_gate_ref[...], wg_ref[:, here]) + product(d_up_ref[...], wu_ref[:, here])
+        terms = terms.astype(jnp.bfloat16)
+        own_ref[:, here] = terms[:rows]
+        other_ref[:, here] = terms[rows:]
+
+
+def feed(mid, cot, wg, wu, wd):
+    arrays = []
+    plans = []
+    for pieces in (mid, cot):
+        plan = []
+        for rows in pieces:
+            index = next((n for n, held in enumerate(arrays) if held is rows.array), None)
+            if index is None:
+                index = len(arrays)
+                arrays.append(rows.array)
+            plan.append((index, rows.start, rows.count))
+        plans.append(tuple(plan))
+    count = sum(rows.count for rows in mid)
+    hidden, width = wg.shape
+    low = jax.ShapeDtypeStruct((count, hidden), jnp.bfloat16)
+    terms = jax.ShapeDtypeStruct((count // 2, width), jnp.bfloat16)
+    return pl.pallas_call(
+        functools.partial(feed_kernel, *plans),
+        out_shape=[low, low, low, terms, terms]
+        + [jax.ShapeDtypeStruct((count, width), jnp.bfloat16)] * 2,
+        compiler_params=pltpu.CompilerParams(vmem_limit_bytes=24 * 2**20),
+        cost_estimate=LONG,
+        name="feed",
+    )(*arrays, wg, wu, wd)
+
+
 def add_kernel(*refs):
     count = len(refs) // 3
     for kept_ref, got_ref, out_ref in zip(refs[:count], refs[count : 2 * count], refs[2 * count :]):
-        rows = out_ref.shape[0]
-        out_ref[...] = kept_ref[:rows, :] + got_ref[:rows, :].astype(jnp.float32)
+        total = kept_ref[...] + got_ref[...].astype(jnp.float32)
+        out_ref[...] = total[: out_ref.shape[0]]
 
 
 def add_all(kept, got, rows):
@@ -965,7 +1025,7 @@
         in_specs=[spec] * (2 * count),
         out_specs=[pl.BlockSpec((rows, block), lambda i: (0, i))] * count,
         out_shape=[jax.ShapeDtypeStruct((rows, width), jnp.float32)] * count,
-        compiler_params=pltpu.CompilerParams(vmem_limit_bytes=40 * 2**20),
+        compiler_params=pltpu.CompilerParams(vmem_limit_bytes=20 * 2**20),
         cost_estimate=LONG,
         name="add_all",
     )(*kept, *got)
@@ -986,7 +1046,7 @@
             out_specs=pl.BlockSpec(block, lambda i, dp: (i, 0)),
         ),
         out_shape=jax.ShapeDtypeStruct(rows.shape, rows.dtype),
-        compiler_params=pltpu.CompilerParams(vmem_limit_bytes=16 * 2**20),
+        compiler_params=pltpu.CompilerParams(vmem_limit_bytes=8 * 2**20),
         cost_estimate=FREE,
         name="own_first",
     )(dp.reshape(1).astype(jnp.int32), rows)
@@ -1021,7 +1081,7 @@
             return 2 * (i % 2) + 1 - i // 2
 
         by_block = pl.BlockSpec((count, block), lambda i, dp: (0, dp[0] ^ of_step(i)))
-        given, self.kept = pl.pallas_call(
+        *given, self.kept = pl.pallas_call(
             column_grads_kernel,
             grid_spec=pltpu.PrefetchScalarGridSpec(
                 num_scalar_prefetch=1,
@@ -1032,33 +1092,40 @@
                     pl.BlockSpec((rows, 2 * mine), lambda i, dp: (0, 0)),
                 ],
                 out_specs=[
-                    pl.BlockSpec((1, block, 3 * mine), lambda i, dp: (jnp.minimum(i, 1), 0, 0)),
+                    *(
+                        pl.BlockSpec((block, width_of * mine), lambda i, dp: (0, 0))
+                        for width_of in (1, 2, 1, 2)
+                    ),
                     pl.BlockSpec((1, block, 3 * mine), lambda i, dp: (jnp.maximum(i, 2) - 2, 0, 0)),
                 ],
             ),
             out_shape=[
-                jax.ShapeDtypeStruct((2, block, 3 * mine), jnp.bfloat16),
+                *(
+                    jax.ShapeDtypeStruct((block, width_of * mine), jnp.bfloat16)
+                    for width_of in (1, 2, 1, 2)
+                ),
                 jax.ShapeDtypeStruct((2, block, 3 * mine), jnp.float32),
             ],
-            compiler_params=pltpu.CompilerParams(vmem_limit_bytes=40 * 2**20),
+            compiler_params=pltpu.CompilerParams(vmem_limit_bytes=20 * 2**20),
             cost_estimate=LONG,
             name="column_grads",
         )(self.dp.reshape(1).astype(jnp.int32), *sources, *hiddens, d_queries, d_pairs)
-        self.from_core = core_swap(given)
-        return [given]
+        self.from_core = [core_swap(value) for value in given]
+        return given
 
     def along_y(self, *gate):
-        given = self.kept[1] + after(self.from_core, *gate)[1].astype(jnp.float32)
+        got = after(tuple(self.from_core[2:]), *gate)
+        given = self.kept[1] + jnp.concatenate(got, axis=1).astype(jnp.float32)
         given = given.astype(jnp.bfloat16)
         self.from_y = y_swap(given)
         return [given]
 
     def along_fsdp(self, *gate):
-        total = self.kept[0] + self.from_core[0].astype(jnp.float32)
+        total = self.kept[0] + jnp.concatenate(self.from_core[:2], axis=1).astype(jnp.float32)
         total = (total + after(self.from_y, *gate).astype(jnp.float32)).astype(jnp.bfloat16)
         each, columns = total.shape[0] // 8, total.shape[1]
         gain = self.gain.astype(jnp.bfloat16).reshape(8, 1, each)
-        gain = jnp.pad(gain, ((0, 0), (0, 7), (0, columns - each)))
+        gain = jnp.pad(gain, ((0, 0), (0, 15), (0, columns - each)))
         given = jnp.concatenate([total.reshape(8, each, columns), gain], axis=1)
         self.got = lax.all_to_all(given, "fsdp", 0, 0, tiled=True)
         return [given], [self.got]
@@ -1077,10 +1144,10 @@
                 flat,
                 column,
                 column,
-                jax.ShapeDtypeStruct((8, 128), jnp.float32),
+                jax.ShapeDtypeStruct((16, 128), jnp.float32),
                 flat,
             ],
-            compiler_params=pltpu.CompilerParams(vmem_limit_bytes=32 * 2**20),
+            compiler_params=pltpu.CompilerParams(vmem_limit_bytes=8 * 2**20),
             cost_estimate=FREE,
             name="own_grads",
         )(got, *weights, flag, out_grads.kept, out_got)
@@ -1122,25 +1189,96 @@
         self.from_x = lax.ppermute(given.astype(jnp.bfloat16), ("dp", "fsdp"), pairs)
 
 
-def hidden_units(own, padded, dp, *gate):
-    rows = jnp.pad(own, ((0, padded - own.shape[0]), (0, 0)))
+def hidden_units(rows, dp, *gate):
     return own_first(lax.all_gather(after(rows, *gate), "dp", axis=0, tiled=True), dp)
 
 
+def hidden_core_kernel(count, *refs):
+    units, rows, out_refs = refs[:count], refs[count : 2 * count], refs[2 * count :]
+    half = units[0].shape[1] // 2
+    total = sum(
+        columns_by_columns(unit_ref[:, half:], row_ref[...]) for unit_ref, row_ref in zip(units, rows)
+    ).astype(jnp.bfloat16)
+    out_refs[0][...] = total[: half // 2]
+    out_refs[1][...] = total[half // 2 :]
+
+
+def hidden_y_kernel(count, *refs):
+    units, rows = refs[:count], refs[count : 2 * count]
+    own_got_ref, y_got_ref, kept_ref, given_ref = refs[2 * count :]
+    half = units[0].shape[1] // 2
+    total = sum(
+        columns_by_columns(unit_ref[:, :half], row_ref[...]) for unit_ref, row_ref in zip(units, rows)
+    )
+    kept_ref[...] = total[: half // 2] + own_got_ref[...].astype(jnp.float32)
+    given = total[half // 2 :] + y_got_ref[...].astype(jnp.float32)
+    given_ref[...] = given.astype(jnp.bfloat16)
+
+
+def out_grad_kernel(att_ref, *refs):
+    *rows, out_ref = refs
+    count = rows[0].shape[0]
+    out_ref[...] = sum(
+        columns_by_columns(att_ref[count * place : count * (place + 1), :], row_ref[...])
+        for place, row_ref in enumerate(rows)
+    )
+
+
+def out_grad(attended, pieces):
+    width = pieces[0].shape[1]
+    block = width // 2
+    return pl.pallas_call(
+        out_grad_kernel,
+        grid=(2,),
+        in_specs=[whole_block(attended)]
+        + [pl.BlockSpec((rows.shape[0], block), lambda i: (0, i)) for rows in pieces],
+        out_specs=pl.BlockSpec((attended.shape[1], block), lambda i: (0, i)),
+        out_shape=jax.ShapeDtypeStruct((attended.shape[1], width), jnp.float32),
+        compiler_params=pltpu.CompilerParams(vmem_limit_bytes=20 * 2**20),
+        cost_estimate=FREE,
+        name="out_grad",
+    )(attended, *pieces)
+
+
 class HiddenGrads:
-    def along_core(self, units, rows):
-        self.units, self.rows = units, rows
-        half = units.shape[1] // 2
-        given = columns_by_columns(units[:, half:], rows).astype(jnp.bfloat16)
-        self.from_core = core_swap(given)
-        return [given]
+    def __init__(self, units, rows):
+        self.units, self.rows = list(units), list(rows)
+
+    def call(self, kernel, got, outs, *gate):
+        width = self.rows[0].shape[1]
+        block = width // 2
+        units = after(tuple(self.units), *gate)
+
+        def spec(rows):
+            return pl.BlockSpec((rows, block), lambda i: (0, i))
+
+        return pl.pallas_call(
+            functools.partial(kernel, len(self.units)),
+            grid=(2,),
+            in_specs=[whole_block(unit) for unit in units]
+            + [spec(rows.shape[0]) for rows in self.rows]
+            + [spec(rows.shape[0]) for rows in got],
+            out_specs=[spec(rows) for rows, dtype in outs],
+            out_shape=[jax.ShapeDtypeStruct((rows, width), dtype) for rows, dtype in outs],
+            compiler_params=pltpu.CompilerParams(vmem_limit_bytes=24 * 2**20),
+            cost_estimate=LONG,
+            name="hidden_grads",
+        )(*units, *self.rows, *got)
+
+    def along_core(self, *gate):
+        half = self.units[0].shape[1] // 2
+        given = self.call(hidden_core_kernel, [], [(half // 2, jnp.bfloat16)] * 2, *gate)
+        self.from_core = [core_swap(value) for value in given]
+        return given
 
     def along_y(self, *gate):
-        half = self.units.shape[1] // 2
-        units, got = after((self.units, self.from_core), *gate)
-        total = columns_by_columns(units[:, :half], self.rows) + got.astype(jnp.float32)
-        given = total[half // 2 :].astype(jnp.bfloat16)
-        self.kept = total
+        half = self.units[0].shape[1] // 2
+        self.kept, given = self.call(
+            hidden_y_kernel,
+            self.from_core,
+            [(half // 2, jnp.float32), (half // 2, jnp.bfloat16)],
+            *gate,
+        )
         self.from_y = y_swap(given)
         return [given]
 
@@ -1205,16 +1343,19 @@
     wa = columns.along_fsdp()
     s1 = move([inputs])
     wy = columns.along_y(*s1)
-    s2 = move([inputs], *s1, *wa, *layout())
+    units = w_gate.shape[0]
+    padded = -(-units // 64) * 64
+    own_units = [
+        jnp.pad(own, ((0, padded - units), (0, 0))) for own in (w_gate, w_up, w_down)
+    ]
+    s2 = move([inputs], *s1, *wa, *layout(), *own_units)
     wc = columns.along_core(*wy)
     s3 = move([inputs], *s2)
     wq, w_kv, gains = columns.whole()
     kv_gain_full, attn_gain_full, ffn_gain_full = (
         gains[:, which * each : (which + 1) * each].reshape(1, width) for which in range(3)
     )
-    units = w_gate.shape[0]
-    padded = -(-units // 64) * 64
-    wg, wu, wd = (hidden_units(own, padded, dp, *s2, *wy) for own in (w_gate, w_up, w_down))
+    wg, wu, wd = (hidden_units(own, dp, *s2, *wy) for own in own_units)
 
     hidden_f = hidden.astype(jnp.float32)
     d_out = cotangent.astype(jnp.float32) * own_live
@@ -1238,7 +1379,7 @@
     attended_f, attended_low, lse = attend(
         *after((queries, pairs), *c1), first, last, place_of_key, head
     )
-    wo = out_rows(after(w_out, *s3), x, y, c, s4, c1)
+    wo = out_rows(after(w_out, *s2), x, y, c, s3, c1)
 
     def rows_of(array, step):
         return array[2 * step * local_rows : 2 * (step + 1) * local_rows]
@@ -1256,69 +1397,61 @@
     middle_unit = middle * middle_scale
     mids = Gather((middle_unit * ffn_gain_full).astype(jnp.bfloat16))
 
-    inners, d_gates, d_ups = [], [], []
-
-    def feed(step):
-        mid = mids.piece(step)
-        gate_value = rows_by_rows(mid, wg)
-        up_value = rows_by_rows(mid, wu)
-        sigmoid_gate = jax.nn.sigmoid(gate_value)
-        swished = gate_value * sigmoid_gate
-        d_inner = rows_by_rows(cots.piece(step), wd)
-        inners.append((swished * up_value).astype(jnp.bfloat16))
-        d_gates.append(
-            (d_inner * up_value * sigmoid_gate * (1.0 + gate_value * (1.0 - sigmoid_gate))).astype(
-                jnp.bfloat16
-            )
-        )
-        d_ups.append((d_inner * swished).astype(jnp.bfloat16))
-        return (product(d_gates[step], wg) + product(d_ups[step], wu)).astype(jnp.bfloat16)
-
+    fed = []
+
+    def feed_piece(step, *gate):
+        weights = after((wg, wu, wd), *gate)
+        fed.append(feed(mids.pieces[step], cots.pieces[step], *weights))
+
+    def terms_of(step):
+        own, other = fed[step][3:5]
+        return back.of_rows(rows_in(own), rows_in(other))
+
+    back = Scatter()
     m1 = move([mids])
     m2 = move([mids], *m1)
-    t0 = feed(0)
-    m3 = move([mids], *m2, t0)
-    t1 = feed(1)
-    back = Scatter()
-    d1 = move([mids, back.of(t1)], *m3)
-    t2 = feed(2)
-    d2 = move([back.of(t2)], *d1)
-    t3 = feed(3)
-    d3 = move([back.of(t3)], *d2)
-    d_gates, d_ups, inners = (jnp.concatenate(value, axis=0) for value in (d_gates, d_ups, inners))
-    all_mids = jnp.concatenate([mids.piece(step) for step in range(4)], axis=0)
-    all_cots = jnp.concatenate([cots.piece(step) for step in range(4)], axis=0)
-    gate_sums, up_sums, down_sums = (HiddenGrads() for which in range(3))
-    h1 = gate_sums.along_core(after(d_gates, *d2), all_mids)
-    d4 = move([back.of(t0)], *d3, *h1)
-    h2 = up_sums.along_core(after(d_ups, *d3), all_mids)
-    h3 = down_sums.along_core(after(inners, *d3), all_cots)
-    d_normed = after(back.total(), *h2, *h3)
+    feed_piece(0)
+    m3 = move([mids], *m2, fed[0][0])
+    feed_piece(1, *m2)
+    d1 = move([mids, terms_of(1)], *m3)
+    feed_piece(2, *m3)
+    d2 = move([terms_of(2)], *d1)
+    feed_piece(3, *d1)
+    d3 = move([terms_of(3)], *d2)
+    inners, d_gates, d_ups, _, _, all_mids, all_cots = zip(*fed)
+    gate_sums = HiddenGrads(d_gates, all_mids)
+    up_sums = HiddenGrads(d_ups, all_mids)
+    down_sums = HiddenGrads(inners, all_cots)
+    h1 = gate_sums.along_core(*d2)
+    d4 = move([terms_of(0)], *d3, *h1)
+    h2 = up_sums.along_core(*d3)
+    d_normed = after(back.total(), *h2)
     d_middle = d_out + norm_backward(middle, middle_scale, ffn_gain_full, d_normed)
     d_branch_low = d_middle.astype(jnp.bfloat16)
     outs = Gather(d_branch_low)
     e1 = move([outs])
+    def result_terms(step, *gate):
+        return product(after(inners[step], *gate), wd).astype(jnp.bfloat16)
+
     h1 = gate_sums.along_y(d_branch_low)
-    e2 = move([outs], *e1, *h1)
+    h3 = down_sums.along_core(*h1)
+    e2 = move([outs], *e1, *h3)
     h2 = up_sums.along_y(*e1)
-    e3 = move([outs], *e2, *h2)
+    first_result = result_terms(1, *e1, *h2)
+    ffn_gain_part = jnp.sum(after(d_normed * middle_unit, first_result), axis=0)
+    column_grads = ColumnGrads(dp)
+    column_grads.gain_core(ffn_gain_part)
+    column_grads.gain_y()
+    e3 = move([outs], *e2, *h2, ffn_gain_part)
     h3 = down_sums.along_y(*e2)
 
-    def result_terms(step, *gate):
-        return product(after(rows_of(inners, step), *gate), wd).astype(jnp.bfloat16)
-
     result = Scatter()
-    first_result = result_terms(1, *e2, *h3)
-    ffn_gain_part = jnp.sum(after(d_normed * middle_unit, first_result), axis=0)
-    e4 = move([outs, result.of(first_result)], *e3, ffn_gain_part, gate_sums.from_y)
-    column_grads = ColumnGrads(dp)
-    column_grads.gain_core(ffn_gain_part, *e3)
-    column_grads.gain_y(*e4)
+    e4 = move([outs, result.of(first_result)], *e3, *h3, gate_sums.from_y, column_grads.gain)
     d_branches = [outs.piece(step) for step in range(4)]
     d_attended = jnp.concatenate(
         [rows_by_rows(rows, wo).astype(jnp.bfloat16) for rows in d_branches], axis=0
     )
-    o2 = move([result.of(result_terms(2, *e3))], *e4, up_sums.from_y, down_sums.from_y, column_grads.gain)
+    o2 = move([result.of(result_terms(2, *e3))], *e4)
     d_queries, d_pairs = attend_back(
         queries, pairs, first, last, place_of_key, lse, attended_f, d_attended, head
     )
@@ -1328,23 +1461,29 @@
     def terms(step, *gate, result=()):
         parts = [d_src, d_hid, *result[:1]]
         rows = after((d_pairs, d_queries), *gate)
-        weights = (*result[1:], inners, wd) if result else ()
+        weights = (inners[result[1]], wd) if result else ()
         return back_terms(parts, step, *rows, w_kv, wq, weights)
 
     first_terms = terms(1)
     started = d_hid.own.array
-    i1 = move(first_terms, *o2)
-    sources, hiddens = after((tuple(src_low), tuple(hid_low)), started)
+    sent = []
+    i1 = move(first_terms, *o2, up_sums.from_y, down_sums.from_y, payload=sent)
+    sources, hiddens = after((tuple(src_low), tuple(hid_low)), *sent)
     column_grads.along_core(sources, hiddens, d_queries, d_pairs)
+    second_terms = terms(2, started, result=(result, 3))
+    i2 = move(second_terms, *i1)
     py = column_grads.along_y()
-    i2 = move(terms(2, started, result=(result, 3)), *i1)
+    next_terms = terms(3, *py, result=(result, 0))
     out_grads = OutGrads(
-        columns_by_columns(after(attended_low, *i1), jnp.concatenate(d_branches, axis=0)), x, y, c
+        out_grad(after(attended_low, *py), d_branches),
+        x,
+        y,
+        c,
     )
     out_grads.along_core()
     oy = out_grads.along_y(column_grads.from_y)
     pz, got_z = column_grads.along_fsdp()
-    i3 = move(terms(3, *i1, result=(result, 0)), *i2, *oy, *pz)
+    i3 = move(next_terms, *i2, *oy)
     out_grads.along_x(*i2)
     i4 = move(terms(0, *i2), *i3)
     grad_gate, grad_up, grad_down = add_all(

time: 590 us -> 578 us (0.980)
  Pallas kernels: 71.2 us -> 112 us
  matrix products: 47.2 us -> 8.29 us
  local copies, waits for them, and re-layouts: 78.9 us -> 66.2 us
    pallas_call x4 -> x15, Pallas kernels: 7.85 us -> 46.3 us  [the longest x4 20 us: feed(): pl.pallas_call(functools.partial(feed_kernel, *plans), out_shape=[low, lo...]
    ppermute x27, waiting for transfers between devices: 149 us -> 128 us  [x_swap(): return lax.ppermute(value, 'fsdp', swap_pairs(8, 1))]
    dot_general x16 -> x4, matrix products: 23 us -> 3.55 us  [rows_by_rows(): lax.dot_general(left, right, (((1,), (1,)), ((), ())), preferred_element_...]
    dot_general x7 -> x0, matrix products: 12.5 us -> none  [columns_by_columns(): lax.dot_general(left, right, (((0,), (0,)), ((), ())), preferred_element_...]
    ppermute x6, waiting for transfers between devices: 18.3 us -> 29.4 us  [y_swap(): return lax.ppermute(value, 'dp', swap_pairs(4, 2))]
    dot_general x14 -> x6, matrix products: 11.7 us -> 4.74 us  [product(): return jnp.dot(left, right, preferred_element_type=jnp.float32)]
    unnamed x319 -> x374, local copies, waits for them, and re-layouts: 59.1 us -> 52.6 us
    all_to_all x1, waiting for transfers between devices: 1.5 us -> 7.64 us  [along_fsdp(): self.got = lax.all_to_all(given, 'fsdp', 0, 0, tiled=True)]
  transfers between devices with their start and end apart: 76 -> 82, of which waited for: 48 -> 49; matrix products, arithmetic and copies ran while one was open for 18% -> 9% of each run, Pallas kernels for 10% -> 19%
where the time goes in v4:
time: 578 us; the launch traced here: 569 us
  waiting for transfers between devices  253 us (44%)
  Pallas kernels  112 us (19%)
  starting transfers between devices  85.2 us (15%)
  local copies, waits for them, and re-layouts  66.2 us (11%)
  other arithmetic  27.3 us (5%)
  between operations  16.5 us (3%)
  matrix products  8.29 us (1%)
    ppermute x27, waiting for transfers between devices, x_swap(): return lax.ppermute(value, 'fsdp', swap_pairs(8, 1))  128 us
    ppermute x26, waiting for transfers between devices, ring_step(): return lax.ppermute(value, 'fsdp', ring_pairs())  68.6 us
    unnamed x374, local copies, waits for them, and re-layouts  52.6 us
    ppermute x26, starting transfers between devices, ring_step(): return lax.ppermute(value, 'fsdp', ring_pairs())  33.5 us
    ppermute x27, starting transfers between devices, x_swap(): return lax.ppermute(value, 'fsdp', swap_pairs(8, 1))  30.2 us
    ppermute x6, waiting for transfers between devices, y_swap(): return lax.ppermute(value, 'dp', swap_pairs(4, 2))  29.4 us
    pallas_call x4, Pallas kernels, feed(): pl.pallas_call(functools.partial(feed_kernel, *plans), out_shape=[low, lo...  20 us
    pallas_call x6, Pallas kernels, call(): pl.pallas_call(functools.partial(kernel, len(self.units)), grid=(2,), in_...  16.6 us
  transfers between devices with their start and end apart: 82, of which 49 were waited for; matrix products, arithmetic and copies ran while one was open for 9% of the time, Pallas kernels for 19%

profile of v4, /device:TPU:0, one launch (start us, length us, event | category | flops | bytes accessed | tf_op | source)
XLA Modules:
  0.0 569.1 jit_solution(6019006048051965816)
XLA Ops:
  9.5 3.1 collective-permute-start.1
  16.2 3.9 all-to-all-start
  32.6 5.0 collective-permute-done.1.held_ref
  37.6 3.4 collective-permute-done.refs_0_
  41.0 14.0 %all-to-all-done = bf16[8,208,256]{2,1,0:T(8,128)(2,1)S(1)} async-done(((bf16[8,208,256]{2,1,0:T(8,128)(2,1)}), bf16[8,208,256]{2,1,0:T(8,128)(2,1)S(1)}, u32[]{:S(2)}, u32[]{:S(2)}) %all-to-all-start) | async-done | bytes 852000 | tf_op jit(solution)/shard_map/all_to_all | solution.py:703
  60.8 18.0 %collective-permute-done.2.refs_2_ = bf16[1664,256]{1,0:T(8,128)(2,1)S(1)} collective-permute-done((bf16[1664,256]{1,0:T(8,128)(2,1)S(1)}, bf16[1664,256]{1,0:T(8,128)(2,1)S(1)}, u32[]{:S(2)}, u32[]{:S(2)}) %collective-permute-start.2) | collective-permute-done | bytes 852000 | tf_op jit(solution)/shard_map/ppermute | solution.py:346
  106.3 6.9 %collective-permute-done.7.refs_0_.refs_1_ = bf16[256,2048]{1,0:T(8,128)(2,1)} collective-permute-done((bf16[256,2048]{1,0:T(8,128)(2,1)}, bf16[256,2048]{1,0:T(8,128)(2,1)}, u32[]{:S(2)}, u32[]{:S(2)}) %collective-permute-start.7) | collective-permute-done | bytes 1048608 | tf_op jit(solution)/shard_map/ppermute | solution.py:338
  113.2 3.7 collective-permute-start.14
  120.6 3.0 project.6
  124.7 7.2 %collective-permute-done.9.refs_0_ = bf16[128,2048]{1,0:T(8,128)(2,1)S(1)} collective-permute-done((bf16[128,2048]{1,0:T(8,128)(2,1)S(1)}, bf16[128,2048]{1,0:T(8,128)(2,1)S(1)}, u32[]{:S(2)}, u32[]{:S(2)}) %collective-permute-start.9) | collective-permute-done | bytes 524320 | tf_op jit(solution)/shard_map/ppermute | solution.py:338
  140.1 4.8 collective-permute-done.11.refs_3_
  148.9 7.6 %attend.1 = (f32[1024,256]{1,0:T(8,128)S(1)}, bf16[1024,256]{1,0:T(8,128)(2,1)S(1)}, f32[2,1024,1]{2,1,0:T(8,128)S(1)}) custom-call(bf16[1024,256]{1,0:T(8,128)(2,1)S(1)} %constant_dynamic-update-slice_fusion.2.q_ref, bf16[1024,512]{1,0:T(8,128)(2,1)S(1)} %constant_dynamic-update-slice_fusion.6.k_ref.v_ref, ...), custom_call_target="tpu_custom_call" | custom-call | flops 20000000000 | tf_op jit(solution)/shard_map/attend/pallas_call | solution.py:594
  157.8 4.8 collective-permute-done.16.refs_1_.refs_2_
  166.7 16.1 %collective-permute-done.18.refs_1_.refs_3_ = bf16[192,2048]{1,0:T(8,128)(2,1)S(1)} collective-permute-done((bf16[192,2048]{1,0:T(8,128)(2,1)S(1)}, bf16[192,2048]{1,0:T(8,128)(2,1)S(1)}, u32[]{:S(2)}, u32[]{:S(2)}) %collective-permute-start.18) | collective-permute-done | bytes 786464 | tf_op jit(solution)/shard_map/ppermute | solution.py:342
  187.8 15.0 %collective-permute-done.20.refs_2_.refs_4_ = bf16[192,2048]{1,0:T(8,128)(2,1)S(1)} collective-permute-done((bf16[192,2048]{1,0:T(8,128)(2,1)S(1)}, bf16[192,2048]{1,0:T(8,128)(2,1)S(1)}, u32[]{:S(2)}, u32[]{:S(2)}) %collective-permute-start.20) | collective-permute-done | bytes 786464 | tf_op jit(solution)/shard_map/ppermute | solution.py:338
  207.1 8.1 %collective-permute-done.22.refs_2_ = bf16[128,2048]{1,0:T(8,128)(2,1)S(1)} collective-permute-done((bf16[128,2048]{1,0:T(8,128)(2,1)S(1)}, bf16[128,2048]{1,0:T(8,128)(2,1)S(1)}, u32[]{:S(2)}, u32[]{:S(2)}) %collective-permute-start.22) | collective-permute-done | bytes 524320 | tf_op jit(solution)/shard_map/ppermute | solution.py:338
  219.5 8.8 %collective-permute-done.24 = bf16[128,2048]{1,0:T(8,128)(2,1)} collective-permute-done((bf16[128,2048]{1,0:T(8,128)(2,1)}, bf16[128,2048]{1,0:T(8,128)(2,1)}, u32[]{:S(2)}, u32[]{:S(2)}) %collective-permute-start.24) | collective-permute-done | bytes 524320 | tf_op jit(solution)/shard_map/ppermute | solution.py:338
  246.6 3.4 collective-permute-start.29
  252.1 5.7 %feed.4 = (bf16[256,768]{1,0:T(8,128)(2,1)S(1)}, bf16[256,768]{1,0:T(8,128)(2,1)S(1)}, bf16[256,768]{1,0:T(8,128)(2,1)S(1)}, bf16[128,2048]{1,0:T(8,128)(2,1)S(1...) custom-call(bf16[128,2048]{1,0:T(8,128)(2,1)} %multiply_convert_fusion.refs_0_, ...), custom_call_target="tpu_custom_call" | custom-call | flops 20000000000 | tf_op jit(solution)/shard_map/feed/pallas_call | solution.py:1000
  261.7 5.5 feed.5
  268.7 3.2 collective-permute-done.31.refs_0_
  275.1 4.4 feed.6
  279.6 5.0 collective-permute-done.32.refs_1_.refs_3_
  288.5 4.4 feed.7
  293.0 7.4 %collective-permute-done.34.refs_1_ = bf16[128,2048]{1,0:T(8,128)(2,1)S(1)} collective-permute-done((bf16[128,2048]{1,0:T(8,128)(2,1)S(1)}, bf16[128,2048]{1,0:T(8,128)(2,1)S(1)}, u32[]{:S(2)}, u32[]{:S(2)}) %collective-permute-start.34) | collective-permute-done | bytes 524320 | tf_op jit(solution)/shard_map/ppermute | solution.py:338
  308.2 5.7 %collective-permute-done.36.refs_1_ = bf16[128,2048]{1,0:T(8,128)(2,1)S(1)} collective-permute-done((bf16[128,2048]{1,0:T(8,128)(2,1)S(1)}, bf16[128,2048]{1,0:T(8,128)(2,1)S(1)}, u32[]{:S(2)}, u32[]{:S(2)}) %collective-permute-start.36) | collective-permute-done | bytes 524320 | tf_op jit(solution)/shard_map/ppermute | solution.py:338
  319.9 5.8 %collective-permute-done.38 = bf16[128,2048]{1,0:T(8,128)(2,1)S(1)} collective-permute-done((bf16[128,2048]{1,0:T(8,128)(2,1)S(1)}, bf16[128,2048]{1,0:T(8,128)(2,1)S(1)}, u32[]{:S(2)}, u32[]{:S(2)}) %collective-permute-start.38) | collective-permute-done | bytes 524320 | tf_op jit(solution)/shard_map/ppermute | solution.py:338
  335.4 3.2 hidden_grads.10
  338.5 5.3 collective-permute-done.43
  357.2 7.3 %collective-permute-done.46 = bf16[128,2048]{1,0:T(8,128)(2,1)S(1)} collective-permute-done((bf16[128,2048]{1,0:T(8,128)(2,1)}, bf16[128,2048]{1,0:T(8,128)(2,1)S(1)}, u32[]{:S(2)}, u32[]{:S(2)}) %collective-permute-start.46) | collective-permute-done | bytes 524320 | tf_op jit(solution)/shard_map/ppermute | solution.py:338
  370.2 3.5 hidden_grads.11
  376.0 3.0 collective-permute-done.51.refs_2_
  384.5 7.9 %collective-permute-done.55.refs_3_ = bf16[128,2048]{1,0:T(8,128)(2,1)S(1)} collective-permute-done((bf16[128,2048]{1,0:T(8,128)(2,1)S(1)}, bf16[128,2048]{1,0:T(8,128)(2,1)S(1)}, u32[]{:S(2)}, u32[]{:S(2)}) %collective-permute-start.55) | collective-permute-done | bytes 524320 | tf_op jit(solution)/shard_map/ppermute | solution.py:338
  397.9 10.0 %attend_back.1 = (bf16[1024,256]{1,0:T(8,128)(2,1)S(1)}, bf16[1024,512]{1,0:T(8,128)(2,1)S(1)}) custom-call(bf16[1024,256]{1,0:T(8,128)(2,1)S(1)} %copy-done.95, bf16[1024,512]{1,0:T(8,128)(2,1)S(1)} %copy-done.93, bf16[1024,512]{1,0:T(8,128)(2,1)S(1)} %copy-done.93, s32[1024,1]{1,0:T(8,128)S(1)} %copy-done.72, s32[1024,1]{1,0:T(8,128)S(1)} %copy-done.68, ...), custom_call_target="tpu_custom_call" | custom-call | flops 20000000000 | tf_op jit(solution)/shard_map/attend_back/pallas_call | solution.py:613
  414.0 6.5 %column_grads.1 = (bf16[512,256]{1,0:T(8,128)(2,1)S(1)}, bf16[512,512]{1,0:T(8,128)(2,1)}, bf16[512,256]{1,0:T(8,128)(2,1)S(1)}, bf16[512,512]{1,0:T(8,128)(2,1)}, f32[2,512,768]{2,1,0:T(8,128)S(1)}) custom-call(s32[1]{0:T(128)} %bitcast.dp_ref, bf16[256,2048]{1,0:T(8,128)(2,1)S(1)} %copy-done.99, bf16[256,2048]{1,0:T(8,128)(2,1)S(1)} %copy-done.103, ...), custom_call_target="tpu_custom_call" | custom-call | flops 20000000000 | tf_op jit(solution)/shard_map/column_grads/pallas_call | solution.py:1084
  430.6 3.2 mix.27
  453.2 9.9 %collective-permute-done.68 = bf16[512,768]{1,0:T(8,128)(2,1)} collective-permute-done((bf16[512,768]{1,0:T(8,128)(2,1)}, bf16[512,768]{1,0:T(8,128)(2,1)}, u32[]{:S(2)}, u32[]{:S(2)}) %collective-permute-start.68) | collective-permute-done | bytes 786464 | tf_op jit(solution)/shard_map/ppermute | solution.py:346
  463.1 7.6 %collective-permute-done.65.refs_1_ = bf16[384,2048]{1,0:T(8,128)(2,1)} collective-permute-done((bf16[384,2048]{1,0:T(8,128)(2,1)}, bf16[384,2048]{1,0:T(8,128)(2,1)}, u32[]{:S(2)}, u32[]{:S(2)}) %collective-permute-start.65) | collective-permute-done | bytes 1572896 | tf_op jit(solution)/shard_map/ppermute | solution.py:338
  472.5 3.6 mix.28
  482.2 5.8 %all-to-all-start.1 = ((bf16[8,80,768]{2,1,0:T(8,128)(2,1)}), bf16[8,80,768]{2,1,0:T(8,128)(2,1)}, u32[]{:S(2)}, u32[]{:S(2)}) async-start(bf16[8,80,768]{2,1,0:T(8,128)(2,1)} %fusion.5), calls=%async_computation.1 | async-start | bytes 1966080 | tf_op jit(solution)/shard_map/all_to_all | solution.py:1130
  488.0 4.2 collective-permute-done.75
  498.5 16.4 %collective-permute-done.69.x_ref.refs_1_ = bf16[384,2048]{1,0:T(8,128)(2,1)} collective-permute-done((bf16[384,2048]{1,0:T(8,128)(2,1)}, bf16[384,2048]{1,0:T(8,128)(2,1)}, u32[]{:S(2)}, u32[]{:S(2)}) %collective-permute-start.69) | collective-permute-done | bytes 1572896 | tf_op jit(solution)/shard_map/ppermute | solution.py:338
  517.2 3.4 mix.29
  520.6 3.5 collective-permute-start.71
  529.3 7.6 %all-to-all-done.1.got_ref = bf16[8,80,768]{2,1,0:T(8,128)(2,1)} async-done(((bf16[8,80,768]{2,1,0:T(8,128)(2,1)}), bf16[8,80,768]{2,1,0:T(8,128)(2,1)}, u32[]{:S(2)}, u32[]{:S(2)}) %all-to-all-start.1) | async-done | bytes 983072 | tf_op jit(solution)/shard_map/all_to_all | solution.py:1130
  542.6 3.5 result.1
  549.3 8.1 %collective-permute-done.72.refs_2_.refs_5_ = bf16[256,2048]{1,0:T(8,128)(2,1)} collective-permute-done((bf16[256,2048]{1,0:T(8,128)(2,1)}, bf16[256,2048]{1,0:T(8,128)(2,1)}, u32[]{:S(2)}, u32[]{:S(2)}) %collective-permute-start.72) | collective-permute-done | bytes 1048608 | tf_op jit(solution)/shard_map/ppermute | solution.py:342
  557.3 4.8 input_grads.1
  (622 shorter events, 240.5 us)
Async XLA Ops:
  9.5 28.1 %collective-permute-start.1 = (bf16[256,2048]{1,0:T(8,128)(2,1)S(1)}, bf16[256,2048]{1,0:T(8,128)(2,1)S(1)}, u32[]{:S(2)}, u32[]{:S(2)}) collective-permute-start(bf16[256,2048]{1,0:T(8,128)(2,1)S(1)} %constant_dynamic-update-slice_fusion.held_ref), channel_id=1, source_target_pairs={{0,2},{1,3},{2,6},{3,7},{6,4},{7,5},{4,0},{5,1},{8,10},{9,11},{10,... | collective-permute-start | bytes 3145736 | tf_op jit(solution)/shard_map/ppermute | solution.py:342
  12.5 28.5 %collective-permute-start = (bf16[256,2048]{1,0:T(8,128)(2,1)S(1)}, bf16[256,2048]{1,0:T(8,128)(2,1)}, u32[]{:S(2)}, u32[]{:S(2)}) collective-permute-start(bf16[256,2048]{1,0:T(8,128)(2,1)S(1)} %constant_dynamic-update-slice_fusion.held_ref), channel_id=1, source_target_pairs={{0,1},{1,0},{2,3},{3,2},{4,5},{5,4},{6,7},{7,6},{8,9},{9,8},{10,11... | collective-permute-start | bytes 3145736 | tf_op jit(solution)/shard_map/ppermute | solution.py:338
  16.2 38.8 %all-to-all-start = ((bf16[8,208,256]{2,1,0:T(8,128)(2,1)}), bf16[8,208,256]{2,1,0:T(8,128)(2,1)S(1)}, u32[]{:S(2)}, u32[]{:S(2)}) async-start(bf16[8,208,256]{2,1,0:T(8,128)(2,1)} %bitcast.85), calls=%async_computation | async-start | bytes 1703936 | tf_op jit(solution)/shard_map/all_to_all | solution.py:703
  20.0 215.8 %all-gather.4.cloned.1.call-start = ((), (), s32[]{:S(2)}) async-start(), calls=%async_computation.2 | async-start | bytes 3932160 | tf_op jit(solution)/shard_map/all_gather | solution.py:1193
  55.0 24.3 %collective-permute-start.5 = (bf16[256,2048]{1,0:T(8,128)(2,1)S(1)}, bf16[256,2048]{1,0:T(8,128)(2,1)S(1)}, u32[]{:S(2)}, u32[]{:S(2)}) collective-permute-start(bf16[256,2048]{1,0:T(8,128)(2,1)S(1)} %collective-permute-done.1.held_ref), channel_id=1, source_target_pairs={{0,1},{1,0},{2,3},{3,2},{4,5},{5,4},{6,7},{7,6},{8,9},{9,8},{10,11... | collective-permute-start | bytes 3145736 | tf_op jit(solution)/shard_map/ppermute | solution.py:338
  56.6 24.5 %collective-permute-start.6 = (bf16[256,2048]{1,0:T(8,128)(2,1)S(1)}, bf16[256,2048]{1,0:T(8,128)(2,1)}, u32[]{:S(2)}, u32[]{:S(2)}) collective-permute-start(bf16[256,2048]{1,0:T(8,128)(2,1)S(1)} %collective-permute-done.1.held_ref), channel_id=1, source_target_pairs={{0,2},{1,3},{2,6},{3,7},{6,4},{7,5},{4,0},{5,1},{8,10},{9,11},{10,... | collective-permute-start | bytes 3145736 | tf_op jit(solution)/shard_map/ppermute | solution.py:342
  57.5 21.4 %collective-permute-start.2 = (bf16[1664,256]{1,0:T(8,128)(2,1)S(1)}, bf16[1664,256]{1,0:T(8,128)(2,1)S(1)}, u32[]{:S(2)}, u32[]{:S(2)}) collective-permute-start(bf16[1664,256]{1,0:T(8,128)(2,1)S(1)} %bitcast.83), channel_id=1, source_target_pairs={{0,16},{8,24},{16,0},{24,8},{1,17},{9,25},{17,1},{25,9},{2,18},{10... | collective-permute-start | bytes 2555912 | tf_op jit(solution)/shard_map/ppermute | solution.py:346
  81.0 158.7 %all-gather.6.cloned.1.call-start = ((), (), s32[]{:S(2)}) async-start(), calls=%async_computation.3 | async-start | bytes 3932160 | tf_op jit(solution)/shard_map/all_gather | solution.py:1193
  81.8 161.7 %all-gather.8.cloned.1.call-start = ((), (), s32[]{:S(2)}) async-start(), calls=%async_computation.4 | async-start | bytes 3932160 | tf_op jit(solution)/shard_map/all_gather | solution.py:1193
  86.1 27.1 %collective-permute-start.7 = (bf16[256,2048]{1,0:T(8,128)(2,1)}, bf16[256,2048]{1,0:T(8,128)(2,1)}, u32[]{:S(2)}, u32[]{:S(2)}) collective-permute-start(bf16[256,2048]{1,0:T(8,128)(2,1)} %collective-permute-done.6.held_ref), channel_id=1, source_target_pairs={{0,1},{1,0},{2,3},{3,2},{4,5},{5,4},{6,7},{7,6},{8,9},{9,8},{10,11... | collective-permute-start | bytes 3145736 | tf_op jit(solution)/shard_map/ppermute | solution.py:338
  87.0 26.2 %collective-permute-start.8 = (bf16[256,2048]{1,0:T(8,128)(2,1)}, bf16[256,2048]{1,0:T(8,128)(2,1)}, u32[]{:S(2)}, u32[]{:S(2)}) collective-permute-start(bf16[256,2048]{1,0:T(8,128)(2,1)} %collective-permute-done.6.held_ref), channel_id=1, source_target_pairs={{0,2},{1,3},{2,6},{3,7},{6,4},{7,5},{4,0},{5,1},{8,10},{9,11},{10,... | collective-permute-start | bytes 3145736 | tf_op jit(solution)/shard_map/ppermute | solution.py:342
  113.2 26.9 %collective-permute-start.14 = (bf16[128,2048]{1,0:T(8,128)(2,1)S(1)}, bf16[128,2048]{1,0:T(8,128)(2,1)S(1)}, u32[]{:S(2)}, u32[]{:S(2)}) collective-permute-start(bf16[128,2048]{1,0:T(8,128)(2,1)S(1)} %copy-done.169), channel_id=1, source_target_pairs={{0,16},{2,18},{4,20},{6,22},{8,24},{10,26},{12,28},{14,30},{17,1},... | collective-permute-start | bytes 1572872 | tf_op jit(solution)/shard_map/ppermute | solution.py:1160
  118.8 14.0 %collective-permute-start.10 = (bf16[128,2048]{1,0:T(8,128)(2,1)S(1)}, bf16[128,2048]{1,0:T(8,128)(2,1)S(1)}, u32[]{:S(2)}, u32[]{:S(2)}) collective-permute-start(bf16[128,2048]{1,0:T(8,128)(2,1)S(1)} %get-tuple-element.274), channel_id=1, source_target_pairs={{0,2},{1,3},{2,6},{3,7},{6,4},{7,5},{4,0},{5,1},{8,10},{9,11},{10,... | collective-permute-start | bytes 1572872 | tf_op jit(solution)/shard_map/ppermute | solution.py:342
  147.2 15.4 %collective-permute-start.16 = (bf16[128,2048]{1,0:T(8,128)(2,1)S(1)}, bf16[128,2048]{1,0:T(8,128)(2,1)S(1)}, u32[]{:S(2)}, u32[]{:S(2)}) collective-permute-start(bf16[128,2048]{1,0:T(8,128)(2,1)S(1)} %collective-permute-done.12.refs_2_), channel_id=1, source_target_pairs={{0,2},{1,3},{2,6},{3,7},{6,4},{7,5},{4,0},{5,1},{8,10},{9,11},{10,... | collective-permute-start | bytes 1572872 | tf_op jit(solution)/shard_map/ppermute | solution.py:342
  148.2 14.5 %collective-permute-start.17 = (bf16[128,2048]{1,0:T(8,128)(2,1)S(1)}, bf16[128,2048]{1,0:T(8,128)(2,1)S(1)}, u32[]{:S(2)}, u32[]{:S(2)}) collective-permute-start(bf16[128,2048]{1,0:T(8,128)(2,1)S(1)} %collective-permute-done.12.refs_2_), channel_id=1, source_target_pairs={{0,1},{1,0},{2,3},{3,2},{4,5},{5,4},{6,7},{7,6},{8,9},{9,8},{10,11... | collective-permute-start | bytes 1572872 | tf_op jit(solution)/shard_map/ppermute | solution.py:338
  162.7 20.0 %collective-permute-start.18 = (bf16[192,2048]{1,0:T(8,128)(2,1)S(1)}, bf16[192,2048]{1,0:T(8,128)(2,1)S(1)}, u32[]{:S(2)}, u32[]{:S(2)}) collective-permute-start(bf16[192,2048]{1,0:T(8,128)(2,1)S(1)} %get-tuple-element.295), channel_id=1, source_target_pairs={{0,2},{1,3},{2,6},{3,7},{6,4},{7,5},{4,0},{5,1},{8,10},{9,11},{10,... | collective-permute-start | bytes 2359304 | tf_op jit(solution)/shard_map/ppermute | solution.py:342
  165.6 18.6 %collective-permute-start.19 = (bf16[192,2048]{1,0:T(8,128)(2,1)S(1)}, bf16[192,2048]{1,0:T(8,128)(2,1)S(1)}, u32[]{:S(2)}, u32[]{:S(2)}) collective-permute-start(bf16[192,2048]{1,0:T(8,128)(2,1)S(1)} %get-tuple-element.296), channel_id=1, source_target_pairs={{0,1},{1,0},{2,3},{3,2},{4,5},{5,4},{6,7},{7,6},{8,9},{9,8},{10,11... | collective-permute-start | bytes 2359304 | tf_op jit(solution)/shard_map/ppermute | solution.py:338
  185.1 17.7 %collective-permute-start.20 = (bf16[192,2048]{1,0:T(8,128)(2,1)S(1)}, bf16[192,2048]{1,0:T(8,128)(2,1)S(1)}, u32[]{:S(2)}, u32[]{:S(2)}) collective-permute-start(bf16[192,2048]{1,0:T(8,128)(2,1)S(1)} %get-tuple-element.299), channel_id=1, source_target_pairs={{0,1},{1,0},{2,3},{3,2},{4,5},{5,4},{6,7},{7,6},{8,9},{9,8},{10,11... | collective-permute-start | bytes 2359304 | tf_op jit(solution)/shard_map/ppermute | solution.py:338
  185.7 18.3 %collective-permute-start.21 = (bf16[192,2048]{1,0:T(8,128)(2,1)S(1)}, bf16[192,2048]{1,0:T(8,128)(2,1)S(1)}, u32[]{:S(2)}, u32[]{:S(2)}) collective-permute-start(bf16[192,2048]{1,0:T(8,128)(2,1)S(1)} %get-tuple-element.300), channel_id=1, source_target_pairs={{0,2},{1,3},{2,6},{3,7},{6,4},{7,5},{4,0},{5,1},{8,10},{9,11},{10,... | collective-permute-start | bytes 2359304 | tf_op jit(solution)/shard_map/ppermute | solution.py:342
  272.8 13.5 %collective-permute-start.33 = (bf16[128,2048]{1,0:T(8,128)(2,1)S(1)}, bf16[128,2048]{1,0:T(8,128)(2,1)S(1)}, u32[]{:S(2)}, u32[]{:S(2)}) collective-permute-start(bf16[128,2048]{1,0:T(8,128)(2,1)S(1)} %get-tuple-element.332), channel_id=1, source_target_pairs={{0,2},{1,3},{2,6},{3,7},{6,4},{7,5},{4,0},{5,1},{8,10},{9,11},{10,... | collective-permute-start | bytes 1572872 | tf_op jit(solution)/shard_map/ppermute | solution.py:342
  286.5 13.8 %collective-permute-start.34 = (bf16[128,2048]{1,0:T(8,128)(2,1)S(1)}, bf16[128,2048]{1,0:T(8,128)(2,1)S(1)}, u32[]{:S(2)}, u32[]{:S(2)}) collective-permute-start(bf16[128,2048]{1,0:T(8,128)(2,1)S(1)} %get-tuple-element.346), channel_id=1, source_target_pairs={{0,1},{1,0},{2,3},{3,2},{4,5},{5,4},{6,7},{7,6},{8,9},{9,8},{10,11... | collective-permute-start | bytes 1572872 | tf_op jit(solution)/shard_map/ppermute | solution.py:338
  287.8 15.3 %collective-permute-start.35 = (bf16[128,2048]{1,0:T(8,128)(2,1)S(1)}, bf16[128,2048]{1,0:T(8,128)(2,1)S(1)}, u32[]{:S(2)}, u32[]{:S(2)}) collective-permute-start(bf16[128,2048]{1,0:T(8,128)(2,1)S(1)} %get-tuple-element.347), channel_id=1, source_target_pairs={{0,2},{1,3},{2,6},{3,7},{6,4},{7,5},{4,0},{5,1},{8,10},{9,11},{10,... | collective-permute-start | bytes 1572872 | tf_op jit(solution)/shard_map/ppermute | solution.py:342
  307.6 22.7 %collective-permute-start.40 = (bf16[192,2048]{1,0:T(8,128)(2,1)S(1)}, bf16[192,2048]{1,0:T(8,128)(2,1)S(1)}, u32[]{:S(2)}, u32[]{:S(2)}) collective-permute-start(bf16[192,2048]{1,0:T(8,128)(2,1)S(1)} %get-tuple-element.358), channel_id=1, source_target_pairs={{0,8},{8,0},{16,24},{24,16},{1,9},{9,1},{17,25},{25,17},{2,10},{10... | collective-permute-start | bytes 2359304 | tf_op jit(solution)/shard_map/ppermute | solution.py:350
  307.7 23.9 %collective-permute-start.41 = (bf16[192,2048]{1,0:T(8,128)(2,1)S(1)}, bf16[192,2048]{1,0:T(8,128)(2,1)S(1)}, u32[]{:S(2)}, u32[]{:S(2)}) collective-permute-start(bf16[192,2048]{1,0:T(8,128)(2,1)S(1)} %get-tuple-element.359), channel_id=1, source_target_pairs={{0,8},{8,0},{16,24},{24,16},{1,9},{9,1},{17,25},{25,17},{2,10},{10... | collective-permute-start | bytes 2359304 | tf_op jit(solution)/shard_map/ppermute | solution.py:350
  319.8 24.1 %collective-permute-start.44 = (bf16[192,2048]{1,0:T(8,128)(2,1)S(1)}, bf16[192,2048]{1,0:T(8,128)(2,1)S(1)}, u32[]{:S(2)}, u32[]{:S(2)}) collective-permute-start(bf16[192,2048]{1,0:T(8,128)(2,1)S(1)} %get-tuple-element.370), channel_id=1, source_target_pairs={{0,8},{8,0},{16,24},{24,16},{1,9},{9,1},{17,25},{25,17},{2,10},{10... | collective-permute-start | bytes 2359304 | tf_op jit(solution)/shard_map/ppermute | solution.py:350
  325.6 18.2 %collective-permute-start.45 = (bf16[192,2048]{1,0:T(8,128)(2,1)S(1)}, bf16[192,2048]{1,0:T(8,128)(2,1)S(1)}, u32[]{:S(2)}, u32[]{:S(2)}) collective-permute-start(bf16[192,2048]{1,0:T(8,128)(2,1)S(1)} %get-tuple-element.371), channel_id=1, source_target_pairs={{0,8},{8,0},{16,24},{24,16},{1,9},{9,1},{17,25},{25,17},{2,10},{10... | collective-permute-start | bytes 2359304 | tf_op jit(solution)/shard_map/ppermute | solution.py:350
  338.5 28.8 %collective-permute-start.48 = (bf16[192,2048]{1,0:T(8,128)(2,1)}, bf16[192,2048]{1,0:T(8,128)(2,1)}, u32[]{:S(2)}, u32[]{:S(2)}) collective-permute-start(bf16[192,2048]{1,0:T(8,128)(2,1)} %get-tuple-element.395), channel_id=1, source_target_pairs={{0,8},{8,0},{16,24},{24,16},{1,9},{9,1},{17,25},{25,17},{2,10},{10... | collective-permute-start | bytes 2359304 | tf_op jit(solution)/shard_map/ppermute | solution.py:350
  343.8 23.9 %collective-permute-start.49 = (bf16[192,2048]{1,0:T(8,128)(2,1)}, bf16[192,2048]{1,0:T(8,128)(2,1)}, u32[]{:S(2)}, u32[]{:S(2)}) collective-permute-start(bf16[192,2048]{1,0:T(8,128)(2,1)} %get-tuple-element.396), channel_id=1, source_target_pairs={{0,8},{8,0},{16,24},{24,16},{1,9},{9,1},{17,25},{25,17},{2,10},{10... | collective-permute-start | bytes 2359304 | tf_op jit(solution)/shard_map/ppermute | solution.py:350
  350.4 14.1 %collective-permute-start.46 = (bf16[128,2048]{1,0:T(8,128)(2,1)}, bf16[128,2048]{1,0:T(8,128)(2,1)S(1)}, u32[]{:S(2)}, u32[]{:S(2)}) collective-permute-start(bf16[128,2048]{1,0:T(8,128)(2,1)} %copy-done.168), channel_id=1, source_target_pairs={{0,1},{1,0},{2,3},{3,2},{4,5},{5,4},{6,7},{7,6},{8,9},{9,8},{10,11... | collective-permute-start | bytes 1572872 | tf_op jit(solution)/shard_map/ppermute | solution.py:338
  351.3 14.9 %collective-permute-start.47 = (bf16[128,2048]{1,0:T(8,128)(2,1)}, bf16[128,2048]{1,0:T(8,128)(2,1)S(1)}, u32[]{:S(2)}, u32[]{:S(2)}) collective-permute-start(bf16[128,2048]{1,0:T(8,128)(2,1)} %copy-done.168), channel_id=1, source_target_pairs={{0,2},{1,3},{2,6},{3,7},{6,4},{7,5},{4,0},{5,1},{8,10},{9,11},{10,... | collective-permute-start | bytes 1572872 | tf_op jit(solution)/shard_map/ppermute | solution.py:342
  356.7 24.1 %collective-permute-start.50 = (bf16[192,2048]{1,0:T(8,128)(2,1)S(1)}, bf16[192,2048]{1,0:T(8,128)(2,1)S(1)}, u32[]{:S(2)}, u32[]{:S(2)}) collective-permute-start(bf16[192,2048]{1,0:T(8,128)(2,1)S(1)} %copy-done.115), channel_id=1, source_target_pairs={{0,16},{8,24},{16,0},{24,8},{1,17},{9,25},{17,1},{25,9},{2,18},{10... | collective-permute-start | bytes 2359304 | tf_op jit(solution)/shard_map/ppermute | solution.py:346
  364.5 45.6 %collective-permute-start.59 = (bf16[192,2048]{1,0:T(8,128)(2,1)S(1)}, bf16[192,2048]{1,0:T(8,128)(2,1)S(1)}, u32[]{:S(2)}, u32[]{:S(2)}) collective-permute-start(bf16[192,2048]{1,0:T(8,128)(2,1)S(1)} %copy-done.113), channel_id=1, source_target_pairs={{0,16},{8,24},{16,0},{24,8},{1,17},{9,25},{17,1},{25,9},{2,18},{10... | collective-permute-start | bytes 2359304 | tf_op jit(solution)/shard_map/ppermute | solution.py:346
  373.7 36.4 %collective-permute-start.60 = (bf16[192,2048]{1,0:T(8,128)(2,1)S(1)}, bf16[192,2048]{1,0:T(8,128)(2,1)S(1)}, u32[]{:S(2)}, u32[]{:S(2)}) collective-permute-start(bf16[192,2048]{1,0:T(8,128)(2,1)S(1)} %get-tuple-element.413), channel_id=1, source_target_pairs={{0,16},{8,24},{16,0},{24,8},{1,17},{9,25},{17,1},{25,9},{2,18},{10... | collective-permute-start | bytes 2359304 | tf_op jit(solution)/shard_map/ppermute | solution.py:346
  394.1 13.8 %collective-permute-start.57 = (bf16[128,2048]{1,0:T(8,128)(2,1)S(1)}, bf16[128,2048]{1,0:T(8,128)(2,1)S(1)}, u32[]{:S(2)}, u32[]{:S(2)}) collective-permute-start(bf16[128,2048]{1,0:T(8,128)(2,1)S(1)} %get-tuple-element.421), channel_id=1, source_target_pairs={{0,1},{1,0},{2,3},{3,2},{4,5},{5,4},{6,7},{7,6},{8,9},{9,8},{10,11... | collective-permute-start | bytes 1572872 | tf_op jit(solution)/shard_map/ppermute | solution.py:338
  410.1 20.4 %collective-permute-start.64 = (bf16[128,2048]{1,0:T(8,128)(2,1)}, bf16[128,2048]{1,0:T(8,128)(2,1)}, u32[]{:S(2)}, u32[]{:S(2)}) collective-permute-start(bf16[128,2048]{1,0:T(8,128)(2,1)} %get-tuple-element.436), channel_id=1, source_target_pairs={{0,1},{1,0},{2,3},{3,2},{4,5},{5,4},{6,7},{7,6},{8,9},{9,8},{10,11... | collective-permute-start | bytes 1572872 | tf_op jit(solution)/shard_map/ppermute | solution.py:338
  411.1 19.4 %collective-permute-start.63 = (bf16[128,2048]{1,0:T(8,128)(2,1)}, bf16[128,2048]{1,0:T(8,128)(2,1)}, u32[]{:S(2)}, u32[]{:S(2)}) collective-permute-start(bf16[128,2048]{1,0:T(8,128)(2,1)} %get-tuple-element.437), channel_id=1, source_target_pairs={{0,2},{1,3},{2,6},{3,7},{6,4},{7,5},{4,0},{5,1},{8,10},{9,11},{10,... | collective-permute-start | bytes 1572872 | tf_op jit(solution)/shard_map/ppermute | solution.py:342
  433.8 37.0 %collective-permute-start.65 = (bf16[384,2048]{1,0:T(8,128)(2,1)}, bf16[384,2048]{1,0:T(8,128)(2,1)}, u32[]{:S(2)}, u32[]{:S(2)}) collective-permute-start(bf16[384,2048]{1,0:T(8,128)(2,1)} %get-tuple-element.459), channel_id=1, source_target_pairs={{0,1},{1,0},{2,3},{3,2},{4,5},{5,4},{6,7},{7,6},{8,9},{9,8},{10,11... | collective-permute-start | bytes 4718600 | tf_op jit(solution)/shard_map/ppermute | solution.py:338
  434.6 37.8 %collective-permute-start.66 = (bf16[384,2048]{1,0:T(8,128)(2,1)}, bf16[384,2048]{1,0:T(8,128)(2,1)}, u32[]{:S(2)}, u32[]{:S(2)}) collective-permute-start(bf16[384,2048]{1,0:T(8,128)(2,1)} %get-tuple-element.460), channel_id=1, source_target_pairs={{0,2},{1,3},{2,6},{3,7},{6,4},{7,5},{4,0},{5,1},{8,10},{9,11},{10,... | collective-permute-start | bytes 4718600 | tf_op jit(solution)/shard_map/ppermute | solution.py:342
  442.9 20.3 %collective-permute-start.68 = (bf16[512,768]{1,0:T(8,128)(2,1)}, bf16[512,768]{1,0:T(8,128)(2,1)}, u32[]{:S(2)}, u32[]{:S(2)}) collective-permute-start(bf16[512,768]{1,0:T(8,128)(2,1)} %fusion.3), channel_id=1, source_target_pairs={{0,16},{8,24},{16,0},{24,8},{1,17},{9,25},{17,1},{25,9},{2,18},{10... | collective-permute-start | bytes 2359304 | tf_op jit(solution)/shard_map/ppermute | solution.py:346
  443.0 36.1 %collective-permute-start.73 = (bf16[512,256]{1,0:T(8,128)(2,1)}, bf16[512,256]{1,0:T(8,128)(2,1)}, u32[]{:S(2)}, u32[]{:S(2)}) collective-permute-start(bf16[512,256]{1,0:T(8,128)(2,1)} %copy-done.122), channel_id=1, source_target_pairs={{0,8},{8,0},{16,24},{24,16},{1,9},{9,1},{17,25},{25,17},{2,10},{10... | collective-permute-start | bytes 786440 | tf_op jit(solution)/shard_map/ppermute | solution.py:350
  450.5 28.5 %collective-permute-start.74 = (bf16[512,512]{1,0:T(8,128)(2,1)}, bf16[512,512]{1,0:T(8,128)(2,1)}, u32[]{:S(2)}, u32[]{:S(2)}) collective-permute-start(bf16[512,512]{1,0:T(8,128)(2,1)} %get-tuple-element.480), channel_id=1, source_target_pairs={{0,8},{8,0},{16,24},{24,16},{1,9},{9,1},{17,25},{25,17},{2,10},{10... | collective-permute-start | bytes 1572872 | tf_op jit(solution)/shard_map/ppermute | solution.py:350
  476.1 38.9 %collective-permute-start.69 = (bf16[384,2048]{1,0:T(8,128)(2,1)}, bf16[384,2048]{1,0:T(8,128)(2,1)}, u32[]{:S(2)}, u32[]{:S(2)}) collective-permute-start(bf16[384,2048]{1,0:T(8,128)(2,1)} %get-tuple-element.463), channel_id=1, source_target_pairs={{0,1},{1,0},{2,3},{3,2},{4,5},{5,4},{6,7},{7,6},{8,9},{9,8},{10,11... | collective-permute-start | bytes 4718600 | tf_op jit(solution)/shard_map/ppermute | solution.py:338
  477.3 39.9 %collective-permute-start.70 = (bf16[384,2048]{1,0:T(8,128)(2,1)}, bf16[384,2048]{1,0:T(8,128)(2,1)}, u32[]{:S(2)}, u32[]{:S(2)}) collective-permute-start(bf16[384,2048]{1,0:T(8,128)(2,1)} %mix.28), channel_id=1, source_target_pairs={{0,2},{1,3},{2,6},{3,7},{6,4},{7,5},{4,0},{5,1},{8,10},{9,11},{10,... | collective-permute-start | bytes 4718600 | tf_op jit(solution)/shard_map/ppermute | solution.py:342
  477.5 14.8 %collective-permute-start.75 = (bf16[128,2048]{1,0:T(8,128)(2,1)}, bf16[128,2048]{1,0:T(8,128)(2,1)}, u32[]{:S(2)}, u32[]{:S(2)}) collective-permute-start(bf16[128,2048]{1,0:T(8,128)(2,1)} %fusion.6), channel_id=1, source_target_pairs={{1,17},{3,19},{5,21},{7,23},{9,25},{11,27},{13,29},{15,31},{16,0},... | collective-permute-start | bytes 1572872 | tf_op jit(solution)/shard_map/ppermute | solution.py:1180
  482.2 54.7 %all-to-all-start.1 = ((bf16[8,80,768]{2,1,0:T(8,128)(2,1)}), bf16[8,80,768]{2,1,0:T(8,128)(2,1)}, u32[]{:S(2)}, u32[]{:S(2)}) async-start(bf16[8,80,768]{2,1,0:T(8,128)(2,1)} %fusion.5), calls=%async_computation.1 | async-start | bytes 1966080 | tf_op jit(solution)/shard_map/all_to_all | solution.py:1130
  494.0 34.5 %collective-permute-start.76 = (bf16[64,2048]{1,0:T(8,128)(2,1)S(1)}, bf16[64,2048]{1,0:T(8,128)(2,1)S(1)}, u32[]{:S(2)}, u32[]{:S(2)}) collective-permute-start(bf16[64,2048]{1,0:T(8,128)(2,1)S(1)} %dynamic-slice_convert_fusion.1), channel_id=1, source_target_pairs={{0,1},{2,3},{4,5},{6,7},{8,9},{10,11},{12,13},{14,15},{17,16},{19,... | collective-permute-start | bytes 786440 | tf_op jit(solution)/shard_map/ppermute | solution.py:1189
  520.6 28.6 %collective-permute-start.71 = (bf16[256,2048]{1,0:T(8,128)(2,1)}, bf16[256,2048]{1,0:T(8,128)(2,1)}, u32[]{:S(2)}, u32[]{:S(2)}) collective-permute-start(bf16[256,2048]{1,0:T(8,128)(2,1)} %get-tuple-element.475), channel_id=1, source_target_pairs={{0,1},{1,0},{2,3},{3,2},{4,5},{5,4},{6,7},{7,6},{8,9},{9,8},{10,11... | collective-permute-start | bytes 3145736 | tf_op jit(solution)/shard_map/ppermute | solution.py:338
  524.1 33.2 %collective-permute-start.72 = (bf16[256,2048]{1,0:T(8,128)(2,1)}, bf16[256,2048]{1,0:T(8,128)(2,1)}, u32[]{:S(2)}, u32[]{:S(2)}) collective-permute-start(bf16[256,2048]{1,0:T(8,128)(2,1)} %mix.29), channel_id=1, source_target_pairs={{0,2},{1,3},{2,6},{3,7},{6,4},{7,5},{4,0},{5,1},{8,10},{9,11},{10,... | collective-permute-start | bytes 3145736 | tf_op jit(solution)/shard_map/ppermute | solution.py:342
  (216 other events, 2424.0 us)
Sparse Core Ops, SparseCore 0:
  81.2 29.1 all-gather.3
  111.9 32.9 all-gather.5
  146.4 31.6 all-gather.7

commit v5 on v4

--- a/solution.py
+++ b/solution.py
@@ -1005,6 +1005,29 @@
         cost_estimate=LONG,
         name="feed",
     )(*arrays, wg, wu, wd)
+
+
+def branch_back_kernel(plan, *refs):
+    *arrays, wo_ref, rows_ref, att_ref = refs
+    first = 0
+    for (start, count), array in zip(plan, arrays):
+        rows_ref[first : first + count, :] = array[start : start + count, :]
+        first += count
+    att_ref[...] = rows_by_rows(rows_ref[...], wo_ref[...]).astype(jnp.bfloat16)
+
+
+def branch_back(pieces, wo):
+    count = sum(rows.count for rows in pieces)
+    return pl.pallas_call(
+        functools.partial(branch_back_kernel, tuple((rows.start, rows.count) for rows in pieces)),
+        out_shape=[
+            jax.ShapeDtypeStruct((count, wo.shape[1]), jnp.bfloat16),
+            jax.ShapeDtypeStruct((count, wo.shape[0]), jnp.bfloat16),
+        ],
+        compiler_params=pltpu.CompilerParams(vmem_limit_bytes=16 * 2**20),
+        cost_estimate=FREE,
+        name="branch_back",
+    )(*(rows.array for rows in pieces), wo)
 
 
 def add_kernel(*refs):
@@ -1332,8 +1355,10 @@
     place_of_key = jnp.where(live, position, -1)[None, :]
     own_live = live[:local_rows].astype(jnp.float32)[:, None]
 
-    def layout():
-        return first, last, place_of_key, own_live
+    d_out = cotangent.astype(jnp.float32) * own_live
+    d_out_low = d_out.astype(jnp.bfloat16)
+    layout = lax.optimization_barrier((first, last, place_of_key, own_live, d_out_low))
+    first, last, place_of_key, own_live, d_out_low = layout
 
     each = kv_gain.shape[0]
     inputs = Gather(jnp.concatenate([source, hidden], axis=0))
@@ -1348,7 +1373,7 @@
     own_units = [
         jnp.pad(own, ((0, padded - units), (0, 0))) for own in (w_gate, w_up, w_down)
     ]
-    s2 = move([inputs], *s1, *wa, *layout(), *own_units)
+    s2 = move([inputs], *s1, *wa, *layout, *own_units)
     wc = columns.along_core(*wy)
     s3 = move([inputs], *s2)
     wq, w_kv, gains = columns.whole()
@@ -1358,7 +1383,6 @@
     wg, wu, wd = (hidden_units(own, dp, *s2, *wy) for own in own_units)
 
     hidden_f = hidden.astype(jnp.float32)
-    d_out = cotangent.astype(jnp.float32) * own_live
     projected = []
 
     def project_piece(step, cost, *gate):
@@ -1369,7 +1393,7 @@
     project_piece(1, FREE)
     s4 = move([inputs], *s3)
     project_piece(2, LONG, *s3)
-    cots = Gather(d_out.astype(jnp.bfloat16))
+    cots = Gather(d_out_low)
     c1 = move([cots], *s4, projected[2][3])
     project_piece(3, LONG)
     src_low, hid_low, pairs, queries = zip(*projected)
@@ -1447,10 +1471,8 @@
 
     result = Scatter()
     e4 = move([outs, result.of(first_result)], *e3, *h3, gate_sums.from_y, column_grads.gain)
-    d_branches = [outs.piece(step) for step in range(4)]
-    d_attended = jnp.concatenate(
-        [rows_by_rows(rows, wo).astype(jnp.bfloat16) for rows in d_branches], axis=0
-    )
+    d_branches, d_attended = zip(*(branch_back(outs.pieces[step], wo) for step in range(4)))
+    d_attended = jnp.concatenate(d_attended, axis=0)
     o2 = move([result.of(result_terms(2, *e3))], *e4)
     d_queries, d_pairs = attend_back(
         queries, pairs, first, last, place_of_key, lse, attended_f, d_attended, head
@@ -1467,11 +1489,11 @@
     first_terms = terms(1)
     started = d_hid.own.array
     sent = []
-    i1 = move(first_terms, *o2, up_sums.from_y, down_sums.from_y, payload=sent)
-    sources, hiddens = after((tuple(src_low), tuple(hid_low)), *sent)
+    i1 = move(first_terms, *o2, up_sums.from_y, payload=sent)
+    second_terms = terms(2, started, result=(result, 3))
+    sources, hiddens = after((tuple(src_low), tuple(hid_low)), *sent, result.own.array)
     column_grads.along_core(sources, hiddens, d_queries, d_pairs)
-    second_terms = terms(2, started, result=(result, 3))
-    i2 = move(second_terms, *i1)
+    i2 = move(second_terms, *i1, down_sums.from_y)
     py = column_grads.along_y()
     next_terms = terms(3, *py, result=(result, 0))
     out_grads = OutGrads(

time: 578 us -> 567 us (0.981)
  waiting for transfers between devices: 253 us -> 246 us
    ppermute x27, waiting for transfers between devices: 128 us -> 111 us  [x_swap(): return lax.ppermute(value, 'fsdp', swap_pairs(8, 1))]
    unnamed x374 -> x342, local copies, waits for them, and re-layouts: 52.6 us -> 56 us
  transfers between devices with their start and end apart: 82 -> 82, of which waited for: 49 -> 50; matrix products, arithmetic and copies ran while one was open for 9% -> 7% of each run, Pallas kernels for 19% -> 20%
where the time goes in v5:
time: 567 us; the launch traced here: 558 us
  waiting for transfers between devices  246 us (43%)
  Pallas kernels  116 us (20%)
  starting transfers between devices  83.9 us (15%)
  local copies, waits for them, and re-layouts  66.4 us (12%)
  other arithmetic  25.2 us (4%)
  between operations  16.3 us (3%)
    ppermute x27, waiting for transfers between devices, x_swap(): return lax.ppermute(value, 'fsdp', swap_pairs(8, 1))  111 us
    ppermute x26, waiting for transfers between devices, ring_step(): return lax.ppermute(value, 'fsdp', ring_pairs())  72.2 us
    unnamed x342, local copies, waits for them, and re-layouts  56 us
    ppermute x6, waiting for transfers between devices, y_swap(): return lax.ppermute(value, 'dp', swap_pairs(4, 2))  32.7 us
    ppermute x26, starting transfers between devices, ring_step(): return lax.ppermute(value, 'fsdp', ring_pairs())  32.4 us
    ppermute x27, starting transfers between devices, x_swap(): return lax.ppermute(value, 'fsdp', swap_pairs(8, 1))  30.2 us
    pallas_call x4, Pallas kernels, feed(): pl.pallas_call(functools.partial(feed_kernel, *plans), out_shape=[low, lo...  20 us
    pallas_call x6, Pallas kernels, call(): pl.pallas_call(functools.partial(kernel, len(self.units)), grid=(2,), in_...  16.8 us
  transfers between devices with their start and end apart: 82, of which 50 were waited for; matrix products, arithmetic and copies ran while one was open for 7% of the time, Pallas kernels for 20%

profile of v5, /device:TPU:0, one launch (start us, length us, event | category | flops | bytes accessed | tf_op | source)
XLA Modules:
  0.0 557.7 jit_solution(5104287743090828154)
XLA Ops:
  9.5 3.1 collective-permute-start.1
  15.3 3.9 all-to-all-start
  28.7 9.0 %collective-permute-done.1.held_ref = bf16[256,2048]{1,0:T(8,128)(2,1)} collective-permute-done((bf16[256,2048]{1,0:T(8,128)(2,1)S(1)}, bf16[256,2048]{1,0:T(8,128)(2,1)}, u32[]{:S(2)}, u32[]{:S(2)}) %collective-permute-start.1) | collective-permute-done | bytes 1048608 | tf_op jit(solution)/shard_map/ppermute | solution.py:342
  37.7 3.3 collective-permute-done.refs_0_
  41.1 14.0 %all-to-all-done = bf16[8,208,256]{2,1,0:T(8,128)(2,1)S(1)} async-done(((bf16[8,208,256]{2,1,0:T(8,128)(2,1)}), bf16[8,208,256]{2,1,0:T(8,128)(2,1)S(1)}, u32[]{:S(2)}, u32[]{:S(2)}) %all-to-all-start) | async-done | bytes 852000 | tf_op jit(solution)/shard_map/all_to_all | solution.py:703
  59.9 19.0 %collective-permute-done.2.refs_2_ = bf16[1664,256]{1,0:T(8,128)(2,1)S(1)} collective-permute-done((bf16[1664,256]{1,0:T(8,128)(2,1)S(1)}, bf16[1664,256]{1,0:T(8,128)(2,1)S(1)}, u32[]{:S(2)}, u32[]{:S(2)}) %collective-permute-start.2) | collective-permute-done | bytes 852000 | tf_op jit(solution)/shard_map/ppermute | solution.py:346
  107.3 4.0 collective-permute-done.7.refs_0_.refs_1_
  111.7 3.7 collective-permute-start.14
  119.7 3.4 project.6
  124.2 5.9 %collective-permute-done.9.refs_0_ = bf16[128,2048]{1,0:T(8,128)(2,1)S(1)} collective-permute-done((bf16[128,2048]{1,0:T(8,128)(2,1)S(1)}, bf16[128,2048]{1,0:T(8,128)(2,1)S(1)}, u32[]{:S(2)}, u32[]{:S(2)}) %collective-permute-start.9) | collective-permute-done | bytes 524320 | tf_op jit(solution)/shard_map/ppermute | solution.py:338
  138.6 4.5 collective-permute-done.11.refs_3_
  147.1 7.5 %attend.1 = (f32[1024,256]{1,0:T(8,128)S(1)}, bf16[1024,256]{1,0:T(8,128)(2,1)S(1)}, f32[2,1024,1]{2,1,0:T(8,128)S(1)}) custom-call(bf16[1024,256]{1,0:T(8,128)(2,1)S(1)} %constant_dynamic-update-slice_fusion.2.q_ref, bf16[1024,512]{1,0:T(8,128)(2,1)S(1)} %constant_dynamic-update-slice_fusion.6.k_ref.v_ref, ...), custom_call_target="tpu_custom_call" | custom-call | flops 20000000000 | tf_op jit(solution)/shard_map/attend/pallas_call | solution.py:594
  155.9 4.9 collective-permute-done.16.refs_1_.refs_2_
  164.9 16.1 %collective-permute-done.18.refs_1_.refs_3_ = bf16[192,2048]{1,0:T(8,128)(2,1)S(1)} collective-permute-done((bf16[192,2048]{1,0:T(8,128)(2,1)S(1)}, bf16[192,2048]{1,0:T(8,128)(2,1)S(1)}, u32[]{:S(2)}, u32[]{:S(2)}) %collective-permute-start.18) | collective-permute-done | bytes 786464 | tf_op jit(solution)/shard_map/ppermute | solution.py:342
  186.0 15.0 %collective-permute-done.20.refs_2_.refs_4_ = bf16[192,2048]{1,0:T(8,128)(2,1)S(1)} collective-permute-done((bf16[192,2048]{1,0:T(8,128)(2,1)S(1)}, bf16[192,2048]{1,0:T(8,128)(2,1)S(1)}, u32[]{:S(2)}, u32[]{:S(2)}) %collective-permute-start.20) | collective-permute-done | bytes 786464 | tf_op jit(solution)/shard_map/ppermute | solution.py:338
  205.3 8.1 %collective-permute-done.22.refs_2_ = bf16[128,2048]{1,0:T(8,128)(2,1)S(1)} collective-permute-done((bf16[128,2048]{1,0:T(8,128)(2,1)S(1)}, bf16[128,2048]{1,0:T(8,128)(2,1)S(1)}, u32[]{:S(2)}, u32[]{:S(2)}) %collective-permute-start.22) | collective-permute-done | bytes 524320 | tf_op jit(solution)/shard_map/ppermute | solution.py:338
  217.7 8.8 %collective-permute-done.24 = bf16[128,2048]{1,0:T(8,128)(2,1)} collective-permute-done((bf16[128,2048]{1,0:T(8,128)(2,1)}, bf16[128,2048]{1,0:T(8,128)(2,1)}, u32[]{:S(2)}, u32[]{:S(2)}) %collective-permute-start.24) | collective-permute-done | bytes 524320 | tf_op jit(solution)/shard_map/ppermute | solution.py:338
  244.8 3.4 collective-permute-start.29
  250.3 5.7 %feed.4 = (bf16[256,768]{1,0:T(8,128)(2,1)S(1)}, bf16[256,768]{1,0:T(8,128)(2,1)S(1)}, bf16[256,768]{1,0:T(8,128)(2,1)S(1)}, bf16[128,2048]{1,0:T(8,128)(2,1)S(1...) custom-call(bf16[128,2048]{1,0:T(8,128)(2,1)} %multiply_convert_fusion.refs_0_, ...), custom_call_target="tpu_custom_call" | custom-call | flops 20000000000 | tf_op jit(solution)/shard_map/feed/pallas_call | solution.py:1000
  259.9 5.5 feed.5
  267.0 3.1 collective-permute-done.31.refs_0_
  273.2 4.4 feed.6
  277.6 5.1 collective-permute-done.32.refs_1_.refs_3_
  286.5 4.4 feed.7
  291.0 7.6 %collective-permute-done.34.refs_1_ = bf16[128,2048]{1,0:T(8,128)(2,1)S(1)} collective-permute-done((bf16[128,2048]{1,0:T(8,128)(2,1)S(1)}, bf16[128,2048]{1,0:T(8,128)(2,1)S(1)}, u32[]{:S(2)}, u32[]{:S(2)}) %collective-permute-start.34) | collective-permute-done | bytes 524320 | tf_op jit(solution)/shard_map/ppermute | solution.py:338
  306.2 5.9 %collective-permute-done.36.refs_1_ = bf16[128,2048]{1,0:T(8,128)(2,1)S(1)} collective-permute-done((bf16[128,2048]{1,0:T(8,128)(2,1)S(1)}, bf16[128,2048]{1,0:T(8,128)(2,1)S(1)}, u32[]{:S(2)}, u32[]{:S(2)}) %collective-permute-start.36) | collective-permute-done | bytes 524320 | tf_op jit(solution)/shard_map/ppermute | solution.py:338
  318.1 5.8 %collective-permute-done.38 = bf16[128,2048]{1,0:T(8,128)(2,1)S(1)} collective-permute-done((bf16[128,2048]{1,0:T(8,128)(2,1)S(1)}, bf16[128,2048]{1,0:T(8,128)(2,1)S(1)}, u32[]{:S(2)}, u32[]{:S(2)}) %collective-permute-start.38) | collective-permute-done | bytes 524320 | tf_op jit(solution)/shard_map/ppermute | solution.py:338
  333.6 3.2 hidden_grads.10
  336.8 5.3 collective-permute-done.43.refs_0_
  351.8 3.6 collective-permute-done.54
  355.4 4.2 collective-permute-done.46.refs_1_
  370.3 3.6 hidden_grads.11
  393.4 10.0 %attend_back.1 = (bf16[1024,256]{1,0:T(8,128)(2,1)S(1)}, bf16[1024,512]{1,0:T(8,128)(2,1)S(1)}) custom-call(bf16[1024,256]{1,0:T(8,128)(2,1)S(1)} %copy-done.87, bf16[1024,512]{1,0:T(8,128)(2,1)S(1)} %copy-done.85, bf16[1024,512]{1,0:T(8,128)(2,1)S(1)} %copy-done.85, s32[1024,1]{1,0:T(8,128)S(1)} %copy-done.67, s32[1024,1]{1,0:T(8,128)S(1)} %copy-done.63, ...), custom_call_target="tpu_custom_call" | custom-call | flops 20000000000 | tf_op jit(solution)/shard_map/attend_back/pallas_call | solution.py:613
  405.4 3.3 collective-permute-start.62
  411.8 6.5 %column_grads.1 = (bf16[512,256]{1,0:T(8,128)(2,1)S(1)}, bf16[512,512]{1,0:T(8,128)(2,1)}, bf16[512,256]{1,0:T(8,128)(2,1)}, bf16[512,512]{1,0:T(8,128)(2,1)}, f32[2,512,768]{2,1,0:T(8,128)S(1)}) custom-call(s32[1]{0:T(128)} %bitcast.dp_ref, bf16[256,2048]{1,0:T(8,128)(2,1)S(1)} %copy-done.91, bf16[256,2048]{1,0:T(8,128)(2,1)S(1)} %copy-done.95, ...), custom_call_target="tpu_custom_call" | custom-call | flops 20000000000 | tf_op jit(solution)/shard_map/column_grads/pallas_call | solution.py:1107
  438.5 3.0 back_terms.6
  443.9 10.1 %collective-permute-done.68 = bf16[512,768]{1,0:T(8,128)(2,1)} collective-permute-done((bf16[512,768]{1,0:T(8,128)(2,1)}, bf16[512,768]{1,0:T(8,128)(2,1)}, u32[]{:S(2)}, u32[]{:S(2)}) %collective-permute-start.68) | collective-permute-done | bytes 786464 | tf_op jit(solution)/shard_map/ppermute | solution.py:346
  454.1 6.0 %collective-permute-done.65.refs_1_ = bf16[384,2048]{1,0:T(8,128)(2,1)} collective-permute-done((bf16[384,2048]{1,0:T(8,128)(2,1)}, bf16[384,2048]{1,0:T(8,128)(2,1)}, u32[]{:S(2)}, u32[]{:S(2)}) %collective-permute-start.65) | collective-permute-done | bytes 1572896 | tf_op jit(solution)/shard_map/ppermute | solution.py:338
  461.7 3.6 mix.28
  470.9 5.4 all-to-all-start.1
  476.4 4.5 collective-permute-done.75
  487.1 17.8 %collective-permute-done.69.x_ref.refs_1_ = bf16[384,2048]{1,0:T(8,128)(2,1)} collective-permute-done((bf16[384,2048]{1,0:T(8,128)(2,1)}, bf16[384,2048]{1,0:T(8,128)(2,1)}, u32[]{:S(2)}, u32[]{:S(2)}) %collective-permute-start.69) | collective-permute-done | bytes 1572896 | tf_op jit(solution)/shard_map/ppermute | solution.py:338
  506.7 3.4 mix.29
  510.0 3.5 collective-permute-start.71
  518.1 7.9 %all-to-all-done.1.got_ref = bf16[8,80,768]{2,1,0:T(8,128)(2,1)} async-done(((bf16[8,80,768]{2,1,0:T(8,128)(2,1)}), bf16[8,80,768]{2,1,0:T(8,128)(2,1)}, u32[]{:S(2)}, u32[]{:S(2)}) %all-to-all-start.1) | async-done | bytes 983072 | tf_op jit(solution)/shard_map/all_to_all | solution.py:1153
  534.1 3.5 result.1
  538.6 7.4 %collective-permute-done.72.refs_2_.refs_5_ = bf16[256,2048]{1,0:T(8,128)(2,1)} collective-permute-done((bf16[256,2048]{1,0:T(8,128)(2,1)}, bf16[256,2048]{1,0:T(8,128)(2,1)}, u32[]{:S(2)}, u32[]{:S(2)}) %collective-permute-start.72) | collective-permute-done | bytes 1048608 | tf_op jit(solution)/shard_map/ppermute | solution.py:342
  546.0 4.8 input_grads.1
  (585 shorter events, 235.7 us)
Async XLA Ops:
  9.5 28.2 %collective-permute-start.1 = (bf16[256,2048]{1,0:T(8,128)(2,1)S(1)}, bf16[256,2048]{1,0:T(8,128)(2,1)}, u32[]{:S(2)}, u32[]{:S(2)}) collective-permute-start(bf16[256,2048]{1,0:T(8,128)(2,1)S(1)} %constant_dynamic-update-slice_fusion.held_ref), channel_id=1, source_target_pairs={{0,2},{1,3},{2,6},{3,7},{6,4},{7,5},{4,0},{5,1},{8,10},{9,11},{10,... | collective-permute-start | bytes 3145736 | tf_op jit(solution)/shard_map/ppermute | solution.py:342
  12.6 28.5 %collective-permute-start = (bf16[256,2048]{1,0:T(8,128)(2,1)S(1)}, bf16[256,2048]{1,0:T(8,128)(2,1)}, u32[]{:S(2)}, u32[]{:S(2)}) collective-permute-start(bf16[256,2048]{1,0:T(8,128)(2,1)S(1)} %constant_dynamic-update-slice_fusion.held_ref), channel_id=1, source_target_pairs={{0,1},{1,0},{2,3},{3,2},{4,5},{5,4},{6,7},{7,6},{8,9},{9,8},{10,11... | collective-permute-start | bytes 3145736 | tf_op jit(solution)/shard_map/ppermute | solution.py:338
  15.3 39.8 %all-to-all-start = ((bf16[8,208,256]{2,1,0:T(8,128)(2,1)}), bf16[8,208,256]{2,1,0:T(8,128)(2,1)S(1)}, u32[]{:S(2)}, u32[]{:S(2)}) async-start(bf16[8,208,256]{2,1,0:T(8,128)(2,1)} %bitcast.83), calls=%async_computation | async-start | bytes 1703936 | tf_op jit(solution)/shard_map/all_to_all | solution.py:703
  19.2 214.8 %all-gather.4.cloned.1.call-start = ((), (), s32[]{:S(2)}) async-start(), calls=%async_computation.2 | async-start | bytes 3932160 | tf_op jit(solution)/shard_map/all_gather | solution.py:1216
  55.1 24.6 %collective-permute-start.5 = (bf16[256,2048]{1,0:T(8,128)(2,1)}, bf16[256,2048]{1,0:T(8,128)(2,1)S(1)}, u32[]{:S(2)}, u32[]{:S(2)}) collective-permute-start(bf16[256,2048]{1,0:T(8,128)(2,1)} %collective-permute-done.1.held_ref), channel_id=1, source_target_pairs={{0,1},{1,0},{2,3},{3,2},{4,5},{5,4},{6,7},{7,6},{8,9},{9,8},{10,11... | collective-permute-start | bytes 3145736 | tf_op jit(solution)/shard_map/ppermute | solution.py:338
  56.6 24.7 %collective-permute-start.6 = (bf16[256,2048]{1,0:T(8,128)(2,1)}, bf16[256,2048]{1,0:T(8,128)(2,1)}, u32[]{:S(2)}, u32[]{:S(2)}) collective-permute-start(bf16[256,2048]{1,0:T(8,128)(2,1)} %collective-permute-done.1.held_ref), channel_id=1, source_target_pairs={{0,2},{1,3},{2,6},{3,7},{6,4},{7,5},{4,0},{5,1},{8,10},{9,11},{10,... | collective-permute-start | bytes 3145736 | tf_op jit(solution)/shard_map/ppermute | solution.py:342
  57.5 21.4 %collective-permute-start.2 = (bf16[1664,256]{1,0:T(8,128)(2,1)S(1)}, bf16[1664,256]{1,0:T(8,128)(2,1)S(1)}, u32[]{:S(2)}, u32[]{:S(2)}) collective-permute-start(bf16[1664,256]{1,0:T(8,128)(2,1)S(1)} %bitcast.81), channel_id=1, source_target_pairs={{0,16},{8,24},{16,0},{24,8},{1,17},{9,25},{17,1},{25,9},{2,18},{10... | collective-permute-start | bytes 2555912 | tf_op jit(solution)/shard_map/ppermute | solution.py:346
  81.3 156.6 %all-gather.6.cloned.1.call-start = ((), (), s32[]{:S(2)}) async-start(), calls=%async_computation.3 | async-start | bytes 3932160 | tf_op jit(solution)/shard_map/all_gather | solution.py:1216
  82.0 159.6 %all-gather.8.cloned.1.call-start = ((), (), s32[]{:S(2)}) async-start(), calls=%async_computation.4 | async-start | bytes 3932160 | tf_op jit(solution)/shard_map/all_gather | solution.py:1216
  84.3 27.0 %collective-permute-start.7 = (bf16[256,2048]{1,0:T(8,128)(2,1)}, bf16[256,2048]{1,0:T(8,128)(2,1)}, u32[]{:S(2)}, u32[]{:S(2)}) collective-permute-start(bf16[256,2048]{1,0:T(8,128)(2,1)} %collective-permute-done.6.held_ref), channel_id=1, source_target_pairs={{0,1},{1,0},{2,3},{3,2},{4,5},{5,4},{6,7},{7,6},{8,9},{9,8},{10,11... | collective-permute-start | bytes 3145736 | tf_op jit(solution)/shard_map/ppermute | solution.py:338
  85.2 26.5 %collective-permute-start.8 = (bf16[256,2048]{1,0:T(8,128)(2,1)}, bf16[256,2048]{1,0:T(8,128)(2,1)}, u32[]{:S(2)}, u32[]{:S(2)}) collective-permute-start(bf16[256,2048]{1,0:T(8,128)(2,1)} %collective-permute-done.6.held_ref), channel_id=1, source_target_pairs={{0,2},{1,3},{2,6},{3,7},{6,4},{7,5},{4,0},{5,1},{8,10},{9,11},{10,... | collective-permute-start | bytes 3145736 | tf_op jit(solution)/shard_map/ppermute | solution.py:342
  111.7 26.9 %collective-permute-start.14 = (bf16[128,2048]{1,0:T(8,128)(2,1)S(1)}, bf16[128,2048]{1,0:T(8,128)(2,1)S(1)}, u32[]{:S(2)}, u32[]{:S(2)}) collective-permute-start(bf16[128,2048]{1,0:T(8,128)(2,1)S(1)} %copy-done.155), channel_id=1, source_target_pairs={{0,16},{2,18},{4,20},{6,22},{8,24},{10,26},{12,28},{14,30},{17,1},... | collective-permute-start | bytes 1572872 | tf_op jit(solution)/shard_map/ppermute | solution.py:1183
  117.2 13.9 %collective-permute-start.10 = (bf16[128,2048]{1,0:T(8,128)(2,1)S(1)}, bf16[128,2048]{1,0:T(8,128)(2,1)S(1)}, u32[]{:S(2)}, u32[]{:S(2)}) collective-permute-start(bf16[128,2048]{1,0:T(8,128)(2,1)S(1)} %get-tuple-element.292), channel_id=1, source_target_pairs={{0,2},{1,3},{2,6},{3,7},{6,4},{7,5},{4,0},{5,1},{8,10},{9,11},{10,... | collective-permute-start | bytes 1572872 | tf_op jit(solution)/shard_map/ppermute | solution.py:342
  145.4 15.4 %collective-permute-start.16 = (bf16[128,2048]{1,0:T(8,128)(2,1)S(1)}, bf16[128,2048]{1,0:T(8,128)(2,1)S(1)}, u32[]{:S(2)}, u32[]{:S(2)}) collective-permute-start(bf16[128,2048]{1,0:T(8,128)(2,1)S(1)} %collective-permute-done.12.refs_2_), channel_id=1, source_target_pairs={{0,2},{1,3},{2,6},{3,7},{6,4},{7,5},{4,0},{5,1},{8,10},{9,11},{10,... | collective-permute-start | bytes 1572872 | tf_op jit(solution)/shard_map/ppermute | solution.py:342
  146.4 14.5 %collective-permute-start.17 = (bf16[128,2048]{1,0:T(8,128)(2,1)S(1)}, bf16[128,2048]{1,0:T(8,128)(2,1)S(1)}, u32[]{:S(2)}, u32[]{:S(2)}) collective-permute-start(bf16[128,2048]{1,0:T(8,128)(2,1)S(1)} %collective-permute-done.12.refs_2_), channel_id=1, source_target_pairs={{0,1},{1,0},{2,3},{3,2},{4,5},{5,4},{6,7},{7,6},{8,9},{9,8},{10,11... | collective-permute-start | bytes 1572872 | tf_op jit(solution)/shard_map/ppermute | solution.py:338
  160.9 20.0 %collective-permute-start.18 = (bf16[192,2048]{1,0:T(8,128)(2,1)S(1)}, bf16[192,2048]{1,0:T(8,128)(2,1)S(1)}, u32[]{:S(2)}, u32[]{:S(2)}) collective-permute-start(bf16[192,2048]{1,0:T(8,128)(2,1)S(1)} %get-tuple-element.313), channel_id=1, source_target_pairs={{0,2},{1,3},{2,6},{3,7},{6,4},{7,5},{4,0},{5,1},{8,10},{9,11},{10,... | collective-permute-start | bytes 2359304 | tf_op jit(solution)/shard_map/ppermute | solution.py:342
  163.8 18.6 %collective-permute-start.19 = (bf16[192,2048]{1,0:T(8,128)(2,1)S(1)}, bf16[192,2048]{1,0:T(8,128)(2,1)S(1)}, u32[]{:S(2)}, u32[]{:S(2)}) collective-permute-start(bf16[192,2048]{1,0:T(8,128)(2,1)S(1)} %get-tuple-element.314), channel_id=1, source_target_pairs={{0,1},{1,0},{2,3},{3,2},{4,5},{5,4},{6,7},{7,6},{8,9},{9,8},{10,11... | collective-permute-start | bytes 2359304 | tf_op jit(solution)/shard_map/ppermute | solution.py:338
  183.3 17.7 %collective-permute-start.20 = (bf16[192,2048]{1,0:T(8,128)(2,1)S(1)}, bf16[192,2048]{1,0:T(8,128)(2,1)S(1)}, u32[]{:S(2)}, u32[]{:S(2)}) collective-permute-start(bf16[192,2048]{1,0:T(8,128)(2,1)S(1)} %get-tuple-element.317), channel_id=1, source_target_pairs={{0,1},{1,0},{2,3},{3,2},{4,5},{5,4},{6,7},{7,6},{8,9},{9,8},{10,11... | collective-permute-start | bytes 2359304 | tf_op jit(solution)/shard_map/ppermute | solution.py:338
  183.9 18.3 %collective-permute-start.21 = (bf16[192,2048]{1,0:T(8,128)(2,1)S(1)}, bf16[192,2048]{1,0:T(8,128)(2,1)S(1)}, u32[]{:S(2)}, u32[]{:S(2)}) collective-permute-start(bf16[192,2048]{1,0:T(8,128)(2,1)S(1)} %get-tuple-element.318), channel_id=1, source_target_pairs={{0,2},{1,3},{2,6},{3,7},{6,4},{7,5},{4,0},{5,1},{8,10},{9,11},{10,... | collective-permute-start | bytes 2359304 | tf_op jit(solution)/shard_map/ppermute | solution.py:342
  271.1 13.5 %collective-permute-start.33 = (bf16[128,2048]{1,0:T(8,128)(2,1)S(1)}, bf16[128,2048]{1,0:T(8,128)(2,1)S(1)}, u32[]{:S(2)}, u32[]{:S(2)}) collective-permute-start(bf16[128,2048]{1,0:T(8,128)(2,1)S(1)} %get-tuple-element.350), channel_id=1, source_target_pairs={{0,2},{1,3},{2,6},{3,7},{6,4},{7,5},{4,0},{5,1},{8,10},{9,11},{10,... | collective-permute-start | bytes 1572872 | tf_op jit(solution)/shard_map/ppermute | solution.py:342
  284.7 13.8 %collective-permute-start.34 = (bf16[128,2048]{1,0:T(8,128)(2,1)S(1)}, bf16[128,2048]{1,0:T(8,128)(2,1)S(1)}, u32[]{:S(2)}, u32[]{:S(2)}) collective-permute-start(bf16[128,2048]{1,0:T(8,128)(2,1)S(1)} %get-tuple-element.364), channel_id=1, source_target_pairs={{0,1},{1,0},{2,3},{3,2},{4,5},{5,4},{6,7},{7,6},{8,9},{9,8},{10,11... | collective-permute-start | bytes 1572872 | tf_op jit(solution)/shard_map/ppermute | solution.py:338
  286.0 15.3 %collective-permute-start.35 = (bf16[128,2048]{1,0:T(8,128)(2,1)S(1)}, bf16[128,2048]{1,0:T(8,128)(2,1)S(1)}, u32[]{:S(2)}, u32[]{:S(2)}) collective-permute-start(bf16[128,2048]{1,0:T(8,128)(2,1)S(1)} %get-tuple-element.365), channel_id=1, source_target_pairs={{0,2},{1,3},{2,6},{3,7},{6,4},{7,5},{4,0},{5,1},{8,10},{9,11},{10,... | collective-permute-start | bytes 1572872 | tf_op jit(solution)/shard_map/ppermute | solution.py:342
  305.6 23.0 %collective-permute-start.40 = (bf16[192,2048]{1,0:T(8,128)(2,1)S(1)}, bf16[192,2048]{1,0:T(8,128)(2,1)S(1)}, u32[]{:S(2)}, u32[]{:S(2)}) collective-permute-start(bf16[192,2048]{1,0:T(8,128)(2,1)S(1)} %get-tuple-element.376), channel_id=1, source_target_pairs={{0,8},{8,0},{16,24},{24,16},{1,9},{9,1},{17,25},{25,17},{2,10},{10... | collective-permute-start | bytes 2359304 | tf_op jit(solution)/shard_map/ppermute | solution.py:350
  305.7 24.1 %collective-permute-start.41 = (bf16[192,2048]{1,0:T(8,128)(2,1)S(1)}, bf16[192,2048]{1,0:T(8,128)(2,1)S(1)}, u32[]{:S(2)}, u32[]{:S(2)}) collective-permute-start(bf16[192,2048]{1,0:T(8,128)(2,1)S(1)} %get-tuple-element.377), channel_id=1, source_target_pairs={{0,8},{8,0},{16,24},{24,16},{1,9},{9,1},{17,25},{25,17},{2,10},{10... | collective-permute-start | bytes 2359304 | tf_op jit(solution)/shard_map/ppermute | solution.py:350
  318.1 24.1 %collective-permute-start.44 = (bf16[192,2048]{1,0:T(8,128)(2,1)S(1)}, bf16[192,2048]{1,0:T(8,128)(2,1)S(1)}, u32[]{:S(2)}, u32[]{:S(2)}) collective-permute-start(bf16[192,2048]{1,0:T(8,128)(2,1)S(1)} %get-tuple-element.388), channel_id=1, source_target_pairs={{0,8},{8,0},{16,24},{24,16},{1,9},{9,1},{17,25},{25,17},{2,10},{10... | collective-permute-start | bytes 2359304 | tf_op jit(solution)/shard_map/ppermute | solution.py:350
  323.9 18.3 %collective-permute-start.45 = (bf16[192,2048]{1,0:T(8,128)(2,1)S(1)}, bf16[192,2048]{1,0:T(8,128)(2,1)S(1)}, u32[]{:S(2)}, u32[]{:S(2)}) collective-permute-start(bf16[192,2048]{1,0:T(8,128)(2,1)S(1)} %get-tuple-element.389), channel_id=1, source_target_pairs={{0,8},{8,0},{16,24},{24,16},{1,9},{9,1},{17,25},{25,17},{2,10},{10... | collective-permute-start | bytes 2359304 | tf_op jit(solution)/shard_map/ppermute | solution.py:350
  336.8 25.5 %collective-permute-start.48 = (bf16[192,2048]{1,0:T(8,128)(2,1)}, bf16[192,2048]{1,0:T(8,128)(2,1)}, u32[]{:S(2)}, u32[]{:S(2)}) collective-permute-start(bf16[192,2048]{1,0:T(8,128)(2,1)} %get-tuple-element.413), channel_id=1, source_target_pairs={{0,8},{8,0},{16,24},{24,16},{1,9},{9,1},{17,25},{25,17},{2,10},{10... | collective-permute-start | bytes 2359304 | tf_op jit(solution)/shard_map/ppermute | solution.py:350
  342.1 20.2 %collective-permute-start.49 = (bf16[192,2048]{1,0:T(8,128)(2,1)}, bf16[192,2048]{1,0:T(8,128)(2,1)}, u32[]{:S(2)}, u32[]{:S(2)}) collective-permute-start(bf16[192,2048]{1,0:T(8,128)(2,1)} %get-tuple-element.414), channel_id=1, source_target_pairs={{0,8},{8,0},{16,24},{24,16},{1,9},{9,1},{17,25},{25,17},{2,10},{10... | collective-permute-start | bytes 2359304 | tf_op jit(solution)/shard_map/ppermute | solution.py:350
  344.8 14.7 %collective-permute-start.46 = (bf16[128,2048]{1,0:T(8,128)(2,1)}, bf16[128,2048]{1,0:T(8,128)(2,1)}, u32[]{:S(2)}, u32[]{:S(2)}) collective-permute-start(bf16[128,2048]{1,0:T(8,128)(2,1)} %collective-permute-done.43.refs_0_), channel_id=1, source_target_pairs={{0,1},{1,0},{2,3},{3,2},{4,5},{5,4},{6,7},{7,6},{8,9},{9,8},{10,11... | collective-permute-start | bytes 1572872 | tf_op jit(solution)/shard_map/ppermute | solution.py:338
  345.8 15.5 %collective-permute-start.47 = (bf16[128,2048]{1,0:T(8,128)(2,1)}, bf16[128,2048]{1,0:T(8,128)(2,1)}, u32[]{:S(2)}, u32[]{:S(2)}) collective-permute-start(bf16[128,2048]{1,0:T(8,128)(2,1)} %collective-permute-done.43.refs_0_), channel_id=1, source_target_pairs={{0,2},{1,3},{2,6},{3,7},{6,4},{7,5},{4,0},{5,1},{8,10},{9,11},{10,... | collective-permute-start | bytes 1572872 | tf_op jit(solution)/shard_map/ppermute | solution.py:342
  355.3 21.2 %collective-permute-start.50 = (bf16[192,2048]{1,0:T(8,128)(2,1)}, bf16[192,2048]{1,0:T(8,128)(2,1)S(1)}, u32[]{:S(2)}, u32[]{:S(2)}) collective-permute-start(bf16[192,2048]{1,0:T(8,128)(2,1)} %copy-done.106), channel_id=1, source_target_pairs={{0,16},{8,24},{16,0},{24,8},{1,17},{9,25},{17,1},{25,9},{2,18},{10... | collective-permute-start | bytes 2359304 | tf_op jit(solution)/shard_map/ppermute | solution.py:346
  362.4 14.1 %collective-permute-start.52 = (bf16[128,2048]{1,0:T(8,128)(2,1)}, bf16[128,2048]{1,0:T(8,128)(2,1)S(1)}, u32[]{:S(2)}, u32[]{:S(2)}) collective-permute-start(bf16[128,2048]{1,0:T(8,128)(2,1)} %collective-permute-done.47.refs_0_), channel_id=1, source_target_pairs={{0,2},{1,3},{2,6},{3,7},{6,4},{7,5},{4,0},{5,1},{8,10},{9,11},{10,... | collective-permute-start | bytes 1572872 | tf_op jit(solution)/shard_map/ppermute | solution.py:342
  377.7 26.9 %collective-permute-start.59 = (bf16[192,2048]{1,0:T(8,128)(2,1)S(1)}, bf16[192,2048]{1,0:T(8,128)(2,1)S(1)}, u32[]{:S(2)}, u32[]{:S(2)}) collective-permute-start(bf16[192,2048]{1,0:T(8,128)(2,1)S(1)} %copy-done.105), channel_id=1, source_target_pairs={{0,16},{8,24},{16,0},{24,8},{1,17},{9,25},{17,1},{25,9},{2,18},{10... | collective-permute-start | bytes 2359304 | tf_op jit(solution)/shard_map/ppermute | solution.py:346
  379.4 43.0 %collective-permute-start.64 = (bf16[192,2048]{1,0:T(8,128)(2,1)S(1)}, bf16[192,2048]{1,0:T(8,128)(2,1)S(1)}, u32[]{:S(2)}, u32[]{:S(2)}) collective-permute-start(bf16[192,2048]{1,0:T(8,128)(2,1)S(1)} %get-tuple-element.434), channel_id=1, source_target_pairs={{0,16},{8,24},{16,0},{24,8},{1,17},{9,25},{17,1},{25,9},{2,18},{10... | collective-permute-start | bytes 2359304 | tf_op jit(solution)/shard_map/ppermute | solution.py:346
  404.7 15.9 %collective-permute-start.63 = (bf16[128,2048]{1,0:T(8,128)(2,1)S(1)}, bf16[128,2048]{1,0:T(8,128)(2,1)S(1)}, u32[]{:S(2)}, u32[]{:S(2)}) collective-permute-start(bf16[128,2048]{1,0:T(8,128)(2,1)S(1)} %get-tuple-element.458), channel_id=1, source_target_pairs={{0,1},{1,0},{2,3},{3,2},{4,5},{5,4},{6,7},{7,6},{8,9},{9,8},{10,11... | collective-permute-start | bytes 1572872 | tf_op jit(solution)/shard_map/ppermute | solution.py:338
  405.4 15.1 %collective-permute-start.62 = (bf16[128,2048]{1,0:T(8,128)(2,1)S(1)}, bf16[128,2048]{1,0:T(8,128)(2,1)S(1)}, u32[]{:S(2)}, u32[]{:S(2)}) collective-permute-start(bf16[128,2048]{1,0:T(8,128)(2,1)S(1)} %get-tuple-element.459), channel_id=1, source_target_pairs={{0,2},{1,3},{2,6},{3,7},{6,4},{7,5},{4,0},{5,1},{8,10},{9,11},{10,... | collective-permute-start | bytes 1572872 | tf_op jit(solution)/shard_map/ppermute | solution.py:342
  423.4 36.6 %collective-permute-start.65 = (bf16[384,2048]{1,0:T(8,128)(2,1)}, bf16[384,2048]{1,0:T(8,128)(2,1)}, u32[]{:S(2)}, u32[]{:S(2)}) collective-permute-start(bf16[384,2048]{1,0:T(8,128)(2,1)} %get-tuple-element.481), channel_id=1, source_target_pairs={{0,1},{1,0},{2,3},{3,2},{4,5},{5,4},{6,7},{7,6},{8,9},{9,8},{10,11... | collective-permute-start | bytes 4718600 | tf_op jit(solution)/shard_map/ppermute | solution.py:338
  424.4 37.2 %collective-permute-start.66 = (bf16[384,2048]{1,0:T(8,128)(2,1)}, bf16[384,2048]{1,0:T(8,128)(2,1)}, u32[]{:S(2)}, u32[]{:S(2)}) collective-permute-start(bf16[384,2048]{1,0:T(8,128)(2,1)} %get-tuple-element.482), channel_id=1, source_target_pairs={{0,2},{1,3},{2,6},{3,7},{6,4},{7,5},{4,0},{5,1},{8,10},{9,11},{10,... | collective-permute-start | bytes 4718600 | tf_op jit(solution)/shard_map/ppermute | solution.py:342
  433.8 20.3 %collective-permute-start.68 = (bf16[512,768]{1,0:T(8,128)(2,1)}, bf16[512,768]{1,0:T(8,128)(2,1)}, u32[]{:S(2)}, u32[]{:S(2)}) collective-permute-start(bf16[512,768]{1,0:T(8,128)(2,1)} %fusion.3), channel_id=1, source_target_pairs={{0,16},{8,24},{16,0},{24,8},{1,17},{9,25},{17,1},{25,9},{2,18},{10... | collective-permute-start | bytes 2359304 | tf_op jit(solution)/shard_map/ppermute | solution.py:346
  433.8 34.0 %collective-permute-start.73 = (bf16[512,256]{1,0:T(8,128)(2,1)}, bf16[512,256]{1,0:T(8,128)(2,1)}, u32[]{:S(2)}, u32[]{:S(2)}) collective-permute-start(bf16[512,256]{1,0:T(8,128)(2,1)} %copy-done.113), channel_id=1, source_target_pairs={{0,8},{8,0},{16,24},{24,16},{1,9},{9,1},{17,25},{25,17},{2,10},{10... | collective-permute-start | bytes 786440 | tf_op jit(solution)/shard_map/ppermute | solution.py:350
  441.4 26.4 %collective-permute-start.74 = (bf16[512,512]{1,0:T(8,128)(2,1)}, bf16[512,512]{1,0:T(8,128)(2,1)}, u32[]{:S(2)}, u32[]{:S(2)}) collective-permute-start(bf16[512,512]{1,0:T(8,128)(2,1)} %get-tuple-element.506), channel_id=1, source_target_pairs={{0,8},{8,0},{16,24},{24,16},{1,9},{9,1},{17,25},{25,17},{2,10},{10... | collective-permute-start | bytes 1572872 | tf_op jit(solution)/shard_map/ppermute | solution.py:350
  465.3 39.6 %collective-permute-start.69 = (bf16[384,2048]{1,0:T(8,128)(2,1)}, bf16[384,2048]{1,0:T(8,128)(2,1)}, u32[]{:S(2)}, u32[]{:S(2)}) collective-permute-start(bf16[384,2048]{1,0:T(8,128)(2,1)} %get-tuple-element.489), channel_id=1, source_target_pairs={{0,1},{1,0},{2,3},{3,2},{4,5},{5,4},{6,7},{7,6},{8,9},{9,8},{10,11... | collective-permute-start | bytes 4718600 | tf_op jit(solution)/shard_map/ppermute | solution.py:338
  466.3 40.3 %collective-permute-start.70 = (bf16[384,2048]{1,0:T(8,128)(2,1)}, bf16[384,2048]{1,0:T(8,128)(2,1)}, u32[]{:S(2)}, u32[]{:S(2)}) collective-permute-start(bf16[384,2048]{1,0:T(8,128)(2,1)} %mix.28), channel_id=1, source_target_pairs={{0,2},{1,3},{2,6},{3,7},{6,4},{7,5},{4,0},{5,1},{8,10},{9,11},{10,... | collective-permute-start | bytes 4718600 | tf_op jit(solution)/shard_map/ppermute | solution.py:342
  466.3 14.6 %collective-permute-start.75 = (bf16[128,2048]{1,0:T(8,128)(2,1)}, bf16[128,2048]{1,0:T(8,128)(2,1)}, u32[]{:S(2)}, u32[]{:S(2)}) collective-permute-start(bf16[128,2048]{1,0:T(8,128)(2,1)} %fusion.6), channel_id=1, source_target_pairs={{1,17},{3,19},{5,21},{7,23},{9,25},{11,27},{13,29},{15,31},{16,0},... | collective-permute-start | bytes 1572872 | tf_op jit(solution)/shard_map/ppermute | solution.py:1203
  470.9 55.0 %all-to-all-start.1 = ((bf16[8,80,768]{2,1,0:T(8,128)(2,1)}), bf16[8,80,768]{2,1,0:T(8,128)(2,1)}, u32[]{:S(2)}, u32[]{:S(2)}) async-start(bf16[8,80,768]{2,1,0:T(8,128)(2,1)} %fusion.5), calls=%async_computation.1 | async-start | bytes 1966080 | tf_op jit(solution)/shard_map/all_to_all | solution.py:1153
  482.7 34.7 %collective-permute-start.76 = (bf16[64,2048]{1,0:T(8,128)(2,1)S(1)}, bf16[64,2048]{1,0:T(8,128)(2,1)S(1)}, u32[]{:S(2)}, u32[]{:S(2)}) collective-permute-start(bf16[64,2048]{1,0:T(8,128)(2,1)S(1)} %dynamic-slice_convert_fusion.1), channel_id=1, source_target_pairs={{0,1},{2,3},{4,5},{6,7},{8,9},{10,11},{12,13},{14,15},{17,16},{19,... | collective-permute-start | bytes 786440 | tf_op jit(solution)/shard_map/ppermute | solution.py:1212
  510.0 28.6 %collective-permute-start.71 = (bf16[256,2048]{1,0:T(8,128)(2,1)}, bf16[256,2048]{1,0:T(8,128)(2,1)}, u32[]{:S(2)}, u32[]{:S(2)}) collective-permute-start(bf16[256,2048]{1,0:T(8,128)(2,1)} %get-tuple-element.501), channel_id=1, source_target_pairs={{0,1},{1,0},{2,3},{3,2},{4,5},{5,4},{6,7},{7,6},{8,9},{9,8},{10,11... | collective-permute-start | bytes 3145736 | tf_op jit(solution)/shard_map/ppermute | solution.py:338
  513.6 32.4 %collective-permute-start.72 = (bf16[256,2048]{1,0:T(8,128)(2,1)}, bf16[256,2048]{1,0:T(8,128)(2,1)}, u32[]{:S(2)}, u32[]{:S(2)}) collective-permute-start(bf16[256,2048]{1,0:T(8,128)(2,1)} %mix.29), channel_id=1, source_target_pairs={{0,2},{1,3},{2,6},{3,7},{6,4},{7,5},{4,0},{5,1},{8,10},{9,11},{10,... | collective-permute-start | bytes 3145736 | tf_op jit(solution)/shard_map/ppermute | solution.py:342
  (201 other events, 2224.5 us)
Sparse Core Ops, SparseCore 0:
  81.4 29.1 all-gather.3
  112.1 30.9 all-gather.5
  144.7 31.6 all-gather.7

commit v6 on v5

--- a/solution.py
+++ b/solution.py
@@ -486,7 +486,7 @@
     return pl.pallas_call(
         functools.partial(mix_kernel, tuple(plans)),
         out_shape=[jax.ShapeDtypeStruct((count, width), jnp.bfloat16) for count in counts],
-        compiler_params=pltpu.CompilerParams(vmem_limit_bytes=16 * 2**20),
+        compiler_params=pltpu.CompilerParams(vmem_limit_bytes=10 * 2**20),
         cost_estimate=FREE,
         name="mix",
     )(*arrays)
@@ -630,7 +630,7 @@
             jax.ShapeDtypeStruct((count, 2 * width), jnp.bfloat16),
         ],
         scratch_shapes=[pltpu.VMEM((count, head), jnp.float32)] * 2,
-        compiler_params=pltpu.CompilerParams(vmem_limit_bytes=20 * 2**20),
+        compiler_params=pltpu.CompilerParams(vmem_limit_bytes=14 * 2**20),
         cost_estimate=LONG,
         name="attend_back",
     )(queries, pairs, pairs, first, last, place, lse, attended, d_attended)
@@ -846,7 +846,7 @@
             jax.ShapeDtypeStruct((rows, w_kv.shape[1]), low),
             jax.ShapeDtypeStruct((rows, wq.shape[1]), low),
         ],
-        compiler_params=pltpu.CompilerParams(vmem_limit_bytes=16 * 2**20),
+        compiler_params=pltpu.CompilerParams(vmem_limit_bytes=12 * 2**20),
         cost_estimate=cost,
         name="project",
     )(*piece, kv_gain, attn_gain, w_kv, wq)
@@ -876,7 +876,7 @@
     own, other = pl.pallas_call(
         functools.partial(terms_kernel, step),
         out_shape=[out, out],
-        compiler_params=pltpu.CompilerParams(vmem_limit_bytes=20 * 2**20),
+        compiler_params=pltpu.CompilerParams(vmem_limit_bytes=14 * 2**20),
         cost_estimate=FREE,
         name="back_terms",
     )(d_pairs, d_queries, w_kv, wq, *result)
@@ -911,7 +911,7 @@
         + [row_blocks(part, block) for part in sums],
         out_specs=pl.BlockSpec((block, width), lambda i: (i, 0)),
         out_shape=jax.ShapeDtypeStruct((rows, width), jnp.bfloat16),
-        compiler_params=pltpu.CompilerParams(vmem_limit_bytes=8 * 2**20),
+        compiler_params=pltpu.CompilerParams(vmem_limit_bytes=6 * 2**20),
         cost_estimate=FREE,
         name="result",
     )(middle, live, *(part.array for part in sums))
@@ -944,7 +944,7 @@
         + [row_blocks(part, block) for part in sums],
         out_specs=[spec, spec],
         out_shape=[jax.ShapeDtypeStruct((rows, width), jnp.bfloat16)] * 2,
-        compiler_params=pltpu.CompilerParams(vmem_limit_bytes=56 * 2**20),
+        compiler_params=pltpu.CompilerParams(vmem_limit_bytes=8 * 2**20),
         cost_estimate=FREE,
         name="input_grads",
     )(hidden, source, d_middle, attn_gain, kv_gain, *(part.array for part in sums))
@@ -1001,7 +1001,7 @@
         functools.partial(feed_kernel, *plans),
         out_shape=[low, low, low, terms, terms]
         + [jax.ShapeDtypeStruct((count, width), jnp.bfloat16)] * 2,
-        compiler_params=pltpu.CompilerParams(vmem_limit_bytes=24 * 2**20),
+        compiler_params=pltpu.CompilerParams(vmem_limit_bytes=20 * 2**20),
         cost_estimate=LONG,
         name="feed",
     )(*arrays, wg, wu, wd)
@@ -1048,7 +1048,7 @@
         in_specs=[spec] * (2 * count),
         out_specs=[pl.BlockSpec((rows, block), lambda i: (0, i))] * count,
         out_shape=[jax.ShapeDtypeStruct((rows, width), jnp.float32)] * count,
-        compiler_params=pltpu.CompilerParams(vmem_limit_bytes=20 * 2**20),
+        compiler_params=pltpu.CompilerParams(vmem_limit_bytes=8 * 2**20),
         cost_estimate=LONG,
         name="add_all",
     )(*kept, *got)
@@ -1129,7 +1129,7 @@
                 ),
                 jax.ShapeDtypeStruct((2, block, 3 * mine), jnp.float32),
             ],
-            compiler_params=pltpu.CompilerParams(vmem_limit_bytes=20 * 2**20),
+            compiler_params=pltpu.CompilerParams(vmem_limit_bytes=16 * 2**20),
             cost_estimate=LONG,
             name="column_grads",
         )(self.dp.reshape(1).astype(jnp.int32), *sources, *hiddens, d_queries, d_pairs)
@@ -1170,7 +1170,7 @@
                 jax.ShapeDtypeStruct((16, 128), jnp.float32),
                 flat,
             ],
-            compiler_params=pltpu.CompilerParams(vmem_limit_bytes=8 * 2**20),
+            compiler_params=pltpu.CompilerParams(vmem_limit_bytes=6 * 2**20),
             cost_estimate=FREE,
             name="own_grads",
         )(got, *weights, flag, out_grads.kept, out_got)
@@ -1257,7 +1257,7 @@
         + [pl.BlockSpec((rows.shape[0], block), lambda i: (0, i)) for rows in pieces],
         out_specs=pl.BlockSpec((attended.shape[1], block), lambda i: (0, i)),
         out_shape=jax.ShapeDtypeStruct((attended.shape[1], width), jnp.float32),
-        compiler_params=pltpu.CompilerParams(vmem_limit_bytes=20 * 2**20),
+        compiler_params=pltpu.CompilerParams(vmem_limit_bytes=10 * 2**20),
         cost_estimate=FREE,
         name="out_grad",
     )(attended, *pieces)
@@ -1283,7 +1283,7 @@
             + [spec(rows.shape[0]) for rows in got],
             out_specs=[spec(rows) for rows, dtype in outs],
             out_shape=[jax.ShapeDtypeStruct((rows, width), dtype) for rows, dtype in outs],
-            compiler_params=pltpu.CompilerParams(vmem_limit_bytes=24 * 2**20),
+            compiler_params=pltpu.CompilerParams(vmem_limit_bytes=14 * 2**20),
             cost_estimate=LONG,
             name="hidden_grads",
         )(*units, *self.rows, *got)

time: 567 us -> 567 us (level)
    unnamed x342 -> x358, local copies, waits for them, and re-layouts: 56 us -> 56.4 us
where the time goes in v6:
time: 567 us; the launch traced here: 557 us
  waiting for transfers between devices  244 us (43%)
  Pallas kernels  116 us (20%)
  starting transfers between devices  84.4 us (15%)
  local copies, waits for them, and re-layouts  66.8 us (12%)
  other arithmetic  25.2 us (4%)
  between operations  16.4 us (3%)
    ppermute x27, waiting for transfers between devices, x_swap(): return lax.ppermute(value, 'fsdp', swap_pairs(8, 1))  112 us
    ppermute x26, waiting for transfers between devices, ring_step(): return lax.ppermute(value, 'fsdp', ring_pairs())  72 us
    unnamed x358, local copies, waits for them, and re-layouts  56.4 us
    ppermute x6, waiting for transfers between devices, y_swap(): return lax.ppermute(value, 'dp', swap_pairs(4, 2))  32.7 us
    ppermute x26, starting transfers between devices, ring_step(): return lax.ppermute(value, 'fsdp', ring_pairs())  31.9 us
    ppermute x27, starting transfers between devices, x_swap(): return lax.ppermute(value, 'fsdp', swap_pairs(8, 1))  30.7 us
    pallas_call x4, Pallas kernels, feed(): pl.pallas_call(functools.partial(feed_kernel, *plans), out_shape=[low, lo...  20 us
    pallas_call x6, Pallas kernels, call(): pl.pallas_call(functools.partial(kernel, len(self.units)), grid=(2,), in_...  16.8 us
  transfers between devices with their start and end apart: 82, of which 50 were waited for; matrix products, arithmetic and copies ran while one was open for 7% of the time, Pallas kernels for 20%

profile of v6, /device:TPU:0, one launch (start us, length us, event | category | flops | bytes accessed | tf_op | source)
XLA Modules:
  0.0 557.4 jit_solution(15618308017820757394)
XLA Ops:
  9.5 3.1 collective-permute-start.1
  15.3 3.9 all-to-all-start
  28.7 9.0 %collective-permute-done.1.held_ref = bf16[256,2048]{1,0:T(8,128)(2,1)} collective-permute-done((bf16[256,2048]{1,0:T(8,128)(2,1)S(1)}, bf16[256,2048]{1,0:T(8,128)(2,1)}, u32[]{:S(2)}, u32[]{:S(2)}) %collective-permute-start.1) | collective-permute-done | bytes 1048608 | tf_op jit(solution)/shard_map/ppermute | solution.py:342
  37.7 3.3 collective-permute-done.refs_0_
  41.1 14.0 %all-to-all-done = bf16[8,208,256]{2,1,0:T(8,128)(2,1)S(1)} async-done(((bf16[8,208,256]{2,1,0:T(8,128)(2,1)}), bf16[8,208,256]{2,1,0:T(8,128)(2,1)S(1)}, u32[]{:S(2)}, u32[]{:S(2)}) %all-to-all-start) | async-done | bytes 852000 | tf_op jit(solution)/shard_map/all_to_all | solution.py:703
  59.9 19.0 %collective-permute-done.2.refs_2_ = bf16[1664,256]{1,0:T(8,128)(2,1)S(1)} collective-permute-done((bf16[1664,256]{1,0:T(8,128)(2,1)S(1)}, bf16[1664,256]{1,0:T(8,128)(2,1)S(1)}, u32[]{:S(2)}, u32[]{:S(2)}) %collective-permute-start.2) | collective-permute-done | bytes 852000 | tf_op jit(solution)/shard_map/ppermute | solution.py:346
  102.6 3.1 project.5
  105.8 5.5 collective-permute-done.7.refs_0_.refs_1_
  111.7 3.7 collective-permute-start.14
  119.7 3.4 project.6
  124.2 5.9 %collective-permute-done.9.refs_0_ = bf16[128,2048]{1,0:T(8,128)(2,1)S(1)} collective-permute-done((bf16[128,2048]{1,0:T(8,128)(2,1)S(1)}, bf16[128,2048]{1,0:T(8,128)(2,1)S(1)}, u32[]{:S(2)}, u32[]{:S(2)}) %collective-permute-start.9) | collective-permute-done | bytes 524320 | tf_op jit(solution)/shard_map/ppermute | solution.py:338
  138.6 4.5 collective-permute-done.11.refs_3_
  147.1 7.5 %attend.1 = (f32[1024,256]{1,0:T(8,128)S(1)}, bf16[1024,256]{1,0:T(8,128)(2,1)S(1)}, f32[2,1024,1]{2,1,0:T(8,128)S(1)}) custom-call(bf16[1024,256]{1,0:T(8,128)(2,1)S(1)} %constant_dynamic-update-slice_fusion.2.q_ref, bf16[1024,512]{1,0:T(8,128)(2,1)S(1)} %constant_dynamic-update-slice_fusion.6.k_ref.v_ref, ...), custom_call_target="tpu_custom_call" | custom-call | flops 20000000000 | tf_op jit(solution)/shard_map/attend/pallas_call | solution.py:594
  155.9 4.8 collective-permute-done.16.refs_1_.refs_2_
  164.9 16.1 %collective-permute-done.18.refs_1_.refs_3_ = bf16[192,2048]{1,0:T(8,128)(2,1)S(1)} collective-permute-done((bf16[192,2048]{1,0:T(8,128)(2,1)S(1)}, bf16[192,2048]{1,0:T(8,128)(2,1)S(1)}, u32[]{:S(2)}, u32[]{:S(2)}) %collective-permute-start.18) | collective-permute-done | bytes 786464 | tf_op jit(solution)/shard_map/ppermute | solution.py:342
  186.0 15.0 %collective-permute-done.20.refs_2_.refs_4_ = bf16[192,2048]{1,0:T(8,128)(2,1)S(1)} collective-permute-done((bf16[192,2048]{1,0:T(8,128)(2,1)S(1)}, bf16[192,2048]{1,0:T(8,128)(2,1)S(1)}, u32[]{:S(2)}, u32[]{:S(2)}) %collective-permute-start.20) | collective-permute-done | bytes 786464 | tf_op jit(solution)/shard_map/ppermute | solution.py:338
  205.3 8.1 %collective-permute-done.22.refs_2_ = bf16[128,2048]{1,0:T(8,128)(2,1)S(1)} collective-permute-done((bf16[128,2048]{1,0:T(8,128)(2,1)S(1)}, bf16[128,2048]{1,0:T(8,128)(2,1)S(1)}, u32[]{:S(2)}, u32[]{:S(2)}) %collective-permute-start.22) | collective-permute-done | bytes 524320 | tf_op jit(solution)/shard_map/ppermute | solution.py:338
  217.6 8.8 %collective-permute-done.24 = bf16[128,2048]{1,0:T(8,128)(2,1)} collective-permute-done((bf16[128,2048]{1,0:T(8,128)(2,1)}, bf16[128,2048]{1,0:T(8,128)(2,1)}, u32[]{:S(2)}, u32[]{:S(2)}) %collective-permute-start.24) | collective-permute-done | bytes 524320 | tf_op jit(solution)/shard_map/ppermute | solution.py:338
  244.7 3.4 collective-permute-start.29
  250.2 5.7 %feed.4 = (bf16[256,768]{1,0:T(8,128)(2,1)S(1)}, bf16[256,768]{1,0:T(8,128)(2,1)S(1)}, bf16[256,768]{1,0:T(8,128)(2,1)S(1)}, bf16[128,2048]{1,0:T(8,128)(2,1)S(1...) custom-call(bf16[128,2048]{1,0:T(8,128)(2,1)} %multiply_convert_fusion.refs_0_, ...), custom_call_target="tpu_custom_call" | custom-call | flops 20000000000 | tf_op jit(solution)/shard_map/feed/pallas_call | solution.py:1000
  259.9 5.5 feed.5
  266.9 3.2 collective-permute-done.31.refs_0_
  273.3 4.4 feed.6
  277.7 5.0 collective-permute-done.32.refs_1_.refs_3_
  286.7 4.4 feed.7
  291.1 7.3 %collective-permute-done.34.refs_1_ = bf16[128,2048]{1,0:T(8,128)(2,1)S(1)} collective-permute-done((bf16[128,2048]{1,0:T(8,128)(2,1)S(1)}, bf16[128,2048]{1,0:T(8,128)(2,1)S(1)}, u32[]{:S(2)}, u32[]{:S(2)}) %collective-permute-start.34) | collective-permute-done | bytes 524320 | tf_op jit(solution)/shard_map/ppermute | solution.py:338
  306.3 5.7 %collective-permute-done.36.refs_1_ = bf16[128,2048]{1,0:T(8,128)(2,1)S(1)} collective-permute-done((bf16[128,2048]{1,0:T(8,128)(2,1)S(1)}, bf16[128,2048]{1,0:T(8,128)(2,1)S(1)}, u32[]{:S(2)}, u32[]{:S(2)}) %collective-permute-start.36) | collective-permute-done | bytes 524320 | tf_op jit(solution)/shard_map/ppermute | solution.py:338
  318.1 5.7 %collective-permute-done.38 = bf16[128,2048]{1,0:T(8,128)(2,1)S(1)} collective-permute-done((bf16[128,2048]{1,0:T(8,128)(2,1)S(1)}, bf16[128,2048]{1,0:T(8,128)(2,1)S(1)}, u32[]{:S(2)}, u32[]{:S(2)}) %collective-permute-start.38) | collective-permute-done | bytes 524320 | tf_op jit(solution)/shard_map/ppermute | solution.py:338
  333.4 3.2 hidden_grads.10
  336.6 5.3 collective-permute-done.43.refs_0_
  352.1 3.6 collective-permute-done.54
  355.7 4.8 collective-permute-done.46.refs_1_
  371.2 3.6 hidden_grads.11
  394.0 10.0 %attend_back.1 = (bf16[1024,256]{1,0:T(8,128)(2,1)S(1)}, bf16[1024,512]{1,0:T(8,128)(2,1)S(1)}) custom-call(bf16[1024,256]{1,0:T(8,128)(2,1)S(1)} %copy-done.94, bf16[1024,512]{1,0:T(8,128)(2,1)S(1)} %copy-done.92, bf16[1024,512]{1,0:T(8,128)(2,1)S(1)} %copy-done.92, s32[1024,1]{1,0:T(8,128)S(1)} %copy-done.71, s32[1024,1]{1,0:T(8,128)S(1)} %copy-done.67, ...), custom_call_target="tpu_custom_call" | custom-call | flops 20000000000 | tf_op jit(solution)/shard_map/attend_back/pallas_call | solution.py:613
  412.0 6.5 %column_grads.1 = (bf16[512,256]{1,0:T(8,128)(2,1)S(1)}, bf16[512,512]{1,0:T(8,128)(2,1)}, bf16[512,256]{1,0:T(8,128)(2,1)}, bf16[512,512]{1,0:T(8,128)(2,1)}, f32[2,512,768]{2,1,0:T(8,128)S(1)}) custom-call(s32[1]{0:T(128)} %bitcast.dp_ref, bf16[256,2048]{1,0:T(8,128)(2,1)S(1)} %copy-done.98, bf16[256,2048]{1,0:T(8,128)(2,1)S(1)} %copy-done.102, ...), custom_call_target="tpu_custom_call" | custom-call | flops 20000000000 | tf_op jit(solution)/shard_map/column_grads/pallas_call | solution.py:1107
  438.9 3.0 back_terms.6
  444.4 10.1 %collective-permute-done.68 = bf16[512,768]{1,0:T(8,128)(2,1)} collective-permute-done((bf16[512,768]{1,0:T(8,128)(2,1)}, bf16[512,768]{1,0:T(8,128)(2,1)}, u32[]{:S(2)}, u32[]{:S(2)}) %collective-permute-start.68) | collective-permute-done | bytes 786464 | tf_op jit(solution)/shard_map/ppermute | solution.py:346
  454.5 5.7 %collective-permute-done.65.refs_1_ = bf16[384,2048]{1,0:T(8,128)(2,1)} collective-permute-done((bf16[384,2048]{1,0:T(8,128)(2,1)}, bf16[384,2048]{1,0:T(8,128)(2,1)}, u32[]{:S(2)}, u32[]{:S(2)}) %collective-permute-start.65) | collective-permute-done | bytes 1572896 | tf_op jit(solution)/shard_map/ppermute | solution.py:338
  462.1 3.7 mix.28
  471.2 5.9 %all-to-all-start.1 = ((bf16[8,80,768]{2,1,0:T(8,128)(2,1)}), bf16[8,80,768]{2,1,0:T(8,128)(2,1)}, u32[]{:S(2)}, u32[]{:S(2)}) async-start(bf16[8,80,768]{2,1,0:T(8,128)(2,1)} %fusion.5), calls=%async_computation.1 | async-start | bytes 1966080 | tf_op jit(solution)/shard_map/all_to_all | solution.py:1153
  477.1 4.0 collective-permute-done.75
  487.3 17.9 %collective-permute-done.69.x_ref.refs_1_ = bf16[384,2048]{1,0:T(8,128)(2,1)} collective-permute-done((bf16[384,2048]{1,0:T(8,128)(2,1)}, bf16[384,2048]{1,0:T(8,128)(2,1)}, u32[]{:S(2)}, u32[]{:S(2)}) %collective-permute-start.69) | collective-permute-done | bytes 1572896 | tf_op jit(solution)/shard_map/ppermute | solution.py:338
  506.5 3.4 mix.29
  509.9 3.9 collective-permute-start.71
  519.2 7.0 %all-to-all-done.1.got_ref = bf16[8,80,768]{2,1,0:T(8,128)(2,1)} async-done(((bf16[8,80,768]{2,1,0:T(8,128)(2,1)}), bf16[8,80,768]{2,1,0:T(8,128)(2,1)}, u32[]{:S(2)}, u32[]{:S(2)}) %all-to-all-start.1) | async-done | bytes 983072 | tf_op jit(solution)/shard_map/all_to_all | solution.py:1153
  534.4 3.6 result.1
  539.1 7.1 %collective-permute-done.72.refs_2_.refs_5_ = bf16[256,2048]{1,0:T(8,128)(2,1)} collective-permute-done((bf16[256,2048]{1,0:T(8,128)(2,1)}, bf16[256,2048]{1,0:T(8,128)(2,1)}, u32[]{:S(2)}, u32[]{:S(2)}) %collective-permute-start.72) | collective-permute-done | bytes 1048608 | tf_op jit(solution)/shard_map/ppermute | solution.py:342
  546.2 4.2 input_grads.1
  (601 shorter events, 235.2 us)
Async XLA Ops:
  9.5 28.2 %collective-permute-start.1 = (bf16[256,2048]{1,0:T(8,128)(2,1)S(1)}, bf16[256,2048]{1,0:T(8,128)(2,1)}, u32[]{:S(2)}, u32[]{:S(2)}) collective-permute-start(bf16[256,2048]{1,0:T(8,128)(2,1)S(1)} %constant_dynamic-update-slice_fusion.held_ref), channel_id=1, source_target_pairs={{0,2},{1,3},{2,6},{3,7},{6,4},{7,5},{4,0},{5,1},{8,10},{9,11},{10,... | collective-permute-start | bytes 3145736 | tf_op jit(solution)/shard_map/ppermute | solution.py:342
  12.6 28.5 %collective-permute-start = (bf16[256,2048]{1,0:T(8,128)(2,1)S(1)}, bf16[256,2048]{1,0:T(8,128)(2,1)}, u32[]{:S(2)}, u32[]{:S(2)}) collective-permute-start(bf16[256,2048]{1,0:T(8,128)(2,1)S(1)} %constant_dynamic-update-slice_fusion.held_ref), channel_id=1, source_target_pairs={{0,1},{1,0},{2,3},{3,2},{4,5},{5,4},{6,7},{7,6},{8,9},{9,8},{10,11... | collective-permute-start | bytes 3145736 | tf_op jit(solution)/shard_map/ppermute | solution.py:338
  15.3 39.8 %all-to-all-start = ((bf16[8,208,256]{2,1,0:T(8,128)(2,1)}), bf16[8,208,256]{2,1,0:T(8,128)(2,1)S(1)}, u32[]{:S(2)}, u32[]{:S(2)}) async-start(bf16[8,208,256]{2,1,0:T(8,128)(2,1)} %bitcast.83), calls=%async_computation | async-start | bytes 1703936 | tf_op jit(solution)/shard_map/all_to_all | solution.py:703
  19.2 214.8 %all-gather.4.cloned.1.call-start = ((), (), s32[]{:S(2)}) async-start(), calls=%async_computation.2 | async-start | bytes 3932160 | tf_op jit(solution)/shard_map/all_gather | solution.py:1216
  55.1 24.6 %collective-permute-start.5 = (bf16[256,2048]{1,0:T(8,128)(2,1)}, bf16[256,2048]{1,0:T(8,128)(2,1)S(1)}, u32[]{:S(2)}, u32[]{:S(2)}) collective-permute-start(bf16[256,2048]{1,0:T(8,128)(2,1)} %collective-permute-done.1.held_ref), channel_id=1, source_target_pairs={{0,1},{1,0},{2,3},{3,2},{4,5},{5,4},{6,7},{7,6},{8,9},{9,8},{10,11... | collective-permute-start | bytes 3145736 | tf_op jit(solution)/shard_map/ppermute | solution.py:338
  56.6 24.7 %collective-permute-start.6 = (bf16[256,2048]{1,0:T(8,128)(2,1)}, bf16[256,2048]{1,0:T(8,128)(2,1)}, u32[]{:S(2)}, u32[]{:S(2)}) collective-permute-start(bf16[256,2048]{1,0:T(8,128)(2,1)} %collective-permute-done.1.held_ref), channel_id=1, source_target_pairs={{0,2},{1,3},{2,6},{3,7},{6,4},{7,5},{4,0},{5,1},{8,10},{9,11},{10,... | collective-permute-start | bytes 3145736 | tf_op jit(solution)/shard_map/ppermute | solution.py:342
  57.5 21.4 %collective-permute-start.2 = (bf16[1664,256]{1,0:T(8,128)(2,1)S(1)}, bf16[1664,256]{1,0:T(8,128)(2,1)S(1)}, u32[]{:S(2)}, u32[]{:S(2)}) collective-permute-start(bf16[1664,256]{1,0:T(8,128)(2,1)S(1)} %bitcast.81), channel_id=1, source_target_pairs={{0,16},{8,24},{16,0},{24,8},{1,17},{9,25},{17,1},{25,9},{2,18},{10... | collective-permute-start | bytes 2555912 | tf_op jit(solution)/shard_map/ppermute | solution.py:346
  81.3 156.6 %all-gather.6.cloned.1.call-start = ((), (), s32[]{:S(2)}) async-start(), calls=%async_computation.3 | async-start | bytes 3932160 | tf_op jit(solution)/shard_map/all_gather | solution.py:1216
  82.0 159.6 %all-gather.8.cloned.1.call-start = ((), (), s32[]{:S(2)}) async-start(), calls=%async_computation.4 | async-start | bytes 3932160 | tf_op jit(solution)/shard_map/all_gather | solution.py:1216
  84.3 27.0 %collective-permute-start.7 = (bf16[256,2048]{1,0:T(8,128)(2,1)}, bf16[256,2048]{1,0:T(8,128)(2,1)}, u32[]{:S(2)}, u32[]{:S(2)}) collective-permute-start(bf16[256,2048]{1,0:T(8,128)(2,1)} %collective-permute-done.6.held_ref), channel_id=1, source_target_pairs={{0,1},{1,0},{2,3},{3,2},{4,5},{5,4},{6,7},{7,6},{8,9},{9,8},{10,11... | collective-permute-start | bytes 3145736 | tf_op jit(solution)/shard_map/ppermute | solution.py:338
  85.2 26.5 %collective-permute-start.8 = (bf16[256,2048]{1,0:T(8,128)(2,1)}, bf16[256,2048]{1,0:T(8,128)(2,1)}, u32[]{:S(2)}, u32[]{:S(2)}) collective-permute-start(bf16[256,2048]{1,0:T(8,128)(2,1)} %collective-permute-done.6.held_ref), channel_id=1, source_target_pairs={{0,2},{1,3},{2,6},{3,7},{6,4},{7,5},{4,0},{5,1},{8,10},{9,11},{10,... | collective-permute-start | bytes 3145736 | tf_op jit(solution)/shard_map/ppermute | solution.py:342
  111.7 26.9 %collective-permute-start.14 = (bf16[128,2048]{1,0:T(8,128)(2,1)S(1)}, bf16[128,2048]{1,0:T(8,128)(2,1)S(1)}, u32[]{:S(2)}, u32[]{:S(2)}) collective-permute-start(bf16[128,2048]{1,0:T(8,128)(2,1)S(1)} %copy-done.163), channel_id=1, source_target_pairs={{0,16},{2,18},{4,20},{6,22},{8,24},{10,26},{12,28},{14,30},{17,1},... | collective-permute-start | bytes 1572872 | tf_op jit(solution)/shard_map/ppermute | solution.py:1183
  117.2 13.9 %collective-permute-start.10 = (bf16[128,2048]{1,0:T(8,128)(2,1)S(1)}, bf16[128,2048]{1,0:T(8,128)(2,1)S(1)}, u32[]{:S(2)}, u32[]{:S(2)}) collective-permute-start(bf16[128,2048]{1,0:T(8,128)(2,1)S(1)} %get-tuple-element.292), channel_id=1, source_target_pairs={{0,2},{1,3},{2,6},{3,7},{6,4},{7,5},{4,0},{5,1},{8,10},{9,11},{10,... | collective-permute-start | bytes 1572872 | tf_op jit(solution)/shard_map/ppermute | solution.py:342
  145.4 15.4 %collective-permute-start.16 = (bf16[128,2048]{1,0:T(8,128)(2,1)S(1)}, bf16[128,2048]{1,0:T(8,128)(2,1)S(1)}, u32[]{:S(2)}, u32[]{:S(2)}) collective-permute-start(bf16[128,2048]{1,0:T(8,128)(2,1)S(1)} %collective-permute-done.12.refs_2_), channel_id=1, source_target_pairs={{0,2},{1,3},{2,6},{3,7},{6,4},{7,5},{4,0},{5,1},{8,10},{9,11},{10,... | collective-permute-start | bytes 1572872 | tf_op jit(solution)/shard_map/ppermute | solution.py:342
  146.4 14.5 %collective-permute-start.17 = (bf16[128,2048]{1,0:T(8,128)(2,1)S(1)}, bf16[128,2048]{1,0:T(8,128)(2,1)S(1)}, u32[]{:S(2)}, u32[]{:S(2)}) collective-permute-start(bf16[128,2048]{1,0:T(8,128)(2,1)S(1)} %collective-permute-done.12.refs_2_), channel_id=1, source_target_pairs={{0,1},{1,0},{2,3},{3,2},{4,5},{5,4},{6,7},{7,6},{8,9},{9,8},{10,11... | collective-permute-start | bytes 1572872 | tf_op jit(solution)/shard_map/ppermute | solution.py:338
  160.9 20.0 %collective-permute-start.18 = (bf16[192,2048]{1,0:T(8,128)(2,1)S(1)}, bf16[192,2048]{1,0:T(8,128)(2,1)S(1)}, u32[]{:S(2)}, u32[]{:S(2)}) collective-permute-start(bf16[192,2048]{1,0:T(8,128)(2,1)S(1)} %get-tuple-element.313), channel_id=1, source_target_pairs={{0,2},{1,3},{2,6},{3,7},{6,4},{7,5},{4,0},{5,1},{8,10},{9,11},{10,... | collective-permute-start | bytes 2359304 | tf_op jit(solution)/shard_map/ppermute | solution.py:342
  163.8 18.6 %collective-permute-start.19 = (bf16[192,2048]{1,0:T(8,128)(2,1)S(1)}, bf16[192,2048]{1,0:T(8,128)(2,1)S(1)}, u32[]{:S(2)}, u32[]{:S(2)}) collective-permute-start(bf16[192,2048]{1,0:T(8,128)(2,1)S(1)} %get-tuple-element.314), channel_id=1, source_target_pairs={{0,1},{1,0},{2,3},{3,2},{4,5},{5,4},{6,7},{7,6},{8,9},{9,8},{10,11... | collective-permute-start | bytes 2359304 | tf_op jit(solution)/shard_map/ppermute | solution.py:338
  183.3 17.7 %collective-permute-start.20 = (bf16[192,2048]{1,0:T(8,128)(2,1)S(1)}, bf16[192,2048]{1,0:T(8,128)(2,1)S(1)}, u32[]{:S(2)}, u32[]{:S(2)}) collective-permute-start(bf16[192,2048]{1,0:T(8,128)(2,1)S(1)} %get-tuple-element.317), channel_id=1, source_target_pairs={{0,1},{1,0},{2,3},{3,2},{4,5},{5,4},{6,7},{7,6},{8,9},{9,8},{10,11... | collective-permute-start | bytes 2359304 | tf_op jit(solution)/shard_map/ppermute | solution.py:338
  183.9 18.3 %collective-permute-start.21 = (bf16[192,2048]{1,0:T(8,128)(2,1)S(1)}, bf16[192,2048]{1,0:T(8,128)(2,1)S(1)}, u32[]{:S(2)}, u32[]{:S(2)}) collective-permute-start(bf16[192,2048]{1,0:T(8,128)(2,1)S(1)} %get-tuple-element.318), channel_id=1, source_target_pairs={{0,2},{1,3},{2,6},{3,7},{6,4},{7,5},{4,0},{5,1},{8,10},{9,11},{10,... | collective-permute-start | bytes 2359304 | tf_op jit(solution)/shard_map/ppermute | solution.py:342
  271.0 13.5 %collective-permute-start.33 = (bf16[128,2048]{1,0:T(8,128)(2,1)S(1)}, bf16[128,2048]{1,0:T(8,128)(2,1)S(1)}, u32[]{:S(2)}, u32[]{:S(2)}) collective-permute-start(bf16[128,2048]{1,0:T(8,128)(2,1)S(1)} %get-tuple-element.350), channel_id=1, source_target_pairs={{0,2},{1,3},{2,6},{3,7},{6,4},{7,5},{4,0},{5,1},{8,10},{9,11},{10,... | collective-permute-start | bytes 1572872 | tf_op jit(solution)/shard_map/ppermute | solution.py:342
  284.7 13.8 %collective-permute-start.34 = (bf16[128,2048]{1,0:T(8,128)(2,1)S(1)}, bf16[128,2048]{1,0:T(8,128)(2,1)S(1)}, u32[]{:S(2)}, u32[]{:S(2)}) collective-permute-start(bf16[128,2048]{1,0:T(8,128)(2,1)S(1)} %get-tuple-element.364), channel_id=1, source_target_pairs={{0,1},{1,0},{2,3},{3,2},{4,5},{5,4},{6,7},{7,6},{8,9},{9,8},{10,11... | collective-permute-start | bytes 1572872 | tf_op jit(solution)/shard_map/ppermute | solution.py:338
  286.0 15.3 %collective-permute-start.35 = (bf16[128,2048]{1,0:T(8,128)(2,1)S(1)}, bf16[128,2048]{1,0:T(8,128)(2,1)S(1)}, u32[]{:S(2)}, u32[]{:S(2)}) collective-permute-start(bf16[128,2048]{1,0:T(8,128)(2,1)S(1)} %get-tuple-element.365), channel_id=1, source_target_pairs={{0,2},{1,3},{2,6},{3,7},{6,4},{7,5},{4,0},{5,1},{8,10},{9,11},{10,... | collective-permute-start | bytes 1572872 | tf_op jit(solution)/shard_map/ppermute | solution.py:342
  305.8 22.8 %collective-permute-start.40 = (bf16[192,2048]{1,0:T(8,128)(2,1)S(1)}, bf16[192,2048]{1,0:T(8,128)(2,1)S(1)}, u32[]{:S(2)}, u32[]{:S(2)}) collective-permute-start(bf16[192,2048]{1,0:T(8,128)(2,1)S(1)} %get-tuple-element.376), channel_id=1, source_target_pairs={{0,8},{8,0},{16,24},{24,16},{1,9},{9,1},{17,25},{25,17},{2,10},{10... | collective-permute-start | bytes 2359304 | tf_op jit(solution)/shard_map/ppermute | solution.py:350
  305.8 23.8 %collective-permute-start.41 = (bf16[192,2048]{1,0:T(8,128)(2,1)S(1)}, bf16[192,2048]{1,0:T(8,128)(2,1)S(1)}, u32[]{:S(2)}, u32[]{:S(2)}) collective-permute-start(bf16[192,2048]{1,0:T(8,128)(2,1)S(1)} %get-tuple-element.377), channel_id=1, source_target_pairs={{0,8},{8,0},{16,24},{24,16},{1,9},{9,1},{17,25},{25,17},{2,10},{10... | collective-permute-start | bytes 2359304 | tf_op jit(solution)/shard_map/ppermute | solution.py:350
  318.0 24.0 %collective-permute-start.44 = (bf16[192,2048]{1,0:T(8,128)(2,1)S(1)}, bf16[192,2048]{1,0:T(8,128)(2,1)S(1)}, u32[]{:S(2)}, u32[]{:S(2)}) collective-permute-start(bf16[192,2048]{1,0:T(8,128)(2,1)S(1)} %get-tuple-element.388), channel_id=1, source_target_pairs={{0,8},{8,0},{16,24},{24,16},{1,9},{9,1},{17,25},{25,17},{2,10},{10... | collective-permute-start | bytes 2359304 | tf_op jit(solution)/shard_map/ppermute | solution.py:350
  323.7 18.3 %collective-permute-start.45 = (bf16[192,2048]{1,0:T(8,128)(2,1)S(1)}, bf16[192,2048]{1,0:T(8,128)(2,1)S(1)}, u32[]{:S(2)}, u32[]{:S(2)}) collective-permute-start(bf16[192,2048]{1,0:T(8,128)(2,1)S(1)} %get-tuple-element.389), channel_id=1, source_target_pairs={{0,8},{8,0},{16,24},{24,16},{1,9},{9,1},{17,25},{25,17},{2,10},{10... | collective-permute-start | bytes 2359304 | tf_op jit(solution)/shard_map/ppermute | solution.py:350
  336.6 26.7 %collective-permute-start.48 = (bf16[192,2048]{1,0:T(8,128)(2,1)}, bf16[192,2048]{1,0:T(8,128)(2,1)}, u32[]{:S(2)}, u32[]{:S(2)}) collective-permute-start(bf16[192,2048]{1,0:T(8,128)(2,1)} %get-tuple-element.413), channel_id=1, source_target_pairs={{0,8},{8,0},{16,24},{24,16},{1,9},{9,1},{17,25},{25,17},{2,10},{10... | collective-permute-start | bytes 2359304 | tf_op jit(solution)/shard_map/ppermute | solution.py:350
  342.0 21.3 %collective-permute-start.49 = (bf16[192,2048]{1,0:T(8,128)(2,1)}, bf16[192,2048]{1,0:T(8,128)(2,1)}, u32[]{:S(2)}, u32[]{:S(2)}) collective-permute-start(bf16[192,2048]{1,0:T(8,128)(2,1)} %get-tuple-element.414), channel_id=1, source_target_pairs={{0,8},{8,0},{16,24},{24,16},{1,9},{9,1},{17,25},{25,17},{2,10},{10... | collective-permute-start | bytes 2359304 | tf_op jit(solution)/shard_map/ppermute | solution.py:350
  345.8 14.6 %collective-permute-start.46 = (bf16[128,2048]{1,0:T(8,128)(2,1)}, bf16[128,2048]{1,0:T(8,128)(2,1)}, u32[]{:S(2)}, u32[]{:S(2)}) collective-permute-start(bf16[128,2048]{1,0:T(8,128)(2,1)} %collective-permute-done.43.refs_0_), channel_id=1, source_target_pairs={{0,1},{1,0},{2,3},{3,2},{4,5},{5,4},{6,7},{7,6},{8,9},{9,8},{10,11... | collective-permute-start | bytes 1572872 | tf_op jit(solution)/shard_map/ppermute | solution.py:338
  346.8 15.5 %collective-permute-start.47 = (bf16[128,2048]{1,0:T(8,128)(2,1)}, bf16[128,2048]{1,0:T(8,128)(2,1)}, u32[]{:S(2)}, u32[]{:S(2)}) collective-permute-start(bf16[128,2048]{1,0:T(8,128)(2,1)} %collective-permute-done.43.refs_0_), channel_id=1, source_target_pairs={{0,2},{1,3},{2,6},{3,7},{6,4},{7,5},{4,0},{5,1},{8,10},{9,11},{10,... | collective-permute-start | bytes 1572872 | tf_op jit(solution)/shard_map/ppermute | solution.py:342
  355.6 21.8 %collective-permute-start.50 = (bf16[192,2048]{1,0:T(8,128)(2,1)}, bf16[192,2048]{1,0:T(8,128)(2,1)S(1)}, u32[]{:S(2)}, u32[]{:S(2)}) collective-permute-start(bf16[192,2048]{1,0:T(8,128)(2,1)} %copy-done.113), channel_id=1, source_target_pairs={{0,16},{8,24},{16,0},{24,8},{1,17},{9,25},{17,1},{25,9},{2,18},{10... | collective-permute-start | bytes 2359304 | tf_op jit(solution)/shard_map/ppermute | solution.py:346
  363.3 14.1 %collective-permute-start.52 = (bf16[128,2048]{1,0:T(8,128)(2,1)}, bf16[128,2048]{1,0:T(8,128)(2,1)S(1)}, u32[]{:S(2)}, u32[]{:S(2)}) collective-permute-start(bf16[128,2048]{1,0:T(8,128)(2,1)} %collective-permute-done.47.refs_0_), channel_id=1, source_target_pairs={{0,2},{1,3},{2,6},{3,7},{6,4},{7,5},{4,0},{5,1},{8,10},{9,11},{10,... | collective-permute-start | bytes 1572872 | tf_op jit(solution)/shard_map/ppermute | solution.py:342
  378.6 26.6 %collective-permute-start.59 = (bf16[192,2048]{1,0:T(8,128)(2,1)S(1)}, bf16[192,2048]{1,0:T(8,128)(2,1)S(1)}, u32[]{:S(2)}, u32[]{:S(2)}) collective-permute-start(bf16[192,2048]{1,0:T(8,128)(2,1)S(1)} %copy-done.112), channel_id=1, source_target_pairs={{0,16},{8,24},{16,0},{24,8},{1,17},{9,25},{17,1},{25,9},{2,18},{10... | collective-permute-start | bytes 2359304 | tf_op jit(solution)/shard_map/ppermute | solution.py:346
  380.3 42.4 %collective-permute-start.64 = (bf16[192,2048]{1,0:T(8,128)(2,1)S(1)}, bf16[192,2048]{1,0:T(8,128)(2,1)S(1)}, u32[]{:S(2)}, u32[]{:S(2)}) collective-permute-start(bf16[192,2048]{1,0:T(8,128)(2,1)S(1)} %get-tuple-element.434), channel_id=1, source_target_pairs={{0,16},{8,24},{16,0},{24,8},{1,17},{9,25},{17,1},{25,9},{2,18},{10... | collective-permute-start | bytes 2359304 | tf_op jit(solution)/shard_map/ppermute | solution.py:346
  405.3 15.5 %collective-permute-start.63 = (bf16[128,2048]{1,0:T(8,128)(2,1)S(1)}, bf16[128,2048]{1,0:T(8,128)(2,1)S(1)}, u32[]{:S(2)}, u32[]{:S(2)}) collective-permute-start(bf16[128,2048]{1,0:T(8,128)(2,1)S(1)} %get-tuple-element.458), channel_id=1, source_target_pairs={{0,1},{1,0},{2,3},{3,2},{4,5},{5,4},{6,7},{7,6},{8,9},{9,8},{10,11... | collective-permute-start | bytes 1572872 | tf_op jit(solution)/shard_map/ppermute | solution.py:338
  406.4 14.4 %collective-permute-start.62 = (bf16[128,2048]{1,0:T(8,128)(2,1)S(1)}, bf16[128,2048]{1,0:T(8,128)(2,1)S(1)}, u32[]{:S(2)}, u32[]{:S(2)}) collective-permute-start(bf16[128,2048]{1,0:T(8,128)(2,1)S(1)} %get-tuple-element.459), channel_id=1, source_target_pairs={{0,2},{1,3},{2,6},{3,7},{6,4},{7,5},{4,0},{5,1},{8,10},{9,11},{10,... | collective-permute-start | bytes 1572872 | tf_op jit(solution)/shard_map/ppermute | solution.py:342
  423.6 36.6 %collective-permute-start.65 = (bf16[384,2048]{1,0:T(8,128)(2,1)}, bf16[384,2048]{1,0:T(8,128)(2,1)}, u32[]{:S(2)}, u32[]{:S(2)}) collective-permute-start(bf16[384,2048]{1,0:T(8,128)(2,1)} %get-tuple-element.481), channel_id=1, source_target_pairs={{0,1},{1,0},{2,3},{3,2},{4,5},{5,4},{6,7},{7,6},{8,9},{9,8},{10,11... | collective-permute-start | bytes 4718600 | tf_op jit(solution)/shard_map/ppermute | solution.py:338
  424.8 37.2 %collective-permute-start.66 = (bf16[384,2048]{1,0:T(8,128)(2,1)}, bf16[384,2048]{1,0:T(8,128)(2,1)}, u32[]{:S(2)}, u32[]{:S(2)}) collective-permute-start(bf16[384,2048]{1,0:T(8,128)(2,1)} %get-tuple-element.482), channel_id=1, source_target_pairs={{0,2},{1,3},{2,6},{3,7},{6,4},{7,5},{4,0},{5,1},{8,10},{9,11},{10,... | collective-permute-start | bytes 4718600 | tf_op jit(solution)/shard_map/ppermute | solution.py:342
  434.2 20.3 %collective-permute-start.68 = (bf16[512,768]{1,0:T(8,128)(2,1)}, bf16[512,768]{1,0:T(8,128)(2,1)}, u32[]{:S(2)}, u32[]{:S(2)}) collective-permute-start(bf16[512,768]{1,0:T(8,128)(2,1)} %fusion.3), channel_id=1, source_target_pairs={{0,16},{8,24},{16,0},{24,8},{1,17},{9,25},{17,1},{25,9},{2,18},{10... | collective-permute-start | bytes 2359304 | tf_op jit(solution)/shard_map/ppermute | solution.py:346
  434.3 33.8 %collective-permute-start.73 = (bf16[512,256]{1,0:T(8,128)(2,1)}, bf16[512,256]{1,0:T(8,128)(2,1)}, u32[]{:S(2)}, u32[]{:S(2)}) collective-permute-start(bf16[512,256]{1,0:T(8,128)(2,1)} %copy-done.120), channel_id=1, source_target_pairs={{0,8},{8,0},{16,24},{24,16},{1,9},{9,1},{17,25},{25,17},{2,10},{10... | collective-permute-start | bytes 786440 | tf_op jit(solution)/shard_map/ppermute | solution.py:350
  441.9 26.2 %collective-permute-start.74 = (bf16[512,512]{1,0:T(8,128)(2,1)}, bf16[512,512]{1,0:T(8,128)(2,1)}, u32[]{:S(2)}, u32[]{:S(2)}) collective-permute-start(bf16[512,512]{1,0:T(8,128)(2,1)} %get-tuple-element.506), channel_id=1, source_target_pairs={{0,8},{8,0},{16,24},{24,16},{1,9},{9,1},{17,25},{25,17},{2,10},{10... | collective-permute-start | bytes 1572872 | tf_op jit(solution)/shard_map/ppermute | solution.py:350
  465.8 39.4 %collective-permute-start.69 = (bf16[384,2048]{1,0:T(8,128)(2,1)}, bf16[384,2048]{1,0:T(8,128)(2,1)}, u32[]{:S(2)}, u32[]{:S(2)}) collective-permute-start(bf16[384,2048]{1,0:T(8,128)(2,1)} %get-tuple-element.489), channel_id=1, source_target_pairs={{0,1},{1,0},{2,3},{3,2},{4,5},{5,4},{6,7},{7,6},{8,9},{9,8},{10,11... | collective-permute-start | bytes 4718600 | tf_op jit(solution)/shard_map/ppermute | solution.py:338
  466.6 39.9 %collective-permute-start.70 = (bf16[384,2048]{1,0:T(8,128)(2,1)}, bf16[384,2048]{1,0:T(8,128)(2,1)}, u32[]{:S(2)}, u32[]{:S(2)}) collective-permute-start(bf16[384,2048]{1,0:T(8,128)(2,1)} %mix.28), channel_id=1, source_target_pairs={{0,2},{1,3},{2,6},{3,7},{6,4},{7,5},{4,0},{5,1},{8,10},{9,11},{10,... | collective-permute-start | bytes 4718600 | tf_op jit(solution)/shard_map/ppermute | solution.py:342
  466.6 14.6 %collective-permute-start.75 = (bf16[128,2048]{1,0:T(8,128)(2,1)}, bf16[128,2048]{1,0:T(8,128)(2,1)}, u32[]{:S(2)}, u32[]{:S(2)}) collective-permute-start(bf16[128,2048]{1,0:T(8,128)(2,1)} %fusion.6), channel_id=1, source_target_pairs={{1,17},{3,19},{5,21},{7,23},{9,25},{11,27},{13,29},{15,31},{16,0},... | collective-permute-start | bytes 1572872 | tf_op jit(solution)/shard_map/ppermute | solution.py:1203
  471.2 55.0 %all-to-all-start.1 = ((bf16[8,80,768]{2,1,0:T(8,128)(2,1)}), bf16[8,80,768]{2,1,0:T(8,128)(2,1)}, u32[]{:S(2)}, u32[]{:S(2)}) async-start(bf16[8,80,768]{2,1,0:T(8,128)(2,1)} %fusion.5), calls=%async_computation.1 | async-start | bytes 1966080 | tf_op jit(solution)/shard_map/all_to_all | solution.py:1153
  482.9 35.6 %collective-permute-start.76 = (bf16[64,2048]{1,0:T(8,128)(2,1)S(1)}, bf16[64,2048]{1,0:T(8,128)(2,1)S(1)}, u32[]{:S(2)}, u32[]{:S(2)}) collective-permute-start(bf16[64,2048]{1,0:T(8,128)(2,1)S(1)} %dynamic-slice_convert_fusion.1), channel_id=1, source_target_pairs={{0,1},{2,3},{4,5},{6,7},{8,9},{10,11},{12,13},{14,15},{17,16},{19,... | collective-permute-start | bytes 786440 | tf_op jit(solution)/shard_map/ppermute | solution.py:1212
  509.9 29.2 %collective-permute-start.71 = (bf16[256,2048]{1,0:T(8,128)(2,1)}, bf16[256,2048]{1,0:T(8,128)(2,1)}, u32[]{:S(2)}, u32[]{:S(2)}) collective-permute-start(bf16[256,2048]{1,0:T(8,128)(2,1)} %get-tuple-element.501), channel_id=1, source_target_pairs={{0,1},{1,0},{2,3},{3,2},{4,5},{5,4},{6,7},{7,6},{8,9},{9,8},{10,11... | collective-permute-start | bytes 3145736 | tf_op jit(solution)/shard_map/ppermute | solution.py:338
  513.8 32.5 %collective-permute-start.72 = (bf16[256,2048]{1,0:T(8,128)(2,1)}, bf16[256,2048]{1,0:T(8,128)(2,1)}, u32[]{:S(2)}, u32[]{:S(2)}) collective-permute-start(bf16[256,2048]{1,0:T(8,128)(2,1)} %mix.29), channel_id=1, source_target_pairs={{0,2},{1,3},{2,6},{3,7},{6,4},{7,5},{4,0},{5,1},{8,10},{9,11},{10,... | collective-permute-start | bytes 3145736 | tf_op jit(solution)/shard_map/ppermute | solution.py:342
  (209 other events, 2314.1 us)
Sparse Core Ops, SparseCore 0:
  81.4 29.1 all-gather.3
  112.1 30.9 all-gather.5
  144.7 31.6 all-gather.7

commit v7 on v6

--- a/solution.py
+++ b/solution.py
@@ -1028,6 +1028,20 @@
         cost_estimate=FREE,
         name="branch_back",
     )(*(rows.array for rows in pieces), wo)
+
+
+def result_terms_kernel(inner_ref, weights_ref, out_ref):
+    out_ref[...] = product(inner_ref[...], weights_ref[...]).astype(jnp.bfloat16)
+
+
+def result_terms_of(inner, weights):
+    return pl.pallas_call(
+        result_terms_kernel,
+        out_shape=jax.ShapeDtypeStruct((inner.shape[0], weights.shape[1]), jnp.bfloat16),
+        compiler_params=pltpu.CompilerParams(vmem_limit_bytes=12 * 2**20),
+        cost_estimate=FREE,
+        name="result_terms",
+    )(inner, weights)
 
 
 def add_kernel(*refs):
@@ -1455,7 +1469,7 @@
     outs = Gather(d_branch_low)
     e1 = move([outs])
     def result_terms(step, *gate):
-        return product(after(inners[step], *gate), wd).astype(jnp.bfloat16)
+        return result_terms_of(after(inners[step], *gate), wd)
 
     h1 = gate_sums.along_y(d_branch_low)
     h3 = down_sums.along_core(*h1)

time: 567 us -> 564 us (level)
    unnamed x358 -> x368, local copies, waits for them, and re-layouts: 56.4 us -> 53.3 us
  transfers between devices with their start and end apart: 82 -> 82, of which waited for: 50 -> 54; matrix products, arithmetic and copies ran while one was open for 7% -> 7% of each run, Pallas kernels for 20% -> 20%
where the time goes in v7:
time: 564 us; the launch traced here: 554 us
  waiting for transfers between devices  243 us (43%)
  Pallas kernels  115 us (20%)
  starting transfers between devices  86.7 us (15%)
  local copies, waits for them, and re-layouts  65.9 us (12%)
  other arithmetic  25.3 us (4%)
  between operations  16.4 us (3%)
    ppermute x27, waiting for transfers between devices, x_swap(): return lax.ppermute(value, 'fsdp', swap_pairs(8, 1))  116 us
    ppermute x26, waiting for transfers between devices, ring_step(): return lax.ppermute(value, 'fsdp', ring_pairs())  70.2 us
    unnamed x368, local copies, waits for them, and re-layouts  53.3 us
    ppermute x6, waiting for transfers between devices, y_swap(): return lax.ppermute(value, 'dp', swap_pairs(4, 2))  31.9 us
    ppermute x26, starting transfers between devices, ring_step(): return lax.ppermute(value, 'fsdp', ring_pairs())  31.5 us
    ppermute x27, starting transfers between devices, x_swap(): return lax.ppermute(value, 'fsdp', swap_pairs(8, 1))  30.4 us
    pallas_call x4, Pallas kernels, feed(): pl.pallas_call(functools.partial(feed_kernel, *plans), out_shape=[low, lo...  20 us
    pallas_call x6, Pallas kernels, call(): pl.pallas_call(functools.partial(kernel, len(self.units)), grid=(2,), in_...  16.7 us
  transfers between devices with their start and end apart: 82, of which 54 were waited for; matrix products, arithmetic and copies ran while one was open for 7% of the time, Pallas kernels for 20%

profile of v7, /device:TPU:0, one launch (start us, length us, event | category | flops | bytes accessed | tf_op | source)
XLA Modules:
  0.0 554.4 jit_solution(11602945754959052455)
XLA Ops:
  9.5 3.1 collective-permute-start.1
  15.3 3.9 all-to-all-start
  32.7 5.0 collective-permute-done.1.held_ref
  37.6 3.4 collective-permute-done.refs_0_
  41.0 14.0 %all-to-all-done = bf16[8,208,256]{2,1,0:T(8,128)(2,1)S(1)} async-done(((bf16[8,208,256]{2,1,0:T(8,128)(2,1)}), bf16[8,208,256]{2,1,0:T(8,128)(2,1)S(1)}, u32[]{:S(2)}, u32[]{:S(2)}) %all-to-all-start) | async-done | bytes 852000 | tf_op jit(solution)/shard_map/all_to_all | solution.py:703
  60.8 18.2 %collective-permute-done.2.refs_2_ = bf16[1664,256]{1,0:T(8,128)(2,1)} collective-permute-done((bf16[1664,256]{1,0:T(8,128)(2,1)S(1)}, bf16[1664,256]{1,0:T(8,128)(2,1)}, u32[]{:S(2)}, u32[]{:S(2)}) %collective-permute-start.2) | collective-permute-done | bytes 852000 | tf_op jit(solution)/shard_map/ppermute | solution.py:346
  86.2 3.1 collective-permute-done.13
  103.9 7.0 %collective-permute-done.7.refs_0_.refs_1_ = bf16[256,2048]{1,0:T(8,128)(2,1)} collective-permute-done((bf16[256,2048]{1,0:T(8,128)(2,1)}, bf16[256,2048]{1,0:T(8,128)(2,1)}, u32[]{:S(2)}, u32[]{:S(2)}) %collective-permute-start.7) | collective-permute-done | bytes 1048608 | tf_op jit(solution)/shard_map/ppermute | solution.py:338
  111.5 3.7 collective-permute-start.14
  118.9 3.1 project.6
  124.1 5.8 %collective-permute-done.9.refs_0_ = bf16[128,2048]{1,0:T(8,128)(2,1)S(1)} collective-permute-done((bf16[128,2048]{1,0:T(8,128)(2,1)S(1)}, bf16[128,2048]{1,0:T(8,128)(2,1)S(1)}, u32[]{:S(2)}, u32[]{:S(2)}) %collective-permute-start.9) | collective-permute-done | bytes 524320 | tf_op jit(solution)/shard_map/ppermute | solution.py:338
  136.1 6.8 %collective-permute-done.11.refs_3_ = bf16[128,2048]{1,0:T(8,128)(2,1)S(1)} collective-permute-done((bf16[128,2048]{1,0:T(8,128)(2,1)S(1)}, bf16[128,2048]{1,0:T(8,128)(2,1)S(1)}, u32[]{:S(2)}, u32[]{:S(2)}) %collective-permute-start.11) | collective-permute-done | bytes 524320 | tf_op jit(solution)/shard_map/ppermute | solution.py:338
  146.8 7.5 %attend.1 = (f32[1024,256]{1,0:T(8,128)S(1)}, bf16[1024,256]{1,0:T(8,128)(2,1)S(1)}, f32[2,1024,1]{2,1,0:T(8,128)S(1)}) custom-call(bf16[1024,256]{1,0:T(8,128)(2,1)S(1)} %constant_dynamic-update-slice_fusion.2.q_ref, bf16[1024,512]{1,0:T(8,128)(2,1)S(1)} %constant_dynamic-update-slice_fusion.6.k_ref.v_ref, ...), custom_call_target="tpu_custom_call" | custom-call | flops 20000000000 | tf_op jit(solution)/shard_map/attend/pallas_call | solution.py:594
  155.7 4.8 collective-permute-done.16.refs_1_.refs_2_
  164.7 16.1 %collective-permute-done.18.refs_1_.refs_3_ = bf16[192,2048]{1,0:T(8,128)(2,1)S(1)} collective-permute-done((bf16[192,2048]{1,0:T(8,128)(2,1)S(1)}, bf16[192,2048]{1,0:T(8,128)(2,1)S(1)}, u32[]{:S(2)}, u32[]{:S(2)}) %collective-permute-start.18) | collective-permute-done | bytes 786464 | tf_op jit(solution)/shard_map/ppermute | solution.py:342
  185.7 15.0 %collective-permute-done.20.refs_2_.refs_4_ = bf16[192,2048]{1,0:T(8,128)(2,1)S(1)} collective-permute-done((bf16[192,2048]{1,0:T(8,128)(2,1)S(1)}, bf16[192,2048]{1,0:T(8,128)(2,1)S(1)}, u32[]{:S(2)}, u32[]{:S(2)}) %collective-permute-start.20) | collective-permute-done | bytes 786464 | tf_op jit(solution)/shard_map/ppermute | solution.py:338
  205.0 8.1 %collective-permute-done.22.refs_2_ = bf16[128,2048]{1,0:T(8,128)(2,1)S(1)} collective-permute-done((bf16[128,2048]{1,0:T(8,128)(2,1)S(1)}, bf16[128,2048]{1,0:T(8,128)(2,1)S(1)}, u32[]{:S(2)}, u32[]{:S(2)}) %collective-permute-start.22) | collective-permute-done | bytes 524320 | tf_op jit(solution)/shard_map/ppermute | solution.py:338
  216.6 8.5 %collective-permute-done.24 = bf16[128,2048]{1,0:T(8,128)(2,1)S(1)} collective-permute-done((bf16[128,2048]{1,0:T(8,128)(2,1)S(1)}, bf16[128,2048]{1,0:T(8,128)(2,1)S(1)}, u32[]{:S(2)}, u32[]{:S(2)}) %collective-permute-start.24) | collective-permute-done | bytes 524320 | tf_op jit(solution)/shard_map/ppermute | solution.py:338
  242.9 3.5 collective-permute-start.29
  248.5 5.7 %feed.4 = (bf16[256,768]{1,0:T(8,128)(2,1)S(1)}, bf16[256,768]{1,0:T(8,128)(2,1)S(1)}, bf16[256,768]{1,0:T(8,128)(2,1)S(1)}, bf16[128,2048]{1,0:T(8,128)(2,1)S(1...) custom-call(bf16[128,2048]{1,0:T(8,128)(2,1)} %multiply_convert_fusion.refs_0_, ...), custom_call_target="tpu_custom_call" | custom-call | flops 20000000000 | tf_op jit(solution)/shard_map/feed/pallas_call | solution.py:1000
  259.2 5.5 feed.5
  266.7 3.3 collective-permute-done.31.refs_0_
  272.2 4.4 feed.6
  276.6 6.8 %collective-permute-done.32.refs_1_.refs_3_ = bf16[128,2048]{1,0:T(8,128)(2,1)S(1)} collective-permute-done((bf16[128,2048]{1,0:T(8,128)(2,1)S(1)}, bf16[128,2048]{1,0:T(8,128)(2,1)S(1)}, u32[]{:S(2)}, u32[]{:S(2)}) %collective-permute-start.32) | collective-permute-done | bytes 524320 | tf_op jit(solution)/shard_map/ppermute | solution.py:338
  287.2 4.4 feed.7
  291.7 8.2 %collective-permute-done.34.refs_1_ = bf16[128,2048]{1,0:T(8,128)(2,1)S(1)} collective-permute-done((bf16[128,2048]{1,0:T(8,128)(2,1)S(1)}, bf16[128,2048]{1,0:T(8,128)(2,1)S(1)}, u32[]{:S(2)}, u32[]{:S(2)}) %collective-permute-start.34) | collective-permute-done | bytes 524320 | tf_op jit(solution)/shard_map/ppermute | solution.py:338
  306.3 8.1 %collective-permute-done.36.refs_1_ = bf16[128,2048]{1,0:T(8,128)(2,1)S(1)} collective-permute-done((bf16[128,2048]{1,0:T(8,128)(2,1)S(1)}, bf16[128,2048]{1,0:T(8,128)(2,1)S(1)}, u32[]{:S(2)}, u32[]{:S(2)}) %collective-permute-start.36) | collective-permute-done | bytes 524320 | tf_op jit(solution)/shard_map/ppermute | solution.py:338
  320.1 4.7 collective-permute-done.38
  334.5 3.2 hidden_grads.10
  337.7 5.3 collective-permute-done.43.refs_0_
  354.7 3.6 collective-permute-done.54
  368.8 3.6 hidden_grads.11
  386.8 2.9 collective-permute-done.55.refs_1_.refs_3_
  393.7 10.0 %attend_back.1 = (bf16[1024,256]{1,0:T(8,128)(2,1)S(1)}, bf16[1024,512]{1,0:T(8,128)(2,1)S(1)}) custom-call(bf16[1024,256]{1,0:T(8,128)(2,1)S(1)} %copy-done.105, bf16[1024,512]{1,0:T(8,128)(2,1)S(1)} %copy-done.103, bf16[1024,512]{1,0:T(8,128)(2,1)S(1)} %copy-done.103, s32[1024,1]{1,0:T(8,128)S(1)} %copy-done.77, s32[1024,1]{1,0:T(8,128)S(1)} %copy-done.73, ...), custom_call_target="tpu_custom_call" | custom-call | flops 20000000000 | tf_op jit(solution)/shard_map/attend_back/pallas_call | solution.py:613
  411.2 6.5 %column_grads.1 = (bf16[512,256]{1,0:T(8,128)(2,1)S(1)}, bf16[512,512]{1,0:T(8,128)(2,1)}, bf16[512,256]{1,0:T(8,128)(2,1)}, bf16[512,512]{1,0:T(8,128)(2,1)}, f32[2,512,768]{2,1,0:T(8,128)S(1)}) custom-call(s32[1]{0:T(128)} %bitcast.dp_ref, bf16[256,2048]{1,0:T(8,128)(2,1)S(1)} %copy-done.109, bf16[256,2048]{1,0:T(8,128)(2,1)S(1)} %copy-done.113, ...), custom_call_target="tpu_custom_call" | custom-call | flops 20000000000 | tf_op jit(solution)/shard_map/column_grads/pallas_call | solution.py:1121
  439.8 3.0 back_terms.6
  445.8 8.1 %collective-permute-done.68 = bf16[512,768]{1,0:T(8,128)(2,1)} collective-permute-done((bf16[512,768]{1,0:T(8,128)(2,1)}, bf16[512,768]{1,0:T(8,128)(2,1)}, u32[]{:S(2)}, u32[]{:S(2)}) %collective-permute-start.68) | collective-permute-done | bytes 786464 | tf_op jit(solution)/shard_map/ppermute | solution.py:346
  453.9 3.8 collective-permute-done.65.refs_1_
  460.0 3.7 mix.28
  468.5 7.3 %all-to-all-start.1 = ((bf16[8,80,768]{2,1,0:T(8,128)(2,1)}), bf16[8,80,768]{2,1,0:T(8,128)(2,1)}, u32[]{:S(2)}, u32[]{:S(2)}) async-start(bf16[8,80,768]{2,1,0:T(8,128)(2,1)} %fusion.5), calls=%async_computation.1 | async-start | bytes 1966080 | tf_op jit(solution)/shard_map/all_to_all | solution.py:1167
  484.9 18.6 %collective-permute-done.69.x_ref.refs_1_ = bf16[384,2048]{1,0:T(8,128)(2,1)} collective-permute-done((bf16[384,2048]{1,0:T(8,128)(2,1)}, bf16[384,2048]{1,0:T(8,128)(2,1)}, u32[]{:S(2)}, u32[]{:S(2)}) %collective-permute-start.69) | collective-permute-done | bytes 1572896 | tf_op jit(solution)/shard_map/ppermute | solution.py:338
  504.0 3.4 mix.29
  507.3 4.4 collective-permute-start.71
  513.9 2.9 add_all.1
  517.5 6.2 %all-to-all-done.1.got_ref = bf16[8,80,768]{2,1,0:T(8,128)(2,1)} async-done(((bf16[8,80,768]{2,1,0:T(8,128)(2,1)}), bf16[8,80,768]{2,1,0:T(8,128)(2,1)}, u32[]{:S(2)}, u32[]{:S(2)}) %all-to-all-start.1) | async-done | bytes 983072 | tf_op jit(solution)/shard_map/all_to_all | solution.py:1167
  529.4 3.6 result.1
  535.1 8.1 %collective-permute-done.72.refs_2_.refs_5_ = bf16[256,2048]{1,0:T(8,128)(2,1)} collective-permute-done((bf16[256,2048]{1,0:T(8,128)(2,1)}, bf16[256,2048]{1,0:T(8,128)(2,1)}, u32[]{:S(2)}, u32[]{:S(2)}) %collective-permute-start.72) | collective-permute-done | bytes 1048608 | tf_op jit(solution)/shard_map/ppermute | solution.py:342
  543.2 4.2 input_grads.1
  (611 shorter events, 234.0 us)
Async XLA Ops:
  9.5 28.1 %collective-permute-start.1 = (bf16[256,2048]{1,0:T(8,128)(2,1)S(1)}, bf16[256,2048]{1,0:T(8,128)(2,1)S(1)}, u32[]{:S(2)}, u32[]{:S(2)}) collective-permute-start(bf16[256,2048]{1,0:T(8,128)(2,1)S(1)} %constant_dynamic-update-slice_fusion.held_ref), channel_id=1, source_target_pairs={{0,2},{1,3},{2,6},{3,7},{6,4},{7,5},{4,0},{5,1},{8,10},{9,11},{10,... | collective-permute-start | bytes 3145736 | tf_op jit(solution)/shard_map/ppermute | solution.py:342
  12.6 28.5 %collective-permute-start = (bf16[256,2048]{1,0:T(8,128)(2,1)S(1)}, bf16[256,2048]{1,0:T(8,128)(2,1)}, u32[]{:S(2)}, u32[]{:S(2)}) collective-permute-start(bf16[256,2048]{1,0:T(8,128)(2,1)S(1)} %constant_dynamic-update-slice_fusion.held_ref), channel_id=1, source_target_pairs={{0,1},{1,0},{2,3},{3,2},{4,5},{5,4},{6,7},{7,6},{8,9},{9,8},{10,11... | collective-permute-start | bytes 3145736 | tf_op jit(solution)/shard_map/ppermute | solution.py:338
  15.3 39.8 %all-to-all-start = ((bf16[8,208,256]{2,1,0:T(8,128)(2,1)}), bf16[8,208,256]{2,1,0:T(8,128)(2,1)S(1)}, u32[]{:S(2)}, u32[]{:S(2)}) async-start(bf16[8,208,256]{2,1,0:T(8,128)(2,1)} %bitcast.79), calls=%async_computation | async-start | bytes 1703936 | tf_op jit(solution)/shard_map/all_to_all | solution.py:703
  19.1 213.0 %all-gather.4.cloned.1.call-start = ((), (), s32[]{:S(2)}) async-start(), calls=%async_computation.2 | async-start | bytes 3932160 | tf_op jit(solution)/shard_map/all_gather | solution.py:1230
  55.0 24.3 %collective-permute-start.5 = (bf16[256,2048]{1,0:T(8,128)(2,1)S(1)}, bf16[256,2048]{1,0:T(8,128)(2,1)S(1)}, u32[]{:S(2)}, u32[]{:S(2)}) collective-permute-start(bf16[256,2048]{1,0:T(8,128)(2,1)S(1)} %collective-permute-done.1.held_ref), channel_id=1, source_target_pairs={{0,1},{1,0},{2,3},{3,2},{4,5},{5,4},{6,7},{7,6},{8,9},{9,8},{10,11... | collective-permute-start | bytes 3145736 | tf_op jit(solution)/shard_map/ppermute | solution.py:338
  56.6 24.5 %collective-permute-start.6 = (bf16[256,2048]{1,0:T(8,128)(2,1)S(1)}, bf16[256,2048]{1,0:T(8,128)(2,1)}, u32[]{:S(2)}, u32[]{:S(2)}) collective-permute-start(bf16[256,2048]{1,0:T(8,128)(2,1)S(1)} %collective-permute-done.1.held_ref), channel_id=1, source_target_pairs={{0,2},{1,3},{2,6},{3,7},{6,4},{7,5},{4,0},{5,1},{8,10},{9,11},{10,... | collective-permute-start | bytes 3145736 | tf_op jit(solution)/shard_map/ppermute | solution.py:342
  57.5 21.5 %collective-permute-start.2 = (bf16[1664,256]{1,0:T(8,128)(2,1)S(1)}, bf16[1664,256]{1,0:T(8,128)(2,1)}, u32[]{:S(2)}, u32[]{:S(2)}) collective-permute-start(bf16[1664,256]{1,0:T(8,128)(2,1)S(1)} %bitcast.77), channel_id=1, source_target_pairs={{0,16},{8,24},{16,0},{24,8},{1,17},{9,25},{17,1},{25,9},{2,18},{10... | collective-permute-start | bytes 2555912 | tf_op jit(solution)/shard_map/ppermute | solution.py:346
  81.1 155.0 %all-gather.6.cloned.1.call-start = ((), (), s32[]{:S(2)}) async-start(), calls=%async_computation.3 | async-start | bytes 3932160 | tf_op jit(solution)/shard_map/all_gather | solution.py:1230
  81.8 158.2 %all-gather.8.cloned.1.call-start = ((), (), s32[]{:S(2)}) async-start(), calls=%async_computation.4 | async-start | bytes 3932160 | tf_op jit(solution)/shard_map/all_gather | solution.py:1230
  84.1 26.8 %collective-permute-start.7 = (bf16[256,2048]{1,0:T(8,128)(2,1)}, bf16[256,2048]{1,0:T(8,128)(2,1)}, u32[]{:S(2)}, u32[]{:S(2)}) collective-permute-start(bf16[256,2048]{1,0:T(8,128)(2,1)} %collective-permute-done.6.held_ref), channel_id=1, source_target_pairs={{0,1},{1,0},{2,3},{3,2},{4,5},{5,4},{6,7},{7,6},{8,9},{9,8},{10,11... | collective-permute-start | bytes 3145736 | tf_op jit(solution)/shard_map/ppermute | solution.py:338
  85.0 26.5 %collective-permute-start.8 = (bf16[256,2048]{1,0:T(8,128)(2,1)}, bf16[256,2048]{1,0:T(8,128)(2,1)}, u32[]{:S(2)}, u32[]{:S(2)}) collective-permute-start(bf16[256,2048]{1,0:T(8,128)(2,1)} %collective-permute-done.6.held_ref), channel_id=1, source_target_pairs={{0,2},{1,3},{2,6},{3,7},{6,4},{7,5},{4,0},{5,1},{8,10},{9,11},{10,... | collective-permute-start | bytes 3145736 | tf_op jit(solution)/shard_map/ppermute | solution.py:342
  111.5 24.6 %collective-permute-start.14 = (bf16[128,2048]{1,0:T(8,128)(2,1)S(1)}, bf16[128,2048]{1,0:T(8,128)(2,1)S(1)}, u32[]{:S(2)}, u32[]{:S(2)}) collective-permute-start(bf16[128,2048]{1,0:T(8,128)(2,1)S(1)} %copy-done.168), channel_id=1, source_target_pairs={{0,16},{2,18},{4,20},{6,22},{8,24},{10,26},{12,28},{14,30},{17,1},... | collective-permute-start | bytes 1572872 | tf_op jit(solution)/shard_map/ppermute | solution.py:1197
  117.0 13.9 %collective-permute-start.10 = (bf16[128,2048]{1,0:T(8,128)(2,1)S(1)}, bf16[128,2048]{1,0:T(8,128)(2,1)S(1)}, u32[]{:S(2)}, u32[]{:S(2)}) collective-permute-start(bf16[128,2048]{1,0:T(8,128)(2,1)S(1)} %get-tuple-element.292), channel_id=1, source_target_pairs={{0,2},{1,3},{2,6},{3,7},{6,4},{7,5},{4,0},{5,1},{8,10},{9,11},{10,... | collective-permute-start | bytes 1572872 | tf_op jit(solution)/shard_map/ppermute | solution.py:342
  145.1 15.4 %collective-permute-start.16 = (bf16[128,2048]{1,0:T(8,128)(2,1)S(1)}, bf16[128,2048]{1,0:T(8,128)(2,1)S(1)}, u32[]{:S(2)}, u32[]{:S(2)}) collective-permute-start(bf16[128,2048]{1,0:T(8,128)(2,1)S(1)} %collective-permute-done.12.refs_2_), channel_id=1, source_target_pairs={{0,2},{1,3},{2,6},{3,7},{6,4},{7,5},{4,0},{5,1},{8,10},{9,11},{10,... | collective-permute-start | bytes 1572872 | tf_op jit(solution)/shard_map/ppermute | solution.py:342
  146.2 14.5 %collective-permute-start.17 = (bf16[128,2048]{1,0:T(8,128)(2,1)S(1)}, bf16[128,2048]{1,0:T(8,128)(2,1)S(1)}, u32[]{:S(2)}, u32[]{:S(2)}) collective-permute-start(bf16[128,2048]{1,0:T(8,128)(2,1)S(1)} %collective-permute-done.12.refs_2_), channel_id=1, source_target_pairs={{0,1},{1,0},{2,3},{3,2},{4,5},{5,4},{6,7},{7,6},{8,9},{9,8},{10,11... | collective-permute-start | bytes 1572872 | tf_op jit(solution)/shard_map/ppermute | solution.py:338
  160.7 20.0 %collective-permute-start.18 = (bf16[192,2048]{1,0:T(8,128)(2,1)S(1)}, bf16[192,2048]{1,0:T(8,128)(2,1)S(1)}, u32[]{:S(2)}, u32[]{:S(2)}) collective-permute-start(bf16[192,2048]{1,0:T(8,128)(2,1)S(1)} %get-tuple-element.313), channel_id=1, source_target_pairs={{0,2},{1,3},{2,6},{3,7},{6,4},{7,5},{4,0},{5,1},{8,10},{9,11},{10,... | collective-permute-start | bytes 2359304 | tf_op jit(solution)/shard_map/ppermute | solution.py:342
  163.6 18.6 %collective-permute-start.19 = (bf16[192,2048]{1,0:T(8,128)(2,1)S(1)}, bf16[192,2048]{1,0:T(8,128)(2,1)S(1)}, u32[]{:S(2)}, u32[]{:S(2)}) collective-permute-start(bf16[192,2048]{1,0:T(8,128)(2,1)S(1)} %get-tuple-element.314), channel_id=1, source_target_pairs={{0,1},{1,0},{2,3},{3,2},{4,5},{5,4},{6,7},{7,6},{8,9},{9,8},{10,11... | collective-permute-start | bytes 2359304 | tf_op jit(solution)/shard_map/ppermute | solution.py:338
  183.0 17.7 %collective-permute-start.20 = (bf16[192,2048]{1,0:T(8,128)(2,1)S(1)}, bf16[192,2048]{1,0:T(8,128)(2,1)S(1)}, u32[]{:S(2)}, u32[]{:S(2)}) collective-permute-start(bf16[192,2048]{1,0:T(8,128)(2,1)S(1)} %get-tuple-element.317), channel_id=1, source_target_pairs={{0,1},{1,0},{2,3},{3,2},{4,5},{5,4},{6,7},{7,6},{8,9},{9,8},{10,11... | collective-permute-start | bytes 2359304 | tf_op jit(solution)/shard_map/ppermute | solution.py:338
  183.7 18.3 %collective-permute-start.21 = (bf16[192,2048]{1,0:T(8,128)(2,1)S(1)}, bf16[192,2048]{1,0:T(8,128)(2,1)S(1)}, u32[]{:S(2)}, u32[]{:S(2)}) collective-permute-start(bf16[192,2048]{1,0:T(8,128)(2,1)S(1)} %get-tuple-element.318), channel_id=1, source_target_pairs={{0,2},{1,3},{2,6},{3,7},{6,4},{7,5},{4,0},{5,1},{8,10},{9,11},{10,... | collective-permute-start | bytes 2359304 | tf_op jit(solution)/shard_map/ppermute | solution.py:342
  256.4 13.6 %collective-permute-start.31 = (bf16[128,2048]{1,0:T(8,128)(2,1)S(1)}, bf16[128,2048]{1,0:T(8,128)(2,1)S(1)}, u32[]{:S(2)}, u32[]{:S(2)}) collective-permute-start(bf16[128,2048]{1,0:T(8,128)(2,1)S(1)} %collective-permute-done.29.refs_0_), channel_id=1, source_target_pairs={{0,2},{1,3},{2,6},{3,7},{6,4},{7,5},{4,0},{5,1},{8,10},{9,11},{10,... | collective-permute-start | bytes 1572872 | tf_op jit(solution)/shard_map/ppermute | solution.py:342
  270.8 14.3 %collective-permute-start.33 = (bf16[128,2048]{1,0:T(8,128)(2,1)S(1)}, bf16[128,2048]{1,0:T(8,128)(2,1)S(1)}, u32[]{:S(2)}, u32[]{:S(2)}) collective-permute-start(bf16[128,2048]{1,0:T(8,128)(2,1)S(1)} %get-tuple-element.350), channel_id=1, source_target_pairs={{0,2},{1,3},{2,6},{3,7},{6,4},{7,5},{4,0},{5,1},{8,10},{9,11},{10,... | collective-permute-start | bytes 1572872 | tf_op jit(solution)/shard_map/ppermute | solution.py:342
  285.2 14.6 %collective-permute-start.34 = (bf16[128,2048]{1,0:T(8,128)(2,1)S(1)}, bf16[128,2048]{1,0:T(8,128)(2,1)S(1)}, u32[]{:S(2)}, u32[]{:S(2)}) collective-permute-start(bf16[128,2048]{1,0:T(8,128)(2,1)S(1)} %get-tuple-element.364), channel_id=1, source_target_pairs={{0,1},{1,0},{2,3},{3,2},{4,5},{5,4},{6,7},{7,6},{8,9},{9,8},{10,11... | collective-permute-start | bytes 1572872 | tf_op jit(solution)/shard_map/ppermute | solution.py:338
  286.7 15.7 %collective-permute-start.35 = (bf16[128,2048]{1,0:T(8,128)(2,1)S(1)}, bf16[128,2048]{1,0:T(8,128)(2,1)S(1)}, u32[]{:S(2)}, u32[]{:S(2)}) collective-permute-start(bf16[128,2048]{1,0:T(8,128)(2,1)S(1)} %get-tuple-element.365), channel_id=1, source_target_pairs={{0,2},{1,3},{2,6},{3,7},{6,4},{7,5},{4,0},{5,1},{8,10},{9,11},{10,... | collective-permute-start | bytes 1572872 | tf_op jit(solution)/shard_map/ppermute | solution.py:342
  305.7 24.9 %collective-permute-start.40 = (bf16[192,2048]{1,0:T(8,128)(2,1)S(1)}, bf16[192,2048]{1,0:T(8,128)(2,1)S(1)}, u32[]{:S(2)}, u32[]{:S(2)}) collective-permute-start(bf16[192,2048]{1,0:T(8,128)(2,1)S(1)} %get-tuple-element.376), channel_id=1, source_target_pairs={{0,8},{8,0},{16,24},{24,16},{1,9},{9,1},{17,25},{25,17},{2,10},{10... | collective-permute-start | bytes 2359304 | tf_op jit(solution)/shard_map/ppermute | solution.py:350
  305.8 25.0 %collective-permute-start.41 = (bf16[192,2048]{1,0:T(8,128)(2,1)S(1)}, bf16[192,2048]{1,0:T(8,128)(2,1)S(1)}, u32[]{:S(2)}, u32[]{:S(2)}) collective-permute-start(bf16[192,2048]{1,0:T(8,128)(2,1)S(1)} %get-tuple-element.377), channel_id=1, source_target_pairs={{0,8},{8,0},{16,24},{24,16},{1,9},{9,1},{17,25},{25,17},{2,10},{10... | collective-permute-start | bytes 2359304 | tf_op jit(solution)/shard_map/ppermute | solution.py:350
  320.0 25.2 %collective-permute-start.44 = (bf16[192,2048]{1,0:T(8,128)(2,1)S(1)}, bf16[192,2048]{1,0:T(8,128)(2,1)S(1)}, u32[]{:S(2)}, u32[]{:S(2)}) collective-permute-start(bf16[192,2048]{1,0:T(8,128)(2,1)S(1)} %get-tuple-element.388), channel_id=1, source_target_pairs={{0,8},{8,0},{16,24},{24,16},{1,9},{9,1},{17,25},{25,17},{2,10},{10... | collective-permute-start | bytes 2359304 | tf_op jit(solution)/shard_map/ppermute | solution.py:350
  324.7 22.3 %collective-permute-start.45 = (bf16[192,2048]{1,0:T(8,128)(2,1)S(1)}, bf16[192,2048]{1,0:T(8,128)(2,1)S(1)}, u32[]{:S(2)}, u32[]{:S(2)}) collective-permute-start(bf16[192,2048]{1,0:T(8,128)(2,1)S(1)} %get-tuple-element.389), channel_id=1, source_target_pairs={{0,8},{8,0},{16,24},{24,16},{1,9},{9,1},{17,25},{25,17},{2,10},{10... | collective-permute-start | bytes 2359304 | tf_op jit(solution)/shard_map/ppermute | solution.py:350
  337.7 23.2 %collective-permute-start.48 = (bf16[192,2048]{1,0:T(8,128)(2,1)}, bf16[192,2048]{1,0:T(8,128)(2,1)}, u32[]{:S(2)}, u32[]{:S(2)}) collective-permute-start(bf16[192,2048]{1,0:T(8,128)(2,1)} %get-tuple-element.413), channel_id=1, source_target_pairs={{0,8},{8,0},{16,24},{24,16},{1,9},{9,1},{17,25},{25,17},{2,10},{10... | collective-permute-start | bytes 2359304 | tf_op jit(solution)/shard_map/ppermute | solution.py:350
  343.1 17.9 %collective-permute-start.49 = (bf16[192,2048]{1,0:T(8,128)(2,1)}, bf16[192,2048]{1,0:T(8,128)(2,1)}, u32[]{:S(2)}, u32[]{:S(2)}) collective-permute-start(bf16[192,2048]{1,0:T(8,128)(2,1)} %get-tuple-element.414), channel_id=1, source_target_pairs={{0,8},{8,0},{16,24},{24,16},{1,9},{9,1},{17,25},{25,17},{2,10},{10... | collective-permute-start | bytes 2359304 | tf_op jit(solution)/shard_map/ppermute | solution.py:350
  343.1 15.3 %collective-permute-start.46 = (bf16[128,2048]{1,0:T(8,128)(2,1)}, bf16[128,2048]{1,0:T(8,128)(2,1)}, u32[]{:S(2)}, u32[]{:S(2)}) collective-permute-start(bf16[128,2048]{1,0:T(8,128)(2,1)} %collective-permute-done.43.refs_0_), channel_id=1, source_target_pairs={{0,1},{1,0},{2,3},{3,2},{4,5},{5,4},{6,7},{7,6},{8,9},{9,8},{10,11... | collective-permute-start | bytes 1572872 | tf_op jit(solution)/shard_map/ppermute | solution.py:338
  345.2 15.4 %collective-permute-start.47 = (bf16[128,2048]{1,0:T(8,128)(2,1)}, bf16[128,2048]{1,0:T(8,128)(2,1)}, u32[]{:S(2)}, u32[]{:S(2)}) collective-permute-start(bf16[128,2048]{1,0:T(8,128)(2,1)} %collective-permute-done.43.refs_0_), channel_id=1, source_target_pairs={{0,2},{1,3},{2,6},{3,7},{6,4},{7,5},{4,0},{5,1},{8,10},{9,11},{10,... | collective-permute-start | bytes 1572872 | tf_op jit(solution)/shard_map/ppermute | solution.py:342
  358.3 19.1 %collective-permute-start.50 = (bf16[192,2048]{1,0:T(8,128)(2,1)}, bf16[192,2048]{1,0:T(8,128)(2,1)S(1)}, u32[]{:S(2)}, u32[]{:S(2)}) collective-permute-start(bf16[192,2048]{1,0:T(8,128)(2,1)} %copy-done.124), channel_id=1, source_target_pairs={{0,16},{8,24},{16,0},{24,8},{1,17},{9,25},{17,1},{25,9},{2,18},{10... | collective-permute-start | bytes 2359304 | tf_op jit(solution)/shard_map/ppermute | solution.py:346
  360.6 13.4 %collective-permute-start.51 = (bf16[128,2048]{1,0:T(8,128)(2,1)}, bf16[128,2048]{1,0:T(8,128)(2,1)S(1)}, u32[]{:S(2)}, u32[]{:S(2)}) collective-permute-start(bf16[128,2048]{1,0:T(8,128)(2,1)} %collective-permute-done.47.refs_0_), channel_id=1, source_target_pairs={{0,1},{1,0},{2,3},{3,2},{4,5},{5,4},{6,7},{7,6},{8,9},{9,8},{10,11... | collective-permute-start | bytes 1572872 | tf_op jit(solution)/shard_map/ppermute | solution.py:338
  360.9 14.3 %collective-permute-start.52 = (bf16[128,2048]{1,0:T(8,128)(2,1)}, bf16[128,2048]{1,0:T(8,128)(2,1)S(1)}, u32[]{:S(2)}, u32[]{:S(2)}) collective-permute-start(bf16[128,2048]{1,0:T(8,128)(2,1)} %collective-permute-done.47.refs_0_), channel_id=1, source_target_pairs={{0,2},{1,3},{2,6},{3,7},{6,4},{7,5},{4,0},{5,1},{8,10},{9,11},{10,... | collective-permute-start | bytes 1572872 | tf_op jit(solution)/shard_map/ppermute | solution.py:342
  379.0 26.6 %collective-permute-start.59 = (bf16[192,2048]{1,0:T(8,128)(2,1)S(1)}, bf16[192,2048]{1,0:T(8,128)(2,1)S(1)}, u32[]{:S(2)}, u32[]{:S(2)}) collective-permute-start(bf16[192,2048]{1,0:T(8,128)(2,1)S(1)} %copy-done.123), channel_id=1, source_target_pairs={{0,16},{8,24},{16,0},{24,8},{1,17},{9,25},{17,1},{25,9},{2,18},{10... | collective-permute-start | bytes 2359304 | tf_op jit(solution)/shard_map/ppermute | solution.py:346
  380.8 40.4 %collective-permute-start.64 = (bf16[192,2048]{1,0:T(8,128)(2,1)S(1)}, bf16[192,2048]{1,0:T(8,128)(2,1)S(1)}, u32[]{:S(2)}, u32[]{:S(2)}) collective-permute-start(bf16[192,2048]{1,0:T(8,128)(2,1)S(1)} %get-tuple-element.434), channel_id=1, source_target_pairs={{0,16},{8,24},{16,0},{24,8},{1,17},{9,25},{17,1},{25,9},{2,18},{10... | collective-permute-start | bytes 2359304 | tf_op jit(solution)/shard_map/ppermute | solution.py:346
  422.1 35.6 %collective-permute-start.65 = (bf16[384,2048]{1,0:T(8,128)(2,1)}, bf16[384,2048]{1,0:T(8,128)(2,1)}, u32[]{:S(2)}, u32[]{:S(2)}) collective-permute-start(bf16[384,2048]{1,0:T(8,128)(2,1)} %get-tuple-element.481), channel_id=1, source_target_pairs={{0,1},{1,0},{2,3},{3,2},{4,5},{5,4},{6,7},{7,6},{8,9},{9,8},{10,11... | collective-permute-start | bytes 4718600 | tf_op jit(solution)/shard_map/ppermute | solution.py:338
  423.2 36.8 %collective-permute-start.66 = (bf16[384,2048]{1,0:T(8,128)(2,1)}, bf16[384,2048]{1,0:T(8,128)(2,1)}, u32[]{:S(2)}, u32[]{:S(2)}) collective-permute-start(bf16[384,2048]{1,0:T(8,128)(2,1)} %get-tuple-element.482), channel_id=1, source_target_pairs={{0,2},{1,3},{2,6},{3,7},{6,4},{7,5},{4,0},{5,1},{8,10},{9,11},{10,... | collective-permute-start | bytes 4718600 | tf_op jit(solution)/shard_map/ppermute | solution.py:342
  433.6 20.3 %collective-permute-start.68 = (bf16[512,768]{1,0:T(8,128)(2,1)}, bf16[512,768]{1,0:T(8,128)(2,1)}, u32[]{:S(2)}, u32[]{:S(2)}) collective-permute-start(bf16[512,768]{1,0:T(8,128)(2,1)} %fusion.3), channel_id=1, source_target_pairs={{0,16},{8,24},{16,0},{24,8},{1,17},{9,25},{17,1},{25,9},{2,18},{10... | collective-permute-start | bytes 2359304 | tf_op jit(solution)/shard_map/ppermute | solution.py:346
  434.5 31.3 %collective-permute-start.73 = (bf16[512,256]{1,0:T(8,128)(2,1)}, bf16[512,256]{1,0:T(8,128)(2,1)}, u32[]{:S(2)}, u32[]{:S(2)}) collective-permute-start(bf16[512,256]{1,0:T(8,128)(2,1)} %copy-done.131), channel_id=1, source_target_pairs={{0,8},{8,0},{16,24},{24,16},{1,9},{9,1},{17,25},{25,17},{2,10},{10... | collective-permute-start | bytes 786440 | tf_op jit(solution)/shard_map/ppermute | solution.py:350
  442.8 23.0 %collective-permute-start.74 = (bf16[512,512]{1,0:T(8,128)(2,1)}, bf16[512,512]{1,0:T(8,128)(2,1)}, u32[]{:S(2)}, u32[]{:S(2)}) collective-permute-start(bf16[512,512]{1,0:T(8,128)(2,1)} %get-tuple-element.506), channel_id=1, source_target_pairs={{0,8},{8,0},{16,24},{24,16},{1,9},{9,1},{17,25},{25,17},{2,10},{10... | collective-permute-start | bytes 1572872 | tf_op jit(solution)/shard_map/ppermute | solution.py:350
  463.7 39.7 %collective-permute-start.69 = (bf16[384,2048]{1,0:T(8,128)(2,1)}, bf16[384,2048]{1,0:T(8,128)(2,1)}, u32[]{:S(2)}, u32[]{:S(2)}) collective-permute-start(bf16[384,2048]{1,0:T(8,128)(2,1)} %get-tuple-element.489), channel_id=1, source_target_pairs={{0,1},{1,0},{2,3},{3,2},{4,5},{5,4},{6,7},{7,6},{8,9},{9,8},{10,11... | collective-permute-start | bytes 4718600 | tf_op jit(solution)/shard_map/ppermute | solution.py:338
  464.0 39.9 %collective-permute-start.70 = (bf16[384,2048]{1,0:T(8,128)(2,1)}, bf16[384,2048]{1,0:T(8,128)(2,1)}, u32[]{:S(2)}, u32[]{:S(2)}) collective-permute-start(bf16[384,2048]{1,0:T(8,128)(2,1)} %mix.28), channel_id=1, source_target_pairs={{0,2},{1,3},{2,6},{3,7},{6,4},{7,5},{4,0},{5,1},{8,10},{9,11},{10,... | collective-permute-start | bytes 4718600 | tf_op jit(solution)/shard_map/ppermute | solution.py:342
  464.3 14.0 %collective-permute-start.75 = (bf16[128,2048]{1,0:T(8,128)(2,1)}, bf16[128,2048]{1,0:T(8,128)(2,1)}, u32[]{:S(2)}, u32[]{:S(2)}) collective-permute-start(bf16[128,2048]{1,0:T(8,128)(2,1)} %fusion.6), channel_id=1, source_target_pairs={{1,17},{3,19},{5,21},{7,23},{9,25},{11,27},{13,29},{15,31},{16,0},... | collective-permute-start | bytes 1572872 | tf_op jit(solution)/shard_map/ppermute | solution.py:1217
  468.5 55.2 %all-to-all-start.1 = ((bf16[8,80,768]{2,1,0:T(8,128)(2,1)}), bf16[8,80,768]{2,1,0:T(8,128)(2,1)}, u32[]{:S(2)}, u32[]{:S(2)}) async-start(bf16[8,80,768]{2,1,0:T(8,128)(2,1)} %fusion.5), calls=%async_computation.1 | async-start | bytes 1966080 | tf_op jit(solution)/shard_map/all_to_all | solution.py:1167
  479.7 37.1 %collective-permute-start.76 = (bf16[64,2048]{1,0:T(8,128)(2,1)S(1)}, bf16[64,2048]{1,0:T(8,128)(2,1)S(1)}, u32[]{:S(2)}, u32[]{:S(2)}) collective-permute-start(bf16[64,2048]{1,0:T(8,128)(2,1)S(1)} %dynamic-slice_convert_fusion.1), channel_id=1, source_target_pairs={{0,1},{2,3},{4,5},{6,7},{8,9},{10,11},{12,13},{14,15},{17,16},{19,... | collective-permute-start | bytes 786440 | tf_op jit(solution)/shard_map/ppermute | solution.py:1226
  507.3 27.8 %collective-permute-start.71 = (bf16[256,2048]{1,0:T(8,128)(2,1)}, bf16[256,2048]{1,0:T(8,128)(2,1)}, u32[]{:S(2)}, u32[]{:S(2)}) collective-permute-start(bf16[256,2048]{1,0:T(8,128)(2,1)} %get-tuple-element.501), channel_id=1, source_target_pairs={{0,1},{1,0},{2,3},{3,2},{4,5},{5,4},{6,7},{7,6},{8,9},{9,8},{10,11... | collective-permute-start | bytes 3145736 | tf_op jit(solution)/shard_map/ppermute | solution.py:338
  511.7 31.5 %collective-permute-start.72 = (bf16[256,2048]{1,0:T(8,128)(2,1)}, bf16[256,2048]{1,0:T(8,128)(2,1)}, u32[]{:S(2)}, u32[]{:S(2)}) collective-permute-start(bf16[256,2048]{1,0:T(8,128)(2,1)} %mix.29), channel_id=1, source_target_pairs={{0,2},{1,3},{2,6},{3,7},{6,4},{7,5},{4,0},{5,1},{8,10},{9,11},{10,... | collective-permute-start | bytes 3145736 | tf_op jit(solution)/shard_map/ppermute | solution.py:342
  (214 other events, 2391.0 us)
Sparse Core Ops, SparseCore 0:
  81.2 29.1 all-gather.3
  111.9 30.9 all-gather.5
  144.5 31.6 all-gather.7
